TPU v7x, 32 devices: a whole 2x2x4 slice. The times are simulated.
32 devices in a mesh: lat: 4 (over y, core), lon: 8 (over z, x).
Axes of the slice: x: 2, y: 2, z: 4, core: 2. Of those that a mesh axis runs over, the one named last changes fastest.
Arguments:
- tendency: bfloat16 [2, 16, 512, 2048], P(None, None, 'lat', 'lon'), may hold values from -6 to 6
- thickness: float32 [16], replicated, may hold values from 0.03 to 0.3
- level_count: int32 [512, 2048], P('lat', 'lon'), may hold values from 0 to 16, as said below
- block_mask: int32 [32, 8], P('lat', 'lon'), may hold values from 0 to 1, as said below
- owner: int32 [32, 8], P('lat', 'lon'), may hold values from -1 to 7, as said below
- inertia: float32 [512, 2048], P('lat', 'lon'), may hold values from 0.2 to 2
Outputs:
- barotropic_forcing: float32 [4, 8, 8, 2, 16, 256], P('lat', 'lon')
- pressure: float32 [512, 2048], P('lat', 'lon')
- residual: float32 [512, 2048], P('lat', 'lon')
Inputs may be any that keep to these rules, and one draw needn't show every extreme that they name: `block_mask`: each latitude index holds exactly 48 ocean blocks among its 64. -1 exactly on land blocks; on ocean blocks the owner's longitude index within the same latitude index. A device's ocean blocks go to distinct owners, and every owner receives exactly 6 blocks. `level_count`: 0 exactly on the cells of land blocks, 1 to 16 on ocean cells; 16 is reached on every ocean block.
All inputs are finite; a program needn't handle non-finite values.
Results may differ from a plain program's by a relative error of at most 0.0003.
Values may be sent and summed in bfloat16 or wider, within the bound.
No kernel may reach another device: no remote copies, remote signals or barrier semaphores. Data moves between devices by JAX's collectives and lax.ppermute only.
A program may use at most 64 MiB of HBM per device.

v0:
```python
import jax
import jax.numpy as jnp
from jax import lax
from jax.sharding import PartitionSpec as P

ITERS = 4


OFFSETS = [(-1, -1), (-1, 0), (-1, 1), (0, -1), (0, 1), (1, -1), (1, 0), (1, 1)]
HIGH = lax.Precision.HIGHEST


def with_halo(block, sides, width):
    for axis, dim in sides:
        count = lax.axis_size(axis)
        forward = [(i, i + 1) for i in range(count - 1)]
        forward.append((count - 1, 0))
        backward = [(target, source) for source, target in forward]
        low = lax.ppermute(
            lax.slice_in_dim(block, block.shape[dim] - width, None, axis=dim), axis, forward
        )
        high = lax.ppermute(lax.slice_in_dim(block, 0, width, axis=dim), axis, backward)
        block = jnp.concatenate([low, block, high], axis=dim)
    return block


def close_ends(padded, axis):
    count = padded.shape[axis]
    where_lat = lax.axis_index("lat")
    first = where_lat == 0
    last = where_lat == lax.axis_size("lat") - 1
    positions = jnp.arange(count)
    keep = jnp.where((positions == 0) & first | (positions == count - 1) & last, 0.0, 1.0)
    shape = [1] * padded.ndim
    shape[axis] = count
    return padded * keep.reshape(shape)


def rim(field):
    padded = with_halo(field, (("lat", 0), ("lon", 1)), 1)
    return close_ends(padded, 0)


def neighbour(padded, row_step, col_step, total_rows, total_cols):
    return padded[
        1 + row_step : 1 + row_step + total_rows, 1 + col_step : 1 + col_step + total_cols
    ]


def operate(field, weights, inertia):
    total_rows, total_cols = field.shape
    padded = rim(field)
    result = inertia * field
    for weight_map, (row_step, col_step) in zip(weights, OFFSETS):
        result = result + weight_map * (
            field - neighbour(padded, row_step, col_step, total_rows, total_cols)
        )
    return result


def paired_sums(residual, scaled, image):
    return lax.psum((jnp.sum(residual * scaled), jnp.sum(scaled * image)), ("lat", "lon"))


def on_device(tendency, thickness, level_count, block_mask, owner, inertia):
    components, depth_levels, local_rows, local_cols = tendency.shape
    blocks_here = block_mask.shape[0]
    block_span = local_rows // blocks_here
    live = jnp.arange(depth_levels)[:, None, None] < level_count[None]
    masked = jnp.where(live[None], tendency, jnp.zeros((), jnp.bfloat16))
    column_depth = jnp.sum(jnp.where(live, thickness[:, None, None], 0.0), axis=0)
    lon_count = lax.axis_size("lon")
    select = (owner[:, 0][None, :] == jnp.arange(lon_count)[:, None]).astype(jnp.float32)
    pieces = masked.reshape(components, depth_levels, blocks_here, block_span, local_cols)
    outgoing = jnp.einsum(
        "dj,cljsx->dclsx", select.astype(jnp.bfloat16), pieces, preferred_element_type=jnp.float32
    ).astype(jnp.bfloat16)
    summed = jnp.einsum(
        "l,dclsx->dcsx",
        thickness,
        lax.all_to_all(outgoing, "lon", split_axis=0, concat_axis=0, tiled=True).astype(
            jnp.float32
        ),
        precision=HIGH,
    )
    returned = lax.all_to_all(summed, "lon", split_axis=0, concat_axis=0, tiled=True)
    forcing = jnp.einsum("dj,dcsx->cjsx", select, returned, precision=HIGH)
    forcing = forcing.reshape(components, local_rows, local_cols)
    barotropic_forcing = summed.reshape((1, 1) + summed.shape)
    padded = with_halo(forcing, (("lat", 1), ("lon", 2)), 1)
    padded = close_ends(padded, 1)
    ocean_rows = jnp.repeat(block_mask[:, 0].astype(jnp.float32), block_span)
    east_west = padded[0, 1:-1, 2:] - padded[0, 1:-1, :-2]
    north_south = padded[1, 2:, 1:-1] - padded[1, :-2, 1:-1]
    source = 0.5 * (east_west + north_south) * ocean_rows[:, None]
    depth_pad = rim(column_depth)
    weights = []
    for row_step, col_step in OFFSETS:
        factor = 1.0 if row_step * col_step == 0 else 0.5
        beside = neighbour(depth_pad, row_step, col_step, local_rows, local_cols)
        weights.append(0.5 * factor * (column_depth + beside))
    diag = inertia + sum(weights)
    pressure = jnp.zeros_like(source)
    residual = source
    scaled = residual / diag
    image = operate(scaled, weights, inertia)
    norm_now, product = paired_sums(residual, scaled, image)
    alpha = norm_now / product
    direction, along = (scaled, image)
    for iteration in range(ITERS):
        pressure = pressure + alpha * direction
        residual = residual - alpha * along
        if iteration + 1 < ITERS:
            scaled = residual / diag
            image = operate(scaled, weights, inertia)
            norm_next, product = paired_sums(residual, scaled, image)
            ratio = norm_next / norm_now
            alpha = norm_next / (product - ratio * norm_next / alpha)
            direction = scaled + ratio * direction
            along = image + ratio * along
            norm_now = norm_next
    return (barotropic_forcing, pressure, residual)


def solution(mesh):
    return jax.shard_map(
        on_device,
        mesh=mesh,
        in_specs=(
            P(None, None, "lat", "lon"),
            P(),
            P("lat", "lon"),
            P("lat", "lon"),
            P("lat", "lon"),
            P("lat", "lon"),
        ),
        out_specs=(P("lat", "lon", None, None, None, None), P("lat", "lon"), P("lat", "lon")),
        check_vma=False,
    )
```

profile of v0, /device:TPU:0, one launch (start us, length us, event | category | flops | bytes accessed | tf_op | source)
XLA Modules:
  0.0 318.2 jit_solution(10367695730303942632)
XLA Ops:
  0.6 1.2 iota_compare_fusion
  1.9 1.9 broadcast_select_fusion
  3.8 1.2 fusion.4
  5.0 1.8 copy.18
  6.8 7.4 %all-to-all-start = ((bf16[8,2,16,16,256]{4,3,2,1,0:T(8,128)(2,1)}), bf16[8,2,16,16,256]{4,3,2,1,0:T(8,128)(2,1)S(1)}, u32[]{:S(2)}, u32[]{:S(2)}) async-start(bf16[8,2,16,16,256]{4,3,2,1,0:T(8,128)(2,1)} %copy.18), calls=%async_computation | async-start | bytes 4194304 | tf_op jit(solution)/shard_map/all_to_all | solution.py:81
  14.2 0.3 select_reduce_fusion
  14.5 47.9 %all-to-all-done = bf16[8,2,16,16,256]{4,3,2,1,0:T(8,128)(2,1)S(1)} async-done(((bf16[8,2,16,16,256]{4,3,2,1,0:T(8,128)(2,1)}), bf16[8,2,16,16,256]{4,3,2,1,0:T(8,128)(2,1)S(1)}, u32[]{:S(2)}, u32[]{:S(2)}) %all-to-all-start) | async-done | bytes 2097184 | tf_op jit(solution)/shard_map/all_to_all | solution.py:81
  62.4 1.3 fusion
  63.7 0.7 copy.37
  64.4 3.6 %all-to-all-start.1 = ((f32[8,2,16,256]{3,2,1,0:T(8,128)}), f32[8,2,16,256]{3,2,1,0:T(8,128)S(1)}, u32[]{:S(2)}, u32[]{:S(2)}) async-start(f32[8,2,16,256]{3,2,1,0:T(8,128)} %bitcast.30), calls=%async_computation.1 | async-start | bytes 524288 | tf_op jit(solution)/shard_map/all_to_all | solution.py:86
  68.2 1.7 collective-permute-start.5
  70.0 1.1 collective-permute-done.4
  71.2 6.0 %all-to-all-done.1 = f32[8,2,16,256]{3,2,1,0:T(8,128)S(1)} async-done(((f32[8,2,16,256]{3,2,1,0:T(8,128)}), f32[8,2,16,256]{3,2,1,0:T(8,128)S(1)}, u32[]{:S(2)}, u32[]{:S(2)}) %all-to-all-start.1) | async-done | bytes 262176 | tf_op jit(solution)/shard_map/all_to_all | solution.py:86
  77.2 0.4 convolution_bitcast_fusion
  77.6 0.1 copy.20
  77.8 1.7 collective-permute-start.1
  79.6 1.5 collective-permute-start.6
  81.0 3.3 %collective-permute-start.7 = (f32[130,1]{1,0:T(8,128)S(1)}, f32[130,1]{1,0:T(8,128)S(1)}, u32[]{:S(2)}, u32[]{:S(2)}) collective-permute-start(f32[130,1]{1,0:T(8,128)S(1)} %get-tuple-element.61), channel_id=1, source_target_pairs={{1,0},{2,1},{3,2},{4,3},{5,4},{6,5},{7,6},{0,7},{9,8},{10,9},{11,1... | collective-permute-start | bytes 1568 | tf_op jit(solution)/shard_map/ppermute | solution.py:22
  84.4 0.1 fusion.107
  84.5 4.7 %collective-permute-start.3 = (f32[2,130,1]{2,1,0:T(8,128)S(1)}, f32[2,130,1]{2,1,0:T(8,128)S(1)}, u32[]{:S(2)}, u32[]{:S(2)}) collective-permute-start(f32[2,130,1]{2,1,0:T(8,128)S(1)} %get-tuple-element.47), channel_id=1, source_target_pairs={{1,0},{2,1},{3,2},{4,3},{5,4},{6,5},{7,6},{0,7},{9,8},{10,9},{11,1... | collective-permute-start | bytes 3128 | tf_op jit(solution)/shard_map/ppermute | solution.py:22
  89.3 0.2 maximum_multiply_fusion.1
  89.4 2.9 collective-permute-done.2
  92.3 0.5 collective-permute-done.3
  92.8 0.2 maximum_multiply_fusion
  93.1 0.4 fusion.97
  93.5 1.7 collective-permute-start.9
  95.2 1.2 collective-permute-done.8
  96.6 0.6 collective-permute-start.10
  97.2 4.2 %collective-permute-start.11 = (f32[130,1]{1,0:T(8,128)S(1)}, f32[130,1]{1,0:T(8,128)S(1)}, u32[]{:S(2)}, u32[]{:S(2)}) collective-permute-start(f32[130,1]{1,0:T(8,128)S(1)} %get-tuple-element.59), channel_id=1, source_target_pairs={{1,0},{2,1},{3,2},{4,3},{5,4},{6,5},{7,6},{0,7},{9,8},{10,9},{11,1... | collective-permute-start | bytes 1568 | tf_op jit(solution)/shard_map/ppermute | solution.py:22
  101.4 2.7 collective-permute-done.10
  104.1 0.2 maximum_multiply_fusion.2
  104.3 0.9 multiply_reduce_fusion.6
  105.1 40.0 %all-reduce.3 = (f32[]{:T(128)}, f32[]{:T(128)}) all-reduce(f32[]{:T(128)} %get-tuple-element.16, f32[]{:T(128)} %get-tuple-element.15), channel_id=1, replica_groups=mesh['lat'=4,'lon'=8] {'lat','lon'}, use_global_device_ids=true, to_apply=%region_2.3 | all-reduce | flops 2 | bytes 16 | tf_op jit(solution)/shard_map/psum | solution.py:62
  146.6 1.7 collective-permute-start.13
  148.3 1.2 collective-permute-done.12
  149.6 0.2 collective-permute-done.13
  149.9 2.2 collective-permute-start.14
  152.1 2.6 collective-permute-start.15
  154.7 2.4 collective-permute-done.14
  157.1 0.1 collective-permute-done.15
  157.2 0.2 maximum_multiply_fusion.3
  157.4 0.9 multiply_reduce_fusion.4
  158.3 41.2 %all-reduce.2 = (f32[]{:T(128)}, f32[]{:T(128)}) all-reduce(f32[]{:T(128)} %get-tuple-element.14, f32[]{:T(128)} %get-tuple-element.13), channel_id=1, replica_groups=mesh['lat'=4,'lon'=8] {'lat','lon'}, use_global_device_ids=true, to_apply=%region_6.7 | all-reduce | flops 2 | bytes 16 | tf_op jit(solution)/shard_map/psum | solution.py:62
  204.2 1.7 collective-permute-start.17
  205.9 1.2 collective-permute-done.16
  207.2 0.2 collective-permute-done.17
  207.5 2.1 collective-permute-start.18
  209.6 2.6 collective-permute-start.19
  212.3 2.4 collective-permute-done.18
  214.7 0.2 collective-permute-done.19
  214.9 0.2 maximum_multiply_fusion.4
  215.1 0.9 multiply_reduce_fusion.2
  215.9 40.8 %all-reduce.1 = (f32[]{:T(128)}, f32[]{:T(128)}) all-reduce(f32[]{:T(128)} %get-tuple-element.12, f32[]{:T(128)} %get-tuple-element.11), channel_id=1, replica_groups=mesh['lat'=4,'lon'=8] {'lat','lon'}, use_global_device_ids=true, to_apply=%region_10.11 | all-reduce | flops 2 | bytes 16 | tf_op jit(solution)/shard_map/psum | solution.py:62
  260.8 1.7 collective-permute-start.21
  262.5 1.2 collective-permute-done.20
  263.8 0.2 collective-permute-done.21
  264.1 2.2 collective-permute-start.22
  266.2 2.6 collective-permute-start.23
  268.9 2.4 collective-permute-done.22
  271.2 0.1 collective-permute-done.23
  271.4 0.2 maximum_multiply_fusion.5
  271.6 0.9 multiply_reduce_fusion
  272.5 41.2 %all-reduce = (f32[]{:T(128)}, f32[]{:T(128)}) all-reduce(f32[]{:T(128)} %get-tuple-element.10, f32[]{:T(128)} %get-tuple-element.9), channel_id=1, replica_groups=mesh['lat'=4,'lon'=8] {'lat','lon'}, use_global_device_ids=true, to_apply=%region_14.15 | all-reduce | flops 2 | bytes 16 | tf_op jit(solution)/shard_map/psum | solution.py:62
  317.4 0.8 multiply_subtract_fusion
  (48 shorter events, 1.4 us)
Async XLA Ops:
  1.8 1.9 copy-start.3
  6.8 7.4 %copy-start.1 = (s32[128,256]{1,0:T(8,128)S(1)}, s32[128,256]{1,0:T(8,128)}, u32[]{:S(2)}) copy-start(s32[128,256]{1,0:T(8,128)} %param.8) | copy-start | bytes 393220
  6.8 7.4 %copy-start.2 = (f32[16]{0:T(128)S(1)}, f32[16]{0:T(128)}, u32[]{:S(2)}) copy-start(f32[16]{0:T(128)} %param.7) | copy-start | bytes 196
  6.8 55.6 %all-to-all-start = ((bf16[8,2,16,16,256]{4,3,2,1,0:T(8,128)(2,1)}), bf16[8,2,16,16,256]{4,3,2,1,0:T(8,128)(2,1)S(1)}, u32[]{:S(2)}, u32[]{:S(2)}) async-start(bf16[8,2,16,16,256]{4,3,2,1,0:T(8,128)(2,1)} %copy.18), calls=%async_computation | async-start | bytes 4194304 | tf_op jit(solution)/shard_map/all_to_all | solution.py:81
  14.2 55.7 %copy-start.4 = (s32[8,1]{0,1:T(1,128)S(1)}, s32[8,1]{0,1:T(1,128)}, u32[]{:S(2)}) copy-start(s32[8,1]{0,1:T(1,128)} %param.9) | copy-start | bytes 100
  64.4 12.7 %all-to-all-start.1 = ((f32[8,2,16,256]{3,2,1,0:T(8,128)}), f32[8,2,16,256]{3,2,1,0:T(8,128)S(1)}, u32[]{:S(2)}, u32[]{:S(2)}) async-start(f32[8,2,16,256]{3,2,1,0:T(8,128)} %bitcast.30), calls=%async_computation.1 | async-start | bytes 524288 | tf_op jit(solution)/shard_map/all_to_all | solution.py:86
  68.1 3.0 collective-permute-start.4
  68.1 24.9 %copy-start = (f32[128,256]{1,0:T(8,128)S(1)}, f32[128,256]{1,0:T(8,128)}, u32[]{:S(2)}) copy-start(f32[128,256]{1,0:T(8,128)} %param.11) | copy-start | bytes 393220
  68.2 3.0 collective-permute-start.5
  77.7 6.7 %collective-permute-start = (f32[2,1,256]{2,1,0:T(1,128)S(1)}, f32[2,1,256]{2,1,0:T(1,128)S(1)}, u32[]{:S(2)}, u32[]{:S(2)}) collective-permute-start(f32[2,1,256]{2,1,0:T(1,128)S(1)} %get-tuple-element.48), channel_id=1, source_target_pairs={{0,8},{8,16},{16,24},{24,0},{1,9},{9,17},{17,25},{25,1},{2,10},{10... | collective-permute-start | bytes 6152 | tf_op jit(solution)/shard_map/ppermute | solution.py:19
  77.8 6.6 %collective-permute-start.1 = (f32[2,1,256]{2,1,0:T(1,128)S(1)}, f32[2,1,256]{2,1,0:T(1,128)S(1)}, u32[]{:S(2)}, u32[]{:S(2)}) collective-permute-start(f32[2,1,256]{2,1,0:T(1,128)S(1)} %get-tuple-element.49), channel_id=1, source_target_pairs={{8,0},{16,8},{24,16},{0,24},{9,1},{17,9},{25,17},{1,25},{10,2},{18... | collective-permute-start | bytes 6152 | tf_op jit(solution)/shard_map/ppermute | solution.py:22
  79.6 9.7 %collective-permute-start.6 = (f32[130,1]{1,0:T(8,128)S(1)}, f32[130,1]{1,0:T(8,128)S(1)}, u32[]{:S(2)}, u32[]{:S(2)}) collective-permute-start(f32[130,1]{1,0:T(8,128)S(1)} %get-tuple-element.60), channel_id=1, source_target_pairs={{0,1},{1,2},{2,3},{3,4},{4,5},{5,6},{6,7},{7,0},{8,9},{9,10},{10,1... | collective-permute-start | bytes 1568 | tf_op jit(solution)/shard_map/ppermute | solution.py:19
  81.0 8.2 %collective-permute-start.7 = (f32[130,1]{1,0:T(8,128)S(1)}, f32[130,1]{1,0:T(8,128)S(1)}, u32[]{:S(2)}, u32[]{:S(2)}) collective-permute-start(f32[130,1]{1,0:T(8,128)S(1)} %get-tuple-element.61), channel_id=1, source_target_pairs={{1,0},{2,1},{3,2},{4,3},{5,4},{6,5},{7,6},{0,7},{9,8},{10,9},{11,1... | collective-permute-start | bytes 1568 | tf_op jit(solution)/shard_map/ppermute | solution.py:22
  84.5 7.9 %collective-permute-start.2 = (f32[2,130,1]{2,1,0:T(8,128)S(1)}, f32[2,130,1]{2,1,0:T(8,128)S(1)}, u32[]{:S(2)}, u32[]{:S(2)}) collective-permute-start(f32[2,130,1]{2,1,0:T(8,128)S(1)} %get-tuple-element.46), channel_id=1, source_target_pairs={{0,1},{1,2},{2,3},{3,4},{4,5},{5,6},{6,7},{7,0},{8,9},{9,10},{10,1... | collective-permute-start | bytes 3128 | tf_op jit(solution)/shard_map/ppermute | solution.py:19
  84.5 8.3 %collective-permute-start.3 = (f32[2,130,1]{2,1,0:T(8,128)S(1)}, f32[2,130,1]{2,1,0:T(8,128)S(1)}, u32[]{:S(2)}, u32[]{:S(2)}) collective-permute-start(f32[2,130,1]{2,1,0:T(8,128)S(1)} %get-tuple-element.47), channel_id=1, source_target_pairs={{1,0},{2,1},{3,2},{4,3},{5,4},{6,5},{7,6},{0,7},{9,8},{10,9},{11,1... | collective-permute-start | bytes 3128 | tf_op jit(solution)/shard_map/ppermute | solution.py:22
  93.5 3.0 collective-permute-start.8
  93.5 3.0 collective-permute-start.9
  96.6 7.5 %collective-permute-start.10 = (f32[130,1]{1,0:T(8,128)S(1)}, f32[130,1]{1,0:T(8,128)S(1)}, u32[]{:S(2)}, u32[]{:S(2)}) collective-permute-start(f32[130,1]{1,0:T(8,128)S(1)} %get-tuple-element.58), channel_id=1, source_target_pairs={{0,1},{1,2},{2,3},{3,4},{4,5},{5,6},{6,7},{7,0},{8,9},{9,10},{10,1... | collective-permute-start | bytes 1568 | tf_op jit(solution)/shard_map/ppermute | solution.py:19
  97.2 6.9 %collective-permute-start.11 = (f32[130,1]{1,0:T(8,128)S(1)}, f32[130,1]{1,0:T(8,128)S(1)}, u32[]{:S(2)}, u32[]{:S(2)}) collective-permute-start(f32[130,1]{1,0:T(8,128)S(1)} %get-tuple-element.59), channel_id=1, source_target_pairs={{1,0},{2,1},{3,2},{4,3},{5,4},{6,5},{7,6},{0,7},{9,8},{10,9},{11,1... | collective-permute-start | bytes 1568 | tf_op jit(solution)/shard_map/ppermute | solution.py:22
  146.6 3.0 collective-permute-start.12
  146.6 3.2 %collective-permute-start.13 = (f32[1,256]{1,0:T(1,128)S(1)}, f32[1,256]{1,0:T(1,128)S(1)}, u32[]{:S(2)}, u32[]{:S(2)}) collective-permute-start(f32[1,256]{1,0:T(1,128)S(1)} %get-tuple-element.67), channel_id=1, source_target_pairs={{8,0},{16,8},{24,16},{0,24},{9,1},{17,9},{25,17},{1,25},{10,2},{18... | collective-permute-start | bytes 3080 | tf_op jit(solution)/shard_map/ppermute | solution.py:22
  149.9 7.2 %collective-permute-start.14 = (f32[130,1]{1,0:T(8,128)S(1)}, f32[130,1]{1,0:T(8,128)S(1)}, u32[]{:S(2)}, u32[]{:S(2)}) collective-permute-start(f32[130,1]{1,0:T(8,128)S(1)} %get-tuple-element.56), channel_id=1, source_target_pairs={{0,1},{1,2},{2,3},{3,4},{4,5},{5,6},{6,7},{7,0},{8,9},{9,10},{10,1... | collective-permute-start | bytes 1568 | tf_op jit(solution)/shard_map/ppermute | solution.py:19
  152.1 5.1 %collective-permute-start.15 = (f32[130,1]{1,0:T(8,128)S(1)}, f32[130,1]{1,0:T(8,128)S(1)}, u32[]{:S(2)}, u32[]{:S(2)}) collective-permute-start(f32[130,1]{1,0:T(8,128)S(1)} %get-tuple-element.57), channel_id=1, source_target_pairs={{1,0},{2,1},{3,2},{4,3},{5,4},{6,5},{7,6},{0,7},{9,8},{10,9},{11,1... | collective-permute-start | bytes 1568 | tf_op jit(solution)/shard_map/ppermute | solution.py:22
  204.1 3.0 collective-permute-start.16
  204.2 3.2 %collective-permute-start.17 = (f32[1,256]{1,0:T(1,128)S(1)}, f32[1,256]{1,0:T(1,128)S(1)}, u32[]{:S(2)}, u32[]{:S(2)}) collective-permute-start(f32[1,256]{1,0:T(1,128)S(1)} %get-tuple-element.65), channel_id=1, source_target_pairs={{8,0},{16,8},{24,16},{0,24},{9,1},{17,9},{25,17},{1,25},{10,2},{18... | collective-permute-start | bytes 3080 | tf_op jit(solution)/shard_map/ppermute | solution.py:22
  207.5 7.2 %collective-permute-start.18 = (f32[130,1]{1,0:T(8,128)S(1)}, f32[130,1]{1,0:T(8,128)S(1)}, u32[]{:S(2)}, u32[]{:S(2)}) collective-permute-start(f32[130,1]{1,0:T(8,128)S(1)} %get-tuple-element.54), channel_id=1, source_target_pairs={{0,1},{1,2},{2,3},{3,4},{4,5},{5,6},{6,7},{7,0},{8,9},{9,10},{10,1... | collective-permute-start | bytes 1568 | tf_op jit(solution)/shard_map/ppermute | solution.py:19
  209.6 5.3 %collective-permute-start.19 = (f32[130,1]{1,0:T(8,128)S(1)}, f32[130,1]{1,0:T(8,128)S(1)}, u32[]{:S(2)}, u32[]{:S(2)}) collective-permute-start(f32[130,1]{1,0:T(8,128)S(1)} %get-tuple-element.55), channel_id=1, source_target_pairs={{1,0},{2,1},{3,2},{4,3},{5,4},{6,5},{7,6},{0,7},{9,8},{10,9},{11,1... | collective-permute-start | bytes 1568 | tf_op jit(solution)/shard_map/ppermute | solution.py:22
  260.7 3.0 collective-permute-start.20
  260.8 3.2 %collective-permute-start.21 = (f32[1,256]{1,0:T(1,128)S(1)}, f32[1,256]{1,0:T(1,128)S(1)}, u32[]{:S(2)}, u32[]{:S(2)}) collective-permute-start(f32[1,256]{1,0:T(1,128)S(1)} %get-tuple-element.63), channel_id=1, source_target_pairs={{8,0},{16,8},{24,16},{0,24},{9,1},{17,9},{25,17},{1,25},{10,2},{18... | collective-permute-start | bytes 3080 | tf_op jit(solution)/shard_map/ppermute | solution.py:22
  264.1 7.2 %collective-permute-start.22 = (f32[130,1]{1,0:T(8,128)S(1)}, f32[130,1]{1,0:T(8,128)S(1)}, u32[]{:S(2)}, u32[]{:S(2)}) collective-permute-start(f32[130,1]{1,0:T(8,128)S(1)} %get-tuple-element.52), channel_id=1, source_target_pairs={{0,1},{1,2},{2,3},{3,4},{4,5},{5,6},{6,7},{7,0},{8,9},{9,10},{10,1... | collective-permute-start | bytes 1568 | tf_op jit(solution)/shard_map/ppermute | solution.py:19
  266.2 5.1 %collective-permute-start.23 = (f32[130,1]{1,0:T(8,128)S(1)}, f32[130,1]{1,0:T(8,128)S(1)}, u32[]{:S(2)}, u32[]{:S(2)}) collective-permute-start(f32[130,1]{1,0:T(8,128)S(1)} %get-tuple-element.53), channel_id=1, source_target_pairs={{1,0},{2,1},{3,2},{4,3},{5,4},{6,5},{7,6},{0,7},{9,8},{10,9},{11,1... | collective-permute-start | bytes 1568 | tf_op jit(solution)/shard_map/ppermute | solution.py:22
where the time goes:
time: 319 us; the launch traced here: 318 us
  blocking collectives  163 us (51%)
  waiting for transfers between devices  74.5 us (23%)
  starting transfers between devices  50.4 us (16%)
  between operations  14.5 us (5%)
  other arithmetic  9.45 us (3%)
  local copies, waits for them, and re-layouts  3.3 us (1%)
    psum x4, blocking collectives, paired_sums(): lax.psum((jnp.sum(residual * scaled), jnp.sum(scaled * image)), ('lat', '...  163 us
    all_to_all x1, waiting for transfers between devices, on_device(): lax.all_to_all(outgoing, 'lon', split_axis=0, concat_axis=0, tiled=True)  47.9 us
    ppermute x12, starting transfers between devices, with_halo(): lax.ppermute(lax.slice_in_dim(block, 0, width, axis=dim), axis, backward)  30.5 us
    ppermute x12, waiting for transfers between devices, with_halo(): lax.ppermute(lax.slice_in_dim(block, block.shape[dim] - width, None, axis...  18.8 us
    ppermute x12, starting transfers between devices, with_halo(): lax.ppermute(lax.slice_in_dim(block, block.shape[dim] - width, None, axis...  8.89 us
    all_to_all x1, starting transfers between devices, on_device(): lax.all_to_all(outgoing, 'lon', split_axis=0, concat_axis=0, tiled=True)  7.38 us
  transfers between devices with their start and end apart: 26, of which 21 were waited for; matrix products, arithmetic and copies ran while one was open for 0% of the time, Pallas kernels for 0%

commit v1 on v0

v1 whole, which is shorter than its diff:
```python
import functools

import jax
import jax.numpy as jnp
from jax import lax
from jax.experimental import pallas as pl
from jax.experimental.pallas import tpu as pltpu
from jax.sharding import PartitionSpec as P

STEPS = 4
RIM = STEPS + 1
ROWS = 8
LANES = 128
CHUNK = 32
FIELDS = 4
SUMS = 16
VMEM_BYTES = 16 * 1024 * 1024


def integrate_kernel(
    thick_ref, owner_ref, count_ref, inertia_ref, tend_ref, fields_ref, head_ref, tail_ref, sent_ref
):
    step = pl.program_id(0)
    levels = tend_ref.shape[1]
    chunk = count_ref.shape[0]
    span = sent_ref.shape[2]
    count = count_ref[...]
    first = jnp.zeros(count.shape, jnp.float32)
    second = jnp.zeros(count.shape, jnp.float32)
    depth = jnp.zeros(count.shape, jnp.float32)
    for level in range(levels):
        layer = jnp.where(count > level, thick_ref[level], 0.0)
        depth = depth + layer
        first = first + layer * tend_ref[0, level].astype(jnp.float32)
        second = second + layer * tend_ref[1, level].astype(jnp.float32)
    inertia = inertia_ref[...]
    for place, values in enumerate((first, second, depth, inertia)):
        fields_ref[place] = values

    @pl.when(step == 0)
    def _():
        sent_ref[...] = jnp.zeros(sent_ref.shape, jnp.float32)
        for place, values in enumerate((first, second, depth, inertia)):
            head_ref[place] = values[:ROWS]

    @pl.when(step == pl.num_programs(0) - 1)
    def _():
        for place, values in enumerate((first, second, depth, inertia)):
            tail_ref[place] = values[chunk - ROWS :]

    for part in range(chunk // span):
        target = owner_ref[step * (chunk // span) + part]

        @pl.when(target >= 0)
        def _(target=target, part=part):
            rows = slice(part * span, (part + 1) * span)
            sent_ref[target, 0] = first[rows]
            sent_ref[target, 1] = second[rows]


def integrate(tendency, thickness, level_count, owner, inertia, lon_count):
    components, levels, rows, cols = tendency.shape
    span = rows // owner.shape[0]
    chunk = max(CHUNK, span)
    whole = lambda step: (0, 0, 0)
    f32 = jnp.float32
    return pl.pallas_call(
        integrate_kernel,
        grid=(rows // chunk,),
        in_specs=[
            pl.BlockSpec(memory_space=pltpu.SMEM),
            pl.BlockSpec(memory_space=pltpu.SMEM),
            pl.BlockSpec((chunk, cols), lambda step: (step, 0)),
            pl.BlockSpec((chunk, cols), lambda step: (step, 0)),
            pl.BlockSpec((components, levels, chunk, cols), lambda step: (0, 0, step, 0)),
        ],
        out_specs=[
            pl.BlockSpec((FIELDS, chunk, cols), lambda step: (0, step, 0)),
            pl.BlockSpec((FIELDS, ROWS, cols), whole),
            pl.BlockSpec((FIELDS, ROWS, cols), whole),
            pl.BlockSpec((lon_count, components, span, cols), lambda step: (0, 0, 0, 0)),
        ],
        out_shape=[
            jax.ShapeDtypeStruct((FIELDS, rows, cols), f32),
            jax.ShapeDtypeStruct((FIELDS, ROWS, cols), f32),
            jax.ShapeDtypeStruct((FIELDS, ROWS, cols), f32),
            jax.ShapeDtypeStruct((lon_count, components, span, cols), f32),
        ],
        compiler_params=pltpu.CompilerParams(vmem_limit_bytes=VMEM_BYTES),
        cost_estimate=pl.CostEstimate(
            flops=6 * components * levels * rows * cols,
            bytes_accessed=2 * components * levels * rows * cols,
            transcendentals=0,
        ),
        name="integrate",
    )(thickness, owner, level_count, inertia, tendency)


def edges_kernel(fields_ref, north_ref, south_ref, out_ref):
    rows = fields_ref.shape[1]
    cols = fields_ref.shape[2]
    half = LANES // 2
    for top, size, ref in ((0, ROWS, north_ref), (ROWS, rows, fields_ref), (ROWS + rows, ROWS, south_ref)):
        lane = lax.broadcasted_iota(jnp.int32, (size, LANES), 1)
        packed = jnp.zeros((size, LANES), jnp.float32)
        for place in range(FIELDS):
            west = ref[place, :, :LANES]
            east = ref[place, :, cols - LANES :]
            at = place * RIM
            west = pltpu.roll(west, at, 1) if at else west
            packed = jnp.where((lane >= at) & (lane < at + RIM), west, packed)
            at = half + place * RIM
            east = pltpu.roll(east, (at + RIM) % LANES, 1)
            packed = jnp.where((lane >= at) & (lane < at + RIM), east, packed)
        out_ref[top : top + size] = packed


def edges(fields, north, south):
    rows = fields.shape[1] + 2 * ROWS
    return pl.pallas_call(
        edges_kernel,
        out_shape=jax.ShapeDtypeStruct((rows, LANES), jnp.float32),
        compiler_params=pltpu.CompilerParams(vmem_limit_bytes=VMEM_BYTES),
        name="edges",
    )(fields, north, south)


def smooth(field):
    rows, cols = field.shape
    tall = field + 0.5 * (pltpu.roll(field, 1, 0) + pltpu.roll(field, rows - 1, 0))
    return tall + 0.5 * (pltpu.roll(tall, 1, 1) + pltpu.roll(tall, cols - 1, 1))


def krylov_kernel(fields_ref, north_ref, south_ref, east_ref, west_ref, w_ref, mw_ref, sums_ref):
    rows = fields_ref.shape[1]
    cols = fields_ref.shape[2]
    tall = rows + 2 * ROWS
    wide = cols + LANES
    half = LANES // 2
    lane = lax.broadcasted_iota(jnp.int32, (tall, LANES), 1)
    from_east = east_ref[...]
    from_west = west_ref[...]
    padded = []
    for place in range(FIELDS):
        middle = jnp.concatenate([north_ref[place], fields_ref[place], south_ref[place]], axis=0)
        at = place * RIM
        high = pltpu.roll(from_east, LANES - at, 1) if at else from_east
        low = pltpu.roll(from_west, half - RIM - at, 1)
        side = jnp.where(lane < RIM, high, jnp.where(lane >= LANES - RIM, low, 0.0))
        padded.append(jnp.concatenate([middle, side], axis=1))
    first, second, depth, inertia = padded
    inside = inertia > 0.0
    east_west = pltpu.roll(first, wide - 1, 1) - pltpu.roll(first, 1, 1)
    north_south = pltpu.roll(second, tall - 1, 0) - pltpu.roll(second, 1, 0)
    source = jnp.where(depth > 0.0, 0.5 * (east_west + north_south), 0.0)
    diag = inertia + 2.0 * depth + smooth(depth)
    inverse = jnp.where(inside, 1.0 / jnp.where(inside, diag, 1.0), 0.0)
    own = (slice(ROWS, ROWS + rows), slice(0, cols))
    scaled = source
    mws = [scaled[own]]
    ws = []
    vector = scaled * inverse
    for step in range(STEPS):
        ws.append(vector[own])
        weighed = depth * vector
        scaled = depth * smooth(vector) + smooth(weighed) - 2.0 * weighed
        mws.append(scaled[own])
        vector = scaled * inverse
    for place, values in enumerate(ws):
        w_ref[place] = values
    for place, values in enumerate(mws):
        mw_ref[place] = values
    images = [mws[place] - mws[place + 1] for place in range(STEPS)]
    pairs = [ws[place] * mws[0] for place in range(STEPS)]
    for low in range(STEPS):
        for high in range(low, STEPS):
            pairs.append(ws[low] * images[high])
    sums_ref[...] = jnp.zeros(sums_ref.shape, jnp.float32)
    for place, product in enumerate(pairs):
        line = jnp.sum(product, axis=0, keepdims=True)
        total = line[:, :LANES]
        for start in range(LANES, cols, LANES):
            total = total + line[:, start : start + LANES]
        sums_ref[place : place + 1, :] = total


def krylov(fields, north, south, east, west):
    _, rows, cols = fields.shape
    f32 = jnp.float32
    return pl.pallas_call(
        krylov_kernel,
        out_shape=[
            jax.ShapeDtypeStruct((STEPS, rows, cols), f32),
            jax.ShapeDtypeStruct((STEPS + 1, rows, cols), f32),
            jax.ShapeDtypeStruct((SUMS, LANES), f32),
        ],
        compiler_params=pltpu.CompilerParams(vmem_limit_bytes=VMEM_BYTES),
        name="krylov",
    )(fields, north, south, east, west)


def combine_kernel(sums_ref, w_ref, mw_ref, pressure_ref, residual_ref):
    totals = jnp.sum(sums_ref[...], axis=1, keepdims=True)
    entry = lambda place: totals[place : place + 1, :]
    right = [entry(place) for place in range(STEPS)]
    matrix = {}
    place = STEPS
    for low in range(STEPS):
        for high in range(low, STEPS):
            matrix[low, high] = entry(place)
            place += 1
    for pivot in range(STEPS):
        inverse = 1.0 / matrix[pivot, pivot]
        for row in range(pivot + 1, STEPS):
            factor = matrix[pivot, row] * inverse
            for col in range(row, STEPS):
                matrix[row, col] = matrix[row, col] - factor * matrix[pivot, col]
            right[row] = right[row] - factor * right[pivot]
        matrix[pivot, pivot] = inverse
    for pivot in reversed(range(STEPS)):
        for col in range(pivot + 1, STEPS):
            right[pivot] = right[pivot] - matrix[pivot, col] * right[col]
        right[pivot] = right[pivot] * matrix[pivot, pivot]
    pressure = right[0] * w_ref[0]
    residual = mw_ref[0] - right[0] * (mw_ref[0] - mw_ref[1])
    for place in range(1, STEPS):
        pressure = pressure + right[place] * w_ref[place]
        residual = residual - right[place] * (mw_ref[place] - mw_ref[place + 1])
    pressure_ref[...] = pressure
    residual_ref[...] = residual


def combine(sums, w, mw):
    shape = jax.ShapeDtypeStruct(w.shape[1:], jnp.float32)
    return pl.pallas_call(
        combine_kernel,
        out_shape=[shape, shape],
        compiler_params=pltpu.CompilerParams(vmem_limit_bytes=VMEM_BYTES),
        name="combine",
    )(sums, w, mw)


def total_over(values, axis):
    count = lax.axis_size(axis)
    if count & (count - 1):
        return lax.psum(values, axis)
    shift = 1
    while shift < count:
        pairs = [(place, place ^ shift) for place in range(count)]
        values = values + lax.ppermute(values, axis, pairs)
        shift *= 2
    return values


def on_device(tendency, thickness, level_count, block_mask, owner, inertia):
    lat_count = lax.axis_size("lat")
    lon_count = lax.axis_size("lon")
    fields, head, tail, sent = integrate(
        tendency, thickness, level_count, owner[:, 0], inertia, lon_count
    )
    south_pairs = [(place, place + 1) for place in range(lat_count - 1)]
    north_pairs = [(place + 1, place) for place in range(lat_count - 1)]
    north = lax.ppermute(tail, "lat", south_pairs)
    south = lax.ppermute(head, "lat", north_pairs)
    packed = edges(fields, north, south)
    east = lax.ppermute(packed, "lon", [((p + 1) % lon_count, p) for p in range(lon_count)])
    west = lax.ppermute(packed, "lon", [(p, (p + 1) % lon_count) for p in range(lon_count)])
    held = lax.all_to_all(sent, "lon", split_axis=0, concat_axis=0, tiled=True)
    w, mw, sums = krylov(fields, north, south, east, west)
    sums = total_over(total_over(sums, "lat"), "lon")
    pressure, residual = combine(sums, w, mw)
    return (held.reshape((1, 1) + held.shape), pressure, residual)


def solution(mesh):
    return jax.shard_map(
        on_device,
        mesh=mesh,
        in_specs=(
            P(None, None, "lat", "lon"),
            P(),
            P("lat", "lon"),
            P("lat", "lon"),
            P("lat", "lon"),
            P("lat", "lon"),
        ),
        out_specs=(P("lat", "lon", None, None, None, None), P("lat", "lon"), P("lat", "lon")),
        check_vma=False,
    )
```

time: 319 us -> 50.5 us (0.16)
  blocking collectives: 163 us -> 0 us
  waiting for transfers between devices: 74.5 us -> 17.4 us
  starting transfers between devices: 50.4 us -> 21.2 us
  between operations: 14.5 us -> 0.69 us
  other arithmetic: 9.45 us -> 0.02 us
  Pallas kernels: 0 us -> 5.44 us
    psum x4 -> x0, blocking collectives: 163 us -> none  [paired_sums(): lax.psum((jnp.sum(residual * scaled), jnp.sum(scaled * image)), ('lat', '...]
    all_to_all x2 -> x1, waiting for transfers between devices: 53.9 us -> 0.01 us  [on_device(): held = lax.all_to_all(sent, 'lon', split_axis=0, concat_axis=0, tiled=True)]
    ppermute x24 -> x9, starting transfers between devices: 39.4 us -> 14 us  [the longest x5 6.4 us: total_over(): values = values + lax.ppermute(values, axis, pairs)]
    pallas_call x0 -> x4, Pallas kernels: none -> 5.44 us  [the longest x1 2.26 us: integrate(): pl.pallas_call(integrate_kernel, grid=(rows // chunk,), in_specs=[pl.Bloc...]
    unnamed x10 -> x11, local copies, waits for them, and re-layouts: 0.03 us -> 5.4 us
    reduce_sum x5 -> x0, other arithmetic: 3.85 us -> none  [the longest x4 3.58 us: paired_sums(): jnp.sum(scaled * image)]
    all_to_all x2 -> x1, starting transfers between devices: 11 us -> 7.25 us  [on_device(): held = lax.all_to_all(sent, 'lon', split_axis=0, concat_axis=0, tiled=True)]
    ppermute x24 -> x9, waiting for transfers between devices: 20.6 us -> 17.4 us  [the longest x5 11.7 us: total_over(): values = values + lax.ppermute(values, axis, pairs)]
  transfers between devices with their start and end apart: 26 -> 10, of which waited for: 21 -> 7; matrix products, arithmetic and copies ran while one was open for 0% -> 0% of each run, Pallas kernels for 0% -> 6%
where the time goes in v1:
time: 50.5 us; the launch traced here: 50.2 us
  starting transfers between devices  21.2 us (42%)
  waiting for transfers between devices  17.4 us (34%)
  Pallas kernels  5.44 us (11%)
  local copies, waits for them, and re-layouts  5.4 us (11%)
  between operations  0.69 us (1%)
    ppermute x5, waiting for transfers between devices, total_over(): values = values + lax.ppermute(values, axis, pairs)  11.7 us
    all_to_all x1, starting transfers between devices, on_device(): held = lax.all_to_all(sent, 'lon', split_axis=0, concat_axis=0, tiled=True)  7.25 us
    ppermute x5, starting transfers between devices, total_over(): values = values + lax.ppermute(values, axis, pairs)  6.4 us
    unnamed x11, local copies, waits for them, and re-layouts  5.4 us
    ppermute x1, waiting for transfers between devices, on_device(): south = lax.ppermute(head, 'lat', north_pairs)  3.38 us
    ppermute x1, starting transfers between devices, on_device(): lax.ppermute(packed, 'lon', [((p + 1) % lon_count, p) for p in range(lon_...  2.77 us
    ppermute x1, waiting for transfers between devices, on_device(): lax.ppermute(packed, 'lon', [(p, (p + 1) % lon_count) for p in range(lon_...  2.37 us
    pallas_call x1, Pallas kernels, integrate(): pl.pallas_call(integrate_kernel, grid=(rows // chunk,), in_specs=[pl.Bloc...  2.26 us
  transfers between devices with their start and end apart: 10, of which 7 were waited for; matrix products, arithmetic and copies ran while one was open for 0% of the time, Pallas kernels for 6%

profile of v1, /device:TPU:0, one launch (start us, length us, event | category | flops | bytes accessed | tf_op | source)
XLA Modules:
  0.0 50.2 jit_solution(3082910950483593824)
XLA Ops:
  0.6 0.0 copy-start
  0.6 1.6 %copy-done = bf16[2,16,128,256]{3,2,1,0:T(8,128)(2,1)S(1)} copy-done((bf16[2,16,128,256]{3,2,1,0:T(8,128)(2,1)S(1)}, bf16[2,16,128,256]{3,2,1,0:T(8,128)(2,1)}, u32[]{:S(2)}) %copy-start) | copy-done | bytes 2097176
  2.2 0.0 copy-start.1
  2.2 0.9 %copy-done.1 = s32[128,256]{1,0:T(8,128)S(1)} copy-done((s32[128,256]{1,0:T(8,128)S(1)}, s32[128,256]{1,0:T(8,128)}, u32[]{:S(2)}) %copy-start.1) | copy-done | bytes 131096
  3.1 0.0 copy-start.2
  3.1 0.9 %copy-done.2 = f32[128,256]{1,0:T(8,128)S(1)} copy-done((f32[128,256]{1,0:T(8,128)S(1)}, f32[128,256]{1,0:T(8,128)}, u32[]{:S(2)}) %copy-start.2) | copy-done | bytes 131096
  4.0 0.0 copy-start.3
  4.0 0.7 %copy-done.3 = f32[16]{0:T(128)S(1)} copy-done((f32[16]{0:T(128)S(1)}, f32[16]{0:T(128)}, u32[]{:S(2)}) %copy-start.3) | copy-done | bytes 88
  4.7 0.0 copy-start.4
  4.7 0.7 %copy-done.4 = s32[8,1]{0,1:T(1,128)S(1)} copy-done((s32[8,1]{0,1:T(1,128)S(1)}, s32[8,1]{0,1:T(1,128)}, u32[]{:S(2)}) %copy-start.4) | copy-done | bytes 56
  5.3 2.3 %integrate.1 = (f32[4,128,256]{2,1,0:T(8,128)S(1)}, f32[4,8,256]{2,1,0:T(8,128)S(1)}, f32[4,8,256]{2,1,0:T(8,128)S(1)}, f32[8,2,16,256]{3,2,1,0:T(8,128)}) custom-call(f32[16]{0:T(128)S(1)} %copy-done.3, s32[8]{0:T(128)S(1)} %bitcast.2, s32[128,256]{1,0:T(8,128)S(1)} %copy-done.1, f32[128,256]{1,0:T(8,128)S(1)} %copy-done.2, ...), custom_call_target="tpu_custom_call" | custom-call | flops 6291456 | bytes 2097152 | tf_op jit(solution)/shard_map/integrate/pallas_call | solution.py:67
  7.6 7.3 %all-to-all-start = ((f32[8,2,16,256]{3,2,1,0:T(8,128)}), f32[8,2,16,256]{3,2,1,0:T(8,128)S(1)}, u32[]{:S(2)}, u32[]{:S(2)}) async-start(f32[8,2,16,256]{3,2,1,0:T(8,128)} %get-tuple-element.12), calls=%async_computation | async-start | bytes 524288 | tf_op jit(solution)/shard_map/all_to_all | solution.py:268
  14.9 1.4 %collective-permute-start = (f32[4,8,256]{2,1,0:T(8,128)S(1)}, f32[4,8,256]{2,1,0:T(8,128)S(1)}, u32[]{:S(2)}, u32[]{:S(2)}) collective-permute-start(f32[4,8,256]{2,1,0:T(8,128)S(1)} %get-tuple-element.14), channel_id=1, source_target_pairs={{0,8},{8,16},{16,24},{1,9},{9,17},{17,25},{2,10},{10,18},{18,26},{... | collective-permute-start | bytes 98312 | tf_op jit(solution)/shard_map/ppermute | solution.py:263
  16.3 1.3 %collective-permute-start.1 = (f32[4,8,256]{2,1,0:T(8,128)S(1)}, f32[4,8,256]{2,1,0:T(8,128)S(1)}, u32[]{:S(2)}, u32[]{:S(2)}) collective-permute-start(f32[4,8,256]{2,1,0:T(8,128)S(1)} %get-tuple-element.15), channel_id=1, source_target_pairs={{8,0},{16,8},{24,16},{9,1},{17,9},{25,17},{10,2},{18,10},{26,18},{... | collective-permute-start | bytes 98312 | tf_op jit(solution)/shard_map/ppermute | solution.py:264
  17.6 0.0 collective-permute-done.north_ref
  17.6 3.4 %collective-permute-done.1.south_ref = f32[4,8,256]{2,1,0:T(8,128)S(1)} collective-permute-done((f32[4,8,256]{2,1,0:T(8,128)S(1)}, f32[4,8,256]{2,1,0:T(8,128)S(1)}, u32[]{:S(2)}, u32[]{:S(2)}) %collective-permute-start.1) | collective-permute-done | bytes 32800 | tf_op jit(solution)/shard_map/ppermute | solution.py:264
  21.0 0.2 edges.1
  21.2 2.1 %collective-permute-start.3 = (f32[144,128]{1,0:T(8,128)S(1)}, f32[144,128]{1,0:T(8,128)S(1)}, u32[]{:S(2)}, u32[]{:S(2)}) collective-permute-start(f32[144,128]{1,0:T(8,128)S(1)} %edges.1), channel_id=1, source_target_pairs={{0,1},{1,2},{2,3},{3,4},{4,5},{5,6},{6,7},{7,0},{8,9},{9,10},{10,1... | collective-permute-start | bytes 221192 | tf_op jit(solution)/shard_map/ppermute | solution.py:267
  23.3 2.8 %collective-permute-start.2 = (f32[144,128]{1,0:T(8,128)S(1)}, f32[144,128]{1,0:T(8,128)S(1)}, u32[]{:S(2)}, u32[]{:S(2)}) collective-permute-start(f32[144,128]{1,0:T(8,128)S(1)} %edges.1), channel_id=1, source_target_pairs={{1,0},{2,1},{3,2},{4,3},{5,4},{6,5},{7,6},{0,7},{9,8},{10,9},{11,1... | collective-permute-start | bytes 221192 | tf_op jit(solution)/shard_map/ppermute | solution.py:266
  26.0 2.4 %collective-permute-done.3.west_ref = f32[144,128]{1,0:T(8,128)S(1)} collective-permute-done((f32[144,128]{1,0:T(8,128)S(1)}, f32[144,128]{1,0:T(8,128)S(1)}, u32[]{:S(2)}, u32[]{:S(2)}) %collective-permute-start.3) | collective-permute-done | bytes 73760 | tf_op jit(solution)/shard_map/ppermute | solution.py:267
  28.4 0.0 collective-permute-done.2.east_ref
  28.4 2.0 %krylov.1 = (f32[4,128,256]{2,1,0:T(8,128)S(1)}, f32[5,128,256]{2,1,0:T(8,128)S(1)}, f32[16,128]{1,0:T(8,128)S(1)}) custom-call(f32[4,128,256]{2,1,0:T(8,128)S(1)} %get-tuple-element.13.fields_ref, f32[4,8,256]{2,1,0:T(8,128)S(1)} %collective-permute-done.north_ref, f32[4,8,256]{2,1,0:T(8,128)S(1)} %collective-permute-done.1.south_ref, ...), custom_call_target="tpu_custom_call" | custom-call | tf_op jit(solution)/shard_map/krylov/pallas_call | solution.py:190
  30.4 1.7 %collective-permute-start.4 = (f32[16,128]{1,0:T(8,128)S(1)}, f32[16,128]{1,0:T(8,128)S(1)}, u32[]{:S(2)}, u32[]{:S(2)}) collective-permute-start(f32[16,128]{1,0:T(8,128)S(1)} %get-tuple-element.16), channel_id=1, source_target_pairs={{0,8},{8,0},{16,24},{24,16},{1,9},{9,1},{17,25},{25,17},{2,10},{10... | collective-permute-start | bytes 24584 | tf_op jit(solution)/shard_map/ppermute | solution.py:250
  32.2 0.8 %collective-permute-done.4 = f32[16,128]{1,0:T(8,128)S(1)} collective-permute-done((f32[16,128]{1,0:T(8,128)S(1)}, f32[16,128]{1,0:T(8,128)S(1)}, u32[]{:S(2)}, u32[]{:S(2)}) %collective-permute-start.4) | collective-permute-done | bytes 8224 | tf_op jit(solution)/shard_map/ppermute | solution.py:250
  33.0 1.2 %collective-permute-start.5 = (f32[16,128]{1,0:T(8,128)S(1)}, f32[16,128]{1,0:T(8,128)S(1)}, u32[]{:S(2)}, u32[]{:S(2)}) collective-permute-start(f32[16,128]{1,0:T(8,128)S(1)} %add.15), channel_id=1, source_target_pairs={{0,16},{8,24},{16,0},{24,8},{1,17},{9,25},{17,1},{25,9},{2,18},{10... | collective-permute-start | bytes 24584 | tf_op jit(solution)/shard_map/ppermute | solution.py:250
  34.2 2.4 %collective-permute-done.5 = f32[16,128]{1,0:T(8,128)S(1)} collective-permute-done((f32[16,128]{1,0:T(8,128)S(1)}, f32[16,128]{1,0:T(8,128)S(1)}, u32[]{:S(2)}, u32[]{:S(2)}) %collective-permute-start.5) | collective-permute-done | bytes 8224 | tf_op jit(solution)/shard_map/ppermute | solution.py:250
  36.7 1.1 %collective-permute-start.6 = (f32[16,128]{1,0:T(8,128)S(1)}, f32[16,128]{1,0:T(8,128)S(1)}, u32[]{:S(2)}, u32[]{:S(2)}) collective-permute-start(f32[16,128]{1,0:T(8,128)S(1)} %add.16), channel_id=1, source_target_pairs={{0,1},{1,0},{2,3},{3,2},{4,5},{5,4},{6,7},{7,6},{8,9},{9,8},{10,11... | collective-permute-start | bytes 24584 | tf_op jit(solution)/shard_map/ppermute | solution.py:250
  37.8 2.5 %collective-permute-done.6 = f32[16,128]{1,0:T(8,128)S(1)} collective-permute-done((f32[16,128]{1,0:T(8,128)S(1)}, f32[16,128]{1,0:T(8,128)S(1)}, u32[]{:S(2)}, u32[]{:S(2)}) %collective-permute-start.6) | collective-permute-done | bytes 8224 | tf_op jit(solution)/shard_map/ppermute | solution.py:250
  40.3 0.7 %collective-permute-start.7 = (f32[16,128]{1,0:T(8,128)S(1)}, f32[16,128]{1,0:T(8,128)S(1)}, u32[]{:S(2)}, u32[]{:S(2)}) collective-permute-start(f32[16,128]{1,0:T(8,128)S(1)} %add.17), channel_id=1, source_target_pairs={{0,2},{1,3},{2,0},{3,1},{4,6},{5,7},{6,4},{7,5},{8,10},{9,11},{10,... | collective-permute-start | bytes 24584 | tf_op jit(solution)/shard_map/ppermute | solution.py:250
  41.0 2.9 %collective-permute-done.7 = f32[16,128]{1,0:T(8,128)S(1)} collective-permute-done((f32[16,128]{1,0:T(8,128)S(1)}, f32[16,128]{1,0:T(8,128)S(1)}, u32[]{:S(2)}, u32[]{:S(2)}) %collective-permute-start.7) | collective-permute-done | bytes 8224 | tf_op jit(solution)/shard_map/ppermute | solution.py:250
  44.0 1.6 %collective-permute-start.8 = (f32[16,128]{1,0:T(8,128)S(1)}, f32[16,128]{1,0:T(8,128)S(1)}, u32[]{:S(2)}, u32[]{:S(2)}) collective-permute-start(f32[16,128]{1,0:T(8,128)S(1)} %add.18), channel_id=1, source_target_pairs={{0,4},{1,5},{2,6},{3,7},{4,0},{5,1},{6,2},{7,3},{8,12},{9,13},{10,... | collective-permute-start | bytes 24584 | tf_op jit(solution)/shard_map/ppermute | solution.py:250
  45.6 2.9 %collective-permute-done.8 = f32[16,128]{1,0:T(8,128)S(1)} collective-permute-done((f32[16,128]{1,0:T(8,128)S(1)}, f32[16,128]{1,0:T(8,128)S(1)}, u32[]{:S(2)}, u32[]{:S(2)}) %collective-permute-start.8) | collective-permute-done | bytes 8224 | tf_op jit(solution)/shard_map/ppermute | solution.py:250
  48.5 1.0 %combine.1 = (f32[128,256]{1,0:T(8,128)}, f32[128,256]{1,0:T(8,128)}) custom-call(f32[16,128]{1,0:T(8,128)S(1)} %add.19.sums_ref, f32[4,128,256]{2,1,0:T(8,128)S(1)} %get-tuple-element.17.w_ref, f32[5,128,256]{2,1,0:T(8,128)S(1)} %get-tuple-element.18.mw_ref), custom_call_target="tpu_custom_call" | custom-call | tf_op jit(solution)/shard_map/combine/pallas_call | solution.py:235
  49.5 0.0 all-to-all-done
  49.5 0.7 %copy.9 = f32[1,1,8,2,16,256]{5,4,3,2,1,0:T(8,128)} copy(f32[1,1,8,2,16,256]{5,4,3,2,1,0:T(8,128)S(1)} %bitcast.3) | data formatting | bytes 524288
  (5 shorter events, 0.0 us)
Async XLA Ops:
  0.6 1.6 %copy-start = (bf16[2,16,128,256]{3,2,1,0:T(8,128)(2,1)S(1)}, bf16[2,16,128,256]{3,2,1,0:T(8,128)(2,1)}, u32[]{:S(2)}) copy-start(bf16[2,16,128,256]{3,2,1,0:T(8,128)(2,1)} %tend_ref.1) | copy-start | bytes 6291460
  2.2 0.9 %copy-start.1 = (s32[128,256]{1,0:T(8,128)S(1)}, s32[128,256]{1,0:T(8,128)}, u32[]{:S(2)}) copy-start(s32[128,256]{1,0:T(8,128)} %count_ref.1) | copy-start | bytes 393220
  3.1 0.9 %copy-start.2 = (f32[128,256]{1,0:T(8,128)S(1)}, f32[128,256]{1,0:T(8,128)}, u32[]{:S(2)}) copy-start(f32[128,256]{1,0:T(8,128)} %inertia_ref.1) | copy-start | bytes 393220
  4.0 0.7 %copy-start.3 = (f32[16]{0:T(128)S(1)}, f32[16]{0:T(128)}, u32[]{:S(2)}) copy-start(f32[16]{0:T(128)} %thick_ref.1) | copy-start | bytes 196
  4.7 0.7 %copy-start.4 = (s32[8,1]{0,1:T(1,128)S(1)}, s32[8,1]{0,1:T(1,128)}, u32[]{:S(2)}) copy-start(s32[8,1]{0,1:T(1,128)} %param.9) | copy-start | bytes 100
  7.6 41.9 %all-to-all-start = ((f32[8,2,16,256]{3,2,1,0:T(8,128)}), f32[8,2,16,256]{3,2,1,0:T(8,128)S(1)}, u32[]{:S(2)}, u32[]{:S(2)}) async-start(f32[8,2,16,256]{3,2,1,0:T(8,128)} %get-tuple-element.12), calls=%async_computation | async-start | bytes 524288 | tf_op jit(solution)/shard_map/all_to_all | solution.py:268
  14.9 2.8 %collective-permute-start = (f32[4,8,256]{2,1,0:T(8,128)S(1)}, f32[4,8,256]{2,1,0:T(8,128)S(1)}, u32[]{:S(2)}, u32[]{:S(2)}) collective-permute-start(f32[4,8,256]{2,1,0:T(8,128)S(1)} %get-tuple-element.14), channel_id=1, source_target_pairs={{0,8},{8,16},{16,24},{1,9},{9,17},{17,25},{2,10},{10,18},{18,26},{... | collective-permute-start | bytes 98312 | tf_op jit(solution)/shard_map/ppermute | solution.py:263
  16.3 4.7 %collective-permute-start.1 = (f32[4,8,256]{2,1,0:T(8,128)S(1)}, f32[4,8,256]{2,1,0:T(8,128)S(1)}, u32[]{:S(2)}, u32[]{:S(2)}) collective-permute-start(f32[4,8,256]{2,1,0:T(8,128)S(1)} %get-tuple-element.15), channel_id=1, source_target_pairs={{8,0},{16,8},{24,16},{9,1},{17,9},{25,17},{10,2},{18,10},{26,18},{... | collective-permute-start | bytes 98312 | tf_op jit(solution)/shard_map/ppermute | solution.py:264
  21.2 7.2 %collective-permute-start.3 = (f32[144,128]{1,0:T(8,128)S(1)}, f32[144,128]{1,0:T(8,128)S(1)}, u32[]{:S(2)}, u32[]{:S(2)}) collective-permute-start(f32[144,128]{1,0:T(8,128)S(1)} %edges.1), channel_id=1, source_target_pairs={{0,1},{1,2},{2,3},{3,4},{4,5},{5,6},{6,7},{7,0},{8,9},{9,10},{10,1... | collective-permute-start | bytes 221192 | tf_op jit(solution)/shard_map/ppermute | solution.py:267
  23.3 5.1 %collective-permute-start.2 = (f32[144,128]{1,0:T(8,128)S(1)}, f32[144,128]{1,0:T(8,128)S(1)}, u32[]{:S(2)}, u32[]{:S(2)}) collective-permute-start(f32[144,128]{1,0:T(8,128)S(1)} %edges.1), channel_id=1, source_target_pairs={{1,0},{2,1},{3,2},{4,3},{5,4},{6,5},{7,6},{0,7},{9,8},{10,9},{11,1... | collective-permute-start | bytes 221192 | tf_op jit(solution)/shard_map/ppermute | solution.py:266
  30.4 2.5 %collective-permute-start.4 = (f32[16,128]{1,0:T(8,128)S(1)}, f32[16,128]{1,0:T(8,128)S(1)}, u32[]{:S(2)}, u32[]{:S(2)}) collective-permute-start(f32[16,128]{1,0:T(8,128)S(1)} %get-tuple-element.16), channel_id=1, source_target_pairs={{0,8},{8,0},{16,24},{24,16},{1,9},{9,1},{17,25},{25,17},{2,10},{10... | collective-permute-start | bytes 24584 | tf_op jit(solution)/shard_map/ppermute | solution.py:250
  33.0 3.7 %collective-permute-start.5 = (f32[16,128]{1,0:T(8,128)S(1)}, f32[16,128]{1,0:T(8,128)S(1)}, u32[]{:S(2)}, u32[]{:S(2)}) collective-permute-start(f32[16,128]{1,0:T(8,128)S(1)} %add.15), channel_id=1, source_target_pairs={{0,16},{8,24},{16,0},{24,8},{1,17},{9,25},{17,1},{25,9},{2,18},{10... | collective-permute-start | bytes 24584 | tf_op jit(solution)/shard_map/ppermute | solution.py:250
  36.7 3.7 %collective-permute-start.6 = (f32[16,128]{1,0:T(8,128)S(1)}, f32[16,128]{1,0:T(8,128)S(1)}, u32[]{:S(2)}, u32[]{:S(2)}) collective-permute-start(f32[16,128]{1,0:T(8,128)S(1)} %add.16), channel_id=1, source_target_pairs={{0,1},{1,0},{2,3},{3,2},{4,5},{5,4},{6,7},{7,6},{8,9},{9,8},{10,11... | collective-permute-start | bytes 24584 | tf_op jit(solution)/shard_map/ppermute | solution.py:250
  40.3 3.7 %collective-permute-start.7 = (f32[16,128]{1,0:T(8,128)S(1)}, f32[16,128]{1,0:T(8,128)S(1)}, u32[]{:S(2)}, u32[]{:S(2)}) collective-permute-start(f32[16,128]{1,0:T(8,128)S(1)} %add.17), channel_id=1, source_target_pairs={{0,2},{1,3},{2,0},{3,1},{4,6},{5,7},{6,4},{7,5},{8,10},{9,11},{10,... | collective-permute-start | bytes 24584 | tf_op jit(solution)/shard_map/ppermute | solution.py:250
  44.0 4.5 %collective-permute-start.8 = (f32[16,128]{1,0:T(8,128)S(1)}, f32[16,128]{1,0:T(8,128)S(1)}, u32[]{:S(2)}, u32[]{:S(2)}) collective-permute-start(f32[16,128]{1,0:T(8,128)S(1)} %add.18), channel_id=1, source_target_pairs={{0,4},{1,5},{2,6},{3,7},{4,0},{5,1},{6,2},{7,3},{8,12},{9,13},{10,... | collective-permute-start | bytes 24584 | tf_op jit(solution)/shard_map/ppermute | solution.py:250

commit v2 on v1

--- a/solution.py
+++ b/solution.py
@@ -13,80 +13,105 @@
 LANES = 128
 CHUNK = 32
 FIELDS = 4
-SUMS = 16
 VMEM_BYTES = 16 * 1024 * 1024
 
 
 def integrate_kernel(
-    thick_ref, owner_ref, count_ref, inertia_ref, tend_ref, fields_ref, head_ref, tail_ref, sent_ref
+    thick_hbm,
+    owner_hbm,
+    count_hbm,
+    inertia_hbm,
+    tend_hbm,
+    fields_ref,
+    head_ref,
+    tail_ref,
+    sent_ref,
+    thick_ref,
+    owner_ref,
+    count_ref,
+    inertia_ref,
+    tend_ref,
+    small_sems,
+    chunk_sems,
 ):
-    step = pl.program_id(0)
-    levels = tend_ref.shape[1]
-    chunk = count_ref.shape[0]
+    levels, rows = tend_hbm.shape[1:3]
     span = sent_ref.shape[2]
-    count = count_ref[...]
-    first = jnp.zeros(count.shape, jnp.float32)
-    second = jnp.zeros(count.shape, jnp.float32)
-    depth = jnp.zeros(count.shape, jnp.float32)
-    for level in range(levels):
-        layer = jnp.where(count > level, thick_ref[level], 0.0)
-        depth = depth + layer
-        first = first + layer * tend_ref[0, level].astype(jnp.float32)
-        second = second + layer * tend_ref[1, level].astype(jnp.float32)
-    inertia = inertia_ref[...]
-    for place, values in enumerate((first, second, depth, inertia)):
-        fields_ref[place] = values
-
-    @pl.when(step == 0)
-    def _():
-        sent_ref[...] = jnp.zeros(sent_ref.shape, jnp.float32)
-        for place, values in enumerate((first, second, depth, inertia)):
-            head_ref[place] = values[:ROWS]
-
-    @pl.when(step == pl.num_programs(0) - 1)
-    def _():
-        for place, values in enumerate((first, second, depth, inertia)):
-            tail_ref[place] = values[chunk - ROWS :]
-
-    for part in range(chunk // span):
-        target = owner_ref[step * (chunk // span) + part]
-
-        @pl.when(target >= 0)
-        def _(target=target, part=part):
-            rows = slice(part * span, (part + 1) * span)
-            sent_ref[target, 0] = first[rows]
-            sent_ref[target, 1] = second[rows]
+    chunk = max(CHUNK, span)
+    small = [
+        pltpu.make_async_copy(source, target, small_sems.at[place])
+        for place, (source, target) in enumerate(
+            (
+                (thick_hbm, thick_ref),
+                (owner_hbm, owner_ref),
+                (count_hbm, count_ref),
+                (inertia_hbm, inertia_ref),
+            )
+        )
+    ]
+    large = []
+    for place in range(rows // chunk):
+        part = pl.ds(place * chunk, chunk)
+        large.append(
+            pltpu.make_async_copy(
+                tend_hbm.at[:, :, part], tend_ref.at[:, :, part], chunk_sems.at[place]
+            )
+        )
+    for copy in small + large:
+        copy.start()
+    sent_ref[...] = jnp.zeros(sent_ref.shape, jnp.float32)
+    for copy in small:
+        copy.wait()
+    for place, copy in enumerate(large):
+        part = slice(place * chunk, (place + 1) * chunk)
+        copy.wait()
+        count = count_ref[part]
+        first = jnp.zeros(count.shape, jnp.float32)
+        second = jnp.zeros(count.shape, jnp.float32)
+        depth = jnp.zeros(count.shape, jnp.float32)
+        for level in range(levels):
+            layer = jnp.where(count > level, thick_ref[level], 0.0)
+            depth = depth + layer
+            first = first + layer * tend_ref[0, level, part].astype(jnp.float32)
+            second = second + layer * tend_ref[1, level, part].astype(jnp.float32)
+        inertia = inertia_ref[part]
+        for field, values in enumerate((first, second, depth, inertia)):
+            fields_ref[field, part] = values
+            if place == 0:
+                head_ref[field] = values[:ROWS]
+            if place == len(large) - 1:
+                tail_ref[field] = values[chunk - ROWS :]
+        for piece in range(chunk // span):
+            target = owner_ref[place * (chunk // span) + piece]
+
+            @pl.when(target >= 0)
+            def _(target=target, piece=piece, first=first, second=second):
+                rows_here = slice(piece * span, (piece + 1) * span)
+                sent_ref[target, 0] = first[rows_here]
+                sent_ref[target, 1] = second[rows_here]
 
 
 def integrate(tendency, thickness, level_count, owner, inertia, lon_count):
     components, levels, rows, cols = tendency.shape
     span = rows // owner.shape[0]
-    chunk = max(CHUNK, span)
-    whole = lambda step: (0, 0, 0)
     f32 = jnp.float32
     return pl.pallas_call(
         integrate_kernel,
-        grid=(rows // chunk,),
-        in_specs=[
-            pl.BlockSpec(memory_space=pltpu.SMEM),
-            pl.BlockSpec(memory_space=pltpu.SMEM),
-            pl.BlockSpec((chunk, cols), lambda step: (step, 0)),
-            pl.BlockSpec((chunk, cols), lambda step: (step, 0)),
-            pl.BlockSpec((components, levels, chunk, cols), lambda step: (0, 0, step, 0)),
-        ],
-        out_specs=[
-            pl.BlockSpec((FIELDS, chunk, cols), lambda step: (0, step, 0)),
-            pl.BlockSpec((FIELDS, ROWS, cols), whole),
-            pl.BlockSpec((FIELDS, ROWS, cols), whole),
-            pl.BlockSpec((lon_count, components, span, cols), lambda step: (0, 0, 0, 0)),
-        ],
+        in_specs=[pl.BlockSpec(memory_space=pltpu.HBM)] * 5,
         out_shape=[
             jax.ShapeDtypeStruct((FIELDS, rows, cols), f32),
             jax.ShapeDtypeStruct((FIELDS, ROWS, cols), f32),
             jax.ShapeDtypeStruct((FIELDS, ROWS, cols), f32),
             jax.ShapeDtypeStruct((lon_count, components, span, cols), f32),
         ],
-        compiler_params=pltpu.CompilerParams(vmem_limit_bytes=VMEM_BYTES),
+        scratch_shapes=[
+            pltpu.SMEM(thickness.shape, f32),
+            pltpu.SMEM(owner.shape, jnp.int32),
+            pltpu.VMEM(level_count.shape, jnp.int32),
+            pltpu.VMEM(inertia.shape, f32),
+            pltpu.VMEM(tendency.shape, tendency.dtype),
+            pltpu.SemaphoreType.DMA((4,)),
+            pltpu.SemaphoreType.DMA((rows // max(CHUNK, span),)),
+        ],
         cost_estimate=pl.CostEstimate(
             flops=6 * components * levels * rows * cols,
             bytes_accessed=2 * components * levels * rows * cols,
@@ -175,16 +200,24 @@
     for low in range(STEPS):
         for high in range(low, STEPS):
             pairs.append(ws[low] * images[high])
-    sums_ref[...] = jnp.zeros(sums_ref.shape, jnp.float32)
-    for place, product in enumerate(pairs):
+    half_lane = lax.broadcasted_iota(jnp.int32, (1, LANES), 1) < half
+    lines = []
+    for product in pairs:
         line = jnp.sum(product, axis=0, keepdims=True)
         total = line[:, :LANES]
         for start in range(LANES, cols, LANES):
             total = total + line[:, start : start + LANES]
-        sums_ref[place : place + 1, :] = total
-
-
-def krylov(fields, north, south, east, west):
+        lines.append(total + pltpu.roll(total, half, 1))
+    packed = [
+        jnp.where(half_lane, lines[place], lines[place + 1]) for place in range(0, len(lines), 2)
+    ]
+    packed.append(jnp.zeros((ROWS - len(packed), LANES), jnp.float32))
+    packed = jnp.concatenate(packed, axis=0)
+    for place in range(sums_ref.shape[0]):
+        sums_ref[place] = packed
+
+
+def krylov(fields, north, south, east, west, devices):
     _, rows, cols = fields.shape
     f32 = jnp.float32
     return pl.pallas_call(
@@ -192,7 +225,7 @@
         out_shape=[
             jax.ShapeDtypeStruct((STEPS, rows, cols), f32),
             jax.ShapeDtypeStruct((STEPS + 1, rows, cols), f32),
-            jax.ShapeDtypeStruct((SUMS, LANES), f32),
+            jax.ShapeDtypeStruct((devices, ROWS, LANES), f32),
         ],
         compiler_params=pltpu.CompilerParams(vmem_limit_bytes=VMEM_BYTES),
         name="krylov",
@@ -200,8 +233,13 @@
 
 
 def combine_kernel(sums_ref, w_ref, mw_ref, pressure_ref, residual_ref):
-    totals = jnp.sum(sums_ref[...], axis=1, keepdims=True)
-    entry = lambda place: totals[place : place + 1, :]
+    packed = jnp.sum(sums_ref[...], axis=0)
+    lower = lax.broadcasted_iota(jnp.int32, packed.shape, 1) < LANES // 2
+    totals = (
+        jnp.sum(jnp.where(lower, packed, 0.0), axis=1, keepdims=True),
+        jnp.sum(jnp.where(lower, 0.0, packed), axis=1, keepdims=True),
+    )
+    entry = lambda place: totals[place % 2][place // 2 : place // 2 + 1, :]
     right = [entry(place) for place in range(STEPS)]
     matrix = {}
     place = STEPS
@@ -240,18 +278,6 @@
     )(sums, w, mw)
 
 
-def total_over(values, axis):
-    count = lax.axis_size(axis)
-    if count & (count - 1):
-        return lax.psum(values, axis)
-    shift = 1
-    while shift < count:
-        pairs = [(place, place ^ shift) for place in range(count)]
-        values = values + lax.ppermute(values, axis, pairs)
-        shift *= 2
-    return values
-
-
 def on_device(tendency, thickness, level_count, block_mask, owner, inertia):
     lat_count = lax.axis_size("lat")
     lon_count = lax.axis_size("lon")
@@ -265,9 +291,10 @@
     packed = edges(fields, north, south)
     east = lax.ppermute(packed, "lon", [((p + 1) % lon_count, p) for p in range(lon_count)])
     west = lax.ppermute(packed, "lon", [(p, (p + 1) % lon_count) for p in range(lon_count)])
+    sent, east, west = lax.optimization_barrier((sent, east, west))
     held = lax.all_to_all(sent, "lon", split_axis=0, concat_axis=0, tiled=True)
-    w, mw, sums = krylov(fields, north, south, east, west)
-    sums = total_over(total_over(sums, "lat"), "lon")
+    w, mw, sums = krylov(fields, north, south, east, west, lat_count * lon_count)
+    sums = lax.all_to_all(sums, ("lat", "lon"), split_axis=0, concat_axis=0, tiled=True)
     pressure, residual = combine(sums, w, mw)
     return (held.reshape((1, 1) + held.shape), pressure, residual)
 

time: 50.5 us -> 50.6 us (level)
  blocking collectives: 0 us -> 14.6 us
  starting transfers between devices: 21.2 us -> 11.8 us
  local copies, waits for them, and re-layouts: 5.4 us -> 1.74 us
  waiting for transfers between devices: 17.4 us -> 14.9 us
  Pallas kernels: 5.44 us -> 6.37 us
    all_to_all x0 -> x1, blocking collectives: none -> 14.6 us  [on_device(): lax.all_to_all(sums, ('lat', 'lon'), split_axis=0, concat_axis=0, tiled=T...]
    ppermute x5 -> x0, waiting for transfers between devices: 11.7 us -> none  [total_over(): values = values + lax.ppermute(values, axis, pairs)]
    all_to_all x1, waiting for transfers between devices: 0.01 us -> 8.41 us  [on_device(): held = lax.all_to_all(sent, 'lon', split_axis=0, concat_axis=0, tiled=True)]
    ppermute x5 -> x0, starting transfers between devices: 6.4 us -> none  [total_over(): values = values + lax.ppermute(values, axis, pairs)]
    all_to_all x1, starting transfers between devices: 7.25 us -> 3.41 us  [on_device(): held = lax.all_to_all(sent, 'lon', split_axis=0, concat_axis=0, tiled=True)]
    unnamed x11 -> x3, local copies, waits for them, and re-layouts: 5.4 us -> 1.74 us
    ppermute x1, starting transfers between devices: 1.45 us -> 2.36 us  [on_device(): north = lax.ppermute(tail, 'lat', south_pairs)]
    pallas_call x1, Pallas kernels: 2.26 us -> 3.15 us  [integrate(): pl.pallas_call(integrate_kernel, in_specs=[pl.BlockSpec(memory_space=pltp...]
  transfers between devices with their start and end apart: 10 -> 5, of which waited for: 7 -> 3; matrix products, arithmetic and copies ran while one was open for 0% -> 0% of each run, Pallas kernels for 6% -> 2%
where the time goes in v2:
time: 50.6 us; the launch traced here: 50.2 us
  waiting for transfers between devices  14.9 us (29%)
  blocking collectives  14.6 us (29%)
  starting transfers between devices  11.8 us (23%)
  Pallas kernels  6.37 us (13%)
  local copies, waits for them, and re-layouts  1.74 us (3%)
  between operations  0.69 us (1%)
    all_to_all x1, blocking collectives, on_device(): lax.all_to_all(sums, ('lat', 'lon'), split_axis=0, concat_axis=0, tiled=T...  14.6 us
    all_to_all x1, waiting for transfers between devices, on_device(): held = lax.all_to_all(sent, 'lon', split_axis=0, concat_axis=0, tiled=True)  8.41 us
    ppermute x1, waiting for transfers between devices, on_device(): south = lax.ppermute(head, 'lat', north_pairs)  4.13 us
    all_to_all x1, starting transfers between devices, on_device(): held = lax.all_to_all(sent, 'lon', split_axis=0, concat_axis=0, tiled=True)  3.41 us
    ppermute x1, starting transfers between devices, on_device(): lax.ppermute(packed, 'lon', [((p + 1) % lon_count, p) for p in range(lon_...  3.23 us
    pallas_call x1, Pallas kernels, integrate(): pl.pallas_call(integrate_kernel, in_specs=[pl.BlockSpec(memory_space=pltp...  3.15 us
    ppermute x1, waiting for transfers between devices, on_device(): lax.ppermute(packed, 'lon', [(p, (p + 1) % lon_count) for p in range(lon_...  2.39 us
    ppermute x1, starting transfers between devices, on_device(): north = lax.ppermute(tail, 'lat', south_pairs)  2.36 us
  transfers between devices with their start and end apart: 5, of which 3 were waited for; matrix products, arithmetic and copies ran while one was open for 0% of the time, Pallas kernels for 2%

profile of v2, /device:TPU:0, one launch (start us, length us, event | category | flops | bytes accessed | tf_op | source)
XLA Modules:
  0.0 50.2 jit_solution(12292294214472381482)
XLA Ops:
  0.6 3.1 %integrate.1 = (f32[4,128,256]{2,1,0:T(8,128)}, f32[4,8,256]{2,1,0:T(8,128)}, f32[4,8,256]{2,1,0:T(8,128)}, f32[8,2,16,256]{3,2,1,0:T(8,128)}) custom-call(f32[16]{0:T(128)} %thick_hbm.1, s32[8]{0:T(128)} %bitcast.3, s32[128,256]{1,0:T(8,128)} %count_hbm.1, f32[128,256]{1,0:T(8,128)} %inertia_hbm.1, bf16[2,16,128,256]{3,2,1,0:T(8,128)(2,1)} %tend_hbm.1), custom_call_target="tpu_custom_call" | custom-call | flops 6291456 | bytes 2097152 | tf_op jit(solution)/shard_map/integrate/pallas_call | solution.py:97
  3.8 2.4 %collective-permute-start = (f32[4,8,256]{2,1,0:T(8,128)}, f32[4,8,256]{2,1,0:T(8,128)S(1)}, u32[]{:S(2)}, u32[]{:S(2)}) collective-permute-start(f32[4,8,256]{2,1,0:T(8,128)} %get-tuple-element.17), channel_id=1, source_target_pairs={{0,8},{8,16},{16,24},{1,9},{9,17},{17,25},{2,10},{10,18},{18,26},{... | collective-permute-start | bytes 98312 | tf_op jit(solution)/shard_map/ppermute | solution.py:289
  6.2 1.3 %collective-permute-start.1 = (f32[4,8,256]{2,1,0:T(8,128)}, f32[4,8,256]{2,1,0:T(8,128)S(1)}, u32[]{:S(2)}, u32[]{:S(2)}) collective-permute-start(f32[4,8,256]{2,1,0:T(8,128)} %get-tuple-element.18), channel_id=1, source_target_pairs={{8,0},{16,8},{24,16},{9,1},{17,9},{25,17},{10,2},{18,10},{26,18},{... | collective-permute-start | bytes 98312 | tf_op jit(solution)/shard_map/ppermute | solution.py:290
  7.5 0.0 collective-permute-done.north_ref
  7.5 4.1 %collective-permute-done.1.south_ref = f32[4,8,256]{2,1,0:T(8,128)S(1)} collective-permute-done((f32[4,8,256]{2,1,0:T(8,128)}, f32[4,8,256]{2,1,0:T(8,128)S(1)}, u32[]{:S(2)}, u32[]{:S(2)}) %collective-permute-start.1) | collective-permute-done | bytes 32800 | tf_op jit(solution)/shard_map/ppermute | solution.py:290
  11.6 0.0 copy-start
  11.6 1.0 %copy-done = f32[4,128,256]{2,1,0:T(8,128)S(1)} copy-done((f32[4,128,256]{2,1,0:T(8,128)S(1)}, f32[4,128,256]{2,1,0:T(8,128)}, u32[]{:S(2)}) %copy-start) | copy-done | bytes 524312
  12.6 0.2 edges.1
  12.8 1.5 %collective-permute-start.3 = (f32[144,128]{1,0:T(8,128)S(1)}, f32[144,128]{1,0:T(8,128)S(1)}, u32[]{:S(2)}, u32[]{:S(2)}) collective-permute-start(f32[144,128]{1,0:T(8,128)S(1)} %edges.1), channel_id=1, source_target_pairs={{0,1},{1,2},{2,3},{3,4},{4,5},{5,6},{6,7},{7,0},{8,9},{9,10},{10,1... | collective-permute-start | bytes 221192 | tf_op jit(solution)/shard_map/ppermute | solution.py:293
  14.4 3.2 %collective-permute-start.2 = (f32[144,128]{1,0:T(8,128)S(1)}, f32[144,128]{1,0:T(8,128)S(1)}, u32[]{:S(2)}, u32[]{:S(2)}) collective-permute-start(f32[144,128]{1,0:T(8,128)S(1)} %edges.1), channel_id=1, source_target_pairs={{1,0},{2,1},{3,2},{4,3},{5,4},{6,5},{7,6},{0,7},{9,8},{10,9},{11,1... | collective-permute-start | bytes 221192 | tf_op jit(solution)/shard_map/ppermute | solution.py:292
  17.6 2.4 %collective-permute-done.3.west_ref = f32[144,128]{1,0:T(8,128)S(1)} collective-permute-done((f32[144,128]{1,0:T(8,128)S(1)}, f32[144,128]{1,0:T(8,128)S(1)}, u32[]{:S(2)}, u32[]{:S(2)}) %collective-permute-start.3) | collective-permute-done | bytes 73760 | tf_op jit(solution)/shard_map/ppermute | solution.py:293
  20.0 0.0 collective-permute-done.2.east_ref
  20.0 2.0 %krylov.1 = (f32[4,128,256]{2,1,0:T(8,128)S(1)}, f32[5,128,256]{2,1,0:T(8,128)S(1)}, f32[32,8,128]{2,1,0:T(8,128)S(1)}) custom-call(f32[4,128,256]{2,1,0:T(8,128)S(1)} %copy-done, f32[4,8,256]{2,1,0:T(8,128)S(1)} %collective-permute-done.north_ref, f32[4,8,256]{2,1,0:T(8,128)S(1)} %collective-permute-done.1.south_ref, ...), custom_call_target="tpu_custom_call" | custom-call | tf_op jit(solution)/shard_map/krylov/pallas_call | solution.py:223
  22.1 14.6 %all_to_all.10.sums_ref = f32[32,8,128]{2,1,0:T(8,128)S(1)} all-to-all(f32[32,8,128]{2,1,0:T(8,128)S(1)} %get-tuple-element.22), channel_id=1, replica_groups=mesh['lat'=4,'lon'=8] {'lat','lon'}, dimensions={0} | all-to-all | bytes 262144 | tf_op jit(solution)/shard_map/all_to_all | solution.py:297
  36.7 3.4 %all-to-all-start = ((f32[8,2,16,256]{3,2,1,0:T(8,128)}), f32[8,2,16,256]{3,2,1,0:T(8,128)S(1)}, u32[]{:S(2)}, u32[]{:S(2)}) async-start(f32[8,2,16,256]{3,2,1,0:T(8,128)} %get-tuple-element.19), calls=%async_computation | async-start | bytes 524288 | tf_op jit(solution)/shard_map/all_to_all | solution.py:295
  40.1 1.0 %combine.1 = (f32[128,256]{1,0:T(8,128)}, f32[128,256]{1,0:T(8,128)}) custom-call(f32[32,8,128]{2,1,0:T(8,128)S(1)} %all_to_all.10.sums_ref, f32[4,128,256]{2,1,0:T(8,128)S(1)} %get-tuple-element.23.w_ref, f32[5,128,256]{2,1,0:T(8,128)S(1)} %get-tuple-element.24.mw_ref), custom_call_target="tpu_custom_call" | custom-call | tf_op jit(solution)/shard_map/combine/pallas_call | solution.py:273
  41.1 8.4 %all-to-all-done = f32[8,2,16,256]{3,2,1,0:T(8,128)S(1)} async-done(((f32[8,2,16,256]{3,2,1,0:T(8,128)}), f32[8,2,16,256]{3,2,1,0:T(8,128)S(1)}, u32[]{:S(2)}, u32[]{:S(2)}) %all-to-all-start) | async-done | bytes 262176 | tf_op jit(solution)/shard_map/all_to_all | solution.py:295
  49.5 0.7 %copy.9 = f32[1,1,8,2,16,256]{5,4,3,2,1,0:T(8,128)} copy(f32[1,1,8,2,16,256]{5,4,3,2,1,0:T(8,128)S(1)} %bitcast.2) | data formatting | bytes 524288
Async XLA Ops:
  3.8 3.7 %collective-permute-start = (f32[4,8,256]{2,1,0:T(8,128)}, f32[4,8,256]{2,1,0:T(8,128)S(1)}, u32[]{:S(2)}, u32[]{:S(2)}) collective-permute-start(f32[4,8,256]{2,1,0:T(8,128)} %get-tuple-element.17), channel_id=1, source_target_pairs={{0,8},{8,16},{16,24},{1,9},{9,17},{17,25},{2,10},{10,18},{18,26},{... | collective-permute-start | bytes 98312 | tf_op jit(solution)/shard_map/ppermute | solution.py:289
  6.2 5.4 %collective-permute-start.1 = (f32[4,8,256]{2,1,0:T(8,128)}, f32[4,8,256]{2,1,0:T(8,128)S(1)}, u32[]{:S(2)}, u32[]{:S(2)}) collective-permute-start(f32[4,8,256]{2,1,0:T(8,128)} %get-tuple-element.18), channel_id=1, source_target_pairs={{8,0},{16,8},{24,16},{9,1},{17,9},{25,17},{10,2},{18,10},{26,18},{... | collective-permute-start | bytes 98312 | tf_op jit(solution)/shard_map/ppermute | solution.py:290
  11.6 1.0 %copy-start = (f32[4,128,256]{2,1,0:T(8,128)S(1)}, f32[4,128,256]{2,1,0:T(8,128)}, u32[]{:S(2)}) copy-start(f32[4,128,256]{2,1,0:T(8,128)} %get-tuple-element.16.fields_ref) | copy-start | bytes 1572868
  12.8 7.2 %collective-permute-start.3 = (f32[144,128]{1,0:T(8,128)S(1)}, f32[144,128]{1,0:T(8,128)S(1)}, u32[]{:S(2)}, u32[]{:S(2)}) collective-permute-start(f32[144,128]{1,0:T(8,128)S(1)} %edges.1), channel_id=1, source_target_pairs={{0,1},{1,2},{2,3},{3,4},{4,5},{5,6},{6,7},{7,0},{8,9},{9,10},{10,1... | collective-permute-start | bytes 221192 | tf_op jit(solution)/shard_map/ppermute | solution.py:293
  14.4 5.6 %collective-permute-start.2 = (f32[144,128]{1,0:T(8,128)S(1)}, f32[144,128]{1,0:T(8,128)S(1)}, u32[]{:S(2)}, u32[]{:S(2)}) collective-permute-start(f32[144,128]{1,0:T(8,128)S(1)} %edges.1), channel_id=1, source_target_pairs={{1,0},{2,1},{3,2},{4,3},{5,4},{6,5},{7,6},{0,7},{9,8},{10,9},{11,1... | collective-permute-start | bytes 221192 | tf_op jit(solution)/shard_map/ppermute | solution.py:292
  36.7 12.8 %all-to-all-start = ((f32[8,2,16,256]{3,2,1,0:T(8,128)}), f32[8,2,16,256]{3,2,1,0:T(8,128)S(1)}, u32[]{:S(2)}, u32[]{:S(2)}) async-start(f32[8,2,16,256]{3,2,1,0:T(8,128)} %get-tuple-element.19), calls=%async_computation | async-start | bytes 524288 | tf_op jit(solution)/shard_map/all_to_all | solution.py:295

commit v3 on v2

--- a/solution.py
+++ b/solution.py
@@ -18,16 +18,14 @@
 
 def integrate_kernel(
     thick_hbm,
-    owner_hbm,
     count_hbm,
     inertia_hbm,
     tend_hbm,
     fields_ref,
     head_ref,
     tail_ref,
-    sent_ref,
+    blocks_ref,
     thick_ref,
-    owner_ref,
     count_ref,
     inertia_ref,
     tend_ref,
@@ -35,14 +33,12 @@
     chunk_sems,
 ):
     levels, rows = tend_hbm.shape[1:3]
-    span = sent_ref.shape[2]
-    chunk = max(CHUNK, span)
+    chunk = CHUNK
     small = [
         pltpu.make_async_copy(source, target, small_sems.at[place])
         for place, (source, target) in enumerate(
             (
                 (thick_hbm, thick_ref),
-                (owner_hbm, owner_ref),
                 (count_hbm, count_ref),
                 (inertia_hbm, inertia_ref),
             )
@@ -58,7 +54,6 @@
         )
     for copy in small + large:
         copy.start()
-    sent_ref[...] = jnp.zeros(sent_ref.shape, jnp.float32)
     for copy in small:
         copy.wait()
     for place, copy in enumerate(large):
@@ -80,37 +75,29 @@
                 head_ref[field] = values[:ROWS]
             if place == len(large) - 1:
                 tail_ref[field] = values[chunk - ROWS :]
-        for piece in range(chunk // span):
-            target = owner_ref[place * (chunk // span) + piece]
-
-            @pl.when(target >= 0)
-            def _(target=target, piece=piece, first=first, second=second):
-                rows_here = slice(piece * span, (piece + 1) * span)
-                sent_ref[target, 0] = first[rows_here]
-                sent_ref[target, 1] = second[rows_here]
-
-
-def integrate(tendency, thickness, level_count, owner, inertia, lon_count):
+        blocks_ref[0, part] = first
+        blocks_ref[1, part] = second
+
+
+def integrate(tendency, thickness, level_count, inertia):
     components, levels, rows, cols = tendency.shape
-    span = rows // owner.shape[0]
     f32 = jnp.float32
     return pl.pallas_call(
         integrate_kernel,
-        in_specs=[pl.BlockSpec(memory_space=pltpu.HBM)] * 5,
+        in_specs=[pl.BlockSpec(memory_space=pltpu.HBM)] * 4,
         out_shape=[
             jax.ShapeDtypeStruct((FIELDS, rows, cols), f32),
             jax.ShapeDtypeStruct((FIELDS, ROWS, cols), f32),
             jax.ShapeDtypeStruct((FIELDS, ROWS, cols), f32),
-            jax.ShapeDtypeStruct((lon_count, components, span, cols), f32),
+            jax.ShapeDtypeStruct((components, rows, cols), f32),
         ],
         scratch_shapes=[
             pltpu.SMEM(thickness.shape, f32),
-            pltpu.SMEM(owner.shape, jnp.int32),
             pltpu.VMEM(level_count.shape, jnp.int32),
             pltpu.VMEM(inertia.shape, f32),
             pltpu.VMEM(tendency.shape, tendency.dtype),
-            pltpu.SemaphoreType.DMA((4,)),
-            pltpu.SemaphoreType.DMA((rows // max(CHUNK, span),)),
+            pltpu.SemaphoreType.DMA((3,)),
+            pltpu.SemaphoreType.DMA((rows // CHUNK,)),
         ],
         cost_estimate=pl.CostEstimate(
             flops=6 * components * levels * rows * cols,
@@ -118,7 +105,7 @@
             transcendentals=0,
         ),
         name="integrate",
-    )(thickness, owner, level_count, inertia, tendency)
+    )(thickness, level_count, inertia, tendency)
 
 
 def edges_kernel(fields_ref, north_ref, south_ref, out_ref):
@@ -156,7 +143,7 @@
     return tall + 0.5 * (pltpu.roll(tall, 1, 1) + pltpu.roll(tall, cols - 1, 1))
 
 
-def krylov_kernel(fields_ref, north_ref, south_ref, east_ref, west_ref, w_ref, mw_ref, sums_ref):
+def krylov_kernel(owner_ref, fields_ref, north_ref, south_ref, east_ref, west_ref, w_ref, mw_ref, sums_ref):
     rows = fields_ref.shape[1]
     cols = fields_ref.shape[2]
     tall = rows + 2 * ROWS
@@ -211,29 +198,36 @@
     packed = [
         jnp.where(half_lane, lines[place], lines[place + 1]) for place in range(0, len(lines), 2)
     ]
-    packed.append(jnp.zeros((ROWS - len(packed), LANES), jnp.float32))
+    if len(packed) < ROWS - 1:
+        packed.append(jnp.zeros((ROWS - 1 - len(packed), LANES), jnp.float32))
+    place_lane = lax.broadcasted_iota(jnp.int32, (1, LANES), 1)
+    owners = jnp.zeros((1, LANES), jnp.float32)
+    for place in range(owner_ref.shape[0]):
+        owners = jnp.where(place_lane == place, owner_ref[place].astype(jnp.float32), owners)
+    packed.append(owners)
     packed = jnp.concatenate(packed, axis=0)
-    for place in range(sums_ref.shape[0]):
-        sums_ref[place] = packed
-
-
-def krylov(fields, north, south, east, west, devices):
+    sums_ref[...] = packed
+
+
+def krylov(owner, fields, north, south, east, west):
     _, rows, cols = fields.shape
     f32 = jnp.float32
     return pl.pallas_call(
         krylov_kernel,
+        in_specs=[pl.BlockSpec(memory_space=pltpu.SMEM)]
+        + [pl.BlockSpec(memory_space=pltpu.VMEM)] * 5,
         out_shape=[
             jax.ShapeDtypeStruct((STEPS, rows, cols), f32),
             jax.ShapeDtypeStruct((STEPS + 1, rows, cols), f32),
-            jax.ShapeDtypeStruct((devices, ROWS, LANES), f32),
+            jax.ShapeDtypeStruct((ROWS, LANES), f32),
         ],
         compiler_params=pltpu.CompilerParams(vmem_limit_bytes=VMEM_BYTES),
         name="krylov",
-    )(fields, north, south, east, west)
+    )(owner, fields, north, south, east, west)
 
 
 def combine_kernel(sums_ref, w_ref, mw_ref, pressure_ref, residual_ref):
-    packed = jnp.sum(sums_ref[...], axis=0)
+    packed = jnp.sum(sums_ref[...], axis=0)[: ROWS - 1]
     lower = lax.broadcasted_iota(jnp.int32, packed.shape, 1) < LANES // 2
     totals = (
         jnp.sum(jnp.where(lower, packed, 0.0), axis=1, keepdims=True),
@@ -278,12 +272,65 @@
     )(sums, w, mw)
 
 
+def pick_kernel(sums_hbm, blocks_hbm, held_ref, owner_ref, owner_sem, sems):
+    band = lax.axis_index("lat")
+    me = lax.axis_index("lon").astype(jnp.float32)
+    homes = owner_ref.shape[0]
+    span = held_ref.shape[2]
+    count = blocks_hbm.shape[2] // span
+    mine = pl.ds(band * homes, homes)
+    owners = pltpu.make_async_copy(
+        sums_hbm.at[mine, pl.ds(ROWS - 1, 1)], owner_ref, owner_sem
+    )
+    owners.start()
+    owners.wait()
+
+    def copy(home, block):
+        rows = pl.ds(pl.multiple_of(block * span, span), span)
+        return pltpu.make_async_copy(blocks_hbm.at[home, :, rows], held_ref.at[home], sems.at[home])
+
+    chosen = []
+    for home in range(homes):
+        block = jnp.int32(-1)
+        for place in range(count):
+            block = jnp.where(owner_ref[home, 0, place] == me, place, block)
+        chosen.append(block)
+
+        @pl.when(block >= 0)
+        def _(home=home, block=block):
+            copy(home, block).start()
+
+        @pl.when(block < 0)
+        def _(home=home):
+            held_ref[home] = jnp.zeros(held_ref.shape[1:], jnp.float32)
+
+    for home in range(homes):
+
+        @pl.when(chosen[home] >= 0)
+        def _(home=home):
+            copy(home, chosen[home]).wait()
+
+
+def pick(sums, blocks, count):
+    homes, components, rows, cols = blocks.shape
+    return pl.pallas_call(
+        pick_kernel,
+        in_specs=[pl.BlockSpec(memory_space=pltpu.HBM)] * 2,
+        out_shape=jax.ShapeDtypeStruct((homes, components, rows // count, cols), jnp.float32),
+        scratch_shapes=[
+            pltpu.SMEM((homes, 1, LANES), jnp.float32),
+            pltpu.SemaphoreType.DMA,
+            pltpu.SemaphoreType.DMA((homes,)),
+        ],
+        name="pick",
+    )(sums, blocks)
+
+
 def on_device(tendency, thickness, level_count, block_mask, owner, inertia):
     lat_count = lax.axis_size("lat")
     lon_count = lax.axis_size("lon")
-    fields, head, tail, sent = integrate(
-        tendency, thickness, level_count, owner[:, 0], inertia, lon_count
-    )
+    fields, head, tail, blocks = integrate(tendency, thickness, level_count, inertia)
+    blocks = lax.all_gather(blocks, "lon")
     south_pairs = [(place, place + 1) for place in range(lat_count - 1)]
     north_pairs = [(place + 1, place) for place in range(lat_count - 1)]
     north = lax.ppermute(tail, "lat", south_pairs)
@@ -291,11 +338,10 @@
     packed = edges(fields, north, south)
     east = lax.ppermute(packed, "lon", [((p + 1) % lon_count, p) for p in range(lon_count)])
     west = lax.ppermute(packed, "lon", [(p, (p + 1) % lon_count) for p in range(lon_count)])
-    sent, east, west = lax.optimization_barrier((sent, east, west))
-    held = lax.all_to_all(sent, "lon", split_axis=0, concat_axis=0, tiled=True)
-    w, mw, sums = krylov(fields, north, south, east, west, lat_count * lon_count)
-    sums = lax.all_to_all(sums, ("lat", "lon"), split_axis=0, concat_axis=0, tiled=True)
+    w, mw, sums = krylov(owner[:, 0], fields, north, south, east, west)
+    sums = lax.all_gather(sums, ("lat", "lon"))
     pressure, residual = combine(sums, w, mw)
+    held = pick(sums, blocks, owner.shape[0])
     return (held.reshape((1, 1) + held.shape), pressure, residual)
 
 

time: 50.6 us -> 111 us (2.19); the launches traced: 50.2 us -> 109 us
  blocking collectives: 14.6 us -> 64.5 us
  between operations: 0.69 us -> 14.1 us
  starting transfers between devices: 11.8 us -> 8.27 us
  Pallas kernels: 6.37 us -> 9.31 us
  waiting for transfers between devices: 14.9 us -> 12.1 us
    all_gather x0 -> x1, blocking collectives: none -> 64.5 us  [on_device(): sums = lax.all_gather(sums, ('lat', 'lon'))]
    all_to_all x1 -> x0, blocking collectives: 14.6 us -> none  [on_device(): lax.all_to_all(sums, ('lat', 'lon'), split_axis=0, concat_axis=0, tiled=T...]
    all_to_all x1 -> x0, waiting for transfers between devices: 8.41 us -> none  [on_device(): held = lax.all_to_all(sent, 'lon', split_axis=0, concat_axis=0, tiled=True)]
    ppermute x1, waiting for transfers between devices: 2.39 us -> 5.87 us  [on_device(): lax.ppermute(packed, 'lon', [(p, (p + 1) % lon_count) for p in range(lon_...]
    all_to_all x1 -> x0, starting transfers between devices: 3.41 us -> none  [on_device(): held = lax.all_to_all(sent, 'lon', split_axis=0, concat_axis=0, tiled=True)]
    pallas_call x1 -> x2, Pallas kernels: 2.04 us -> 5.01 us  [the longest x1 2.64 us: krylov(): pl.pallas_call(krylov_kernel, in_specs=[pl.BlockSpec(memory_space=pltpu.S...]
    ppermute x1, waiting for transfers between devices: 0.01 us -> 2.04 us  [on_device(): lax.ppermute(packed, 'lon', [((p + 1) % lon_count, p) for p in range(lon_...]
    ppermute x1, starting transfers between devices: 1.54 us -> 0.01 us  [on_device(): lax.ppermute(packed, 'lon', [(p, (p + 1) % lon_count) for p in range(lon_...]
  transfers between devices with their start and end apart: 5 -> 5, of which waited for: 3 -> 3; matrix products, arithmetic and copies ran while one was open for 0% -> 0% of each run, Pallas kernels for 2% -> 4%
where the time goes in v3:
time: 111 us; the launch traced here: 109 us
  blocking collectives  64.5 us (58%)
  between operations  14.1 us (13%)
  waiting for transfers between devices  12.1 us (11%)
  Pallas kernels  9.31 us (8%)
  starting transfers between devices  8.27 us (7%)
    all_gather x1, blocking collectives, on_device(): sums = lax.all_gather(sums, ('lat', 'lon'))  64.5 us
    ppermute x1, waiting for transfers between devices, on_device(): lax.ppermute(packed, 'lon', [(p, (p + 1) % lon_count) for p in range(lon_...  5.87 us
    ppermute x1, starting transfers between devices, on_device(): lax.ppermute(packed, 'lon', [((p + 1) % lon_count, p) for p in range(lon_...  4.58 us
    ppermute x1, waiting for transfers between devices, on_device(): south = lax.ppermute(head, 'lat', north_pairs)  4.14 us
    pallas_call x1, Pallas kernels, integrate(): pl.pallas_call(integrate_kernel, in_specs=[pl.BlockSpec(memory_space=pltp...  3.1 us
    pallas_call x1, Pallas kernels, krylov(): pl.pallas_call(krylov_kernel, in_specs=[pl.BlockSpec(memory_space=pltpu.S...  2.64 us
    pallas_call x1, Pallas kernels, pick(): pl.pallas_call(pick_kernel, in_specs=[pl.BlockSpec(memory_space=pltpu.HBM...  2.37 us
    ppermute x1, starting transfers between devices, on_device(): north = lax.ppermute(tail, 'lat', south_pairs)  2.36 us
  transfers between devices with their start and end apart: 5, of which 3 were waited for; matrix products, arithmetic and copies ran while one was open for 0% of the time, Pallas kernels for 4%

profile of v3, /device:TPU:0, one launch (start us, length us, event | category | flops | bytes accessed | tf_op | source)
XLA Modules:
  0.0 109.3 jit_solution(14148018991850411329)
XLA Ops:
  7.2 0.0 copy-start.2
  7.2 0.0 all-gather.4.cloned.1.call-start
  7.2 3.1 %integrate.1 = (f32[4,128,256]{2,1,0:T(8,128)}, f32[4,8,256]{2,1,0:T(8,128)}, f32[4,8,256]{2,1,0:T(8,128)}, f32[2,128,256]{2,1,0:T(8,128)}) custom-call(f32[16]{0:T(128)} %thick_hbm.1, s32[128,256]{1,0:T(8,128)} %count_hbm.1, f32[128,256]{1,0:T(8,128)} %inertia_hbm.1, bf16[2,16,128,256]{3,2,1,0:T(8,128)(2,1)} %tend_hbm.1), custom_call_target="tpu_custom_call" | custom-call | flops 6291456 | bytes 2097152 | tf_op jit(solution)/shard_map/integrate/pallas_call | solution.py:85
  10.3 0.0 all-gather.4.cloned.1.call-update
  10.4 2.4 %collective-permute-start = (f32[4,8,256]{2,1,0:T(8,128)}, f32[4,8,256]{2,1,0:T(8,128)S(1)}, u32[]{:S(2)}, u32[]{:S(2)}) collective-permute-start(f32[4,8,256]{2,1,0:T(8,128)} %get-tuple-element.13), channel_id=1, source_target_pairs={{0,8},{8,16},{16,24},{1,9},{9,17},{17,25},{2,10},{10,18},{18,26},{... | collective-permute-start | bytes 98312 | tf_op jit(solution)/shard_map/ppermute | solution.py:336
  12.7 1.3 %collective-permute-start.1 = (f32[4,8,256]{2,1,0:T(8,128)}, f32[4,8,256]{2,1,0:T(8,128)S(1)}, u32[]{:S(2)}, u32[]{:S(2)}) collective-permute-start(f32[4,8,256]{2,1,0:T(8,128)} %get-tuple-element.14), channel_id=1, source_target_pairs={{8,0},{16,8},{24,16},{9,1},{17,9},{25,17},{10,2},{18,10},{26,18},{... | collective-permute-start | bytes 98312 | tf_op jit(solution)/shard_map/ppermute | solution.py:337
  14.0 0.0 collective-permute-done.north_ref
  14.0 4.1 %collective-permute-done.1.south_ref = f32[4,8,256]{2,1,0:T(8,128)S(1)} collective-permute-done((f32[4,8,256]{2,1,0:T(8,128)}, f32[4,8,256]{2,1,0:T(8,128)S(1)}, u32[]{:S(2)}, u32[]{:S(2)}) %collective-permute-start.1) | collective-permute-done | bytes 32800 | tf_op jit(solution)/shard_map/ppermute | solution.py:337
  18.2 0.0 copy-start
  18.2 1.0 copy-done
  19.2 0.2 edges.1
  19.4 4.6 %collective-permute-start.2 = (f32[144,128]{1,0:T(8,128)S(1)}, f32[144,128]{1,0:T(8,128)S(1)}, u32[]{:S(2)}, u32[]{:S(2)}) collective-permute-start(f32[144,128]{1,0:T(8,128)S(1)} %edges.1), channel_id=1, source_target_pairs={{1,0},{2,1},{3,2},{4,3},{5,4},{6,5},{7,6},{0,7},{9,8},{10,9},{11,1... | collective-permute-start | bytes 221192 | tf_op jit(solution)/shard_map/ppermute | solution.py:339
  24.0 0.0 collective-permute-start.3
  24.0 2.0 %collective-permute-done.2.east_ref = f32[144,128]{1,0:T(8,128)S(1)} collective-permute-done((f32[144,128]{1,0:T(8,128)S(1)}, f32[144,128]{1,0:T(8,128)S(1)}, u32[]{:S(2)}, u32[]{:S(2)}) %collective-permute-start.2) | collective-permute-done | bytes 73760 | tf_op jit(solution)/shard_map/ppermute | solution.py:339
  26.0 5.9 %collective-permute-done.3.west_ref = f32[144,128]{1,0:T(8,128)S(1)} collective-permute-done((f32[144,128]{1,0:T(8,128)S(1)}, f32[144,128]{1,0:T(8,128)S(1)}, u32[]{:S(2)}, u32[]{:S(2)}) %collective-permute-start.3) | collective-permute-done | bytes 73760 | tf_op jit(solution)/shard_map/ppermute | solution.py:340
  31.9 0.0 copy-done.2
  31.9 2.6 %krylov.1 = (f32[4,128,256]{2,1,0:T(8,128)S(1)}, f32[5,128,256]{2,1,0:T(8,128)S(1)}, f32[8,128]{1,0:T(8,128)S(1)}) custom-call(s32[8]{0:T(128)S(1)} %bitcast.6, f32[4,128,256]{2,1,0:T(8,128)S(1)} %copy-done, f32[4,8,256]{2,1,0:T(8,128)S(1)} %collective-permute-done.north_ref, f32[4,8,256]{2,1,0:T(8,128)S(1)} %collective-permute-done.1.south_ref, ...), custom_call_target="tpu_custom_call" | custom-call | tf_op jit(solution)/shard_map/krylov/pallas_call | solution.py:215
  34.6 64.5 %all-gather = f32[256,128]{1,0:T(8,128)S(1)} all-gather(f32[8,128]{1,0:T(8,128)S(1)} %get-tuple-element.15), channel_id=2, replica_groups=mesh['lat'=4,'lon'=8] {'lat','lon'}, dimensions={0}, use_global_device_ids=true | all-gather | bytes 135168 | tf_op jit(solution)/shard_map/all_gather | solution.py:342
  99.0 0.0 copy-start.1
  99.0 1.0 combine.1
  100.0 0.0 all-gather.4.cloned.1.call-done
  100.1 0.0 copy-done.1
  100.1 2.4 %pick.1 = f32[8,2,16,256]{3,2,1,0:T(8,128)} custom-call(f32[32,8,128]{2,1,0:T(8,128)} %bitcast.5, f32[8,2,128,256]{3,2,1,0:T(8,128)} %bitcast.7), custom_call_target="tpu_custom_call" | custom-call | tf_op jit(solution)/shard_map/pick/pallas_call | solution.py:316
Async XLA Ops:
  7.2 24.7 %copy-start.2 = (s32[8,1]{0,1:T(1,128)S(1)}, s32[8,1]{0,1:T(1,128)}, u32[]{:S(2)}) copy-start(s32[8,1]{0,1:T(1,128)} %param.9) | copy-start | bytes 100
  7.2 92.9 %all-gather.4.cloned.1.call-start = ((), (), s32[]{:S(2)}) async-start(), calls=%async_computation | async-start | bytes 2359296 | tf_op jit(solution)/shard_map/all_gather | solution.py:333
  10.4 3.7 %collective-permute-start = (f32[4,8,256]{2,1,0:T(8,128)}, f32[4,8,256]{2,1,0:T(8,128)S(1)}, u32[]{:S(2)}, u32[]{:S(2)}) collective-permute-start(f32[4,8,256]{2,1,0:T(8,128)} %get-tuple-element.13), channel_id=1, source_target_pairs={{0,8},{8,16},{16,24},{1,9},{9,17},{17,25},{2,10},{10,18},{18,26},{... | collective-permute-start | bytes 98312 | tf_op jit(solution)/shard_map/ppermute | solution.py:336
  12.7 5.4 %collective-permute-start.1 = (f32[4,8,256]{2,1,0:T(8,128)}, f32[4,8,256]{2,1,0:T(8,128)S(1)}, u32[]{:S(2)}, u32[]{:S(2)}) collective-permute-start(f32[4,8,256]{2,1,0:T(8,128)} %get-tuple-element.14), channel_id=1, source_target_pairs={{8,0},{16,8},{24,16},{9,1},{17,9},{25,17},{10,2},{18,10},{26,18},{... | collective-permute-start | bytes 98312 | tf_op jit(solution)/shard_map/ppermute | solution.py:337
  18.2 1.0 copy-start
  19.4 6.6 %collective-permute-start.2 = (f32[144,128]{1,0:T(8,128)S(1)}, f32[144,128]{1,0:T(8,128)S(1)}, u32[]{:S(2)}, u32[]{:S(2)}) collective-permute-start(f32[144,128]{1,0:T(8,128)S(1)} %edges.1), channel_id=1, source_target_pairs={{1,0},{2,1},{3,2},{4,3},{5,4},{6,5},{7,6},{0,7},{9,8},{10,9},{11,1... | collective-permute-start | bytes 221192 | tf_op jit(solution)/shard_map/ppermute | solution.py:339
  24.0 7.9 %collective-permute-start.3 = (f32[144,128]{1,0:T(8,128)S(1)}, f32[144,128]{1,0:T(8,128)S(1)}, u32[]{:S(2)}, u32[]{:S(2)}) collective-permute-start(f32[144,128]{1,0:T(8,128)S(1)} %edges.1), channel_id=1, source_target_pairs={{0,1},{1,2},{2,3},{3,4},{4,5},{5,6},{6,7},{7,0},{8,9},{9,10},{10,1... | collective-permute-start | bytes 221192 | tf_op jit(solution)/shard_map/ppermute | solution.py:340
  99.0 1.0 copy-start.1
Sparse Core Ops, SparseCore 0:
  10.7 54.0 all-gather.3

commit v4 on v2

--- a/solution.py
+++ b/solution.py
@@ -14,6 +14,24 @@
 CHUNK = 32
 FIELDS = 4
 VMEM_BYTES = 16 * 1024 * 1024
+
+
+def pack_edges(ref, part):
+    cols = ref.shape[2]
+    packed = None
+    for place in range(FIELDS):
+        west = ref[place, part, :LANES]
+        east = ref[place, part, cols - LANES :]
+        if packed is None:
+            lane = lax.broadcasted_iota(jnp.int32, west.shape, 1)
+            packed = jnp.zeros(west.shape, jnp.float32)
+        at = place * RIM
+        west = pltpu.roll(west, at, 1) if at else west
+        packed = jnp.where((lane >= at) & (lane < at + RIM), west, packed)
+        at = LANES // 2 + place * RIM
+        east = pltpu.roll(east, (at + RIM) % LANES, 1)
+        packed = jnp.where((lane >= at) & (lane < at + RIM), east, packed)
+    return packed
 
 
 def integrate_kernel(
@@ -25,6 +43,7 @@
     fields_ref,
     head_ref,
     tail_ref,
+    side_ref,
     sent_ref,
     thick_ref,
     owner_ref,
@@ -80,6 +99,7 @@
                 head_ref[field] = values[:ROWS]
             if place == len(large) - 1:
                 tail_ref[field] = values[chunk - ROWS :]
+        side_ref[part] = pack_edges(fields_ref, part)
         for piece in range(chunk // span):
             target = owner_ref[place * (chunk // span) + piece]
 
@@ -101,6 +121,7 @@
             jax.ShapeDtypeStruct((FIELDS, rows, cols), f32),
             jax.ShapeDtypeStruct((FIELDS, ROWS, cols), f32),
             jax.ShapeDtypeStruct((FIELDS, ROWS, cols), f32),
+            jax.ShapeDtypeStruct((rows, LANES), f32),
             jax.ShapeDtypeStruct((lon_count, components, span, cols), f32),
         ],
         scratch_shapes=[
@@ -121,33 +142,21 @@
     )(thickness, owner, level_count, inertia, tendency)
 
 
-def edges_kernel(fields_ref, north_ref, south_ref, out_ref):
-    rows = fields_ref.shape[1]
-    cols = fields_ref.shape[2]
-    half = LANES // 2
-    for top, size, ref in ((0, ROWS, north_ref), (ROWS, rows, fields_ref), (ROWS + rows, ROWS, south_ref)):
-        lane = lax.broadcasted_iota(jnp.int32, (size, LANES), 1)
-        packed = jnp.zeros((size, LANES), jnp.float32)
-        for place in range(FIELDS):
-            west = ref[place, :, :LANES]
-            east = ref[place, :, cols - LANES :]
-            at = place * RIM
-            west = pltpu.roll(west, at, 1) if at else west
-            packed = jnp.where((lane >= at) & (lane < at + RIM), west, packed)
-            at = half + place * RIM
-            east = pltpu.roll(east, (at + RIM) % LANES, 1)
-            packed = jnp.where((lane >= at) & (lane < at + RIM), east, packed)
-        out_ref[top : top + size] = packed
-
-
-def edges(fields, north, south):
-    rows = fields.shape[1] + 2 * ROWS
+def edges_kernel(side_ref, north_ref, south_ref, out_ref):
+    rows = side_ref.shape[0]
+    out_ref[:ROWS] = pack_edges(north_ref, slice(None))
+    out_ref[ROWS : ROWS + rows] = side_ref[...]
+    out_ref[ROWS + rows :] = pack_edges(south_ref, slice(None))
+
+
+def edges(side, north, south):
+    rows = side.shape[0] + 2 * ROWS
     return pl.pallas_call(
         edges_kernel,
         out_shape=jax.ShapeDtypeStruct((rows, LANES), jnp.float32),
         compiler_params=pltpu.CompilerParams(vmem_limit_bytes=VMEM_BYTES),
         name="edges",
-    )(fields, north, south)
+    )(side, north, south)
 
 
 def smooth(field):
@@ -217,7 +226,7 @@
         sums_ref[place] = packed
 
 
-def krylov(fields, north, south, east, west, devices):
+def krylov(fields, north, south, east, west, copies):
     _, rows, cols = fields.shape
     f32 = jnp.float32
     return pl.pallas_call(
@@ -225,14 +234,15 @@
         out_shape=[
             jax.ShapeDtypeStruct((STEPS, rows, cols), f32),
             jax.ShapeDtypeStruct((STEPS + 1, rows, cols), f32),
-            jax.ShapeDtypeStruct((devices, ROWS, LANES), f32),
+            jax.ShapeDtypeStruct((copies, ROWS, LANES), f32),
         ],
         compiler_params=pltpu.CompilerParams(vmem_limit_bytes=VMEM_BYTES),
         name="krylov",
     )(fields, north, south, east, west)
 
 
-def combine_kernel(sums_ref, w_ref, mw_ref, pressure_ref, residual_ref):
+def combine_kernel(sums_ref, w_ref, mw_ref, arrived_ref, pressure_ref, residual_ref, held_ref):
+    held_ref[...] = arrived_ref[...]
     packed = jnp.sum(sums_ref[...], axis=0)
     lower = lax.broadcasted_iota(jnp.int32, packed.shape, 1) < LANES // 2
     totals = (
@@ -268,34 +278,36 @@
     residual_ref[...] = residual
 
 
-def combine(sums, w, mw):
+def combine(sums, w, mw, arrived):
     shape = jax.ShapeDtypeStruct(w.shape[1:], jnp.float32)
     return pl.pallas_call(
         combine_kernel,
-        out_shape=[shape, shape],
+        out_shape=[shape, shape, jax.ShapeDtypeStruct(arrived.shape, jnp.float32)],
         compiler_params=pltpu.CompilerParams(vmem_limit_bytes=VMEM_BYTES),
         name="combine",
-    )(sums, w, mw)
+    )(sums, w, mw, arrived)
 
 
 def on_device(tendency, thickness, level_count, block_mask, owner, inertia):
     lat_count = lax.axis_size("lat")
     lon_count = lax.axis_size("lon")
-    fields, head, tail, sent = integrate(
+    fields, head, tail, side, sent = integrate(
         tendency, thickness, level_count, owner[:, 0], inertia, lon_count
     )
     south_pairs = [(place, place + 1) for place in range(lat_count - 1)]
     north_pairs = [(place + 1, place) for place in range(lat_count - 1)]
     north = lax.ppermute(tail, "lat", south_pairs)
     south = lax.ppermute(head, "lat", north_pairs)
-    packed = edges(fields, north, south)
+    packed = edges(side, north, south)
+    sent, packed = lax.optimization_barrier((sent, packed))
     east = lax.ppermute(packed, "lon", [((p + 1) % lon_count, p) for p in range(lon_count)])
     west = lax.ppermute(packed, "lon", [(p, (p + 1) % lon_count) for p in range(lon_count)])
-    sent, east, west = lax.optimization_barrier((sent, east, west))
-    held = lax.all_to_all(sent, "lon", split_axis=0, concat_axis=0, tiled=True)
-    w, mw, sums = krylov(fields, north, south, east, west, lat_count * lon_count)
-    sums = lax.all_to_all(sums, ("lat", "lon"), split_axis=0, concat_axis=0, tiled=True)
-    pressure, residual = combine(sums, w, mw)
+    arrived = lax.all_to_all(sent, "lon", split_axis=0, concat_axis=0, tiled=True)
+    w, mw, sums = krylov(fields, north, south, east, west, lat_count)
+    sums = lax.all_to_all(sums, "lat", split_axis=0, concat_axis=0, tiled=True)
+    sums = jnp.broadcast_to(jnp.sum(sums, axis=0), (lon_count,) + sums.shape[1:])
+    sums = lax.all_to_all(sums, "lon", split_axis=0, concat_axis=0, tiled=True)
+    pressure, residual, held = combine(sums, w, mw, arrived)
     return (held.reshape((1, 1) + held.shape), pressure, residual)
 
 

time: 50.6 us -> 56 us (1.11)
  blocking collectives: 14.6 us -> 31.5 us
  waiting for transfers between devices: 14.9 us -> 6.54 us
  starting transfers between devices: 11.8 us -> 8.4 us
    all_to_all x1 -> x3, blocking collectives: 14.6 us -> 31.5 us  [the longest x1 12.5 us: on_device(): sums = lax.all_to_all(sums, 'lon', split_axis=0, concat_axis=0, tiled=True)]
    all_to_all x1 -> x0, waiting for transfers between devices: 8.41 us -> none  [on_device(): held = lax.all_to_all(sent, 'lon', split_axis=0, concat_axis=0, tiled=True)]
    all_to_all x1 -> x0, starting transfers between devices: 3.41 us -> none  [on_device(): held = lax.all_to_all(sent, 'lon', split_axis=0, concat_axis=0, tiled=True)]
    unnamed x3 -> x4, local copies, waits for them, and re-layouts: 1.74 us -> 1.88 us
  transfers between devices with their start and end apart: 5 -> 4, of which waited for: 3 -> 2; matrix products, arithmetic and copies ran while one was open for 0% -> 0% of each run, Pallas kernels for 2% -> 0%
where the time goes in v4:
time: 56 us; the launch traced here: 55.5 us
  blocking collectives  31.5 us (56%)
  starting transfers between devices  8.4 us (15%)
  waiting for transfers between devices  6.54 us (12%)
  Pallas kernels  6.49 us (12%)
  local copies, waits for them, and re-layouts  1.89 us (3%)
  between operations  0.68 us (1%)
    all_to_all x1, blocking collectives, on_device(): sums = lax.all_to_all(sums, 'lon', split_axis=0, concat_axis=0, tiled=True)  12.5 us
    all_to_all x1, blocking collectives, on_device(): lax.all_to_all(sent, 'lon', split_axis=0, concat_axis=0, tiled=True)  11.5 us
    all_to_all x1, blocking collectives, on_device(): sums = lax.all_to_all(sums, 'lat', split_axis=0, concat_axis=0, tiled=True)  7.49 us
    ppermute x1, waiting for transfers between devices, on_device(): south = lax.ppermute(head, 'lat', north_pairs)  4.14 us
    pallas_call x1, Pallas kernels, integrate(): pl.pallas_call(integrate_kernel, in_specs=[pl.BlockSpec(memory_space=pltp...  3.32 us
    ppermute x1, starting transfers between devices, on_device(): lax.ppermute(packed, 'lon', [((p + 1) % lon_count, p) for p in range(lon_...  3.23 us
    ppermute x1, waiting for transfers between devices, on_device(): lax.ppermute(packed, 'lon', [(p, (p + 1) % lon_count) for p in range(lon_...  2.39 us
    ppermute x1, starting transfers between devices, on_device(): north = lax.ppermute(tail, 'lat', south_pairs)  2.36 us
  transfers between devices with their start and end apart: 4, of which 2 were waited for; matrix products, arithmetic and copies ran while one was open for 0% of the time, Pallas kernels for 0%

profile of v4, /device:TPU:0, one launch (start us, length us, event | category | flops | bytes accessed | tf_op | source)
XLA Modules:
  0.0 55.5 jit_solution(11423095690453019794)
XLA Ops:
  0.6 3.3 %integrate.1 = (f32[4,128,256]{2,1,0:T(8,128)}, f32[4,8,256]{2,1,0:T(8,128)}, f32[4,8,256]{2,1,0:T(8,128)}, f32[128,128]{1,0:T(8,128)}, f32[8,2,16,256]{3,2,1,0:T(8,128)}) custom-call(f32[16]{0:T(128)} %thick_hbm.1, s32[8]{0:T(128)} %bitcast.2, s32[128,256]{1,0:T(8,128)} %count_hbm.1, f32[128,256]{1,0:T(8,128)} %inertia_hbm.1, bf16[2,16,128,256]{3,2,1,0:T(8,128)(2,1)} %tend_hbm.1), custom_call_target="tpu_custom_call" | custom-call | flops 6291456 | bytes 2097152 | tf_op jit(solution)/shard_map/integrate/pallas_call | solution.py:117
  4.0 2.4 %collective-permute-start = (f32[4,8,256]{2,1,0:T(8,128)}, f32[4,8,256]{2,1,0:T(8,128)S(1)}, u32[]{:S(2)}, u32[]{:S(2)}) collective-permute-start(f32[4,8,256]{2,1,0:T(8,128)} %get-tuple-element.17), channel_id=1, source_target_pairs={{0,8},{8,16},{16,24},{1,9},{9,17},{17,25},{2,10},{10,18},{18,26},{... | collective-permute-start | bytes 98312 | tf_op jit(solution)/shard_map/ppermute | solution.py:299
  6.3 1.3 %collective-permute-start.1 = (f32[4,8,256]{2,1,0:T(8,128)}, f32[4,8,256]{2,1,0:T(8,128)S(1)}, u32[]{:S(2)}, u32[]{:S(2)}) collective-permute-start(f32[4,8,256]{2,1,0:T(8,128)} %get-tuple-element.18), channel_id=1, source_target_pairs={{8,0},{16,8},{24,16},{9,1},{17,9},{25,17},{10,2},{18,10},{26,18},{... | collective-permute-start | bytes 98312 | tf_op jit(solution)/shard_map/ppermute | solution.py:300
  7.6 0.0 collective-permute-done.north_ref
  7.6 4.1 %collective-permute-done.1.south_ref = f32[4,8,256]{2,1,0:T(8,128)S(1)} collective-permute-done((f32[4,8,256]{2,1,0:T(8,128)}, f32[4,8,256]{2,1,0:T(8,128)S(1)}, u32[]{:S(2)}, u32[]{:S(2)}) %collective-permute-start.1) | collective-permute-done | bytes 32800 | tf_op jit(solution)/shard_map/ppermute | solution.py:300
  11.8 0.0 copy-start.1
  11.8 0.8 %copy-done.1 = f32[128,128]{1,0:T(8,128)S(1)} copy-done((f32[128,128]{1,0:T(8,128)S(1)}, f32[128,128]{1,0:T(8,128)}, u32[]{:S(2)}) %copy-start.1) | copy-done | bytes 65560
  12.6 0.1 edges.1
  12.7 1.5 %collective-permute-start.3 = (f32[144,128]{1,0:T(8,128)S(1)}, f32[144,128]{1,0:T(8,128)S(1)}, u32[]{:S(2)}, u32[]{:S(2)}) collective-permute-start(f32[144,128]{1,0:T(8,128)S(1)} %edges.1), channel_id=1, source_target_pairs={{0,1},{1,2},{2,3},{3,4},{4,5},{5,6},{6,7},{7,0},{8,9},{9,10},{10,1... | collective-permute-start | bytes 221192 | tf_op jit(solution)/shard_map/ppermute | solution.py:304
  14.2 3.2 %collective-permute-start.2 = (f32[144,128]{1,0:T(8,128)S(1)}, f32[144,128]{1,0:T(8,128)S(1)}, u32[]{:S(2)}, u32[]{:S(2)}) collective-permute-start(f32[144,128]{1,0:T(8,128)S(1)} %edges.1), channel_id=1, source_target_pairs={{1,0},{2,1},{3,2},{4,3},{5,4},{6,5},{7,6},{0,7},{9,8},{10,9},{11,1... | collective-permute-start | bytes 221192 | tf_op jit(solution)/shard_map/ppermute | solution.py:303
  17.4 2.4 %collective-permute-done.3.west_ref = f32[144,128]{1,0:T(8,128)S(1)} collective-permute-done((f32[144,128]{1,0:T(8,128)S(1)}, f32[144,128]{1,0:T(8,128)S(1)}, u32[]{:S(2)}, u32[]{:S(2)}) %collective-permute-start.3) | collective-permute-done | bytes 73760 | tf_op jit(solution)/shard_map/ppermute | solution.py:304
  19.8 0.0 collective-permute-done.2.east_ref
  19.8 0.0 copy-start
  19.8 1.0 %copy-done = f32[4,128,256]{2,1,0:T(8,128)S(1)} copy-done((f32[4,128,256]{2,1,0:T(8,128)S(1)}, f32[4,128,256]{2,1,0:T(8,128)}, u32[]{:S(2)}) %copy-start) | copy-done | bytes 524312
  20.9 2.0 %krylov.1 = (f32[4,128,256]{2,1,0:T(8,128)S(1)}, f32[5,128,256]{2,1,0:T(8,128)S(1)}, f32[4,8,128]{2,1,0:T(8,128)S(1)}) custom-call(f32[4,128,256]{2,1,0:T(8,128)S(1)} %copy-done, f32[4,8,256]{2,1,0:T(8,128)S(1)} %collective-permute-done.north_ref, f32[4,8,256]{2,1,0:T(8,128)S(1)} %collective-permute-done.1.south_ref, ...), custom_call_target="tpu_custom_call" | custom-call | tf_op jit(solution)/shard_map/krylov/pallas_call | solution.py:232
  22.9 7.5 %all_to_all.15 = f32[4,8,128]{2,1,0:T(8,128)S(1)} all-to-all(f32[4,8,128]{2,1,0:T(8,128)S(1)} %get-tuple-element.22), channel_id=1, replica_groups=mesh['lat'=4,'lon'=8] {'lat'}, dimensions={0} | all-to-all | bytes 32768 | tf_op jit(solution)/shard_map/all_to_all | solution.py:307
  30.4 12.5 %all_to_all.16.sums_ref = f32[8,8,128]{2,1,0:T(8,128)S(1)} all-to-all(f32[8,8,128]{2,1,0:T(8,128)S(1)} %broadcast_in_dim.3), channel_id=1, replica_groups=mesh['lat'=4,'lon'=8] {'lon'}, dimensions={0} | all-to-all | bytes 65536 | tf_op jit(solution)/shard_map/all_to_all | solution.py:309
  42.9 11.5 %all_to_all.17.arrived_ref = f32[8,2,16,256]{3,2,1,0:T(8,128)S(1)} all-to-all(f32[8,2,16,256]{3,2,1,0:T(8,128)} %get-tuple-element.25), channel_id=1, replica_groups=mesh['lat'=4,'lon'=8] {'lon'}, dimensions={0} | all-to-all | bytes 524288 | tf_op jit(solution)/shard_map/all_to_all | solution.py:305
  54.4 1.1 %combine.1 = (f32[128,256]{1,0:T(8,128)}, f32[128,256]{1,0:T(8,128)}, f32[8,2,16,256]{3,2,1,0:T(8,128)}) custom-call(f32[8,8,128]{2,1,0:T(8,128)S(1)} %all_to_all.16.sums_ref, f32[4,128,256]{2,1,0:T(8,128)S(1)} %get-tuple-element.23.w_ref, f32[5,128,256]{2,1,0:T(8,128)S(1)} %get-tuple-element.24.mw_ref, f32[8,2,16,256]{3,2,1,0:T(8,128)S(1)} %all_to_all.17.arrived_ref), custom_call_target="tpu_custom_call" | custom-call | tf_op jit(solution)/shard_map/combine/pallas_call | solution.py:283
  (2 shorter events, 0.0 us)
Async XLA Ops:
  4.0 3.7 %collective-permute-start = (f32[4,8,256]{2,1,0:T(8,128)}, f32[4,8,256]{2,1,0:T(8,128)S(1)}, u32[]{:S(2)}, u32[]{:S(2)}) collective-permute-start(f32[4,8,256]{2,1,0:T(8,128)} %get-tuple-element.17), channel_id=1, source_target_pairs={{0,8},{8,16},{16,24},{1,9},{9,17},{17,25},{2,10},{10,18},{18,26},{... | collective-permute-start | bytes 98312 | tf_op jit(solution)/shard_map/ppermute | solution.py:299
  6.3 5.4 %collective-permute-start.1 = (f32[4,8,256]{2,1,0:T(8,128)}, f32[4,8,256]{2,1,0:T(8,128)S(1)}, u32[]{:S(2)}, u32[]{:S(2)}) collective-permute-start(f32[4,8,256]{2,1,0:T(8,128)} %get-tuple-element.18), channel_id=1, source_target_pairs={{8,0},{16,8},{24,16},{9,1},{17,9},{25,17},{10,2},{18,10},{26,18},{... | collective-permute-start | bytes 98312 | tf_op jit(solution)/shard_map/ppermute | solution.py:300
  11.8 0.8 %copy-start.1 = (f32[128,128]{1,0:T(8,128)S(1)}, f32[128,128]{1,0:T(8,128)}, u32[]{:S(2)}) copy-start(f32[128,128]{1,0:T(8,128)} %get-tuple-element.20.side_ref) | copy-start | bytes 196612
  12.7 7.1 %collective-permute-start.3 = (f32[144,128]{1,0:T(8,128)S(1)}, f32[144,128]{1,0:T(8,128)S(1)}, u32[]{:S(2)}, u32[]{:S(2)}) collective-permute-start(f32[144,128]{1,0:T(8,128)S(1)} %edges.1), channel_id=1, source_target_pairs={{0,1},{1,2},{2,3},{3,4},{4,5},{5,6},{6,7},{7,0},{8,9},{9,10},{10,1... | collective-permute-start | bytes 221192 | tf_op jit(solution)/shard_map/ppermute | solution.py:304
  14.2 5.6 %collective-permute-start.2 = (f32[144,128]{1,0:T(8,128)S(1)}, f32[144,128]{1,0:T(8,128)S(1)}, u32[]{:S(2)}, u32[]{:S(2)}) collective-permute-start(f32[144,128]{1,0:T(8,128)S(1)} %edges.1), channel_id=1, source_target_pairs={{1,0},{2,1},{3,2},{4,3},{5,4},{6,5},{7,6},{0,7},{9,8},{10,9},{11,1... | collective-permute-start | bytes 221192 | tf_op jit(solution)/shard_map/ppermute | solution.py:303
  19.8 1.0 %copy-start = (f32[4,128,256]{2,1,0:T(8,128)S(1)}, f32[4,128,256]{2,1,0:T(8,128)}, u32[]{:S(2)}) copy-start(f32[4,128,256]{2,1,0:T(8,128)} %get-tuple-element.16.fields_ref) | copy-start | bytes 1572868

commit v5 on v4

--- a/solution.py
+++ b/solution.py
@@ -14,6 +14,7 @@
 CHUNK = 32
 FIELDS = 4
 VMEM_BYTES = 16 * 1024 * 1024
+INTEGRATE_BYTES = 56350000
 
 
 def pack_edges(ref, part):
@@ -54,7 +55,7 @@
     chunk_sems,
 ):
     levels, rows = tend_hbm.shape[1:3]
-    span = sent_ref.shape[2]
+    span = (sent_ref.shape[1] - ROWS) // 2
     chunk = max(CHUNK, span)
     small = [
         pltpu.make_async_copy(source, target, small_sems.at[place])
@@ -106,8 +107,8 @@
             @pl.when(target >= 0)
             def _(target=target, piece=piece, first=first, second=second):
                 rows_here = slice(piece * span, (piece + 1) * span)
-                sent_ref[target, 0] = first[rows_here]
-                sent_ref[target, 1] = second[rows_here]
+                sent_ref[target, :span] = first[rows_here]
+                sent_ref[target, span : 2 * span] = second[rows_here]
 
 
 def integrate(tendency, thickness, level_count, owner, inertia, lon_count):
@@ -122,7 +123,7 @@
             jax.ShapeDtypeStruct((FIELDS, ROWS, cols), f32),
             jax.ShapeDtypeStruct((FIELDS, ROWS, cols), f32),
             jax.ShapeDtypeStruct((rows, LANES), f32),
-            jax.ShapeDtypeStruct((lon_count, components, span, cols), f32),
+            jax.ShapeDtypeStruct((lon_count, components * span + ROWS, cols), f32),
         ],
         scratch_shapes=[
             pltpu.SMEM(thickness.shape, f32),
@@ -133,6 +134,7 @@
             pltpu.SemaphoreType.DMA((4,)),
             pltpu.SemaphoreType.DMA((rows // max(CHUNK, span),)),
         ],
+        compiler_params=pltpu.CompilerParams(vmem_limit_bytes=INTEGRATE_BYTES),
         cost_estimate=pl.CostEstimate(
             flops=6 * components * levels * rows * cols,
             bytes_accessed=2 * components * levels * rows * cols,
@@ -222,11 +224,10 @@
     ]
     packed.append(jnp.zeros((ROWS - len(packed), LANES), jnp.float32))
     packed = jnp.concatenate(packed, axis=0)
-    for place in range(sums_ref.shape[0]):
-        sums_ref[place] = packed
-
-
-def krylov(fields, north, south, east, west, copies):
+    sums_ref[...] = packed
+
+
+def krylov(fields, north, south, east, west):
     _, rows, cols = fields.shape
     f32 = jnp.float32
     return pl.pallas_call(
@@ -234,16 +235,16 @@
         out_shape=[
             jax.ShapeDtypeStruct((STEPS, rows, cols), f32),
             jax.ShapeDtypeStruct((STEPS + 1, rows, cols), f32),
-            jax.ShapeDtypeStruct((copies, ROWS, LANES), f32),
+            jax.ShapeDtypeStruct((ROWS, LANES), f32),
         ],
         compiler_params=pltpu.CompilerParams(vmem_limit_bytes=VMEM_BYTES),
         name="krylov",
     )(fields, north, south, east, west)
 
 
-def combine_kernel(sums_ref, w_ref, mw_ref, arrived_ref, pressure_ref, residual_ref, held_ref):
-    held_ref[...] = arrived_ref[...]
-    packed = jnp.sum(sums_ref[...], axis=0)
+def combine_kernel(arrived_ref, w_ref, mw_ref, pressure_ref, residual_ref, held_ref):
+    held_ref[...] = arrived_ref[:, : held_ref.shape[1]]
+    packed = jnp.sum(arrived_ref[:, held_ref.shape[1] :, :LANES], axis=0)
     lower = lax.broadcasted_iota(jnp.int32, packed.shape, 1) < LANES // 2
     totals = (
         jnp.sum(jnp.where(lower, packed, 0.0), axis=1, keepdims=True),
@@ -278,14 +279,25 @@
     residual_ref[...] = residual
 
 
-def combine(sums, w, mw, arrived):
+def combine(arrived, w, mw):
+    slots, rows, cols = arrived.shape
     shape = jax.ShapeDtypeStruct(w.shape[1:], jnp.float32)
     return pl.pallas_call(
         combine_kernel,
-        out_shape=[shape, shape, jax.ShapeDtypeStruct(arrived.shape, jnp.float32)],
+        out_shape=[shape, shape, jax.ShapeDtypeStruct((slots, rows - ROWS, cols), jnp.float32)],
         compiler_params=pltpu.CompilerParams(vmem_limit_bytes=VMEM_BYTES),
         name="combine",
-    )(sums, w, mw, arrived)
+    )(arrived, w, mw)
+
+
+def total_over(values, axis):
+    count = lax.axis_size(axis)
+    shift = 1
+    while shift < count:
+        pairs = [(place, place ^ shift) for place in range(count)]
+        values = values + lax.ppermute(values, axis, pairs)
+        shift *= 2
+    return values
 
 
 def on_device(tendency, thickness, level_count, block_mask, owner, inertia):
@@ -299,16 +311,15 @@
     north = lax.ppermute(tail, "lat", south_pairs)
     south = lax.ppermute(head, "lat", north_pairs)
     packed = edges(side, north, south)
-    sent, packed = lax.optimization_barrier((sent, packed))
     east = lax.ppermute(packed, "lon", [((p + 1) % lon_count, p) for p in range(lon_count)])
     west = lax.ppermute(packed, "lon", [(p, (p + 1) % lon_count) for p in range(lon_count)])
+    w, mw, sums = krylov(fields, north, south, east, west)
+    sums = jnp.broadcast_to(total_over(sums, "lat"), (lon_count,) + sums.shape)
+    sent = lax.dynamic_update_slice(sent, sums, (0, sent.shape[1] - ROWS, 0))
     arrived = lax.all_to_all(sent, "lon", split_axis=0, concat_axis=0, tiled=True)
-    w, mw, sums = krylov(fields, north, south, east, west, lat_count)
-    sums = lax.all_to_all(sums, "lat", split_axis=0, concat_axis=0, tiled=True)
-    sums = jnp.broadcast_to(jnp.sum(sums, axis=0), (lon_count,) + sums.shape[1:])
-    sums = lax.all_to_all(sums, "lon", split_axis=0, concat_axis=0, tiled=True)
-    pressure, residual, held = combine(sums, w, mw, arrived)
-    return (held.reshape((1, 1) + held.shape), pressure, residual)
+    pressure, residual, held = combine(arrived, w, mw)
+    held = held.reshape((1, 1, lon_count, 2, held.shape[1] // 2, held.shape[2]))
+    return (held, pressure, residual)
 
 
 def solution(mesh):

time: 56 us -> 47.3 us (0.84)
  blocking collectives: 31.5 us -> 16.1 us
  waiting for transfers between devices: 6.54 us -> 9.46 us
  starting transfers between devices: 8.4 us -> 11.3 us
  local copies, waits for them, and re-layouts: 1.89 us -> 2.97 us
    all_to_all x2 -> x0, blocking collectives: 20 us -> none  [the longest x1 12.5 us: on_device(): sums = lax.all_to_all(sums, 'lon', split_axis=0, concat_axis=0, tiled=True)]
    all_to_all x1, blocking collectives: 11.5 us -> 16.1 us  [on_device(): lax.all_to_all(sent, 'lon', split_axis=0, concat_axis=0, tiled=True)]
    ppermute x0 -> x2, waiting for transfers between devices: none -> 3.14 us  [total_over(): values = values + lax.ppermute(values, axis, pairs)]
    ppermute x0 -> x2, starting transfers between devices: none -> 2.86 us  [total_over(): values = values + lax.ppermute(values, axis, pairs)]
    dynamic_update_slice x0 -> x1, local copies, waits for them, and re-layouts: none -> 0.62 us  [on_device(): sent = lax.dynamic_update_slice(sent, sums, (0, sent.shape[1] - ROWS, 0))]
    unnamed x4 -> x6, local copies, waits for them, and re-layouts: 1.88 us -> 2.35 us
  transfers between devices with their start and end apart: 4 -> 6, of which waited for: 2 -> 4; matrix products, arithmetic and copies ran while one was open for 0% -> 0% of each run, Pallas kernels for 0% -> 0%
where the time goes in v5:
time: 47.3 us; the launch traced here: 47 us
  blocking collectives  16.1 us (34%)
  starting transfers between devices  11.3 us (24%)
  waiting for transfers between devices  9.46 us (20%)
  Pallas kernels  6.53 us (14%)
  local copies, waits for them, and re-layouts  2.97 us (6%)
  between operations  0.69 us (1%)
    all_to_all x1, blocking collectives, on_device(): lax.all_to_all(sent, 'lon', split_axis=0, concat_axis=0, tiled=True)  16.1 us
    ppermute x1, waiting for transfers between devices, on_device(): south = lax.ppermute(head, 'lat', north_pairs)  3.92 us
    pallas_call x1, Pallas kernels, integrate(): pl.pallas_call(integrate_kernel, in_specs=[pl.BlockSpec(memory_space=pltp...  3.32 us
    ppermute x1, starting transfers between devices, on_device(): lax.ppermute(packed, 'lon', [((p + 1) % lon_count, p) for p in range(lon_...  3.23 us
    ppermute x2, waiting for transfers between devices, total_over(): values = values + lax.ppermute(values, axis, pairs)  3.14 us
    ppermute x2, starting transfers between devices, total_over(): values = values + lax.ppermute(values, axis, pairs)  2.86 us
    ppermute x1, waiting for transfers between devices, on_device(): lax.ppermute(packed, 'lon', [(p, (p + 1) % lon_count) for p in range(lon_...  2.39 us
    ppermute x1, starting transfers between devices, on_device(): north = lax.ppermute(tail, 'lat', south_pairs)  2.36 us
  transfers between devices with their start and end apart: 6, of which 4 were waited for; matrix products, arithmetic and copies ran while one was open for 0% of the time, Pallas kernels for 0%

profile of v5, /device:TPU:0, one launch (start us, length us, event | category | flops | bytes accessed | tf_op | source)
XLA Modules:
  0.0 47.0 jit_solution(10117457268138412797)
XLA Ops:
  0.6 0.0 copy-start.1
  0.6 0.6 %copy-done.1 = f32[16]{0:T(128)S(1)} copy-done((f32[16]{0:T(128)S(1)}, f32[16]{0:T(128)}, u32[]{:S(2)}) %copy-start.1) | copy-done | bytes 88
  1.3 0.0 copy-start.2
  1.3 0.7 %copy-done.2 = s32[8,1]{0,1:T(1,128)S(1)} copy-done((s32[8,1]{0,1:T(1,128)S(1)}, s32[8,1]{0,1:T(1,128)}, u32[]{:S(2)}) %copy-start.2) | copy-done | bytes 56
  1.9 3.3 %integrate.1 = (f32[4,128,256]{2,1,0:T(8,128)}, f32[4,8,256]{2,1,0:T(8,128)S(1)}, f32[4,8,256]{2,1,0:T(8,128)S(1)}, f32[128,128]{1,0:T(8,128)S(1)}, f32[8,40,256]{2,1,0:T(8,128)}) custom-call(f32[16]{0:T(128)S(1)} %copy-done.1, s32[8]{0:T(128)S(1)} %bitcast.2, s32[128,256]{1,0:T(8,128)} %count_hbm.1, f32[128,256]{1,0:T(8,128)} %inertia_hbm.1, ...), custom_call_target="tpu_custom_call" | custom-call | flops 6291456 | bytes 2097152 | tf_op jit(solution)/shard_map/integrate/pallas_call | solution.py:118
  5.3 2.4 %collective-permute-start = (f32[4,8,256]{2,1,0:T(8,128)S(1)}, f32[4,8,256]{2,1,0:T(8,128)S(1)}, u32[]{:S(2)}, u32[]{:S(2)}) collective-permute-start(f32[4,8,256]{2,1,0:T(8,128)S(1)} %get-tuple-element.16), channel_id=1, source_target_pairs={{0,8},{8,16},{16,24},{1,9},{9,17},{17,25},{2,10},{10,18},{18,26},{... | collective-permute-start | bytes 98312 | tf_op jit(solution)/shard_map/ppermute | solution.py:311
  7.6 1.3 %collective-permute-start.1 = (f32[4,8,256]{2,1,0:T(8,128)S(1)}, f32[4,8,256]{2,1,0:T(8,128)S(1)}, u32[]{:S(2)}, u32[]{:S(2)}) collective-permute-start(f32[4,8,256]{2,1,0:T(8,128)S(1)} %get-tuple-element.17), channel_id=1, source_target_pairs={{8,0},{16,8},{24,16},{9,1},{17,9},{25,17},{10,2},{18,10},{26,18},{... | collective-permute-start | bytes 98312 | tf_op jit(solution)/shard_map/ppermute | solution.py:312
  8.9 0.0 collective-permute-done.north_ref
  8.9 3.9 %collective-permute-done.1.south_ref = f32[4,8,256]{2,1,0:T(8,128)S(1)} collective-permute-done((f32[4,8,256]{2,1,0:T(8,128)S(1)}, f32[4,8,256]{2,1,0:T(8,128)S(1)}, u32[]{:S(2)}, u32[]{:S(2)}) %collective-permute-start.1) | collective-permute-done | bytes 32800 | tf_op jit(solution)/shard_map/ppermute | solution.py:312
  12.9 0.1 edges.1
  13.0 1.5 %collective-permute-start.3 = (f32[144,128]{1,0:T(8,128)S(1)}, f32[144,128]{1,0:T(8,128)S(1)}, u32[]{:S(2)}, u32[]{:S(2)}) collective-permute-start(f32[144,128]{1,0:T(8,128)S(1)} %edges.1), channel_id=1, source_target_pairs={{0,1},{1,2},{2,3},{3,4},{4,5},{5,6},{6,7},{7,0},{8,9},{9,10},{10,1... | collective-permute-start | bytes 221192 | tf_op jit(solution)/shard_map/ppermute | solution.py:315
  14.5 3.2 %collective-permute-start.2 = (f32[144,128]{1,0:T(8,128)S(1)}, f32[144,128]{1,0:T(8,128)S(1)}, u32[]{:S(2)}, u32[]{:S(2)}) collective-permute-start(f32[144,128]{1,0:T(8,128)S(1)} %edges.1), channel_id=1, source_target_pairs={{1,0},{2,1},{3,2},{4,3},{5,4},{6,5},{7,6},{0,7},{9,8},{10,9},{11,1... | collective-permute-start | bytes 221192 | tf_op jit(solution)/shard_map/ppermute | solution.py:314
  17.7 2.4 %collective-permute-done.3.west_ref = f32[144,128]{1,0:T(8,128)S(1)} collective-permute-done((f32[144,128]{1,0:T(8,128)S(1)}, f32[144,128]{1,0:T(8,128)S(1)}, u32[]{:S(2)}, u32[]{:S(2)}) %collective-permute-start.3) | collective-permute-done | bytes 73760 | tf_op jit(solution)/shard_map/ppermute | solution.py:315
  20.1 0.0 collective-permute-done.2.east_ref
  20.1 0.0 copy-start
  20.1 1.0 %copy-done = f32[4,128,256]{2,1,0:T(8,128)S(1)} copy-done((f32[4,128,256]{2,1,0:T(8,128)S(1)}, f32[4,128,256]{2,1,0:T(8,128)}, u32[]{:S(2)}) %copy-start) | copy-done | bytes 524312
  21.1 2.1 %krylov.1 = (f32[4,128,256]{2,1,0:T(8,128)S(1)}, f32[5,128,256]{2,1,0:T(8,128)S(1)}, f32[8,128]{1,0:T(8,128)S(1)}) custom-call(f32[4,128,256]{2,1,0:T(8,128)S(1)} %copy-done, f32[4,8,256]{2,1,0:T(8,128)S(1)} %collective-permute-done.north_ref, f32[4,8,256]{2,1,0:T(8,128)S(1)} %collective-permute-done.1.south_ref, ...), custom_call_target="tpu_custom_call" | custom-call | tf_op jit(solution)/shard_map/krylov/pallas_call | solution.py:233
  23.2 1.6 %collective-permute-start.4 = (f32[8,128]{1,0:T(8,128)S(1)}, f32[8,128]{1,0:T(8,128)S(1)}, u32[]{:S(2)}, u32[]{:S(2)}) collective-permute-start(f32[8,128]{1,0:T(8,128)S(1)} %get-tuple-element.19), channel_id=1, source_target_pairs={{0,8},{8,0},{16,24},{24,16},{1,9},{9,1},{17,25},{25,17},{2,10},{10... | collective-permute-start | bytes 12296 | tf_op jit(solution)/shard_map/ppermute | solution.py:298
  24.8 0.8 %collective-permute-done.4 = f32[8,128]{1,0:T(8,128)S(1)} collective-permute-done((f32[8,128]{1,0:T(8,128)S(1)}, f32[8,128]{1,0:T(8,128)S(1)}, u32[]{:S(2)}, u32[]{:S(2)}) %collective-permute-start.4) | collective-permute-done | bytes 4128 | tf_op jit(solution)/shard_map/ppermute | solution.py:298
  25.6 1.3 %collective-permute-start.5 = (f32[8,128]{1,0:T(8,128)S(1)}, f32[8,128]{1,0:T(8,128)S(1)}, u32[]{:S(2)}, u32[]{:S(2)}) collective-permute-start(f32[8,128]{1,0:T(8,128)S(1)} %add.6), channel_id=1, source_target_pairs={{0,16},{8,24},{16,0},{24,8},{1,17},{9,25},{17,1},{25,9},{2,18},{10... | collective-permute-start | bytes 12296 | tf_op jit(solution)/shard_map/ppermute | solution.py:298
  26.9 2.3 %collective-permute-done.5 = f32[8,128]{1,0:T(8,128)S(1)} collective-permute-done((f32[8,128]{1,0:T(8,128)S(1)}, f32[8,128]{1,0:T(8,128)S(1)}, u32[]{:S(2)}, u32[]{:S(2)}) %collective-permute-start.5) | collective-permute-done | bytes 4128 | tf_op jit(solution)/shard_map/ppermute | solution.py:298
  29.2 0.6 %broadcast_dynamic-update-slice_fusion = f32[8,40,256]{2,1,0:T(8,128)} fusion(f32[8,40,256]{2,1,0:T(8,128)} %get-tuple-element.14, f32[8,128]{1,0:T(8,128)S(1)} %add.7), kind=kLoop, calls=%fused_computation | loop fusion | bytes 36864 | tf_op jit(solution)/shard_map/dynamic_update_slice | solution.py:318
  29.8 16.1 %all_to_all.5.arrived_ref = f32[8,40,256]{2,1,0:T(8,128)S(1)} all-to-all(f32[8,40,256]{2,1,0:T(8,128)} %broadcast_dynamic-update-slice_fusion), channel_id=1, replica_groups=mesh['lat'=4,'lon'=8] {'lon'}, dimensions={0} | all-to-all | bytes 655360 | tf_op jit(solution)/shard_map/all_to_all | solution.py:319
  45.9 1.1 %combine.1 = (f32[128,256]{1,0:T(8,128)}, f32[128,256]{1,0:T(8,128)}, f32[8,32,256]{2,1,0:T(8,128)}) custom-call(f32[8,40,256]{2,1,0:T(8,128)S(1)} %all_to_all.5.arrived_ref, f32[4,128,256]{2,1,0:T(8,128)S(1)} %get-tuple-element.20.w_ref, f32[5,128,256]{2,1,0:T(8,128)S(1)} %get-tuple-element.21.mw_ref), custom_call_target="tpu_custom_call" | custom-call | tf_op jit(solution)/shard_map/combine/pallas_call | solution.py:285
  (2 shorter events, 0.0 us)
Async XLA Ops:
  0.6 0.7 %copy-start.1 = (f32[16]{0:T(128)S(1)}, f32[16]{0:T(128)}, u32[]{:S(2)}) copy-start(f32[16]{0:T(128)} %thick_hbm.1) | copy-start | bytes 196
  1.3 0.7 %copy-start.2 = (s32[8,1]{0,1:T(1,128)S(1)}, s32[8,1]{0,1:T(1,128)}, u32[]{:S(2)}) copy-start(s32[8,1]{0,1:T(1,128)} %param.9) | copy-start | bytes 100
  5.3 3.7 %collective-permute-start = (f32[4,8,256]{2,1,0:T(8,128)S(1)}, f32[4,8,256]{2,1,0:T(8,128)S(1)}, u32[]{:S(2)}, u32[]{:S(2)}) collective-permute-start(f32[4,8,256]{2,1,0:T(8,128)S(1)} %get-tuple-element.16), channel_id=1, source_target_pairs={{0,8},{8,16},{16,24},{1,9},{9,17},{17,25},{2,10},{10,18},{18,26},{... | collective-permute-start | bytes 98312 | tf_op jit(solution)/shard_map/ppermute | solution.py:311
  7.6 5.2 %collective-permute-start.1 = (f32[4,8,256]{2,1,0:T(8,128)S(1)}, f32[4,8,256]{2,1,0:T(8,128)S(1)}, u32[]{:S(2)}, u32[]{:S(2)}) collective-permute-start(f32[4,8,256]{2,1,0:T(8,128)S(1)} %get-tuple-element.17), channel_id=1, source_target_pairs={{8,0},{16,8},{24,16},{9,1},{17,9},{25,17},{10,2},{18,10},{26,18},{... | collective-permute-start | bytes 98312 | tf_op jit(solution)/shard_map/ppermute | solution.py:312
  13.0 7.1 %collective-permute-start.3 = (f32[144,128]{1,0:T(8,128)S(1)}, f32[144,128]{1,0:T(8,128)S(1)}, u32[]{:S(2)}, u32[]{:S(2)}) collective-permute-start(f32[144,128]{1,0:T(8,128)S(1)} %edges.1), channel_id=1, source_target_pairs={{0,1},{1,2},{2,3},{3,4},{4,5},{5,6},{6,7},{7,0},{8,9},{9,10},{10,1... | collective-permute-start | bytes 221192 | tf_op jit(solution)/shard_map/ppermute | solution.py:315
  14.5 5.6 %collective-permute-start.2 = (f32[144,128]{1,0:T(8,128)S(1)}, f32[144,128]{1,0:T(8,128)S(1)}, u32[]{:S(2)}, u32[]{:S(2)}) collective-permute-start(f32[144,128]{1,0:T(8,128)S(1)} %edges.1), channel_id=1, source_target_pairs={{1,0},{2,1},{3,2},{4,3},{5,4},{6,5},{7,6},{0,7},{9,8},{10,9},{11,1... | collective-permute-start | bytes 221192 | tf_op jit(solution)/shard_map/ppermute | solution.py:314
  20.1 1.0 %copy-start = (f32[4,128,256]{2,1,0:T(8,128)S(1)}, f32[4,128,256]{2,1,0:T(8,128)}, u32[]{:S(2)}) copy-start(f32[4,128,256]{2,1,0:T(8,128)} %get-tuple-element.15.fields_ref) | copy-start | bytes 1572868
  23.2 2.4 %collective-permute-start.4 = (f32[8,128]{1,0:T(8,128)S(1)}, f32[8,128]{1,0:T(8,128)S(1)}, u32[]{:S(2)}, u32[]{:S(2)}) collective-permute-start(f32[8,128]{1,0:T(8,128)S(1)} %get-tuple-element.19), channel_id=1, source_target_pairs={{0,8},{8,0},{16,24},{24,16},{1,9},{9,1},{17,25},{25,17},{2,10},{10... | collective-permute-start | bytes 12296 | tf_op jit(solution)/shard_map/ppermute | solution.py:298
  25.6 3.6 %collective-permute-start.5 = (f32[8,128]{1,0:T(8,128)S(1)}, f32[8,128]{1,0:T(8,128)S(1)}, u32[]{:S(2)}, u32[]{:S(2)}) collective-permute-start(f32[8,128]{1,0:T(8,128)S(1)} %add.6), channel_id=1, source_target_pairs={{0,16},{8,24},{16,0},{24,8},{1,17},{9,25},{17,1},{25,9},{2,18},{10... | collective-permute-start | bytes 12296 | tf_op jit(solution)/shard_map/ppermute | solution.py:298

commit v6 on v5

v6 whole, which is shorter than its diff:
```python
import jax
import jax.numpy as jnp
from jax import lax
from jax.experimental import pallas as pl
from jax.experimental.pallas import tpu as pltpu
from jax.sharding import PartitionSpec as P

STEPS = 4
RIM = STEPS + 1
ROWS = 8
LANES = 128
HALF = LANES // 2
EAST = 48
SEAM = HALF + EAST
CHUNK = 32
FIELDS = 4
VMEM_BYTES = 16 * 1024 * 1024


def lanes_of(shape):
    return lax.broadcasted_iota(jnp.int32, shape, len(shape) - 1)


def turn(values, amount):
    amount = amount % values.shape[1]
    return pltpu.roll(values, amount, 1) if amount else values


def is_even(axis):
    return lax.rem(lax.axis_index(axis), 2) == 0


def pack_edges(ref, part):
    cols = ref.shape[2]
    packed = None
    for place in range(FIELDS):
        west = ref[place, part, :LANES]
        east = ref[place, part, cols - LANES :]
        if packed is None:
            lane = lanes_of(west.shape)
            packed = jnp.zeros(west.shape, jnp.float32)
        at = place * RIM
        packed = jnp.where((lane >= at) & (lane < at + RIM), turn(west, at), packed)
        at = HALF + place * RIM
        packed = jnp.where((lane >= at) & (lane < at + RIM), turn(east, at + RIM), packed)
    return packed


def integrate_kernel(
    thick_hbm,
    owner_hbm,
    count_hbm,
    inertia_hbm,
    tend_hbm,
    fields_ref,
    near_ref,
    far_ref,
    side_ref,
    sent_ref,
    thick_ref,
    owner_ref,
    count_ref,
    inertia_ref,
    tend_ref,
    small_sems,
    chunk_sems,
):
    levels, rows = tend_hbm.shape[1:3]
    span = (sent_ref.shape[1] - ROWS) // 2
    chunk = max(CHUNK, span)
    even = is_even("lat")
    small = [
        pltpu.make_async_copy(source, target, small_sems.at[place])
        for place, (source, target) in enumerate(
            (
                (thick_hbm, thick_ref),
                (owner_hbm, owner_ref),
                (count_hbm, count_ref),
                (inertia_hbm, inertia_ref),
            )
        )
    ]
    large = []
    for place in range(rows // chunk):
        part = pl.ds(place * chunk, chunk)
        large.append(
            pltpu.make_async_copy(
                tend_hbm.at[:, :, part], tend_ref.at[:, :, part], chunk_sems.at[place]
            )
        )
    for copy in small + large:
        copy.start()
    sent_ref[...] = jnp.zeros(sent_ref.shape, jnp.float32)
    for copy in small:
        copy.wait()
    for place, copy in enumerate(large):
        part = slice(place * chunk, (place + 1) * chunk)
        copy.wait()
        count = count_ref[part]
        first = jnp.zeros(count.shape, jnp.float32)
        second = jnp.zeros(count.shape, jnp.float32)
        depth = jnp.zeros(count.shape, jnp.float32)
        for level in range(levels):
            layer = jnp.where(count > level, thick_ref[level], 0.0)
            depth = depth + layer
            first = first + layer * tend_ref[0, level, part].astype(jnp.float32)
            second = second + layer * tend_ref[1, level, part].astype(jnp.float32)
        inertia = inertia_ref[part]
        for field, values in enumerate((first, second, depth, inertia)):
            fields_ref[field, part] = values
        side_ref[part] = pack_edges(fields_ref, part)
        for piece in range(chunk // span):
            target = owner_ref[place * (chunk // span) + piece]

            @pl.when(target >= 0)
            def _(target=target, piece=piece, first=first, second=second):
                rows_here = slice(piece * span, (piece + 1) * span)
                sent_ref[target, :span] = first[rows_here]
                sent_ref[target, span : 2 * span] = second[rows_here]

    for field in range(FIELDS):
        head = fields_ref[field, :ROWS]
        tail = fields_ref[field, rows - ROWS :]
        near_ref[field] = jnp.where(even, tail, head)
        far_ref[field] = jnp.where(even, head, tail)


def integrate(tendency, thickness, level_count, owner, inertia, lon_count):
    components, levels, rows, cols = tendency.shape
    span = rows // owner.shape[0]
    f32 = jnp.float32
    return pl.pallas_call(
        integrate_kernel,
        in_specs=[pl.BlockSpec(memory_space=pltpu.HBM)] * 5,
        out_shape=[
            jax.ShapeDtypeStruct((FIELDS, rows, cols), f32),
            jax.ShapeDtypeStruct((FIELDS, ROWS, cols), f32),
            jax.ShapeDtypeStruct((FIELDS, ROWS, cols), f32),
            jax.ShapeDtypeStruct((rows, LANES), f32),
            jax.ShapeDtypeStruct((lon_count, components * span + ROWS, cols), f32),
        ],
        scratch_shapes=[
            pltpu.SMEM(thickness.shape, f32),
            pltpu.SMEM(owner.shape, jnp.int32),
            pltpu.VMEM(level_count.shape, jnp.int32),
            pltpu.VMEM(inertia.shape, f32),
            pltpu.VMEM(tendency.shape, tendency.dtype),
            pltpu.SemaphoreType.DMA((4,)),
            pltpu.SemaphoreType.DMA((rows // max(CHUNK, span),)),
        ],
        cost_estimate=pl.CostEstimate(
            flops=6 * components * levels * rows * cols,
            bytes_accessed=2 * components * levels * rows * cols,
            transcendentals=0,
        ),
        name="integrate",
    )(thickness, owner, level_count, inertia, tendency)


def edges_kernel(side_ref, near_ref, far_ref, out_ref):
    rows = side_ref.shape[0]
    even = is_even("lat")
    near = pack_edges(near_ref, slice(None))
    far = pack_edges(far_ref, slice(None))
    out_ref[:ROWS] = jnp.where(even, far, near)
    out_ref[ROWS : ROWS + rows] = side_ref[...]
    out_ref[ROWS + rows :] = jnp.where(even, near, far)


def edges(side, near, far):
    rows = side.shape[0] + 2 * ROWS
    return pl.pallas_call(
        edges_kernel,
        out_shape=jax.ShapeDtypeStruct((rows, LANES), jnp.float32),
        name="edges",
    )(side, near, far)


def smooth(field):
    rows, cols = field.shape
    tall = field + 0.5 * (pltpu.roll(field, 1, 0) + pltpu.roll(field, rows - 1, 0))
    return tall + 0.5 * (pltpu.roll(tall, 1, 1) + pltpu.roll(tall, cols - 1, 1))


def basis(first, second, depth, inertia):
    tall, wide = first.shape
    own = slice(ROWS, tall - ROWS)
    inside = inertia > 0.0
    east_west = pltpu.roll(first, wide - 1, 1) - pltpu.roll(first, 1, 1)
    north_south = pltpu.roll(second, tall - 1, 0) - pltpu.roll(second, 1, 0)
    scaled = jnp.where(depth > 0.0, 0.5 * (east_west + north_south), 0.0)
    diag = inertia + 2.0 * depth + smooth(depth)
    inverse = jnp.where(inside, 1.0 / jnp.where(inside, diag, 1.0), 0.0)
    mws = [scaled[own]]
    ws = []
    vector = scaled * inverse
    for step in range(STEPS):
        ws.append(vector[own])
        weighed = depth * vector
        scaled = depth * smooth(vector) + smooth(weighed) - 2.0 * weighed
        mws.append(scaled[own])
        if step + 1 < STEPS:
            vector = scaled * inverse
    return ws, mws


def moments(ws, mws, mask):
    ws = [jnp.where(mask, values, 0.0) for values in ws]
    images = [mws[place] - mws[place + 1] for place in range(STEPS)]
    pairs = [ws[place] * mws[0] for place in range(STEPS)]
    for low in range(STEPS):
        for high in range(low, STEPS):
            pairs.append(ws[low] * images[high])
    lower = lanes_of((1, LANES)) < HALF
    lines = []
    for product in pairs:
        line = jnp.sum(product, axis=0, keepdims=True)
        total = line[:, :LANES]
        for start in range(LANES, line.shape[1], LANES):
            total = total + line[:, start : start + LANES]
        lines.append(total + turn(total, HALF))
    packed = [
        jnp.where(lower, lines[place], lines[place + 1]) for place in range(0, len(lines), 2)
    ]
    packed.append(jnp.zeros((ROWS - len(packed), LANES), jnp.float32))
    return jnp.concatenate(packed, axis=0)


def interior_kernel(fields_ref, near_ref, far_ref, w_ref, mw_ref, strip_ref, sums_ref):
    cols = fields_ref.shape[2]
    even = is_even("lat")
    lane = lanes_of((strip_ref.shape[1], LANES))
    padded = []
    for place in range(FIELDS):
        near = near_ref[place]
        far = far_ref[place]
        north = jnp.where(even, far, near)
        south = jnp.where(even, near, far)
        values = jnp.concatenate([north, fields_ref[place], south], axis=0)
        east = turn(values[:, cols - LANES :], SEAM)
        strip_ref[place] = jnp.where(lane < HALF, values[:, :LANES], east)
        padded.append(values)
    ws, mws = basis(*padded)
    for place, values in enumerate(ws):
        w_ref[place] = values
    for place, values in enumerate(mws):
        mw_ref[place] = values
    lane = lanes_of(ws[0].shape)
    sums_ref[...] = moments(ws, mws, (lane >= RIM) & (lane < cols - RIM))


def interior(fields, near, far):
    _, rows, cols = fields.shape
    f32 = jnp.float32
    return pl.pallas_call(
        interior_kernel,
        out_shape=[
            jax.ShapeDtypeStruct((STEPS, rows, cols), f32),
            jax.ShapeDtypeStruct((STEPS + 1, rows, cols), f32),
            jax.ShapeDtypeStruct((FIELDS, rows + 2 * ROWS, LANES), f32),
            jax.ShapeDtypeStruct((ROWS, LANES), f32),
        ],
        compiler_params=pltpu.CompilerParams(vmem_limit_bytes=VMEM_BYTES),
        cost_estimate=pl.CostEstimate(
            flops=300 * rows * cols, bytes_accessed=64 * rows * cols, transcendentals=0
        ),
        name="interior",
    )(fields, near, far)


def strip_kernel(strip_in_ref, near_ref, far_ref, inner_ref, w_ref, mw_ref, sums_ref):
    even = is_even("lon")
    near = near_ref[...]
    far = far_ref[...]
    from_east = jnp.where(even, near, far)
    from_west = jnp.where(even, far, near)
    lane = lanes_of(near.shape)
    padded = []
    for place in range(FIELDS):
        at = place * RIM
        east = turn(from_east, SEAM - at)
        west = turn(from_west, HALF - RIM - at)
        halo = jnp.where(lane < SEAM + RIM, east, jnp.where(lane >= LANES - RIM, west, 0.0))
        padded.append(jnp.where(lane < SEAM, strip_in_ref[place], halo))
    ws, mws = basis(*padded)
    for place, values in enumerate(ws):
        w_ref[place] = values
    for place, values in enumerate(mws):
        mw_ref[place] = values
    lane = lanes_of(ws[0].shape)
    edge = (lane < RIM) | ((lane >= SEAM - RIM) & (lane < SEAM))
    sums_ref[...] = inner_ref[...] + moments(ws, mws, edge)


def strip(strip_in, near, far, inner):
    rows = strip_in.shape[1] - 2 * ROWS
    f32 = jnp.float32
    return pl.pallas_call(
        strip_kernel,
        out_shape=[
            jax.ShapeDtypeStruct((STEPS, rows, LANES), f32),
            jax.ShapeDtypeStruct((STEPS + 1, rows, LANES), f32),
            jax.ShapeDtypeStruct((ROWS, LANES), f32),
        ],
        compiler_params=pltpu.CompilerParams(vmem_limit_bytes=VMEM_BYTES),
        name="strip",
    )(strip_in, near, far, inner)


def combine_kernel(
    arrived_ref, w_ref, mw_ref, w_edge_ref, mw_edge_ref, pressure_ref, residual_ref, held_ref
):
    held_ref[...] = arrived_ref[:, : held_ref.shape[1]]
    packed = jnp.sum(arrived_ref[:, held_ref.shape[1] :, :LANES], axis=0)
    lower = lanes_of(packed.shape) < HALF
    totals = (
        jnp.sum(jnp.where(lower, packed, 0.0), axis=1, keepdims=True),
        jnp.sum(jnp.where(lower, 0.0, packed), axis=1, keepdims=True),
    )
    entry = lambda place: totals[place % 2][place // 2 : place // 2 + 1, :]
    right = [entry(place) for place in range(STEPS)]
    matrix = {}
    place = STEPS
    for low in range(STEPS):
        for high in range(low, STEPS):
            matrix[low, high] = entry(place)
            place += 1
    for pivot in range(STEPS):
        inverse = 1.0 / matrix[pivot, pivot]
        for row in range(pivot + 1, STEPS):
            factor = matrix[pivot, row] * inverse
            for col in range(row, STEPS):
                matrix[row, col] = matrix[row, col] - factor * matrix[pivot, col]
            right[row] = right[row] - factor * right[pivot]
        matrix[pivot, pivot] = inverse
    for pivot in reversed(range(STEPS)):
        for col in range(pivot + 1, STEPS):
            right[pivot] = right[pivot] - matrix[pivot, col] * right[col]
        right[pivot] = right[pivot] * matrix[pivot, pivot]

    def results(w_ref, mw_ref):
        pressure = right[0] * w_ref[0]
        residual = mw_ref[0] - right[0] * (mw_ref[0] - mw_ref[1])
        for place in range(1, STEPS):
            pressure = pressure + right[place] * w_ref[place]
            residual = residual - right[place] * (mw_ref[place] - mw_ref[place + 1])
        return pressure, residual

    inner = results(w_ref, mw_ref)
    edge = results(w_edge_ref, mw_edge_ref)
    cols = pressure_ref.shape[1]
    lane = lanes_of(edge[0].shape)
    for out_ref, inside, border in zip((pressure_ref, residual_ref), inner, edge):
        out_ref[:, :LANES] = jnp.where(lane < RIM, border, inside[:, :LANES])
        if cols > 2 * LANES:
            out_ref[:, LANES : cols - LANES] = inside[:, LANES : cols - LANES]
        out_ref[:, cols - LANES :] = jnp.where(
            lane >= LANES - RIM, turn(border, -SEAM), inside[:, cols - LANES :]
        )


def combine(arrived, w, mw, w_edge, mw_edge):
    slots, rows, cols = arrived.shape
    shape = jax.ShapeDtypeStruct(w.shape[1:], jnp.float32)
    return pl.pallas_call(
        combine_kernel,
        out_shape=[shape, shape, jax.ShapeDtypeStruct((slots, rows - ROWS, cols), jnp.float32)],
        compiler_params=pltpu.CompilerParams(vmem_limit_bytes=VMEM_BYTES),
        name="combine",
    )(arrived, w, mw, w_edge, mw_edge)


def total_over(values, axis):
    count = lax.axis_size(axis)
    shift = 1
    while shift < count:
        pairs = [(place, place ^ shift) for place in range(count)]
        values = values + lax.ppermute(values, axis, pairs)
        shift *= 2
    return values


def swap(values, axis, first, ring):
    count = lax.axis_size(axis)
    pairs = []
    for place in range(first, count if ring else count - 1, 2):
        beside = (place + 1) % count
        pairs += [(place, beside), (beside, place)]
    return lax.ppermute(values, axis, pairs)


def on_device(tendency, thickness, level_count, block_mask, owner, inertia):
    lon_count = lax.axis_size("lon")
    fields, near, far, side, sent = integrate(
        tendency, thickness, level_count, owner[:, 0], inertia, lon_count
    )
    near = swap(near, "lat", 0, False)
    far = swap(far, "lat", 1, False)
    packed = edges(side, near, far)
    near_edge = swap(packed, "lon", 0, True)
    far_edge = swap(packed, "lon", 1, True)
    w, mw, strip_in, inner = interior(fields, near, far)
    w_edge, mw_edge, sums = strip(strip_in, near_edge, far_edge, inner)
    sums = jnp.broadcast_to(total_over(sums, "lat"), (lon_count,) + sums.shape)
    sent = lax.dynamic_update_slice(sent, sums, (0, sent.shape[1] - ROWS, 0))
    arrived = lax.all_to_all(sent, "lon", split_axis=0, concat_axis=0, tiled=True)
    pressure, residual, held = combine(arrived, w, mw, w_edge, mw_edge)
    held = held.reshape((1, 1, lon_count, 2, held.shape[1] // 2, held.shape[2]))
    return (held, pressure, residual)


def solution(mesh):
    return jax.shard_map(
        on_device,
        mesh=mesh,
        in_specs=(
            P(None, None, "lat", "lon"),
            P(),
            P("lat", "lon"),
            P("lat", "lon"),
            P("lat", "lon"),
            P("lat", "lon"),
        ),
        out_specs=(P("lat", "lon", None, None, None, None), P("lat", "lon"), P("lat", "lon")),
        check_vma=False,
    )
```

time: 47.3 us -> 44.1 us (0.932)
  waiting for transfers between devices: 9.46 us -> 3.36 us
  Pallas kernels: 6.53 us -> 8.41 us
  blocking collectives: 16.1 us -> 14.4 us
  starting transfers between devices: 11.3 us -> 13 us
  local copies, waits for them, and re-layouts: 2.97 us -> 3.8 us
    ppermute x4, waiting for transfers between devices: 6.32 us -> 0.95 us  [swap(): return lax.ppermute(values, axis, pairs)]
    ppermute x2, starting transfers between devices: 2.86 us -> 5.95 us  [total_over(): values = values + lax.ppermute(values, axis, pairs)]
    all_to_all x1, blocking collectives: 16.1 us -> 14.4 us  [on_device(): lax.all_to_all(sent, 'lon', split_axis=0, concat_axis=0, tiled=True)]
    pallas_call x1, Pallas kernels: 0.08 us -> 1.57 us  [edges(): pl.pallas_call(edges_kernel, out_shape=jax.ShapeDtypeStruct((rows, LANES)...]
    ppermute x4, starting transfers between devices: 8.4 us -> 7.05 us  [swap(): return lax.ppermute(values, axis, pairs)]
    unnamed x6 -> x10, local copies, waits for them, and re-layouts: 2.35 us -> 3.18 us
    ppermute x2, waiting for transfers between devices: 3.14 us -> 2.41 us  [total_over(): values = values + lax.ppermute(values, axis, pairs)]
    pallas_call x1 -> x2, Pallas kernels: 2.06 us -> 2.39 us  [the longest x1 1.45 us: interior(): pl.pallas_call(interior_kernel, out_shape=[jax.ShapeDtypeStruct((STEPS, r...]
  transfers between devices with their start and end apart: 6 -> 6, of which waited for: 4 -> 4; matrix products, arithmetic and copies ran while one was open for 0% -> 0% of each run, Pallas kernels for 0% -> 3%
where the time goes in v6:
time: 44.1 us; the launch traced here: 43.6 us
  blocking collectives  14.4 us (33%)
  starting transfers between devices  13 us (29%)
  Pallas kernels  8.41 us (19%)
  local copies, waits for them, and re-layouts  3.8 us (9%)
  waiting for transfers between devices  3.36 us (8%)
  between operations  0.68 us (2%)
    all_to_all x1, blocking collectives, on_device(): lax.all_to_all(sent, 'lon', split_axis=0, concat_axis=0, tiled=True)  14.4 us
    ppermute x4, starting transfers between devices, swap(): return lax.ppermute(values, axis, pairs)  7.05 us
    ppermute x2, starting transfers between devices, total_over(): values = values + lax.ppermute(values, axis, pairs)  5.95 us
    pallas_call x1, Pallas kernels, integrate(): pl.pallas_call(integrate_kernel, in_specs=[pl.BlockSpec(memory_space=pltp...  3.33 us
    unnamed x10, local copies, waits for them, and re-layouts  3.18 us
    ppermute x2, waiting for transfers between devices, total_over(): values = values + lax.ppermute(values, axis, pairs)  2.41 us
    pallas_call x1, Pallas kernels, edges(): pl.pallas_call(edges_kernel, out_shape=jax.ShapeDtypeStruct((rows, LANES)...  1.57 us
    pallas_call x1, Pallas kernels, interior(): pl.pallas_call(interior_kernel, out_shape=[jax.ShapeDtypeStruct((STEPS, r...  1.45 us
  transfers between devices with their start and end apart: 6, of which 4 were waited for; matrix products, arithmetic and copies ran while one was open for 0% of the time, Pallas kernels for 3%

profile of v6, /device:TPU:0, one launch (start us, length us, event | category | flops | bytes accessed | tf_op | source)
XLA Modules:
  0.0 43.6 jit_solution(15706252992444861725)
XLA Ops:
  0.6 3.3 %integrate.1 = (f32[4,128,256]{2,1,0:T(8,128)}, f32[4,8,256]{2,1,0:T(8,128)}, f32[4,8,256]{2,1,0:T(8,128)}, f32[128,128]{1,0:T(8,128)}, f32[8,40,256]{2,1,0:T(8,128)}) custom-call(f32[16]{0:T(128)} %thick_hbm.1, s32[8]{0:T(128)} %bitcast.2, s32[128,256]{1,0:T(8,128)} %count_hbm.1, f32[128,256]{1,0:T(8,128)} %inertia_hbm.1, bf16[2,16,128,256]{3,2,1,0:T(8,128)(2,1)} %tend_hbm.1), custom_call_target="tpu_custom_call" | custom-call | flops 6291456 | bytes 2097152 | tf_op jit(solution)/shard_map/integrate/pallas_call | solution.py:132
  4.0 0.5 %collective-permute-start = (f32[4,8,256]{2,1,0:T(8,128)}, f32[4,8,256]{2,1,0:T(8,128)S(1)}, u32[]{:S(2)}, u32[]{:S(2)}) collective-permute-start(f32[4,8,256]{2,1,0:T(8,128)} %get-tuple-element.20), channel_id=1, source_target_pairs={{0,8},{8,0},{16,24},{24,16},{1,9},{9,1},{17,25},{25,17},{2,10},{10... | collective-permute-start | bytes 98312 | tf_op jit(solution)/shard_map/ppermute | solution.py:389
  4.5 0.7 %collective-permute-start.1 = (f32[4,8,256]{2,1,0:T(8,128)}, f32[4,8,256]{2,1,0:T(8,128)S(1)}, u32[]{:S(2)}, u32[]{:S(2)}) collective-permute-start(f32[4,8,256]{2,1,0:T(8,128)} %get-tuple-element.21), channel_id=1, source_target_pairs={{8,16},{16,8},{9,17},{17,9},{10,18},{18,10},{11,19},{19,11},{12,20... | collective-permute-start | bytes 98312 | tf_op jit(solution)/shard_map/ppermute | solution.py:389
  5.1 0.4 collective-permute-done.near_ref
  5.6 0.0 copy-start.1
  5.6 0.0 collective-permute-done.1.far_ref
  5.6 0.0 copy-start.3
  5.6 0.6 %copy-done.1 = f32[4,8,256]{2,1,0:T(8,128)} copy-done((f32[4,8,256]{2,1,0:T(8,128)}, f32[4,8,256]{2,1,0:T(8,128)S(1)}, u32[]{:S(2)}) %copy-start.1) | copy-done | bytes 32792
  6.2 0.0 copy-done.3
  6.2 1.6 %edges.1 = f32[144,128]{1,0:T(8,128)} custom-call(f32[128,128]{1,0:T(8,128)} %get-tuple-element.23.side_ref, f32[4,8,256]{2,1,0:T(8,128)} %copy-done.1, f32[4,8,256]{2,1,0:T(8,128)} %copy-done.3), custom_call_target="tpu_custom_call" | custom-call | tf_op jit(solution)/shard_map/edges/pallas_call | solution.py:172
  7.8 5.9 %collective-permute-start.3 = (f32[144,128]{1,0:T(8,128)}, f32[144,128]{1,0:T(8,128)S(1)}, u32[]{:S(2)}, u32[]{:S(2)}) collective-permute-start(f32[144,128]{1,0:T(8,128)} %edges.1), channel_id=1, source_target_pairs={{1,2},{2,1},{3,4},{4,3},{5,6},{6,5},{7,0},{0,7},{9,10},{10,9},{11,... | collective-permute-start | bytes 221192 | tf_op jit(solution)/shard_map/ppermute | solution.py:389
  13.6 0.0 collective-permute-start.2
  13.6 0.0 copy-start
  13.6 1.0 %copy-done = f32[4,128,256]{2,1,0:T(8,128)S(1)} copy-done((f32[4,128,256]{2,1,0:T(8,128)S(1)}, f32[4,128,256]{2,1,0:T(8,128)}, u32[]{:S(2)}) %copy-start) | copy-done | bytes 524312
  14.7 0.0 copy-start.2
  14.7 0.8 %copy-done.2 = f32[4,8,256]{2,1,0:T(8,128)S(1)} copy-done((f32[4,8,256]{2,1,0:T(8,128)S(1)}, f32[4,8,256]{2,1,0:T(8,128)}, u32[]{:S(2)}) %copy-start.2) | copy-done | bytes 32792
  15.4 0.0 copy-start.4
  15.4 0.8 %copy-done.4 = f32[4,8,256]{2,1,0:T(8,128)S(1)} copy-done((f32[4,8,256]{2,1,0:T(8,128)S(1)}, f32[4,8,256]{2,1,0:T(8,128)}, u32[]{:S(2)}) %copy-start.4) | copy-done | bytes 32792
  16.2 1.5 %interior.1 = (f32[4,128,256]{2,1,0:T(8,128)S(1)}, f32[5,128,256]{2,1,0:T(8,128)S(1)}, f32[4,144,128]{2,1,0:T(8,128)S(1)}, f32[8,128]{1,0:T(8,128)S(1)}) custom-call(f32[4,128,256]{2,1,0:T(8,128)S(1)} %copy-done, f32[4,8,256]{2,1,0:T(8,128)S(1)} %copy-done.2, f32[4,8,256]{2,1,0:T(8,128)S(1)} %copy-done.4), custom_call_target="tpu_custom_call" | custom-call | flops 9830400 | bytes 2097152 | tf_op jit(solution)/shard_map/interior/pallas_call | solution.py:255
  17.7 0.0 collective-permute-done.3.far_ref
  17.7 0.5 %collective-permute-done.2.near_ref = f32[144,128]{1,0:T(8,128)S(1)} collective-permute-done((f32[144,128]{1,0:T(8,128)}, f32[144,128]{1,0:T(8,128)S(1)}, u32[]{:S(2)}, u32[]{:S(2)}) %collective-permute-start.2) | collective-permute-done | bytes 73760 | tf_op jit(solution)/shard_map/ppermute | solution.py:389
  18.2 0.9 %strip.1 = (f32[4,128,128]{2,1,0:T(8,128)S(1)}, f32[5,128,128]{2,1,0:T(8,128)S(1)}, f32[8,128]{1,0:T(8,128)S(1)}) custom-call(f32[4,144,128]{2,1,0:T(8,128)S(1)} %get-tuple-element.22.strip_in_ref, f32[144,128]{1,0:T(8,128)S(1)} %collective-permute-done.2.near_ref, f32[144,128]{1,0:T(8,128)S(1)} %collective-permute-done.3.far_ref, ...), custom_call_target="tpu_custom_call" | custom-call | tf_op jit(solution)/shard_map/strip/pallas_call | solution.py:298
  19.1 3.8 %collective-permute-start.4 = (f32[8,128]{1,0:T(8,128)S(1)}, f32[8,128]{1,0:T(8,128)S(1)}, u32[]{:S(2)}, u32[]{:S(2)}) collective-permute-start(f32[8,128]{1,0:T(8,128)S(1)} %get-tuple-element.25), channel_id=1, source_target_pairs={{0,8},{8,0},{16,24},{24,16},{1,9},{9,1},{17,25},{25,17},{2,10},{10... | collective-permute-start | bytes 12296 | tf_op jit(solution)/shard_map/ppermute | solution.py:378
  22.9 0.8 %collective-permute-done.4 = f32[8,128]{1,0:T(8,128)S(1)} collective-permute-done((f32[8,128]{1,0:T(8,128)S(1)}, f32[8,128]{1,0:T(8,128)S(1)}, u32[]{:S(2)}, u32[]{:S(2)}) %collective-permute-start.4) | collective-permute-done | bytes 4128 | tf_op jit(solution)/shard_map/ppermute | solution.py:378
  23.8 2.2 %collective-permute-start.5 = (f32[8,128]{1,0:T(8,128)S(1)}, f32[8,128]{1,0:T(8,128)S(1)}, u32[]{:S(2)}, u32[]{:S(2)}) collective-permute-start(f32[8,128]{1,0:T(8,128)S(1)} %add.6), channel_id=1, source_target_pairs={{0,16},{8,24},{16,0},{24,8},{1,17},{9,25},{17,1},{25,9},{2,18},{10... | collective-permute-start | bytes 12296 | tf_op jit(solution)/shard_map/ppermute | solution.py:378
  25.9 1.6 %collective-permute-done.5 = f32[8,128]{1,0:T(8,128)S(1)} collective-permute-done((f32[8,128]{1,0:T(8,128)S(1)}, f32[8,128]{1,0:T(8,128)S(1)}, u32[]{:S(2)}, u32[]{:S(2)}) %collective-permute-start.5) | collective-permute-done | bytes 4128 | tf_op jit(solution)/shard_map/ppermute | solution.py:378
  27.5 0.6 %broadcast_dynamic-update-slice_fusion = f32[8,40,256]{2,1,0:T(8,128)} fusion(f32[8,40,256]{2,1,0:T(8,128)} %get-tuple-element.18, f32[8,128]{1,0:T(8,128)S(1)} %add.7), kind=kLoop, calls=%fused_computation | loop fusion | bytes 36864 | tf_op jit(solution)/shard_map/dynamic_update_slice | solution.py:405
  28.1 14.4 %all_to_all.5.arrived_ref = f32[8,40,256]{2,1,0:T(8,128)S(1)} all-to-all(f32[8,40,256]{2,1,0:T(8,128)} %broadcast_dynamic-update-slice_fusion), channel_id=1, replica_groups=mesh['lat'=4,'lon'=8] {'lon'}, dimensions={0} | all-to-all | bytes 655360 | tf_op jit(solution)/shard_map/all_to_all | solution.py:406
  42.5 1.1 %combine.1 = (f32[128,256]{1,0:T(8,128)}, f32[128,256]{1,0:T(8,128)}, f32[8,32,256]{2,1,0:T(8,128)}) custom-call(f32[8,40,256]{2,1,0:T(8,128)S(1)} %all_to_all.5.arrived_ref, f32[4,128,256]{2,1,0:T(8,128)S(1)} %get-tuple-element.26.w_ref, f32[5,128,256]{2,1,0:T(8,128)S(1)} %get-tuple-element.27.mw_ref, f32[4,128,128]{2,1,0:T(8,128)S(1)} %get-tuple-element.28.w_edge_ref, ...), custom_call_target="tpu_custom_call" | custom-call | tf_op jit(solution)/shard_map/combine/pallas_call | solution.py:365
  (2 shorter events, 0.0 us)
Async XLA Ops:
  4.0 1.6 %collective-permute-start = (f32[4,8,256]{2,1,0:T(8,128)}, f32[4,8,256]{2,1,0:T(8,128)S(1)}, u32[]{:S(2)}, u32[]{:S(2)}) collective-permute-start(f32[4,8,256]{2,1,0:T(8,128)} %get-tuple-element.20), channel_id=1, source_target_pairs={{0,8},{8,0},{16,24},{24,16},{1,9},{9,1},{17,25},{25,17},{2,10},{10... | collective-permute-start | bytes 98312 | tf_op jit(solution)/shard_map/ppermute | solution.py:389
  4.5 1.1 %collective-permute-start.1 = (f32[4,8,256]{2,1,0:T(8,128)}, f32[4,8,256]{2,1,0:T(8,128)S(1)}, u32[]{:S(2)}, u32[]{:S(2)}) collective-permute-start(f32[4,8,256]{2,1,0:T(8,128)} %get-tuple-element.21), channel_id=1, source_target_pairs={{8,16},{16,8},{9,17},{17,9},{10,18},{18,10},{11,19},{19,11},{12,20... | collective-permute-start | bytes 98312 | tf_op jit(solution)/shard_map/ppermute | solution.py:389
  5.6 0.6 %copy-start.1 = (f32[4,8,256]{2,1,0:T(8,128)}, f32[4,8,256]{2,1,0:T(8,128)S(1)}, u32[]{:S(2)}) copy-start(f32[4,8,256]{2,1,0:T(8,128)S(1)} %collective-permute-done.near_ref) | copy-start | bytes 98308
  5.6 0.6 %copy-start.3 = (f32[4,8,256]{2,1,0:T(8,128)}, f32[4,8,256]{2,1,0:T(8,128)S(1)}, u32[]{:S(2)}) copy-start(f32[4,8,256]{2,1,0:T(8,128)S(1)} %collective-permute-done.1.far_ref) | copy-start | bytes 98308
  7.8 9.9 %collective-permute-start.3 = (f32[144,128]{1,0:T(8,128)}, f32[144,128]{1,0:T(8,128)S(1)}, u32[]{:S(2)}, u32[]{:S(2)}) collective-permute-start(f32[144,128]{1,0:T(8,128)} %edges.1), channel_id=1, source_target_pairs={{1,2},{2,1},{3,4},{4,3},{5,6},{6,5},{7,0},{0,7},{9,10},{10,9},{11,... | collective-permute-start | bytes 221192 | tf_op jit(solution)/shard_map/ppermute | solution.py:389
  13.6 4.6 %collective-permute-start.2 = (f32[144,128]{1,0:T(8,128)}, f32[144,128]{1,0:T(8,128)S(1)}, u32[]{:S(2)}, u32[]{:S(2)}) collective-permute-start(f32[144,128]{1,0:T(8,128)} %edges.1), channel_id=1, source_target_pairs={{0,1},{1,0},{2,3},{3,2},{4,5},{5,4},{6,7},{7,6},{8,9},{9,8},{10,11... | collective-permute-start | bytes 221192 | tf_op jit(solution)/shard_map/ppermute | solution.py:389
  13.6 1.0 %copy-start = (f32[4,128,256]{2,1,0:T(8,128)S(1)}, f32[4,128,256]{2,1,0:T(8,128)}, u32[]{:S(2)}) copy-start(f32[4,128,256]{2,1,0:T(8,128)} %get-tuple-element.19.fields_ref) | copy-start | bytes 1572868
  14.7 0.8 %copy-start.2 = (f32[4,8,256]{2,1,0:T(8,128)S(1)}, f32[4,8,256]{2,1,0:T(8,128)}, u32[]{:S(2)}) copy-start(f32[4,8,256]{2,1,0:T(8,128)} %copy-done.1) | copy-start | bytes 98308
  15.4 0.8 %copy-start.4 = (f32[4,8,256]{2,1,0:T(8,128)S(1)}, f32[4,8,256]{2,1,0:T(8,128)}, u32[]{:S(2)}) copy-start(f32[4,8,256]{2,1,0:T(8,128)} %copy-done.3) | copy-start | bytes 98308
  19.1 4.6 %collective-permute-start.4 = (f32[8,128]{1,0:T(8,128)S(1)}, f32[8,128]{1,0:T(8,128)S(1)}, u32[]{:S(2)}, u32[]{:S(2)}) collective-permute-start(f32[8,128]{1,0:T(8,128)S(1)} %get-tuple-element.25), channel_id=1, source_target_pairs={{0,8},{8,0},{16,24},{24,16},{1,9},{9,1},{17,25},{25,17},{2,10},{10... | collective-permute-start | bytes 12296 | tf_op jit(solution)/shard_map/ppermute | solution.py:378
  23.8 3.8 %collective-permute-start.5 = (f32[8,128]{1,0:T(8,128)S(1)}, f32[8,128]{1,0:T(8,128)S(1)}, u32[]{:S(2)}, u32[]{:S(2)}) collective-permute-start(f32[8,128]{1,0:T(8,128)S(1)} %add.6), channel_id=1, source_target_pairs={{0,16},{8,24},{16,0},{24,8},{1,17},{9,25},{17,1},{25,9},{2,18},{10... | collective-permute-start | bytes 12296 | tf_op jit(solution)/shard_map/ppermute | solution.py:378

commit v7 on v6

--- a/solution.py
+++ b/solution.py
@@ -1,3 +1,5 @@
+import functools
+
 import jax
 import jax.numpy as jnp
 from jax import lax
@@ -15,6 +17,7 @@
 CHUNK = 32
 FIELDS = 4
 VMEM_BYTES = 16 * 1024 * 1024
+MIDDLE_BYTES = 56450000
 
 
 def lanes_of(shape):
@@ -46,56 +49,52 @@
     return packed
 
 
-def integrate_kernel(
-    thick_hbm,
-    owner_hbm,
-    count_hbm,
-    inertia_hbm,
-    tend_hbm,
-    fields_ref,
-    near_ref,
-    far_ref,
-    side_ref,
-    sent_ref,
-    thick_ref,
-    owner_ref,
-    count_ref,
-    inertia_ref,
-    tend_ref,
-    small_sems,
-    chunk_sems,
-):
-    levels, rows = tend_hbm.shape[1:3]
-    span = (sent_ref.shape[1] - ROWS) // 2
-    chunk = max(CHUNK, span)
+def integrate_kernel(bands, outer, thick_hbm, count_hbm, inertia_hbm, tend_hbm, *refs):
+    if outer:
+        fields_ref, side_ref, near_ref, far_ref = refs[:4]
+        above = 0
+    else:
+        outer_side_hbm, fields_ref, side_ref = refs[:3]
+        above = outer_side_hbm.shape[0] // 2
+    thick_ref, count_ref, inertia_ref, tend_ref, thick_sem, small_sems, large_sems = refs[-7:]
+    levels = tend_hbm.shape[1]
     even = is_even("lat")
-    small = [
-        pltpu.make_async_copy(source, target, small_sems.at[place])
-        for place, (source, target) in enumerate(
-            (
-                (thick_hbm, thick_ref),
-                (owner_hbm, owner_ref),
-                (count_hbm, count_ref),
-                (inertia_hbm, inertia_ref),
+    copies = [[pltpu.make_async_copy(thick_hbm, thick_ref, thick_sem)]]
+    start = 0
+    for place, (row, size) in enumerate(bands):
+        there = pl.ds(row, size)
+        here = pl.ds(start, size)
+        count_copy = pltpu.make_async_copy(
+            count_hbm.at[there], count_ref.at[here], small_sems.at[0, place]
+        )
+        inertia_copy = pltpu.make_async_copy(
+            inertia_hbm.at[there], inertia_ref.at[here], small_sems.at[1, place]
+        )
+        tend_copy = pltpu.make_async_copy(
+            tend_hbm.at[:, :, there], tend_ref.at[:, :, here], large_sems.at[place]
+        )
+        copies.append([count_copy, inertia_copy, tend_copy])
+        start += size
+    if not outer:
+        for place, row in enumerate((0, above + start)):
+            copies.append(
+                [
+                    pltpu.make_async_copy(
+                        outer_side_hbm.at[pl.ds(place * above, above)],
+                        side_ref.at[pl.ds(row, above)],
+                        small_sems.at[place, len(bands)],
+                    )
+                ]
             )
-        )
-    ]
-    large = []
-    for place in range(rows // chunk):
-        part = pl.ds(place * chunk, chunk)
-        large.append(
-            pltpu.make_async_copy(
-                tend_hbm.at[:, :, part], tend_ref.at[:, :, part], chunk_sems.at[place]
-            )
-        )
-    for copy in small + large:
-        copy.start()
-    sent_ref[...] = jnp.zeros(sent_ref.shape, jnp.float32)
-    for copy in small:
-        copy.wait()
-    for place, copy in enumerate(large):
-        part = slice(place * chunk, (place + 1) * chunk)
-        copy.wait()
+    for group in copies:
+        for copy in group:
+            copy.start()
+    copies[0][0].wait()
+    start = 0
+    for place, (row, size) in enumerate(bands):
+        part = slice(start, start + size)
+        for copy in copies[place + 1]:
+            copy.wait()
         count = count_ref[part]
         first = jnp.zeros(count.shape, jnp.float32)
         second = jnp.zeros(count.shape, jnp.float32)
@@ -105,56 +104,53 @@
             depth = depth + layer
             first = first + layer * tend_ref[0, level, part].astype(jnp.float32)
             second = second + layer * tend_ref[1, level, part].astype(jnp.float32)
-        inertia = inertia_ref[part]
-        for field, values in enumerate((first, second, depth, inertia)):
+        for field, values in enumerate((first, second, depth, inertia_ref[part])):
             fields_ref[field, part] = values
-        side_ref[part] = pack_edges(fields_ref, part)
-        for piece in range(chunk // span):
-            target = owner_ref[place * (chunk // span) + piece]
-
-            @pl.when(target >= 0)
-            def _(target=target, piece=piece, first=first, second=second):
-                rows_here = slice(piece * span, (piece + 1) * span)
-                sent_ref[target, :span] = first[rows_here]
-                sent_ref[target, span : 2 * span] = second[rows_here]
-
-    for field in range(FIELDS):
-        head = fields_ref[field, :ROWS]
-        tail = fields_ref[field, rows - ROWS :]
-        near_ref[field] = jnp.where(even, tail, head)
-        far_ref[field] = jnp.where(even, head, tail)
-
-
-def integrate(tendency, thickness, level_count, owner, inertia, lon_count):
-    components, levels, rows, cols = tendency.shape
-    span = rows // owner.shape[0]
+        side_ref[above + start : above + start + size] = pack_edges(fields_ref, part)
+        start += size
+    for group in copies[len(bands) + 1 :]:
+        for copy in group:
+            copy.wait()
+    if outer:
+        for field in range(FIELDS):
+            head = fields_ref[field, :ROWS]
+            tail = fields_ref[field, start - ROWS :]
+            near_ref[field] = jnp.where(even, tail, head)
+            far_ref[field] = jnp.where(even, head, tail)
+
+
+def integrate(tendency, thickness, level_count, inertia, bands, outer_side=None):
+    outer = outer_side is None
+    around = [] if outer else [outer_side]
+    components, levels, _, cols = tendency.shape
+    rows = sum(size for _, size in bands)
     f32 = jnp.float32
+    halo = jax.ShapeDtypeStruct((FIELDS, ROWS, cols), f32)
     return pl.pallas_call(
-        integrate_kernel,
-        in_specs=[pl.BlockSpec(memory_space=pltpu.HBM)] * 5,
+        functools.partial(integrate_kernel, bands, outer),
+        in_specs=[pl.BlockSpec(memory_space=pltpu.HBM)] * (4 + len(around)),
         out_shape=[
             jax.ShapeDtypeStruct((FIELDS, rows, cols), f32),
-            jax.ShapeDtypeStruct((FIELDS, ROWS, cols), f32),
-            jax.ShapeDtypeStruct((FIELDS, ROWS, cols), f32),
-            jax.ShapeDtypeStruct((rows, LANES), f32),
-            jax.ShapeDtypeStruct((lon_count, components * span + ROWS, cols), f32),
-        ],
+            jax.ShapeDtypeStruct((rows + sum(x.shape[0] for x in around), LANES), f32),
+        ]
+        + ([halo, halo] if outer else []),
         scratch_shapes=[
             pltpu.SMEM(thickness.shape, f32),
-            pltpu.SMEM(owner.shape, jnp.int32),
-            pltpu.VMEM(level_count.shape, jnp.int32),
-            pltpu.VMEM(inertia.shape, f32),
-            pltpu.VMEM(tendency.shape, tendency.dtype),
-            pltpu.SemaphoreType.DMA((4,)),
-            pltpu.SemaphoreType.DMA((rows // max(CHUNK, span),)),
+            pltpu.VMEM((rows, cols), jnp.int32),
+            pltpu.VMEM((rows, cols), f32),
+            pltpu.VMEM((components, levels, rows, cols), tendency.dtype),
+            pltpu.SemaphoreType.DMA,
+            pltpu.SemaphoreType.DMA((2, len(bands) + 1)),
+            pltpu.SemaphoreType.DMA((len(bands),)),
         ],
         cost_estimate=pl.CostEstimate(
             flops=6 * components * levels * rows * cols,
             bytes_accessed=2 * components * levels * rows * cols,
             transcendentals=0,
         ),
-        name="integrate",
-    )(thickness, owner, level_count, inertia, tendency)
+        compiler_params=None if outer else pltpu.CompilerParams(vmem_limit_bytes=MIDDLE_BYTES),
+        name="outer" if outer else "middle",
+    )(thickness, level_count, inertia, tendency, *around)
 
 
 def edges_kernel(side_ref, near_ref, far_ref, out_ref):
@@ -172,6 +168,7 @@
     return pl.pallas_call(
         edges_kernel,
         out_shape=jax.ShapeDtypeStruct((rows, LANES), jnp.float32),
+        compiler_params=pltpu.CompilerParams(vmem_limit_bytes=VMEM_BYTES),
         name="edges",
     )(side, near, far)
 
@@ -226,20 +223,50 @@
     return jnp.concatenate(packed, axis=0)
 
 
-def interior_kernel(fields_ref, near_ref, far_ref, w_ref, mw_ref, strip_ref, sums_ref):
-    cols = fields_ref.shape[2]
+def interior_kernel(
+    owner_ref,
+    outer_ref,
+    middle_ref,
+    near_ref,
+    far_ref,
+    w_ref,
+    mw_ref,
+    strip_ref,
+    sums_ref,
+    sent_ref,
+):
+    half = outer_ref.shape[1] // 2
+    cols = outer_ref.shape[2]
     even = is_even("lat")
     lane = lanes_of((strip_ref.shape[1], LANES))
     padded = []
     for place in range(FIELDS):
         near = near_ref[place]
         far = far_ref[place]
-        north = jnp.where(even, far, near)
-        south = jnp.where(even, near, far)
-        values = jnp.concatenate([north, fields_ref[place], south], axis=0)
+        values = jnp.concatenate(
+            [
+                jnp.where(even, far, near),
+                outer_ref[place, :half],
+                middle_ref[place],
+                outer_ref[place, half:],
+                jnp.where(even, near, far),
+            ],
+            axis=0,
+        )
         east = turn(values[:, cols - LANES :], SEAM)
         strip_ref[place] = jnp.where(lane < HALF, values[:, :LANES], east)
         padded.append(values)
+    span = (sent_ref.shape[1] - ROWS) // 2
+    sent_ref[...] = jnp.zeros(sent_ref.shape, jnp.float32)
+    for block in range(owner_ref.shape[0]):
+        target = owner_ref[block]
+        rows = slice(ROWS + block * span, ROWS + (block + 1) * span)
+
+        @pl.when(target >= 0)
+        def _(target=target, rows=rows):
+            sent_ref[target, :span] = padded[0][rows]
+            sent_ref[target, span : 2 * span] = padded[1][rows]
+
     ws, mws = basis(*padded)
     for place, values in enumerate(ws):
         w_ref[place] = values
@@ -249,23 +276,28 @@
     sums_ref[...] = moments(ws, mws, (lane >= RIM) & (lane < cols - RIM))
 
 
-def interior(fields, near, far):
-    _, rows, cols = fields.shape
+def interior(owner, outer, middle, near, far, lon_count):
+    cols = outer.shape[2]
+    rows = outer.shape[1] + middle.shape[1]
+    span = rows // owner.shape[0]
     f32 = jnp.float32
     return pl.pallas_call(
         interior_kernel,
+        in_specs=[pl.BlockSpec(memory_space=pltpu.SMEM)]
+        + [pl.BlockSpec(memory_space=pltpu.VMEM)] * 4,
         out_shape=[
             jax.ShapeDtypeStruct((STEPS, rows, cols), f32),
             jax.ShapeDtypeStruct((STEPS + 1, rows, cols), f32),
             jax.ShapeDtypeStruct((FIELDS, rows + 2 * ROWS, LANES), f32),
             jax.ShapeDtypeStruct((ROWS, LANES), f32),
+            jax.ShapeDtypeStruct((lon_count, 2 * span + ROWS, cols), f32),
         ],
         compiler_params=pltpu.CompilerParams(vmem_limit_bytes=VMEM_BYTES),
         cost_estimate=pl.CostEstimate(
             flops=300 * rows * cols, bytes_accessed=64 * rows * cols, transcendentals=0
         ),
         name="interior",
-    )(fields, near, far)
+    )(owner, outer, middle, near, far)
 
 
 def strip_kernel(strip_in_ref, near_ref, far_ref, inner_ref, w_ref, mw_ref, sums_ref):
@@ -391,15 +423,18 @@
 
 def on_device(tendency, thickness, level_count, block_mask, owner, inertia):
     lon_count = lax.axis_size("lon")
-    fields, near, far, side, sent = integrate(
-        tendency, thickness, level_count, owner[:, 0], inertia, lon_count
-    )
+    rows = level_count.shape[0]
+    tall = min(CHUNK, rows // 4)
+    inputs = (tendency, thickness, level_count, inertia)
+    outer, outer_side, near, far = integrate(*inputs, ((0, tall), (rows - tall, tall)))
+    bands = tuple((row, tall) for row in range(tall, rows - tall, tall))
+    middle, side = integrate(*inputs, bands, outer_side)
     near = swap(near, "lat", 0, False)
     far = swap(far, "lat", 1, False)
     packed = edges(side, near, far)
     near_edge = swap(packed, "lon", 0, True)
     far_edge = swap(packed, "lon", 1, True)
-    w, mw, strip_in, inner = interior(fields, near, far)
+    w, mw, strip_in, inner, sent = interior(owner[:, 0], outer, middle, near, far, lon_count)
     w_edge, mw_edge, sums = strip(strip_in, near_edge, far_edge, inner)
     sums = jnp.broadcast_to(total_over(sums, "lat"), (lon_count,) + sums.shape)
     sent = lax.dynamic_update_slice(sent, sums, (0, sent.shape[1] - ROWS, 0))

time: 44.1 us -> 40.1 us (0.909)
  starting transfers between devices: 13 us -> 9.75 us
  local copies, waits for them, and re-layouts: 3.8 us -> 1.72 us
  waiting for transfers between devices: 3.36 us -> 4.39 us
  Pallas kernels: 8.41 us -> 8.98 us
    ppermute x2, starting transfers between devices: 5.95 us -> 2.98 us  [total_over(): values = values + lax.ppermute(values, axis, pairs)]
    pallas_call x2 -> x3, Pallas kernels: 4.78 us -> 6.81 us  [the longest x2 4.63 us: integrate(): pl.pallas_call(functools.partial(integrate_kernel, bands, outer), in_spec...]
    pallas_call x1, Pallas kernels: 1.57 us -> 0.08 us  [edges(): pl.pallas_call(edges_kernel, out_shape=jax.ShapeDtypeStruct((rows, LANES)...]
    unnamed x10, local copies, waits for them, and re-layouts: 3.18 us -> 1.71 us
    ppermute x4, waiting for transfers between devices: 0.95 us -> 1.98 us  [swap(): return lax.ppermute(values, axis, pairs)]
    dynamic_update_slice x1, local copies, waits for them, and re-layouts: 0.62 us -> 0.01 us  [on_device(): sent = lax.dynamic_update_slice(sent, sums, (0, sent.shape[1] - ROWS, 0))]
  transfers between devices with their start and end apart: 6 -> 6, of which waited for: 4 -> 3; matrix products, arithmetic and copies ran while one was open for 0% -> 0% of each run, Pallas kernels for 3% -> 11%
where the time goes in v7:
time: 40.1 us; the launch traced here: 39.8 us
  blocking collectives  14.2 us (35%)
  starting transfers between devices  9.75 us (24%)
  Pallas kernels  8.98 us (22%)
  waiting for transfers between devices  4.39 us (11%)
  local copies, waits for them, and re-layouts  1.72 us (4%)
  between operations  0.75 us (2%)
    all_to_all x1, blocking collectives, on_device(): lax.all_to_all(sent, 'lon', split_axis=0, concat_axis=0, tiled=True)  14.2 us
    ppermute x4, starting transfers between devices, swap(): return lax.ppermute(values, axis, pairs)  6.78 us
    pallas_call x2, Pallas kernels, integrate(): pl.pallas_call(functools.partial(integrate_kernel, bands, outer), in_spec...  4.63 us
    ppermute x2, starting transfers between devices, total_over(): values = values + lax.ppermute(values, axis, pairs)  2.98 us
    ppermute x2, waiting for transfers between devices, total_over(): values = values + lax.ppermute(values, axis, pairs)  2.41 us
    pallas_call x1, Pallas kernels, interior(): pl.pallas_call(interior_kernel, in_specs=[pl.BlockSpec(memory_space=pltpu...  2.19 us
    ppermute x4, waiting for transfers between devices, swap(): return lax.ppermute(values, axis, pairs)  1.98 us
    unnamed x10, local copies, waits for them, and re-layouts  1.71 us
  transfers between devices with their start and end apart: 6, of which 3 were waited for; matrix products, arithmetic and copies ran while one was open for 0% of the time, Pallas kernels for 11%

profile of v7, /device:TPU:0, one launch (start us, length us, event | category | flops | bytes accessed | tf_op | source)
XLA Modules:
  0.0 39.8 jit_solution(14042886524298402188)
XLA Ops:
  0.6 0.0 copy-start.3
  0.6 0.0 copy-start.4
  0.7 2.3 %outer.1 = (f32[4,64,256]{2,1,0:T(8,128)}, f32[64,128]{1,0:T(8,128)}, f32[4,8,256]{2,1,0:T(8,128)}, f32[4,8,256]{2,1,0:T(8,128)}) custom-call(f32[16]{0:T(128)} %thick_hbm.3, s32[128,256]{1,0:T(8,128)} %count_hbm.3, f32[128,256]{1,0:T(8,128)} %inertia_hbm.3, bf16[2,16,128,256]{3,2,1,0:T(8,128)(2,1)} %tend_hbm.3), custom_call_target="tpu_custom_call" | custom-call | flops 3145728 | bytes 1048576 | tf_op jit(solution)/shard_map/outer/pallas_call | solution.py:129
  3.0 0.0 copy-start
  3.0 0.5 %collective-permute-start = (f32[4,8,256]{2,1,0:T(8,128)}, f32[4,8,256]{2,1,0:T(8,128)S(1)}, u32[]{:S(2)}, u32[]{:S(2)}) collective-permute-start(f32[4,8,256]{2,1,0:T(8,128)} %get-tuple-element.23), channel_id=1, source_target_pairs={{0,8},{8,0},{16,24},{24,16},{1,9},{9,1},{17,25},{25,17},{2,10},{10... | collective-permute-start | bytes 98312 | tf_op jit(solution)/shard_map/ppermute | solution.py:421
  3.5 0.7 %collective-permute-start.1 = (f32[4,8,256]{2,1,0:T(8,128)}, f32[4,8,256]{2,1,0:T(8,128)S(1)}, u32[]{:S(2)}, u32[]{:S(2)}) collective-permute-start(f32[4,8,256]{2,1,0:T(8,128)} %get-tuple-element.24), channel_id=1, source_target_pairs={{8,16},{16,8},{9,17},{17,9},{10,18},{18,10},{11,19},{19,11},{12,20... | collective-permute-start | bytes 98312 | tf_op jit(solution)/shard_map/ppermute | solution.py:421
  4.2 0.0 copy-done.3
  4.2 0.0 copy-start.2
  4.2 0.7 %copy-done.2 = f32[64,128]{1,0:T(8,128)S(1)} copy-done((f32[64,128]{1,0:T(8,128)S(1)}, f32[64,128]{1,0:T(8,128)}, u32[]{:S(2)}) %copy-start.2) | copy-done | bytes 32792
  4.9 2.3 %middle.1 = (f32[4,64,256]{2,1,0:T(8,128)}, f32[128,128]{1,0:T(8,128)S(1)}) custom-call(f32[16]{0:T(128)S(1)} %copy-done.3, s32[128,256]{1,0:T(8,128)} %count_hbm.3, f32[128,256]{1,0:T(8,128)} %inertia_hbm.3, bf16[2,16,128,256]{3,2,1,0:T(8,128)(2,1)} %tend_hbm.3, f32[64,128]{1,0:T(8,128)S(1)} %copy-done.2), custom_call_target="tpu_custom_call" | custom-call | flops 3145728 | bytes 1048576 | tf_op jit(solution)/shard_map/middle/pallas_call | solution.py:129
  7.3 0.0 collective-permute-done.near_ref
  7.3 0.0 collective-permute-done.1.far_ref
  7.3 0.1 edges.1
  7.4 5.6 %collective-permute-start.3 = (f32[144,128]{1,0:T(8,128)S(1)}, f32[144,128]{1,0:T(8,128)S(1)}, u32[]{:S(2)}, u32[]{:S(2)}) collective-permute-start(f32[144,128]{1,0:T(8,128)S(1)} %edges.1), channel_id=1, source_target_pairs={{1,2},{2,1},{3,4},{4,3},{5,6},{6,5},{7,0},{0,7},{9,10},{10,9},{11,... | collective-permute-start | bytes 221192 | tf_op jit(solution)/shard_map/ppermute | solution.py:421
  13.0 0.0 collective-permute-start.2
  13.0 0.0 copy-done.4
  13.0 0.0 copy-done
  13.0 0.0 copy-start.1
  13.0 0.9 %copy-done.1 = f32[4,64,256]{2,1,0:T(8,128)S(1)} copy-done((f32[4,64,256]{2,1,0:T(8,128)S(1)}, f32[4,64,256]{2,1,0:T(8,128)}, u32[]{:S(2)}) %copy-start.1) | copy-done | bytes 262168
  13.9 2.2 %interior.1 = (f32[4,128,256]{2,1,0:T(8,128)S(1)}, f32[5,128,256]{2,1,0:T(8,128)S(1)}, f32[4,144,128]{2,1,0:T(8,128)S(1)}, f32[8,128]{1,0:T(8,128)S(1)}, f32[8,40,256]{2,1,0:T(8,128)S(1)}) custom-call(s32[8]{0:T(128)S(1)} %bitcast.2, f32[4,64,256]{2,1,0:T(8,128)S(1)} %copy-done, f32[4,64,256]{2,1,0:T(8,128)S(1)} %copy-done.1, ...), custom_call_target="tpu_custom_call" | custom-call | flops 9830400 | bytes 2097152 | tf_op jit(solution)/shard_map/interior/pallas_call | solution.py:284
  16.1 0.0 collective-permute-done.3.far_ref
  16.1 2.0 %collective-permute-done.2.near_ref = f32[144,128]{1,0:T(8,128)S(1)} collective-permute-done((f32[144,128]{1,0:T(8,128)S(1)}, f32[144,128]{1,0:T(8,128)S(1)}, u32[]{:S(2)}, u32[]{:S(2)}) %collective-permute-start.2) | collective-permute-done | bytes 73760 | tf_op jit(solution)/shard_map/ppermute | solution.py:421
  18.1 1.0 %strip.1 = (f32[4,128,128]{2,1,0:T(8,128)S(1)}, f32[5,128,128]{2,1,0:T(8,128)S(1)}, f32[8,128]{1,0:T(8,128)S(1)}) custom-call(f32[4,144,128]{2,1,0:T(8,128)S(1)} %get-tuple-element.26.strip_in_ref, f32[144,128]{1,0:T(8,128)S(1)} %collective-permute-done.2.near_ref, f32[144,128]{1,0:T(8,128)S(1)} %collective-permute-done.3.far_ref, ...), custom_call_target="tpu_custom_call" | custom-call | tf_op jit(solution)/shard_map/strip/pallas_call | solution.py:330
  19.1 0.7 %collective-permute-start.4 = (f32[8,128]{1,0:T(8,128)S(1)}, f32[8,128]{1,0:T(8,128)S(1)}, u32[]{:S(2)}, u32[]{:S(2)}) collective-permute-start(f32[8,128]{1,0:T(8,128)S(1)} %get-tuple-element.29), channel_id=1, source_target_pairs={{0,8},{8,0},{16,24},{24,16},{1,9},{9,1},{17,25},{25,17},{2,10},{10... | collective-permute-start | bytes 12296 | tf_op jit(solution)/shard_map/ppermute | solution.py:410
  19.8 0.8 %collective-permute-done.4 = f32[8,128]{1,0:T(8,128)S(1)} collective-permute-done((f32[8,128]{1,0:T(8,128)S(1)}, f32[8,128]{1,0:T(8,128)S(1)}, u32[]{:S(2)}, u32[]{:S(2)}) %collective-permute-start.4) | collective-permute-done | bytes 4128 | tf_op jit(solution)/shard_map/ppermute | solution.py:410
  20.6 2.3 %collective-permute-start.5 = (f32[8,128]{1,0:T(8,128)S(1)}, f32[8,128]{1,0:T(8,128)S(1)}, u32[]{:S(2)}, u32[]{:S(2)}) collective-permute-start(f32[8,128]{1,0:T(8,128)S(1)} %add.6), channel_id=1, source_target_pairs={{0,16},{8,24},{16,0},{24,8},{1,17},{9,25},{17,1},{25,9},{2,18},{10... | collective-permute-start | bytes 12296 | tf_op jit(solution)/shard_map/ppermute | solution.py:410
  22.9 1.6 %collective-permute-done.5 = f32[8,128]{1,0:T(8,128)S(1)} collective-permute-done((f32[8,128]{1,0:T(8,128)S(1)}, f32[8,128]{1,0:T(8,128)S(1)}, u32[]{:S(2)}, u32[]{:S(2)}) %collective-permute-start.5) | collective-permute-done | bytes 4128 | tf_op jit(solution)/shard_map/ppermute | solution.py:410
  24.5 14.2 %all_to_all.5.arrived_ref = f32[8,40,256]{2,1,0:T(8,128)S(1)} all-to-all(f32[8,40,256]{2,1,0:T(8,128)S(1)} %broadcast_dynamic-update-slice_fusion), channel_id=1, replica_groups=mesh['lat'=4,'lon'=8] {'lon'}, dimensions={0} | all-to-all | bytes 655360 | tf_op jit(solution)/shard_map/all_to_all | solution.py:441
  38.7 1.1 %combine.1 = (f32[128,256]{1,0:T(8,128)}, f32[128,256]{1,0:T(8,128)}, f32[8,32,256]{2,1,0:T(8,128)}) custom-call(f32[8,40,256]{2,1,0:T(8,128)S(1)} %all_to_all.5.arrived_ref, f32[4,128,256]{2,1,0:T(8,128)S(1)} %get-tuple-element.30.w_ref, f32[5,128,256]{2,1,0:T(8,128)S(1)} %get-tuple-element.31.mw_ref, f32[4,128,128]{2,1,0:T(8,128)S(1)} %get-tuple-element.32.w_edge_ref, ...), custom_call_target="tpu_custom_call" | custom-call | tf_op jit(solution)/shard_map/combine/pallas_call | solution.py:397
  (3 shorter events, 0.0 us)
Async XLA Ops:
  0.6 3.5 %copy-start.3 = (f32[16]{0:T(128)S(1)}, f32[16]{0:T(128)}, u32[]{:S(2)}) copy-start(f32[16]{0:T(128)} %thick_hbm.3) | copy-start | bytes 196
  0.6 12.3 %copy-start.4 = (s32[8,1]{0,1:T(1,128)S(1)}, s32[8,1]{0,1:T(1,128)}, u32[]{:S(2)}) copy-start(s32[8,1]{0,1:T(1,128)} %param.9) | copy-start | bytes 100
  3.0 10.0 %copy-start = (f32[4,64,256]{2,1,0:T(8,128)S(1)}, f32[4,64,256]{2,1,0:T(8,128)}, u32[]{:S(2)}) copy-start(f32[4,64,256]{2,1,0:T(8,128)} %get-tuple-element.20.outer_ref) | copy-start | bytes 786436
  3.0 4.3 %collective-permute-start = (f32[4,8,256]{2,1,0:T(8,128)}, f32[4,8,256]{2,1,0:T(8,128)S(1)}, u32[]{:S(2)}, u32[]{:S(2)}) collective-permute-start(f32[4,8,256]{2,1,0:T(8,128)} %get-tuple-element.23), channel_id=1, source_target_pairs={{0,8},{8,0},{16,24},{24,16},{1,9},{9,1},{17,25},{25,17},{2,10},{10... | collective-permute-start | bytes 98312 | tf_op jit(solution)/shard_map/ppermute | solution.py:421
  3.5 3.8 %collective-permute-start.1 = (f32[4,8,256]{2,1,0:T(8,128)}, f32[4,8,256]{2,1,0:T(8,128)S(1)}, u32[]{:S(2)}, u32[]{:S(2)}) collective-permute-start(f32[4,8,256]{2,1,0:T(8,128)} %get-tuple-element.24), channel_id=1, source_target_pairs={{8,16},{16,8},{9,17},{17,9},{10,18},{18,10},{11,19},{19,11},{12,20... | collective-permute-start | bytes 98312 | tf_op jit(solution)/shard_map/ppermute | solution.py:421
  4.2 0.8 %copy-start.2 = (f32[64,128]{1,0:T(8,128)S(1)}, f32[64,128]{1,0:T(8,128)}, u32[]{:S(2)}) copy-start(f32[64,128]{1,0:T(8,128)} %get-tuple-element.21.refs_0_) | copy-start | bytes 98308
  7.4 8.8 %collective-permute-start.3 = (f32[144,128]{1,0:T(8,128)S(1)}, f32[144,128]{1,0:T(8,128)S(1)}, u32[]{:S(2)}, u32[]{:S(2)}) collective-permute-start(f32[144,128]{1,0:T(8,128)S(1)} %edges.1), channel_id=1, source_target_pairs={{1,2},{2,1},{3,4},{4,3},{5,6},{6,5},{7,0},{0,7},{9,10},{10,9},{11,... | collective-permute-start | bytes 221192 | tf_op jit(solution)/shard_map/ppermute | solution.py:421
  13.0 5.1 %collective-permute-start.2 = (f32[144,128]{1,0:T(8,128)S(1)}, f32[144,128]{1,0:T(8,128)S(1)}, u32[]{:S(2)}, u32[]{:S(2)}) collective-permute-start(f32[144,128]{1,0:T(8,128)S(1)} %edges.1), channel_id=1, source_target_pairs={{0,1},{1,0},{2,3},{3,2},{4,5},{5,4},{6,7},{7,6},{8,9},{9,8},{10,11... | collective-permute-start | bytes 221192 | tf_op jit(solution)/shard_map/ppermute | solution.py:421
  13.0 1.0 %copy-start.1 = (f32[4,64,256]{2,1,0:T(8,128)S(1)}, f32[4,64,256]{2,1,0:T(8,128)}, u32[]{:S(2)}) copy-start(f32[4,64,256]{2,1,0:T(8,128)} %get-tuple-element.22.middle_ref) | copy-start | bytes 786436
  19.1 1.5 %collective-permute-start.4 = (f32[8,128]{1,0:T(8,128)S(1)}, f32[8,128]{1,0:T(8,128)S(1)}, u32[]{:S(2)}, u32[]{:S(2)}) collective-permute-start(f32[8,128]{1,0:T(8,128)S(1)} %get-tuple-element.29), channel_id=1, source_target_pairs={{0,8},{8,0},{16,24},{24,16},{1,9},{9,1},{17,25},{25,17},{2,10},{10... | collective-permute-start | bytes 12296 | tf_op jit(solution)/shard_map/ppermute | solution.py:410
  20.6 3.8 %collective-permute-start.5 = (f32[8,128]{1,0:T(8,128)S(1)}, f32[8,128]{1,0:T(8,128)S(1)}, u32[]{:S(2)}, u32[]{:S(2)}) collective-permute-start(f32[8,128]{1,0:T(8,128)S(1)} %add.6), channel_id=1, source_target_pairs={{0,16},{8,24},{16,0},{24,8},{1,17},{9,25},{17,1},{25,9},{2,18},{10... | collective-permute-start | bytes 12296 | tf_op jit(solution)/shard_map/ppermute | solution.py:410

commit v8 on v7

--- a/solution.py
+++ b/solution.py
@@ -12,10 +12,15 @@
 ROWS = 8
 LANES = 128
 HALF = LANES // 2
+QUARTER = LANES // 4
 EAST = 48
 SEAM = HALF + EAST
 CHUNK = 32
 FIELDS = 4
+GROUPS = 6
+PITCH = LANES // GROUPS
+TAIL = 16
+SUM_ROWS = 4
 VMEM_BYTES = 16 * 1024 * 1024
 MIDDLE_BYTES = 56450000
 
@@ -52,10 +57,8 @@
 def integrate_kernel(bands, outer, thick_hbm, count_hbm, inertia_hbm, tend_hbm, *refs):
     if outer:
         fields_ref, side_ref, near_ref, far_ref = refs[:4]
-        above = 0
     else:
-        outer_side_hbm, fields_ref, side_ref = refs[:3]
-        above = outer_side_hbm.shape[0] // 2
+        fields_ref, side_ref = refs[:2]
     thick_ref, count_ref, inertia_ref, tend_ref, thick_sem, small_sems, large_sems = refs[-7:]
     levels = tend_hbm.shape[1]
     even = is_even("lat")
@@ -75,17 +78,6 @@
         )
         copies.append([count_copy, inertia_copy, tend_copy])
         start += size
-    if not outer:
-        for place, row in enumerate((0, above + start)):
-            copies.append(
-                [
-                    pltpu.make_async_copy(
-                        outer_side_hbm.at[pl.ds(place * above, above)],
-                        side_ref.at[pl.ds(row, above)],
-                        small_sems.at[place, len(bands)],
-                    )
-                ]
-            )
     for group in copies:
         for copy in group:
             copy.start()
@@ -106,11 +98,8 @@
             second = second + layer * tend_ref[1, level, part].astype(jnp.float32)
         for field, values in enumerate((first, second, depth, inertia_ref[part])):
             fields_ref[field, part] = values
-        side_ref[above + start : above + start + size] = pack_edges(fields_ref, part)
+        side_ref[part] = pack_edges(fields_ref, part)
         start += size
-    for group in copies[len(bands) + 1 :]:
-        for copy in group:
-            copy.wait()
     if outer:
         for field in range(FIELDS):
             head = fields_ref[field, :ROWS]
@@ -119,19 +108,17 @@
             far_ref[field] = jnp.where(even, head, tail)
 
 
-def integrate(tendency, thickness, level_count, inertia, bands, outer_side=None):
-    outer = outer_side is None
-    around = [] if outer else [outer_side]
+def integrate(tendency, thickness, level_count, inertia, bands, outer):
     components, levels, _, cols = tendency.shape
     rows = sum(size for _, size in bands)
     f32 = jnp.float32
     halo = jax.ShapeDtypeStruct((FIELDS, ROWS, cols), f32)
     return pl.pallas_call(
         functools.partial(integrate_kernel, bands, outer),
-        in_specs=[pl.BlockSpec(memory_space=pltpu.HBM)] * (4 + len(around)),
+        in_specs=[pl.BlockSpec(memory_space=pltpu.HBM)] * 4,
         out_shape=[
             jax.ShapeDtypeStruct((FIELDS, rows, cols), f32),
-            jax.ShapeDtypeStruct((rows + sum(x.shape[0] for x in around), LANES), f32),
+            jax.ShapeDtypeStruct((rows, LANES), f32),
         ]
         + ([halo, halo] if outer else []),
         scratch_shapes=[
@@ -140,7 +127,7 @@
             pltpu.VMEM((rows, cols), f32),
             pltpu.VMEM((components, levels, rows, cols), tendency.dtype),
             pltpu.SemaphoreType.DMA,
-            pltpu.SemaphoreType.DMA((2, len(bands) + 1)),
+            pltpu.SemaphoreType.DMA((2, len(bands))),
             pltpu.SemaphoreType.DMA((len(bands),)),
         ],
         cost_estimate=pl.CostEstimate(
@@ -150,27 +137,48 @@
         ),
         compiler_params=None if outer else pltpu.CompilerParams(vmem_limit_bytes=MIDDLE_BYTES),
         name="outer" if outer else "middle",
-    )(thickness, level_count, inertia, tendency, *around)
-
-
-def edges_kernel(side_ref, near_ref, far_ref, out_ref):
-    rows = side_ref.shape[0]
-    even = is_even("lat")
+    )(thickness, level_count, inertia, tendency)
+
+
+def edges_kernel(outer_ref, middle_ref, near_ref, far_ref, near_out_ref, far_out_ref):
+    even_lat = is_even("lat")
+    even_lon = is_even("lon")
     near = pack_edges(near_ref, slice(None))
     far = pack_edges(far_ref, slice(None))
-    out_ref[:ROWS] = jnp.where(even, far, near)
-    out_ref[ROWS : ROWS + rows] = side_ref[...]
-    out_ref[ROWS + rows :] = jnp.where(even, near, far)
-
-
-def edges(side, near, far):
-    rows = side.shape[0] + 2 * ROWS
+    half = outer_ref.shape[0] // 2
+    packed = jnp.concatenate(
+        [
+            jnp.where(even_lat, far, near),
+            outer_ref[:half],
+            middle_ref[...],
+            outer_ref[half:],
+            jnp.where(even_lat, near, far),
+        ],
+        axis=0,
+    )
+    size = near_out_ref.shape[0]
+    lane = lanes_of(near_out_ref.shape)
+    west = jnp.zeros(near_out_ref.shape, jnp.float32)
+    east = jnp.zeros(near_out_ref.shape, jnp.float32)
+    for group in range(GROUPS):
+        rows = packed[group * size : (group + 1) * size]
+        at = group * PITCH
+        here = (lane >= at) & (lane < at + PITCH)
+        west = jnp.where(here, turn(rows, at), west)
+        east = jnp.where(here, turn(rows, at - HALF), east)
+    near_out_ref[...] = jnp.where(even_lon, east, west)
+    far_out_ref[...] = jnp.where(even_lon, west, east)
+
+
+def edges(outer, middle, near, far):
+    rows = outer.shape[0] + middle.shape[0] + 2 * ROWS
+    message = jax.ShapeDtypeStruct((rows // GROUPS, LANES), jnp.float32)
     return pl.pallas_call(
         edges_kernel,
-        out_shape=jax.ShapeDtypeStruct((rows, LANES), jnp.float32),
+        out_shape=[message, message],
         compiler_params=pltpu.CompilerParams(vmem_limit_bytes=VMEM_BYTES),
         name="edges",
-    )(side, near, far)
+    )(outer, middle, near, far)
 
 
 def smooth(field):
@@ -208,23 +216,26 @@
     for low in range(STEPS):
         for high in range(low, STEPS):
             pairs.append(ws[low] * images[high])
-    lower = lanes_of((1, LANES)) < HALF
     lines = []
     for product in pairs:
         line = jnp.sum(product, axis=0, keepdims=True)
         total = line[:, :LANES]
         for start in range(LANES, line.shape[1], LANES):
             total = total + line[:, start : start + LANES]
-        lines.append(total + turn(total, HALF))
-    packed = [
-        jnp.where(lower, lines[place], lines[place + 1]) for place in range(0, len(lines), 2)
-    ]
+        total = total + turn(total, HALF)
+        lines.append(total + turn(total, QUARTER))
+    quarter = lanes_of((1, LANES)) // QUARTER
+    packed = []
+    for start in range(0, len(lines), 4):
+        row = jnp.zeros((1, LANES), jnp.float32)
+        for place, line in enumerate(lines[start : start + 4]):
+            row = jnp.where(quarter == place, line, row)
+        packed.append(row)
     packed.append(jnp.zeros((ROWS - len(packed), LANES), jnp.float32))
     return jnp.concatenate(packed, axis=0)
 
 
 def interior_kernel(
-    owner_ref,
     outer_ref,
     middle_ref,
     near_ref,
@@ -233,7 +244,6 @@
     mw_ref,
     strip_ref,
     sums_ref,
-    sent_ref,
 ):
     half = outer_ref.shape[1] // 2
     cols = outer_ref.shape[2]
@@ -256,17 +266,6 @@
         east = turn(values[:, cols - LANES :], SEAM)
         strip_ref[place] = jnp.where(lane < HALF, values[:, :LANES], east)
         padded.append(values)
-    span = (sent_ref.shape[1] - ROWS) // 2
-    sent_ref[...] = jnp.zeros(sent_ref.shape, jnp.float32)
-    for block in range(owner_ref.shape[0]):
-        target = owner_ref[block]
-        rows = slice(ROWS + block * span, ROWS + (block + 1) * span)
-
-        @pl.when(target >= 0)
-        def _(target=target, rows=rows):
-            sent_ref[target, :span] = padded[0][rows]
-            sent_ref[target, span : 2 * span] = padded[1][rows]
-
     ws, mws = basis(*padded)
     for place, values in enumerate(ws):
         w_ref[place] = values
@@ -276,28 +275,24 @@
     sums_ref[...] = moments(ws, mws, (lane >= RIM) & (lane < cols - RIM))
 
 
-def interior(owner, outer, middle, near, far, lon_count):
+def interior(outer, middle, near, far):
     cols = outer.shape[2]
     rows = outer.shape[1] + middle.shape[1]
-    span = rows // owner.shape[0]
     f32 = jnp.float32
     return pl.pallas_call(
         interior_kernel,
-        in_specs=[pl.BlockSpec(memory_space=pltpu.SMEM)]
-        + [pl.BlockSpec(memory_space=pltpu.VMEM)] * 4,
         out_shape=[
             jax.ShapeDtypeStruct((STEPS, rows, cols), f32),
             jax.ShapeDtypeStruct((STEPS + 1, rows, cols), f32),
             jax.ShapeDtypeStruct((FIELDS, rows + 2 * ROWS, LANES), f32),
             jax.ShapeDtypeStruct((ROWS, LANES), f32),
-            jax.ShapeDtypeStruct((lon_count, 2 * span + ROWS, cols), f32),
         ],
         compiler_params=pltpu.CompilerParams(vmem_limit_bytes=VMEM_BYTES),
         cost_estimate=pl.CostEstimate(
             flops=300 * rows * cols, bytes_accessed=64 * rows * cols, transcendentals=0
         ),
         name="interior",
-    )(owner, outer, middle, near, far)
+    )(outer, middle, near, far)
 
 
 def strip_kernel(strip_in_ref, near_ref, far_ref, inner_ref, w_ref, mw_ref, sums_ref):
@@ -309,11 +304,15 @@
     lane = lanes_of(near.shape)
     padded = []
     for place in range(FIELDS):
-        at = place * RIM
-        east = turn(from_east, SEAM - at)
-        west = turn(from_west, HALF - RIM - at)
-        halo = jnp.where(lane < SEAM + RIM, east, jnp.where(lane >= LANES - RIM, west, 0.0))
-        padded.append(jnp.where(lane < SEAM, strip_in_ref[place], halo))
+        halo = []
+        for group in range(GROUPS):
+            at = group * PITCH + place * RIM
+            east = turn(from_east, SEAM - at)
+            west = turn(from_west, LANES - RIM - at)
+            west = jnp.where(lane >= LANES - RIM, west, 0.0)
+            halo.append(jnp.where(lane < SEAM + RIM, east, west))
+        halo = jnp.concatenate(halo, axis=0)
+        padded.append(jnp.where(lanes_of(halo.shape) < SEAM, strip_in_ref[place], halo))
     ws, mws = basis(*padded)
     for place, values in enumerate(ws):
         w_ref[place] = values
@@ -339,17 +338,118 @@
     )(strip_in, near, far, inner)
 
 
+def power(exponent):
+    size = jnp.abs(exponent)
+    value = jnp.ones(exponent.shape, jnp.float32)
+    for bit in range(7):
+        up, down = 2.0 ** (1 << bit), 2.0 ** -(1 << bit)
+        factor = jnp.where(exponent < 0, down, up)
+        value = value * jnp.where((size >> bit) & 1 == 1, factor, 1.0)
+    return value
+
+
+def exponent_of(size):
+    bits = jnp.ceil(jnp.log2(jnp.maximum(size, 2.0**-100)))
+    return jnp.clip(bits, -100.0, 100.0).astype(jnp.int32)
+
+
+def nearest(values):
+    return jnp.floor(values + 0.5)
+
+
+def place_kernel(owner_ref, outer_ref, middle_ref, sent_ref, scale_ref):
+    count = owner_ref.shape[0]
+    edge = outer_ref.shape[1] // 2
+    between = middle_ref.shape[1]
+    span = (2 * edge + between) // count
+    sent_ref[...] = jnp.zeros(sent_ref.shape, jnp.int16)
+    scale_ref[...] = jnp.zeros(scale_ref.shape, jnp.float32)
+    for block in range(count):
+        row = block * span
+        if row < edge:
+            ref, row = outer_ref, row
+        elif row < edge + between:
+            ref, row = middle_ref, row - edge
+        else:
+            ref, row = outer_ref, row - between
+        target = owner_ref[block]
+
+        @pl.when(target >= 0)
+        def _(ref=ref, row=row, target=target):
+            for half in range(ref.shape[2] // LANES):
+                cols = slice(half * LANES, (half + 1) * LANES)
+                rows = slice(row, row + span)
+                values = jnp.concatenate([ref[0, rows, cols], ref[1, rows, cols]], axis=0)
+                bits = exponent_of(jnp.max(jnp.abs(values), axis=0, keepdims=True))
+                whole = jnp.clip(nearest(values * power(15 - bits)), -32767.0, 32767.0)
+                there = slice(2 * span * half, 2 * span * (half + 1))
+                sent_ref[target, there] = whole.astype(jnp.int32).astype(jnp.int16)
+                scale_ref[target, half : half + 1] = bits.astype(jnp.float32)
+
+
+def place(owner, outer, middle, lon_count):
+    cols = outer.shape[2]
+    rows = outer.shape[1] + middle.shape[1]
+    span = rows // owner.shape[0]
+    return pl.pallas_call(
+        place_kernel,
+        in_specs=[pl.BlockSpec(memory_space=pltpu.SMEM)]
+        + [pl.BlockSpec(memory_space=pltpu.VMEM)] * 2,
+        out_shape=[
+            jax.ShapeDtypeStruct((lon_count, cols // LANES * 2 * span + TAIL, LANES), jnp.int16),
+            jax.ShapeDtypeStruct((lon_count, ROWS, LANES), jnp.float32),
+        ],
+        compiler_params=pltpu.CompilerParams(vmem_limit_bytes=VMEM_BYTES),
+        cost_estimate=pl.CostEstimate(
+            flops=60 * rows * cols, bytes_accessed=12 * rows * cols, transcendentals=0
+        ),
+        name="place",
+    )(owner, outer, middle)
+
+
+def seal_kernel(sums_ref, other_ref, scale_ref, tail_ref):
+    sums = sums_ref[:SUM_ROWS] + other_ref[:SUM_ROWS]
+    bits = exponent_of(jnp.abs(sums))
+    scaled = sums * power(-bits) * 2.0**14
+    high = nearest(scaled)
+    low = nearest((scaled - high) * 2.0**15)
+    parts = jnp.concatenate([bits.astype(jnp.float32), high, low], axis=0)
+    for slot in range(tail_ref.shape[0]):
+        tile = jnp.concatenate([parts, scale_ref[slot, : TAIL - 3 * SUM_ROWS]], axis=0)
+        tail_ref[slot] = tile.astype(jnp.int32).astype(jnp.int16)
+
+
+def seal(sums, other, scale):
+    return pl.pallas_call(
+        seal_kernel,
+        out_shape=jax.ShapeDtypeStruct((scale.shape[0], TAIL, LANES), jnp.int16),
+        compiler_params=pltpu.CompilerParams(vmem_limit_bytes=VMEM_BYTES),
+        name="seal",
+    )(sums, other, scale)
+
+
 def combine_kernel(
     arrived_ref, w_ref, mw_ref, w_edge_ref, mw_edge_ref, pressure_ref, residual_ref, held_ref
 ):
-    held_ref[...] = arrived_ref[:, : held_ref.shape[1]]
-    packed = jnp.sum(arrived_ref[:, held_ref.shape[1] :, :LANES], axis=0)
-    lower = lanes_of(packed.shape) < HALF
-    totals = (
-        jnp.sum(jnp.where(lower, packed, 0.0), axis=1, keepdims=True),
-        jnp.sum(jnp.where(lower, 0.0, packed), axis=1, keepdims=True),
-    )
-    entry = lambda place: totals[place % 2][place // 2 : place // 2 + 1, :]
+    rows = held_ref.shape[1]
+    packed = jnp.zeros((SUM_ROWS, LANES), jnp.float32)
+    for slot in range(held_ref.shape[0]):
+        tail = arrived_ref[slot, arrived_ref.shape[1] - TAIL :].astype(jnp.int32)
+        digits = tail.astype(jnp.float32)
+        high = digits[SUM_ROWS : 2 * SUM_ROWS]
+        low = digits[2 * SUM_ROWS : 3 * SUM_ROWS]
+        packed = packed + (high + low * 2.0**-15) * power(tail[:SUM_ROWS] - 14)
+        for half in range(held_ref.shape[2] // LANES):
+            at = 3 * SUM_ROWS + half
+            scale = power(tail[at : at + 1] - 15)
+            whole = arrived_ref[slot, half * rows : (half + 1) * rows].astype(jnp.int32)
+            held_ref[slot, :, half * LANES : (half + 1) * LANES] = whole.astype(jnp.float32) * scale
+    quarter = lanes_of(packed.shape) // QUARTER
+    totals = [
+        jnp.sum(jnp.where(quarter == place, packed, 0.0), axis=1, keepdims=True)
+        for place in range(4)
+    ]
+    entry = lambda place: totals[place % 4][place // 4 : place // 4 + 1, :]
     right = [entry(place) for place in range(STEPS)]
     matrix = {}
     place = STEPS
@@ -392,24 +492,20 @@
 
 
 def combine(arrived, w, mw, w_edge, mw_edge):
-    slots, rows, cols = arrived.shape
-    shape = jax.ShapeDtypeStruct(w.shape[1:], jnp.float32)
+    rows, cols = w.shape[1:]
+    shape = jax.ShapeDtypeStruct((rows, cols), jnp.float32)
+    held = (arrived.shape[0], (arrived.shape[1] - TAIL) * LANES // cols, cols)
     return pl.pallas_call(
         combine_kernel,
-        out_shape=[shape, shape, jax.ShapeDtypeStruct((slots, rows - ROWS, cols), jnp.float32)],
+        out_shape=[shape, shape, jax.ShapeDtypeStruct(held, jnp.float32)],
         compiler_params=pltpu.CompilerParams(vmem_limit_bytes=VMEM_BYTES),
         name="combine",
     )(arrived, w, mw, w_edge, mw_edge)
 
 
-def total_over(values, axis):
-    count = lax.axis_size(axis)
-    shift = 1
-    while shift < count:
-        pairs = [(place, place ^ shift) for place in range(count)]
-        values = values + lax.ppermute(values, axis, pairs)
-        shift *= 2
-    return values
+def exchange(values, axis, distance):
+    pairs = [(place, place ^ distance) for place in range(lax.axis_size(axis))]
+    return lax.ppermute(values, axis, pairs)
 
 
 def swap(values, axis, first, ring):
@@ -422,22 +518,28 @@
 
 
 def on_device(tendency, thickness, level_count, block_mask, owner, inertia):
+    lat_count = lax.axis_size("lat")
     lon_count = lax.axis_size("lon")
     rows = level_count.shape[0]
     tall = min(CHUNK, rows // 4)
     inputs = (tendency, thickness, level_count, inertia)
-    outer, outer_side, near, far = integrate(*inputs, ((0, tall), (rows - tall, tall)))
+    outer, outer_side, near, far = integrate(*inputs, ((0, tall), (rows - tall, tall)), True)
     bands = tuple((row, tall) for row in range(tall, rows - tall, tall))
-    middle, side = integrate(*inputs, bands, outer_side)
+    middle, middle_side = integrate(*inputs, bands, False)
     near = swap(near, "lat", 0, False)
     far = swap(far, "lat", 1, False)
-    packed = edges(side, near, far)
-    near_edge = swap(packed, "lon", 0, True)
-    far_edge = swap(packed, "lon", 1, True)
-    w, mw, strip_in, inner, sent = interior(owner[:, 0], outer, middle, near, far, lon_count)
+    near_edge, far_edge = edges(outer_side, middle_side, near, far)
+    near_edge = swap(near_edge, "lon", 0, True)
+    far_edge = swap(far_edge, "lon", 1, True)
+    w, mw, strip_in, inner = interior(outer, middle, near, far)
     w_edge, mw_edge, sums = strip(strip_in, near_edge, far_edge, inner)
-    sums = jnp.broadcast_to(total_over(sums, "lat"), (lon_count,) + sums.shape)
-    sent = lax.dynamic_update_slice(sent, sums, (0, sent.shape[1] - ROWS, 0))
+    sent, scale = place(owner[:, 0], outer, middle, lon_count)
+    shift = 1
+    while 2 * shift < lat_count:
+        sums = sums + exchange(sums, "lat", shift)
+        shift *= 2
+    tail = seal(sums, exchange(sums, "lat", shift), scale)
+    sent = lax.dynamic_update_slice(sent, tail, (0, sent.shape[1] - TAIL, 0))
     arrived = lax.all_to_all(sent, "lon", split_axis=0, concat_axis=0, tiled=True)
     pressure, residual, held = combine(arrived, w, mw, w_edge, mw_edge)
     held = held.reshape((1, 1, lon_count, 2, held.shape[1] // 2, held.shape[2]))

time: 40.1 us -> 37.4 us (0.933)
  waiting for transfers between devices: 4.39 us -> 1.11 us
  starting transfers between devices: 9.75 us -> 11.7 us
  blocking collectives: 14.2 us -> 12.3 us
    all_to_all x1, blocking collectives: 14.2 us -> 12.3 us  [on_device(): lax.all_to_all(sent, 'lon', split_axis=0, concat_axis=0, tiled=True)]
    ppermute x4, waiting for transfers between devices: 1.98 us -> 0.29 us  [swap(): return lax.ppermute(values, axis, pairs)]
    ppermute x2, waiting for transfers between devices: 2.41 us -> 0.83 us  [exchange(): return lax.ppermute(values, axis, pairs)]
    ppermute x2, starting transfers between devices: 2.98 us -> 4.37 us  [exchange(): return lax.ppermute(values, axis, pairs)]
    ppermute x4, starting transfers between devices: 6.78 us -> 7.29 us  [swap(): return lax.ppermute(values, axis, pairs)]
    pallas_call x2 -> x4, Pallas kernels: 2.27 us -> 2.56 us  [the longest x1 1.58 us: interior(): pl.pallas_call(interior_kernel, out_shape=[jax.ShapeDtypeStruct((STEPS, r...]
    unnamed x10 -> x12, local copies, waits for them, and re-layouts: 1.71 us -> 1.92 us
  transfers between devices with their start and end apart: 6 -> 6, of which waited for: 3 -> 2; matrix products, arithmetic and copies ran while one was open for 0% -> 0% of each run, Pallas kernels for 11% -> 12%
where the time goes in v8:
time: 37.4 us; the launch traced here: 37.1 us
  blocking collectives  12.3 us (33%)
  starting transfers between devices  11.7 us (31%)
  Pallas kernels  9.33 us (25%)
  local copies, waits for them, and re-layouts  1.93 us (5%)
  waiting for transfers between devices  1.11 us (3%)
  between operations  0.76 us (2%)
    all_to_all x1, blocking collectives, on_device(): lax.all_to_all(sent, 'lon', split_axis=0, concat_axis=0, tiled=True)  12.3 us
    ppermute x4, starting transfers between devices, swap(): return lax.ppermute(values, axis, pairs)  7.29 us
    pallas_call x2, Pallas kernels, integrate(): pl.pallas_call(functools.partial(integrate_kernel, bands, outer), in_spec...  4.55 us
    ppermute x2, starting transfers between devices, exchange(): return lax.ppermute(values, axis, pairs)  4.37 us
    unnamed x12, local copies, waits for them, and re-layouts  1.92 us
    pallas_call x1, Pallas kernels, interior(): pl.pallas_call(interior_kernel, out_shape=[jax.ShapeDtypeStruct((STEPS, r...  1.58 us
    pallas_call x1, Pallas kernels, combine(): pl.pallas_call(combine_kernel, out_shape=[shape, shape, jax.ShapeDtypeStr...  1.25 us
    pallas_call x1, Pallas kernels, strip(): pl.pallas_call(strip_kernel, out_shape=[jax.ShapeDtypeStruct((STEPS, rows...  0.97 us
  transfers between devices with their start and end apart: 6, of which 2 were waited for; matrix products, arithmetic and copies ran while one was open for 0% of the time, Pallas kernels for 12%

profile of v8, /device:TPU:0, one launch (start us, length us, event | category | flops | bytes accessed | tf_op | source)
XLA Modules:
  0.0 37.1 jit_solution(15046608526597364094)
XLA Ops:
  0.6 0.0 copy-start.4
  0.6 2.3 %outer.1 = (f32[4,64,256]{2,1,0:T(8,128)}, f32[64,128]{1,0:T(8,128)}, f32[4,8,256]{2,1,0:T(8,128)}, f32[4,8,256]{2,1,0:T(8,128)}) custom-call(f32[16]{0:T(128)} %thick_hbm.3, s32[128,256]{1,0:T(8,128)} %count_hbm.3, f32[128,256]{1,0:T(8,128)} %inertia_hbm.3, bf16[2,16,128,256]{3,2,1,0:T(8,128)(2,1)} %tend_hbm.3), custom_call_target="tpu_custom_call" | custom-call | flops 3145728 | bytes 1048576 | tf_op jit(solution)/shard_map/outer/pallas_call | solution.py:116
  2.9 0.0 copy-start.3
  2.9 0.0 copy-start
  3.0 0.0 copy-start.5
  3.0 0.5 %collective-permute-start = (f32[4,8,256]{2,1,0:T(8,128)}, f32[4,8,256]{2,1,0:T(8,128)S(1)}, u32[]{:S(2)}, u32[]{:S(2)}) collective-permute-start(f32[4,8,256]{2,1,0:T(8,128)} %get-tuple-element.26), channel_id=1, source_target_pairs={{0,8},{8,0},{16,24},{24,16},{1,9},{9,1},{17,25},{25,17},{2,10},{10... | collective-permute-start | bytes 98312 | tf_op jit(solution)/shard_map/ppermute | solution.py:517
  3.5 0.7 %collective-permute-start.1 = (f32[4,8,256]{2,1,0:T(8,128)}, f32[4,8,256]{2,1,0:T(8,128)S(1)}, u32[]{:S(2)}, u32[]{:S(2)}) collective-permute-start(f32[4,8,256]{2,1,0:T(8,128)} %get-tuple-element.27), channel_id=1, source_target_pairs={{8,16},{16,8},{9,17},{17,9},{10,18},{18,10},{11,19},{19,11},{12,20... | collective-permute-start | bytes 98312 | tf_op jit(solution)/shard_map/ppermute | solution.py:517
  4.1 0.0 copy-done.4
  4.2 2.3 %middle.1 = (f32[4,64,256]{2,1,0:T(8,128)}, f32[64,128]{1,0:T(8,128)S(1)}) custom-call(f32[16]{0:T(128)S(1)} %copy-done.4, s32[128,256]{1,0:T(8,128)} %count_hbm.3, f32[128,256]{1,0:T(8,128)} %inertia_hbm.3, bf16[2,16,128,256]{3,2,1,0:T(8,128)(2,1)} %tend_hbm.3), custom_call_target="tpu_custom_call" | custom-call | flops 3145728 | bytes 1048576 | tf_op jit(solution)/shard_map/middle/pallas_call | solution.py:116
  6.4 0.0 collective-permute-done.near_ref
  6.4 0.0 collective-permute-done.1.far_ref
  6.5 0.0 copy-done.3
  6.5 0.1 edges.1
  6.6 2.5 %collective-permute-start.2 = (f32[24,128]{1,0:T(8,128)S(1)}, f32[24,128]{1,0:T(8,128)S(1)}, u32[]{:S(2)}, u32[]{:S(2)}) collective-permute-start(f32[24,128]{1,0:T(8,128)S(1)} %get-tuple-element.31), channel_id=1, source_target_pairs={{0,1},{1,0},{2,3},{3,2},{4,5},{5,4},{6,7},{7,6},{8,9},{9,8},{10,11... | collective-permute-start | bytes 36872 | tf_op jit(solution)/shard_map/ppermute | solution.py:517
  9.2 3.6 %collective-permute-start.3 = (f32[24,128]{1,0:T(8,128)S(1)}, f32[24,128]{1,0:T(8,128)S(1)}, u32[]{:S(2)}, u32[]{:S(2)}) collective-permute-start(f32[24,128]{1,0:T(8,128)S(1)} %get-tuple-element.32), channel_id=1, source_target_pairs={{1,2},{2,1},{3,4},{4,3},{5,6},{6,5},{7,0},{0,7},{9,10},{10,9},{11,... | collective-permute-start | bytes 36872 | tf_op jit(solution)/shard_map/ppermute | solution.py:517
  12.7 0.0 copy-done
  12.7 0.0 copy-start.1
  12.7 0.9 %copy-done.1 = f32[4,64,256]{2,1,0:T(8,128)S(1)} copy-done((f32[4,64,256]{2,1,0:T(8,128)S(1)}, f32[4,64,256]{2,1,0:T(8,128)}, u32[]{:S(2)}) %copy-start.1) | copy-done | bytes 262168
  13.7 1.6 %interior.1 = (f32[4,128,256]{2,1,0:T(8,128)S(1)}, f32[5,128,256]{2,1,0:T(8,128)S(1)}, f32[4,144,128]{2,1,0:T(8,128)S(1)}, f32[8,128]{1,0:T(8,128)S(1)}) custom-call(f32[4,64,256]{2,1,0:T(8,128)S(1)} %copy-done, f32[4,64,256]{2,1,0:T(8,128)S(1)} %copy-done.1, f32[4,8,256]{2,1,0:T(8,128)S(1)} %collective-permute-done.near_ref, ...), custom_call_target="tpu_custom_call" | custom-call | flops 9830400 | bytes 2097152 | tf_op jit(solution)/shard_map/interior/pallas_call | solution.py:282
  15.3 0.0 collective-permute-done.2.near_ref
  15.3 0.3 collective-permute-done.3.far_ref
  15.5 1.0 %strip.1 = (f32[4,128,128]{2,1,0:T(8,128)S(1)}, f32[5,128,128]{2,1,0:T(8,128)S(1)}, f32[8,128]{1,0:T(8,128)S(1)}) custom-call(f32[4,144,128]{2,1,0:T(8,128)S(1)} %get-tuple-element.28.strip_in_ref, f32[24,128]{1,0:T(8,128)S(1)} %collective-permute-done.2.near_ref, f32[24,128]{1,0:T(8,128)S(1)} %collective-permute-done.3.far_ref, ...), custom_call_target="tpu_custom_call" | custom-call | tf_op jit(solution)/shard_map/strip/pallas_call | solution.py:329
  16.5 2.2 %collective-permute-start.4 = (f32[8,128]{1,0:T(8,128)S(1)}, f32[8,128]{1,0:T(8,128)S(1)}, u32[]{:S(2)}, u32[]{:S(2)}) collective-permute-start(f32[8,128]{1,0:T(8,128)S(1)} %get-tuple-element.34), channel_id=1, source_target_pairs={{0,8},{8,0},{16,24},{24,16},{1,9},{9,1},{17,25},{25,17},{2,10},{10... | collective-permute-start | bytes 12296 | tf_op jit(solution)/shard_map/ppermute | solution.py:508
  18.7 0.8 %collective-permute-done.4 = f32[8,128]{1,0:T(8,128)S(1)} collective-permute-done((f32[8,128]{1,0:T(8,128)S(1)}, f32[8,128]{1,0:T(8,128)S(1)}, u32[]{:S(2)}, u32[]{:S(2)}) %collective-permute-start.4) | collective-permute-done | bytes 4128 | tf_op jit(solution)/shard_map/ppermute | solution.py:508
  19.5 2.2 %collective-permute-start.5 = (f32[8,128]{1,0:T(8,128)S(1)}, f32[8,128]{1,0:T(8,128)S(1)}, u32[]{:S(2)}, u32[]{:S(2)}) collective-permute-start(f32[8,128]{1,0:T(8,128)S(1)} %add.3.sums_ref), channel_id=1, source_target_pairs={{0,16},{8,24},{16,0},{24,8},{1,17},{9,25},{17,1},{25,9},{2,18},{10... | collective-permute-start | bytes 12296 | tf_op jit(solution)/shard_map/ppermute | solution.py:508
  21.7 0.0 copy-done.5
  21.7 0.0 copy-start.2
  21.7 0.9 %copy-done.2 = f32[4,64,256]{2,1,0:T(8,128)S(1)} copy-done((f32[4,64,256]{2,1,0:T(8,128)S(1)}, f32[4,64,256]{2,1,0:T(8,128)}, u32[]{:S(2)}) %copy-start.2) | copy-done | bytes 262168
  22.7 0.8 %place.1 = (s16[8,80,128]{2,1,0:T(8,128)(2,1)S(1)}, f32[8,8,128]{2,1,0:T(8,128)S(1)}) custom-call(s32[8]{0:T(128)S(1)} %bitcast.2, f32[4,64,256]{2,1,0:T(8,128)S(1)} %copy-done, f32[4,64,256]{2,1,0:T(8,128)S(1)} %copy-done.2), custom_call_target="tpu_custom_call" | custom-call | flops 1966080 | bytes 393216 | tf_op jit(solution)/shard_map/place/pallas_call | solution.py:394
  23.5 0.0 collective-permute-done.5.other_ref
  23.5 12.3 %all_to_all.5.arrived_ref = s16[8,80,128]{2,1,0:T(8,128)(2,1)S(1)} all-to-all(s16[8,80,128]{2,1,0:T(8,128)(2,1)S(1)} %constant_dynamic-update-slice_fusion), channel_id=1, replica_groups=mesh['lat'=4,'lon'=8] {'lon'}, dimensions={0} | all-to-all | bytes 327680 | tf_op jit(solution)/shard_map/all_to_all | solution.py:543
  35.8 1.3 %combine.1 = (f32[128,256]{1,0:T(8,128)}, f32[128,256]{1,0:T(8,128)}, f32[8,32,256]{2,1,0:T(8,128)}) custom-call(s16[8,80,128]{2,1,0:T(8,128)(2,1)S(1)} %all_to_all.5.arrived_ref, f32[4,128,256]{2,1,0:T(8,128)S(1)} %get-tuple-element.36.w_ref, f32[5,128,256]{2,1,0:T(8,128)S(1)} %get-tuple-element.37.mw_ref, f32[4,128,128]{2,1,0:T(8,128)S(1)} %get-tuple-element.38.w_edge_ref, ...), custom_call_target="tpu_custom_call" | custom-call | tf_op jit(solution)/shard_map/combine/pallas_call | solution.py:498
  (3 shorter events, 0.1 us)
Async XLA Ops:
  0.6 3.5 %copy-start.4 = (f32[16]{0:T(128)S(1)}, f32[16]{0:T(128)}, u32[]{:S(2)}) copy-start(f32[16]{0:T(128)} %thick_hbm.3) | copy-start | bytes 196
  2.9 3.5 %copy-start.3 = (f32[64,128]{1,0:T(8,128)S(1)}, f32[64,128]{1,0:T(8,128)}, u32[]{:S(2)}) copy-start(f32[64,128]{1,0:T(8,128)} %get-tuple-element.29.outer_ref) | copy-start | bytes 98308
  2.9 9.8 %copy-start = (f32[4,64,256]{2,1,0:T(8,128)S(1)}, f32[4,64,256]{2,1,0:T(8,128)}, u32[]{:S(2)}) copy-start(f32[4,64,256]{2,1,0:T(8,128)} %get-tuple-element.23.outer_ref) | copy-start | bytes 786436
  3.0 18.8 %copy-start.5 = (s32[8,1]{0,1:T(1,128)S(1)}, s32[8,1]{0,1:T(1,128)}, u32[]{:S(2)}) copy-start(s32[8,1]{0,1:T(1,128)} %param.9) | copy-start | bytes 100
  3.0 3.5 %collective-permute-start = (f32[4,8,256]{2,1,0:T(8,128)}, f32[4,8,256]{2,1,0:T(8,128)S(1)}, u32[]{:S(2)}, u32[]{:S(2)}) collective-permute-start(f32[4,8,256]{2,1,0:T(8,128)} %get-tuple-element.26), channel_id=1, source_target_pairs={{0,8},{8,0},{16,24},{24,16},{1,9},{9,1},{17,25},{25,17},{2,10},{10... | collective-permute-start | bytes 98312 | tf_op jit(solution)/shard_map/ppermute | solution.py:517
  3.5 3.0 %collective-permute-start.1 = (f32[4,8,256]{2,1,0:T(8,128)}, f32[4,8,256]{2,1,0:T(8,128)S(1)}, u32[]{:S(2)}, u32[]{:S(2)}) collective-permute-start(f32[4,8,256]{2,1,0:T(8,128)} %get-tuple-element.27), channel_id=1, source_target_pairs={{8,16},{16,8},{9,17},{17,9},{10,18},{18,10},{11,19},{19,11},{12,20... | collective-permute-start | bytes 98312 | tf_op jit(solution)/shard_map/ppermute | solution.py:517
  6.6 8.7 %collective-permute-start.2 = (f32[24,128]{1,0:T(8,128)S(1)}, f32[24,128]{1,0:T(8,128)S(1)}, u32[]{:S(2)}, u32[]{:S(2)}) collective-permute-start(f32[24,128]{1,0:T(8,128)S(1)} %get-tuple-element.31), channel_id=1, source_target_pairs={{0,1},{1,0},{2,3},{3,2},{4,5},{5,4},{6,7},{7,6},{8,9},{9,8},{10,11... | collective-permute-start | bytes 36872 | tf_op jit(solution)/shard_map/ppermute | solution.py:517
  9.2 6.4 %collective-permute-start.3 = (f32[24,128]{1,0:T(8,128)S(1)}, f32[24,128]{1,0:T(8,128)S(1)}, u32[]{:S(2)}, u32[]{:S(2)}) collective-permute-start(f32[24,128]{1,0:T(8,128)S(1)} %get-tuple-element.32), channel_id=1, source_target_pairs={{1,2},{2,1},{3,4},{4,3},{5,6},{6,5},{7,0},{0,7},{9,10},{10,9},{11,... | collective-permute-start | bytes 36872 | tf_op jit(solution)/shard_map/ppermute | solution.py:517
  12.7 1.0 %copy-start.1 = (f32[4,64,256]{2,1,0:T(8,128)S(1)}, f32[4,64,256]{2,1,0:T(8,128)}, u32[]{:S(2)}) copy-start(f32[4,64,256]{2,1,0:T(8,128)} %get-tuple-element.24.middle_ref) | copy-start | bytes 786436
  16.5 3.0 %collective-permute-start.4 = (f32[8,128]{1,0:T(8,128)S(1)}, f32[8,128]{1,0:T(8,128)S(1)}, u32[]{:S(2)}, u32[]{:S(2)}) collective-permute-start(f32[8,128]{1,0:T(8,128)S(1)} %get-tuple-element.34), channel_id=1, source_target_pairs={{0,8},{8,0},{16,24},{24,16},{1,9},{9,1},{17,25},{25,17},{2,10},{10... | collective-permute-start | bytes 12296 | tf_op jit(solution)/shard_map/ppermute | solution.py:508
  19.5 3.9 %collective-permute-start.5 = (f32[8,128]{1,0:T(8,128)S(1)}, f32[8,128]{1,0:T(8,128)S(1)}, u32[]{:S(2)}, u32[]{:S(2)}) collective-permute-start(f32[8,128]{1,0:T(8,128)S(1)} %add.3.sums_ref), channel_id=1, source_target_pairs={{0,16},{8,24},{16,0},{24,8},{1,17},{9,25},{17,1},{25,9},{2,18},{10... | collective-permute-start | bytes 12296 | tf_op jit(solution)/shard_map/ppermute | solution.py:508
  21.7 1.0 %copy-start.2 = (f32[4,64,256]{2,1,0:T(8,128)S(1)}, f32[4,64,256]{2,1,0:T(8,128)}, u32[]{:S(2)}) copy-start(f32[4,64,256]{2,1,0:T(8,128)} %get-tuple-element.24.middle_ref) | copy-start | bytes 786436

commit v9 on v8

--- a/solution.py
+++ b/solution.py
@@ -19,6 +19,7 @@
 FIELDS = 4
 GROUPS = 6
 PITCH = LANES // GROUPS
+OUTER = 16
 TAIL = 16
 SUM_ROWS = 4
 VMEM_BYTES = 16 * 1024 * 1024
@@ -140,7 +141,7 @@
     )(thickness, level_count, inertia, tendency)
 
 
-def edges_kernel(outer_ref, middle_ref, near_ref, far_ref, near_out_ref, far_out_ref):
+def edges_kernel(outer_ref, middle_ref, far_ref, near_ref, near_out_ref, far_out_ref):
     even_lat = is_even("lat")
     even_lon = is_even("lon")
     near = pack_edges(near_ref, slice(None))
@@ -178,7 +179,7 @@
         out_shape=[message, message],
         compiler_params=pltpu.CompilerParams(vmem_limit_bytes=VMEM_BYTES),
         name="edges",
-    )(outer, middle, near, far)
+    )(outer, middle, far, near)
 
 
 def smooth(field):
@@ -238,8 +239,8 @@
 def interior_kernel(
     outer_ref,
     middle_ref,
+    far_ref,
     near_ref,
-    far_ref,
     w_ref,
     mw_ref,
     strip_ref,
@@ -292,10 +293,10 @@
             flops=300 * rows * cols, bytes_accessed=64 * rows * cols, transcendentals=0
         ),
         name="interior",
-    )(outer, middle, near, far)
-
-
-def strip_kernel(strip_in_ref, near_ref, far_ref, inner_ref, w_ref, mw_ref, sums_ref):
+    )(outer, middle, far, near)
+
+
+def strip_kernel(strip_in_ref, far_ref, near_ref, inner_ref, w_ref, mw_ref, sums_ref):
     even = is_even("lon")
     near = near_ref[...]
     far = far_ref[...]
@@ -335,7 +336,7 @@
         ],
         compiler_params=pltpu.CompilerParams(vmem_limit_bytes=VMEM_BYTES),
         name="strip",
-    )(strip_in, near, far, inner)
+    )(strip_in, far, near, inner)
 
 
 def power(exponent):
@@ -428,9 +429,7 @@
     )(sums, other, scale)
 
 
-def combine_kernel(
-    arrived_ref, w_ref, mw_ref, w_edge_ref, mw_edge_ref, pressure_ref, residual_ref, held_ref
-):
+def unpack_kernel(arrived_ref, held_ref, sums_ref):
     rows = held_ref.shape[1]
     packed = jnp.zeros((SUM_ROWS, LANES), jnp.float32)
     for slot in range(held_ref.shape[0]):
@@ -444,6 +443,27 @@
             scale = power(tail[at : at + 1] - 15)
             whole = arrived_ref[slot, half * rows : (half + 1) * rows].astype(jnp.int32)
             held_ref[slot, :, half * LANES : (half + 1) * LANES] = whole.astype(jnp.float32) * scale
+    sums_ref[:SUM_ROWS] = packed
+    sums_ref[SUM_ROWS:] = jnp.zeros((ROWS - SUM_ROWS, LANES), jnp.float32)
+
+
+def unpack(arrived, cols):
+    held = (arrived.shape[0], (arrived.shape[1] - TAIL) * LANES // cols, cols)
+    return pl.pallas_call(
+        unpack_kernel,
+        out_shape=[
+            jax.ShapeDtypeStruct(held, jnp.float32),
+            jax.ShapeDtypeStruct((ROWS, LANES), jnp.float32),
+        ],
+        compiler_params=pltpu.CompilerParams(vmem_limit_bytes=VMEM_BYTES),
+        name="unpack",
+    )(arrived)
+
+
+def combine_kernel(
+    sums_ref, other_ref, w_ref, mw_ref, w_edge_ref, mw_edge_ref, pressure_ref, residual_ref
+):
+    packed = jnp.where(is_even("lat"), other_ref[:SUM_ROWS], sums_ref[:SUM_ROWS])
     quarter = lanes_of(packed.shape) // QUARTER
     totals = [
         jnp.sum(jnp.where(quarter == place, packed, 0.0), axis=1, keepdims=True)
@@ -491,20 +511,18 @@
         )
 
 
-def combine(arrived, w, mw, w_edge, mw_edge):
-    rows, cols = w.shape[1:]
-    shape = jax.ShapeDtypeStruct((rows, cols), jnp.float32)
-    held = (arrived.shape[0], (arrived.shape[1] - TAIL) * LANES // cols, cols)
+def combine(sums, other, w, mw, w_edge, mw_edge):
+    shape = jax.ShapeDtypeStruct(w.shape[1:], jnp.float32)
     return pl.pallas_call(
         combine_kernel,
-        out_shape=[shape, shape, jax.ShapeDtypeStruct(held, jnp.float32)],
+        out_shape=[shape, shape],
         compiler_params=pltpu.CompilerParams(vmem_limit_bytes=VMEM_BYTES),
         name="combine",
-    )(arrived, w, mw, w_edge, mw_edge)
-
-
-def exchange(values, axis, distance):
-    pairs = [(place, place ^ distance) for place in range(lax.axis_size(axis))]
+    )(sums, other, w, mw, w_edge, mw_edge)
+
+
+def exchange_odd(values, axis, distance):
+    pairs = [(place, place ^ distance) for place in range(1, lax.axis_size(axis), 2)]
     return lax.ppermute(values, axis, pairs)
 
 
@@ -521,27 +539,32 @@
     lat_count = lax.axis_size("lat")
     lon_count = lax.axis_size("lon")
     rows = level_count.shape[0]
-    tall = min(CHUNK, rows // 4)
+    tall = OUTER
     inputs = (tendency, thickness, level_count, inertia)
     outer, outer_side, near, far = integrate(*inputs, ((0, tall), (rows - tall, tall)), True)
-    bands = tuple((row, tall) for row in range(tall, rows - tall, tall))
+    bands = tuple(
+        (row, min(CHUNK, rows - tall - row)) for row in range(tall, rows - tall, CHUNK)
+    )
     middle, middle_side = integrate(*inputs, bands, False)
+    far = swap(far, "lat", 1, False)
     near = swap(near, "lat", 0, False)
-    far = swap(far, "lat", 1, False)
     near_edge, far_edge = edges(outer_side, middle_side, near, far)
+    far_edge = swap(far_edge, "lon", 1, True)
     near_edge = swap(near_edge, "lon", 0, True)
-    far_edge = swap(far_edge, "lon", 1, True)
     w, mw, strip_in, inner = interior(outer, middle, near, far)
     w_edge, mw_edge, sums = strip(strip_in, near_edge, far_edge, inner)
     sent, scale = place(owner[:, 0], outer, middle, lon_count)
-    shift = 1
+    sums = sums + lax.ppermute(sums, "lat", [(p, p + 1) for p in range(0, lat_count, 2)])
+    shift = 2
     while 2 * shift < lat_count:
-        sums = sums + exchange(sums, "lat", shift)
+        sums = sums + exchange_odd(sums, "lat", shift)
         shift *= 2
-    tail = seal(sums, exchange(sums, "lat", shift), scale)
+    tail = seal(sums, exchange_odd(sums, "lat", shift), scale)
     sent = lax.dynamic_update_slice(sent, tail, (0, sent.shape[1] - TAIL, 0))
     arrived = lax.all_to_all(sent, "lon", split_axis=0, concat_axis=0, tiled=True)
-    pressure, residual, held = combine(arrived, w, mw, w_edge, mw_edge)
+    held, sums = unpack(arrived, level_count.shape[1])
+    other = lax.ppermute(sums, "lat", [(p + 1, p) for p in range(0, lat_count, 2)])
+    pressure, residual = combine(sums, other, w, mw, w_edge, mw_edge)
     held = held.reshape((1, 1, lon_count, 2, held.shape[1] // 2, held.shape[2]))
     return (held, pressure, residual)
 

time: 37.4 us -> 41.3 us (1.10)
  waiting for transfers between devices: 1.11 us -> 3.69 us
  starting transfers between devices: 11.7 us -> 13 us
  blocking collectives: 12.3 us -> 11.7 us
  Pallas kernels: 9.33 us -> 9.86 us
    ppermute x4, starting transfers between devices: 7.29 us -> 9.75 us  [swap(): return lax.ppermute(values, axis, pairs)]
    ppermute x2 -> x3, waiting for transfers between devices: 0.83 us -> 2.57 us  [the longest x1 1.76 us: on_device(): lax.ppermute(sums, 'lat', [(p + 1, p) for p in range(0, lat_count, 2)])]
    ppermute x2 -> x3, starting transfers between devices: 4.37 us -> 3.22 us  [the longest x1 1.29 us: on_device(): lax.ppermute(sums, 'lat', [(p, p + 1) for p in range(0, lat_count, 2)])]
    ppermute x4, waiting for transfers between devices: 0.29 us -> 1.12 us  [swap(): return lax.ppermute(values, axis, pairs)]
    all_to_all x1, blocking collectives: 12.3 us -> 11.7 us  [on_device(): lax.all_to_all(sent, 'lon', split_axis=0, concat_axis=0, tiled=True)]
    pallas_call x1 -> x2, Pallas kernels: 1.25 us -> 1.78 us  [the longest x1 1 us: combine(): pl.pallas_call(combine_kernel, out_shape=[shape, shape], compiler_params=...]
  transfers between devices with their start and end apart: 6 -> 7, of which waited for: 2 -> 3; matrix products, arithmetic and copies ran while one was open for 0% -> 0% of each run, Pallas kernels for 12% -> 12%
where the time goes in v9:
time: 41.3 us; the launch traced here: 41 us
  starting transfers between devices  13 us (31%)
  blocking collectives  11.7 us (28%)
  Pallas kernels  9.86 us (24%)
  waiting for transfers between devices  3.69 us (9%)
  local copies, waits for them, and re-layouts  2.02 us (5%)
  between operations  0.79 us (2%)
    all_to_all x1, blocking collectives, on_device(): lax.all_to_all(sent, 'lon', split_axis=0, concat_axis=0, tiled=True)  11.7 us
    ppermute x4, starting transfers between devices, swap(): return lax.ppermute(values, axis, pairs)  9.75 us
    pallas_call x2, Pallas kernels, integrate(): pl.pallas_call(functools.partial(integrate_kernel, bands, outer), in_spec...  4.56 us
    unnamed x12, local copies, waits for them, and re-layouts  2.01 us
    ppermute x1, waiting for transfers between devices, on_device(): lax.ppermute(sums, 'lat', [(p + 1, p) for p in range(0, lat_count, 2)])  1.76 us
    pallas_call x1, Pallas kernels, interior(): pl.pallas_call(interior_kernel, out_shape=[jax.ShapeDtypeStruct((STEPS, r...  1.57 us
    ppermute x1, starting transfers between devices, on_device(): lax.ppermute(sums, 'lat', [(p, p + 1) for p in range(0, lat_count, 2)])  1.29 us
    ppermute x1, starting transfers between devices, on_device(): lax.ppermute(sums, 'lat', [(p + 1, p) for p in range(0, lat_count, 2)])  1.28 us
  transfers between devices with their start and end apart: 7, of which 3 were waited for; matrix products, arithmetic and copies ran while one was open for 0% of the time, Pallas kernels for 12%

profile of v9, /device:TPU:0, one launch (start us, length us, event | category | flops | bytes accessed | tf_op | source)
XLA Modules:
  0.0 41.0 jit_solution(16103995085020615806)
XLA Ops:
  0.6 0.0 copy-start.4
  0.6 2.0 %outer.1 = (f32[4,32,256]{2,1,0:T(8,128)}, f32[32,128]{1,0:T(8,128)}, f32[4,8,256]{2,1,0:T(8,128)}, f32[4,8,256]{2,1,0:T(8,128)}) custom-call(f32[16]{0:T(128)} %thick_hbm.3, s32[128,256]{1,0:T(8,128)} %count_hbm.3, f32[128,256]{1,0:T(8,128)} %inertia_hbm.3, bf16[2,16,128,256]{3,2,1,0:T(8,128)(2,1)} %tend_hbm.3), custom_call_target="tpu_custom_call" | custom-call | flops 1572864 | bytes 524288 | tf_op jit(solution)/shard_map/outer/pallas_call | solution.py:117
  2.6 0.0 copy-start.3
  2.6 0.0 copy-start.2
  2.7 0.0 copy-start.5
  2.7 0.8 %collective-permute-start = (f32[4,8,256]{2,1,0:T(8,128)}, f32[4,8,256]{2,1,0:T(8,128)S(1)}, u32[]{:S(2)}, u32[]{:S(2)}) collective-permute-start(f32[4,8,256]{2,1,0:T(8,128)} %get-tuple-element.27), channel_id=1, source_target_pairs={{8,16},{16,8},{9,17},{17,9},{10,18},{18,10},{11,19},{19,11},{12,20... | collective-permute-start | bytes 98312 | tf_op jit(solution)/shard_map/ppermute | solution.py:535
  3.5 4.4 %collective-permute-start.1 = (f32[4,8,256]{2,1,0:T(8,128)}, f32[4,8,256]{2,1,0:T(8,128)S(1)}, u32[]{:S(2)}, u32[]{:S(2)}) collective-permute-start(f32[4,8,256]{2,1,0:T(8,128)} %get-tuple-element.28), channel_id=1, source_target_pairs={{0,8},{8,0},{16,24},{24,16},{1,9},{9,1},{17,25},{25,17},{2,10},{10... | collective-permute-start | bytes 98312 | tf_op jit(solution)/shard_map/ppermute | solution.py:535
  7.9 0.0 copy-done.4
  7.9 2.6 %middle.1 = (f32[4,96,256]{2,1,0:T(8,128)}, f32[96,128]{1,0:T(8,128)S(1)}) custom-call(f32[16]{0:T(128)S(1)} %copy-done.4, s32[128,256]{1,0:T(8,128)} %count_hbm.3, f32[128,256]{1,0:T(8,128)} %inertia_hbm.3, bf16[2,16,128,256]{3,2,1,0:T(8,128)(2,1)} %tend_hbm.3), custom_call_target="tpu_custom_call" | custom-call | flops 4718592 | bytes 1572864 | tf_op jit(solution)/shard_map/middle/pallas_call | solution.py:117
  10.4 0.0 collective-permute-done.far_ref
  10.5 0.0 collective-permute-done.1.near_ref
  10.5 0.0 copy-done.3
  10.5 0.1 edges.1
  10.6 4.6 %collective-permute-start.2 = (f32[24,128]{1,0:T(8,128)S(1)}, f32[24,128]{1,0:T(8,128)S(1)}, u32[]{:S(2)}, u32[]{:S(2)}) collective-permute-start(f32[24,128]{1,0:T(8,128)S(1)} %get-tuple-element.32), channel_id=1, source_target_pairs={{1,2},{2,1},{3,4},{4,3},{5,6},{6,5},{7,0},{0,7},{9,10},{10,9},{11,... | collective-permute-start | bytes 36872 | tf_op jit(solution)/shard_map/ppermute | solution.py:535
  15.2 0.0 collective-permute-start.3
  15.2 0.0 copy-done.2
  15.2 0.0 copy-start
  15.2 1.0 %copy-done = f32[4,96,256]{2,1,0:T(8,128)S(1)} copy-done((f32[4,96,256]{2,1,0:T(8,128)S(1)}, f32[4,96,256]{2,1,0:T(8,128)}, u32[]{:S(2)}) %copy-start) | copy-done | bytes 393240
  16.2 1.6 %interior.1 = (f32[4,128,256]{2,1,0:T(8,128)S(1)}, f32[5,128,256]{2,1,0:T(8,128)S(1)}, f32[4,144,128]{2,1,0:T(8,128)S(1)}, f32[8,128]{1,0:T(8,128)S(1)}) custom-call(f32[4,32,256]{2,1,0:T(8,128)S(1)} %copy-done.2, f32[4,96,256]{2,1,0:T(8,128)S(1)} %copy-done, f32[4,8,256]{2,1,0:T(8,128)S(1)} %collective-permute-done.far_ref, ...), custom_call_target="tpu_custom_call" | custom-call | flops 9830400 | bytes 2097152 | tf_op jit(solution)/shard_map/interior/pallas_call | solution.py:283
  17.8 0.0 collective-permute-done.2.far_ref
  17.8 1.1 %collective-permute-done.3.near_ref = f32[24,128]{1,0:T(8,128)S(1)} collective-permute-done((f32[24,128]{1,0:T(8,128)S(1)}, f32[24,128]{1,0:T(8,128)S(1)}, u32[]{:S(2)}, u32[]{:S(2)}) %collective-permute-start.3) | collective-permute-done | bytes 12320 | tf_op jit(solution)/shard_map/ppermute | solution.py:535
  18.9 1.0 %strip.1 = (f32[4,128,128]{2,1,0:T(8,128)S(1)}, f32[5,128,128]{2,1,0:T(8,128)S(1)}, f32[8,128]{1,0:T(8,128)S(1)}) custom-call(f32[4,144,128]{2,1,0:T(8,128)S(1)} %get-tuple-element.29.strip_in_ref, f32[24,128]{1,0:T(8,128)S(1)} %collective-permute-done.2.far_ref, f32[24,128]{1,0:T(8,128)S(1)} %collective-permute-done.3.near_ref, ...), custom_call_target="tpu_custom_call" | custom-call | tf_op jit(solution)/shard_map/strip/pallas_call | solution.py:330
  19.9 1.3 %collective-permute-start.4 = (f32[8,128]{1,0:T(8,128)S(1)}, f32[8,128]{1,0:T(8,128)S(1)}, u32[]{:S(2)}, u32[]{:S(2)}) collective-permute-start(f32[8,128]{1,0:T(8,128)S(1)} %get-tuple-element.35), channel_id=1, source_target_pairs={{0,8},{16,24},{1,9},{17,25},{2,10},{18,26},{3,11},{19,27},{4,12},{... | collective-permute-start | bytes 12296 | tf_op jit(solution)/shard_map/ppermute | solution.py:557
  21.1 0.8 %collective-permute-done.4 = f32[8,128]{1,0:T(8,128)S(1)} collective-permute-done((f32[8,128]{1,0:T(8,128)S(1)}, f32[8,128]{1,0:T(8,128)S(1)}, u32[]{:S(2)}, u32[]{:S(2)}) %collective-permute-start.4) | collective-permute-done | bytes 4128 | tf_op jit(solution)/shard_map/ppermute | solution.py:557
  22.0 0.6 %collective-permute-start.5 = (f32[8,128]{1,0:T(8,128)S(1)}, f32[8,128]{1,0:T(8,128)S(1)}, u32[]{:S(2)}, u32[]{:S(2)}) collective-permute-start(f32[8,128]{1,0:T(8,128)S(1)} %add.3.sums_ref), channel_id=1, source_target_pairs={{8,24},{24,8},{9,25},{25,9},{10,26},{26,10},{11,27},{27,11},{12,28... | collective-permute-start | bytes 12296 | tf_op jit(solution)/shard_map/ppermute | solution.py:526
  22.6 0.0 copy-done.5
  22.6 0.0 copy-start.1
  22.6 1.0 %copy-done.1 = f32[4,96,256]{2,1,0:T(8,128)S(1)} copy-done((f32[4,96,256]{2,1,0:T(8,128)S(1)}, f32[4,96,256]{2,1,0:T(8,128)}, u32[]{:S(2)}) %copy-start.1) | copy-done | bytes 393240
  23.6 0.8 %place.1 = (s16[8,80,128]{2,1,0:T(8,128)(2,1)S(1)}, f32[8,8,128]{2,1,0:T(8,128)S(1)}) custom-call(s32[8]{0:T(128)S(1)} %bitcast.2, f32[4,32,256]{2,1,0:T(8,128)S(1)} %copy-done.2, f32[4,96,256]{2,1,0:T(8,128)S(1)} %copy-done.1), custom_call_target="tpu_custom_call" | custom-call | flops 1966080 | bytes 393216 | tf_op jit(solution)/shard_map/place/pallas_call | solution.py:395
  24.4 0.0 collective-permute-done.5.other_ref
  24.5 11.7 %all_to_all.5.arrived_ref = s16[8,80,128]{2,1,0:T(8,128)(2,1)S(1)} all-to-all(s16[8,80,128]{2,1,0:T(8,128)(2,1)S(1)} %constant_dynamic-update-slice_fusion), channel_id=1, replica_groups=mesh['lat'=4,'lon'=8] {'lon'}, dimensions={0} | all-to-all | bytes 327680 | tf_op jit(solution)/shard_map/all_to_all | solution.py:564
  36.2 0.8 %unpack.1 = (f32[8,32,256]{2,1,0:T(8,128)}, f32[8,128]{1,0:T(8,128)S(1)}) custom-call(s16[8,80,128]{2,1,0:T(8,128)(2,1)S(1)} %all_to_all.5.arrived_ref), custom_call_target="tpu_custom_call" | custom-call | tf_op jit(solution)/shard_map/unpack/pallas_call | solution.py:452
  37.0 1.3 %collective-permute-start.6 = (f32[8,128]{1,0:T(8,128)S(1)}, f32[8,128]{1,0:T(8,128)S(1)}, u32[]{:S(2)}, u32[]{:S(2)}) collective-permute-start(f32[8,128]{1,0:T(8,128)S(1)} %get-tuple-element.38.sums_ref), channel_id=1, source_target_pairs={{8,0},{24,16},{9,1},{25,17},{10,2},{26,18},{11,3},{27,19},{12,4},{... | collective-permute-start | bytes 12296 | tf_op jit(solution)/shard_map/ppermute | solution.py:566
  38.3 1.8 %collective-permute-done.6.other_ref = f32[8,128]{1,0:T(8,128)S(1)} collective-permute-done((f32[8,128]{1,0:T(8,128)S(1)}, f32[8,128]{1,0:T(8,128)S(1)}, u32[]{:S(2)}, u32[]{:S(2)}) %collective-permute-start.6) | collective-permute-done | bytes 4128 | tf_op jit(solution)/shard_map/ppermute | solution.py:566
  40.1 1.0 %combine.1 = (f32[128,256]{1,0:T(8,128)}, f32[128,256]{1,0:T(8,128)}) custom-call(f32[8,128]{1,0:T(8,128)S(1)} %get-tuple-element.38.sums_ref, f32[8,128]{1,0:T(8,128)S(1)} %collective-permute-done.6.other_ref, f32[4,128,256]{2,1,0:T(8,128)S(1)} %get-tuple-element.39.w_ref, f32[5,128,256]{2,1,0:T(8,128)S(1)} %get-tuple-element.40.mw_ref, ...), custom_call_target="tpu_custom_call" | custom-call | tf_op jit(solution)/shard_map/combine/pallas_call | solution.py:516
  (3 shorter events, 0.1 us)
Async XLA Ops:
  0.6 7.2 %copy-start.4 = (f32[16]{0:T(128)S(1)}, f32[16]{0:T(128)}, u32[]{:S(2)}) copy-start(f32[16]{0:T(128)} %thick_hbm.3) | copy-start | bytes 196
  2.6 7.8 %copy-start.3 = (f32[32,128]{1,0:T(8,128)S(1)}, f32[32,128]{1,0:T(8,128)}, u32[]{:S(2)}) copy-start(f32[32,128]{1,0:T(8,128)} %get-tuple-element.30.outer_ref) | copy-start | bytes 49156
  2.6 12.6 %copy-start.2 = (f32[4,32,256]{2,1,0:T(8,128)S(1)}, f32[4,32,256]{2,1,0:T(8,128)}, u32[]{:S(2)}) copy-start(f32[4,32,256]{2,1,0:T(8,128)} %get-tuple-element.24.outer_ref) | copy-start | bytes 393220
  2.7 20.0 %copy-start.5 = (s32[8,1]{0,1:T(1,128)S(1)}, s32[8,1]{0,1:T(1,128)}, u32[]{:S(2)}) copy-start(s32[8,1]{0,1:T(1,128)} %param.9) | copy-start | bytes 100
  2.7 7.8 %collective-permute-start = (f32[4,8,256]{2,1,0:T(8,128)}, f32[4,8,256]{2,1,0:T(8,128)S(1)}, u32[]{:S(2)}, u32[]{:S(2)}) collective-permute-start(f32[4,8,256]{2,1,0:T(8,128)} %get-tuple-element.27), channel_id=1, source_target_pairs={{8,16},{16,8},{9,17},{17,9},{10,18},{18,10},{11,19},{19,11},{12,20... | collective-permute-start | bytes 98312 | tf_op jit(solution)/shard_map/ppermute | solution.py:535
  3.5 7.0 %collective-permute-start.1 = (f32[4,8,256]{2,1,0:T(8,128)}, f32[4,8,256]{2,1,0:T(8,128)S(1)}, u32[]{:S(2)}, u32[]{:S(2)}) collective-permute-start(f32[4,8,256]{2,1,0:T(8,128)} %get-tuple-element.28), channel_id=1, source_target_pairs={{0,8},{8,0},{16,24},{24,16},{1,9},{9,1},{17,25},{25,17},{2,10},{10... | collective-permute-start | bytes 98312 | tf_op jit(solution)/shard_map/ppermute | solution.py:535
  10.6 7.1 %collective-permute-start.2 = (f32[24,128]{1,0:T(8,128)S(1)}, f32[24,128]{1,0:T(8,128)S(1)}, u32[]{:S(2)}, u32[]{:S(2)}) collective-permute-start(f32[24,128]{1,0:T(8,128)S(1)} %get-tuple-element.32), channel_id=1, source_target_pairs={{1,2},{2,1},{3,4},{4,3},{5,6},{6,5},{7,0},{0,7},{9,10},{10,9},{11,... | collective-permute-start | bytes 36872 | tf_op jit(solution)/shard_map/ppermute | solution.py:535
  15.2 3.7 %collective-permute-start.3 = (f32[24,128]{1,0:T(8,128)S(1)}, f32[24,128]{1,0:T(8,128)S(1)}, u32[]{:S(2)}, u32[]{:S(2)}) collective-permute-start(f32[24,128]{1,0:T(8,128)S(1)} %get-tuple-element.33), channel_id=1, source_target_pairs={{0,1},{1,0},{2,3},{3,2},{4,5},{5,4},{6,7},{7,6},{8,9},{9,8},{10,11... | collective-permute-start | bytes 36872 | tf_op jit(solution)/shard_map/ppermute | solution.py:535
  15.2 1.0 %copy-start = (f32[4,96,256]{2,1,0:T(8,128)S(1)}, f32[4,96,256]{2,1,0:T(8,128)}, u32[]{:S(2)}) copy-start(f32[4,96,256]{2,1,0:T(8,128)} %get-tuple-element.25.middle_ref) | copy-start | bytes 1179652
  19.9 2.1 %collective-permute-start.4 = (f32[8,128]{1,0:T(8,128)S(1)}, f32[8,128]{1,0:T(8,128)S(1)}, u32[]{:S(2)}, u32[]{:S(2)}) collective-permute-start(f32[8,128]{1,0:T(8,128)S(1)} %get-tuple-element.35), channel_id=1, source_target_pairs={{0,8},{16,24},{1,9},{17,25},{2,10},{18,26},{3,11},{19,27},{4,12},{... | collective-permute-start | bytes 12296 | tf_op jit(solution)/shard_map/ppermute | solution.py:557
  22.0 2.5 %collective-permute-start.5 = (f32[8,128]{1,0:T(8,128)S(1)}, f32[8,128]{1,0:T(8,128)S(1)}, u32[]{:S(2)}, u32[]{:S(2)}) collective-permute-start(f32[8,128]{1,0:T(8,128)S(1)} %add.3.sums_ref), channel_id=1, source_target_pairs={{8,24},{24,8},{9,25},{25,9},{10,26},{26,10},{11,27},{27,11},{12,28... | collective-permute-start | bytes 12296 | tf_op jit(solution)/shard_map/ppermute | solution.py:526
  22.6 1.0 %copy-start.1 = (f32[4,96,256]{2,1,0:T(8,128)S(1)}, f32[4,96,256]{2,1,0:T(8,128)}, u32[]{:S(2)}) copy-start(f32[4,96,256]{2,1,0:T(8,128)} %get-tuple-element.25.middle_ref) | copy-start | bytes 1179652
  37.0 3.0 %collective-permute-start.6 = (f32[8,128]{1,0:T(8,128)S(1)}, f32[8,128]{1,0:T(8,128)S(1)}, u32[]{:S(2)}, u32[]{:S(2)}) collective-permute-start(f32[8,128]{1,0:T(8,128)S(1)} %get-tuple-element.38.sums_ref), channel_id=1, source_target_pairs={{8,0},{24,16},{9,1},{25,17},{10,2},{26,18},{11,3},{27,19},{12,4},{... | collective-permute-start | bytes 12296 | tf_op jit(solution)/shard_map/ppermute | solution.py:566

commit v10 on v8

--- a/solution.py
+++ b/solution.py
@@ -19,10 +19,11 @@
 FIELDS = 4
 GROUPS = 6
 PITCH = LANES // GROUPS
+OUTER = 16
 TAIL = 16
 SUM_ROWS = 4
 VMEM_BYTES = 16 * 1024 * 1024
-MIDDLE_BYTES = 56450000
+WHOLE_BYTES = 56450000
 
 
 def lanes_of(shape):
@@ -55,14 +56,11 @@
 
 
 def integrate_kernel(bands, outer, thick_hbm, count_hbm, inertia_hbm, tend_hbm, *refs):
-    if outer:
-        fields_ref, side_ref, near_ref, far_ref = refs[:4]
-    else:
-        fields_ref, side_ref = refs[:2]
-    thick_ref, count_ref, inertia_ref, tend_ref, thick_sem, small_sems, large_sems = refs[-7:]
+    outs, scratch = refs[:2], refs[2:]
+    thick_ref, count_ref, inertia_ref, tend_ref, thick_sem, small_sems, large_sems = scratch
     levels = tend_hbm.shape[1]
-    even = is_even("lat")
-    copies = [[pltpu.make_async_copy(thick_hbm, thick_ref, thick_sem)]]
+    thick_copy = pltpu.make_async_copy(thick_hbm, thick_ref, thick_sem)
+    copies = []
     start = 0
     for place, (row, size) in enumerate(bands):
         there = pl.ds(row, size)
@@ -76,16 +74,18 @@
         tend_copy = pltpu.make_async_copy(
             tend_hbm.at[:, :, there], tend_ref.at[:, :, here], large_sems.at[place]
         )
-        copies.append([count_copy, inertia_copy, tend_copy])
+        copies.append((count_copy, inertia_copy, tend_copy))
         start += size
+    thick_copy.start()
     for group in copies:
         for copy in group:
             copy.start()
-    copies[0][0].wait()
+    thick_copy.wait()
     start = 0
+    results = []
     for place, (row, size) in enumerate(bands):
         part = slice(start, start + size)
-        for copy in copies[place + 1]:
+        for copy in copies[place]:
             copy.wait()
         count = count_ref[part]
         first = jnp.zeros(count.shape, jnp.float32)
@@ -96,14 +96,21 @@
             depth = depth + layer
             first = first + layer * tend_ref[0, level, part].astype(jnp.float32)
             second = second + layer * tend_ref[1, level, part].astype(jnp.float32)
-        for field, values in enumerate((first, second, depth, inertia_ref[part])):
-            fields_ref[field, part] = values
-        side_ref[part] = pack_edges(fields_ref, part)
+        values = (first, second, depth, inertia_ref[part])
+        if outer:
+            results.append(values)
+        else:
+            fields_ref, side_ref = outs
+            for field in range(FIELDS):
+                fields_ref[field, part] = values[field]
+            side_ref[part] = pack_edges(fields_ref, part)
         start += size
     if outer:
+        near_ref, far_ref = outs
+        even = is_even("lat")
         for field in range(FIELDS):
-            head = fields_ref[field, :ROWS]
-            tail = fields_ref[field, start - ROWS :]
+            head = results[0][field][:ROWS]
+            tail = results[1][field][-ROWS:]
             near_ref[field] = jnp.where(even, tail, head)
             far_ref[field] = jnp.where(even, head, tail)
 
@@ -112,15 +119,17 @@
     components, levels, _, cols = tendency.shape
     rows = sum(size for _, size in bands)
     f32 = jnp.float32
-    halo = jax.ShapeDtypeStruct((FIELDS, ROWS, cols), f32)
-    return pl.pallas_call(
-        functools.partial(integrate_kernel, bands, outer),
-        in_specs=[pl.BlockSpec(memory_space=pltpu.HBM)] * 4,
-        out_shape=[
+    if outer:
+        out_shape = [jax.ShapeDtypeStruct((FIELDS, ROWS, cols), f32)] * 2
+    else:
+        out_shape = [
             jax.ShapeDtypeStruct((FIELDS, rows, cols), f32),
             jax.ShapeDtypeStruct((rows, LANES), f32),
         ]
-        + ([halo, halo] if outer else []),
+    return pl.pallas_call(
+        functools.partial(integrate_kernel, bands, outer),
+        in_specs=[pl.BlockSpec(memory_space=pltpu.HBM)] * 4,
+        out_shape=out_shape,
         scratch_shapes=[
             pltpu.SMEM(thickness.shape, f32),
             pltpu.VMEM((rows, cols), jnp.int32),
@@ -135,27 +144,19 @@
             bytes_accessed=2 * components * levels * rows * cols,
             transcendentals=0,
         ),
-        compiler_params=None if outer else pltpu.CompilerParams(vmem_limit_bytes=MIDDLE_BYTES),
-        name="outer" if outer else "middle",
+        compiler_params=None if outer else pltpu.CompilerParams(vmem_limit_bytes=WHOLE_BYTES),
+        name="outer" if outer else "whole",
     )(thickness, level_count, inertia, tendency)
 
 
-def edges_kernel(outer_ref, middle_ref, near_ref, far_ref, near_out_ref, far_out_ref):
+def edges_kernel(side_ref, far_ref, near_ref, near_out_ref, far_out_ref):
     even_lat = is_even("lat")
     even_lon = is_even("lon")
     near = pack_edges(near_ref, slice(None))
     far = pack_edges(far_ref, slice(None))
-    half = outer_ref.shape[0] // 2
-    packed = jnp.concatenate(
-        [
-            jnp.where(even_lat, far, near),
-            outer_ref[:half],
-            middle_ref[...],
-            outer_ref[half:],
-            jnp.where(even_lat, near, far),
-        ],
-        axis=0,
-    )
+    north = jnp.where(even_lat, far, near)
+    south = jnp.where(even_lat, near, far)
+    packed = jnp.concatenate([north, side_ref[...], south], axis=0)
     size = near_out_ref.shape[0]
     lane = lanes_of(near_out_ref.shape)
     west = jnp.zeros(near_out_ref.shape, jnp.float32)
@@ -170,15 +171,15 @@
     far_out_ref[...] = jnp.where(even_lon, west, east)
 
 
-def edges(outer, middle, near, far):
-    rows = outer.shape[0] + middle.shape[0] + 2 * ROWS
+def edges(side, near, far):
+    rows = side.shape[0] + 2 * ROWS
     message = jax.ShapeDtypeStruct((rows // GROUPS, LANES), jnp.float32)
     return pl.pallas_call(
         edges_kernel,
         out_shape=[message, message],
         compiler_params=pltpu.CompilerParams(vmem_limit_bytes=VMEM_BYTES),
         name="edges",
-    )(outer, middle, near, far)
+    )(side, far, near)
 
 
 def smooth(field):
@@ -236,33 +237,24 @@
 
 
 def interior_kernel(
-    outer_ref,
-    middle_ref,
+    fields_ref,
+    far_ref,
     near_ref,
-    far_ref,
     w_ref,
     mw_ref,
     strip_ref,
     sums_ref,
 ):
-    half = outer_ref.shape[1] // 2
-    cols = outer_ref.shape[2]
+    cols = fields_ref.shape[2]
     even = is_even("lat")
     lane = lanes_of((strip_ref.shape[1], LANES))
     padded = []
     for place in range(FIELDS):
         near = near_ref[place]
         far = far_ref[place]
-        values = jnp.concatenate(
-            [
-                jnp.where(even, far, near),
-                outer_ref[place, :half],
-                middle_ref[place],
-                outer_ref[place, half:],
-                jnp.where(even, near, far),
-            ],
-            axis=0,
-        )
+        north = jnp.where(even, far, near)
+        south = jnp.where(even, near, far)
+        values = jnp.concatenate([north, fields_ref[place], south], axis=0)
         east = turn(values[:, cols - LANES :], SEAM)
         strip_ref[place] = jnp.where(lane < HALF, values[:, :LANES], east)
         padded.append(values)
@@ -275,9 +267,8 @@
     sums_ref[...] = moments(ws, mws, (lane >= RIM) & (lane < cols - RIM))
 
 
-def interior(outer, middle, near, far):
-    cols = outer.shape[2]
-    rows = outer.shape[1] + middle.shape[1]
+def interior(fields, near, far):
+    _, rows, cols = fields.shape
     f32 = jnp.float32
     return pl.pallas_call(
         interior_kernel,
@@ -292,10 +283,10 @@
             flops=300 * rows * cols, bytes_accessed=64 * rows * cols, transcendentals=0
         ),
         name="interior",
-    )(outer, middle, near, far)
-
-
-def strip_kernel(strip_in_ref, near_ref, far_ref, inner_ref, w_ref, mw_ref, sums_ref):
+    )(fields, far, near)
+
+
+def strip_kernel(strip_in_ref, far_ref, near_ref, inner_ref, w_ref, mw_ref, sums_ref):
     even = is_even("lon")
     near = near_ref[...]
     far = far_ref[...]
@@ -335,7 +326,7 @@
         ],
         compiler_params=pltpu.CompilerParams(vmem_limit_bytes=VMEM_BYTES),
         name="strip",
-    )(strip_in, near, far, inner)
+    )(strip_in, far, near, inner)
 
 
 def power(exponent):
@@ -357,29 +348,21 @@
     return jnp.floor(values + 0.5)
 
 
-def place_kernel(owner_ref, outer_ref, middle_ref, sent_ref, scale_ref):
+def place_kernel(owner_ref, fields_ref, sent_ref, scale_ref):
     count = owner_ref.shape[0]
-    edge = outer_ref.shape[1] // 2
-    between = middle_ref.shape[1]
-    span = (2 * edge + between) // count
+    span = fields_ref.shape[1] // count
     sent_ref[...] = jnp.zeros(sent_ref.shape, jnp.int16)
     scale_ref[...] = jnp.zeros(scale_ref.shape, jnp.float32)
     for block in range(count):
-        row = block * span
-        if row < edge:
-            ref, row = outer_ref, row
-        elif row < edge + between:
-            ref, row = middle_ref, row - edge
-        else:
-            ref, row = outer_ref, row - between
         target = owner_ref[block]
 
         @pl.when(target >= 0)
-        def _(ref=ref, row=row, target=target):
-            for half in range(ref.shape[2] // LANES):
+        def _(block=block, target=target):
+            rows = slice(block * span, (block + 1) * span)
+            for half in range(fields_ref.shape[2] // LANES):
                 cols = slice(half * LANES, (half + 1) * LANES)
-                rows = slice(row, row + span)
-                values = jnp.concatenate([ref[0, rows, cols], ref[1, rows, cols]], axis=0)
+                pieces = [fields_ref[0, rows, cols], fields_ref[1, rows, cols]]
+                values = jnp.concatenate(pieces, axis=0)
                 bits = exponent_of(jnp.max(jnp.abs(values), axis=0, keepdims=True))
                 whole = jnp.clip(nearest(values * power(15 - bits)), -32767.0, 32767.0)
                 there = slice(2 * span * half, 2 * span * (half + 1))
@@ -387,14 +370,15 @@
                 scale_ref[target, half : half + 1] = bits.astype(jnp.float32)
 
 
-def place(owner, outer, middle, lon_count):
-    cols = outer.shape[2]
-    rows = outer.shape[1] + middle.shape[1]
+def place(owner, fields, lon_count):
+    _, rows, cols = fields.shape
     span = rows // owner.shape[0]
     return pl.pallas_call(
         place_kernel,
-        in_specs=[pl.BlockSpec(memory_space=pltpu.SMEM)]
-        + [pl.BlockSpec(memory_space=pltpu.VMEM)] * 2,
+        in_specs=[
+            pl.BlockSpec(memory_space=pltpu.SMEM),
+            pl.BlockSpec(memory_space=pltpu.VMEM),
+        ],
         out_shape=[
             jax.ShapeDtypeStruct((lon_count, cols // LANES * 2 * span + TAIL, LANES), jnp.int16),
             jax.ShapeDtypeStruct((lon_count, ROWS, LANES), jnp.float32),
@@ -404,7 +388,7 @@
             flops=60 * rows * cols, bytes_accessed=12 * rows * cols, transcendentals=0
         ),
         name="place",
-    )(owner, outer, middle)
+    )(owner, fields)
 
 
 def seal_kernel(sums_ref, other_ref, scale_ref, tail_ref):
@@ -521,19 +505,18 @@
     lat_count = lax.axis_size("lat")
     lon_count = lax.axis_size("lon")
     rows = level_count.shape[0]
-    tall = min(CHUNK, rows // 4)
     inputs = (tendency, thickness, level_count, inertia)
-    outer, outer_side, near, far = integrate(*inputs, ((0, tall), (rows - tall, tall)), True)
-    bands = tuple((row, tall) for row in range(tall, rows - tall, tall))
-    middle, middle_side = integrate(*inputs, bands, False)
+    near, far = integrate(*inputs, ((0, OUTER), (rows - OUTER, OUTER)), True)
+    bands = tuple((row, CHUNK) for row in range(0, rows, CHUNK))
+    fields, side = integrate(*inputs, bands, False)
+    far = swap(far, "lat", 1, False)
     near = swap(near, "lat", 0, False)
-    far = swap(far, "lat", 1, False)
-    near_edge, far_edge = edges(outer_side, middle_side, near, far)
+    near_edge, far_edge = edges(side, near, far)
+    far_edge = swap(far_edge, "lon", 1, True)
     near_edge = swap(near_edge, "lon", 0, True)
-    far_edge = swap(far_edge, "lon", 1, True)
-    w, mw, strip_in, inner = interior(outer, middle, near, far)
+    w, mw, strip_in, inner = interior(fields, near, far)
     w_edge, mw_edge, sums = strip(strip_in, near_edge, far_edge, inner)
-    sent, scale = place(owner[:, 0], outer, middle, lon_count)
+    sent, scale = place(owner[:, 0], fields, lon_count)
     shift = 1
     while 2 * shift < lat_count:
         sums = sums + exchange(sums, "lat", shift)

time: 37.4 us -> 37.6 us (level)
  waiting for transfers between devices: 1.11 us -> 3.57 us
  starting transfers between devices: 11.7 us -> 10.1 us
  blocking collectives: 12.3 us -> 11.3 us
    ppermute x2, starting transfers between devices: 4.37 us -> 0.49 us  [exchange(): return lax.ppermute(values, axis, pairs)]
    ppermute x4, starting transfers between devices: 7.29 us -> 9.62 us  [swap(): return lax.ppermute(values, axis, pairs)]
    ppermute x2, waiting for transfers between devices: 0.83 us -> 2.48 us  [exchange(): return lax.ppermute(values, axis, pairs)]
    all_to_all x1, blocking collectives: 12.3 us -> 11.3 us  [on_device(): lax.all_to_all(sent, 'lon', split_axis=0, concat_axis=0, tiled=True)]
    ppermute x4, waiting for transfers between devices: 0.29 us -> 1.09 us  [swap(): return lax.ppermute(values, axis, pairs)]
    unnamed x12 -> x8, local copies, waits for them, and re-layouts: 1.92 us -> 2.09 us
  transfers between devices with their start and end apart: 6 -> 6, of which waited for: 2 -> 3; matrix products, arithmetic and copies ran while one was open for 0% -> 0% of each run, Pallas kernels for 12% -> 14%
where the time goes in v10:
time: 37.6 us; the launch traced here: 37.3 us
  blocking collectives  11.3 us (30%)
  starting transfers between devices  10.1 us (27%)
  Pallas kernels  9.48 us (25%)
  waiting for transfers between devices  3.57 us (9%)
  local copies, waits for them, and re-layouts  2.1 us (6%)
  between operations  0.73 us (2%)
    all_to_all x1, blocking collectives, on_device(): lax.all_to_all(sent, 'lon', split_axis=0, concat_axis=0, tiled=True)  11.3 us
    ppermute x4, starting transfers between devices, swap(): return lax.ppermute(values, axis, pairs)  9.62 us
    pallas_call x2, Pallas kernels, integrate(): pl.pallas_call(functools.partial(integrate_kernel, bands, outer), in_spec...  4.72 us
    ppermute x2, waiting for transfers between devices, exchange(): return lax.ppermute(values, axis, pairs)  2.48 us
    unnamed x8, local copies, waits for them, and re-layouts  2.09 us
    pallas_call x1, Pallas kernels, interior(): pl.pallas_call(interior_kernel, out_shape=[jax.ShapeDtypeStruct((STEPS, r...  1.56 us
    pallas_call x1, Pallas kernels, combine(): pl.pallas_call(combine_kernel, out_shape=[shape, shape, jax.ShapeDtypeStr...  1.25 us
    ppermute x4, waiting for transfers between devices, swap(): return lax.ppermute(values, axis, pairs)  1.09 us
  transfers between devices with their start and end apart: 6, of which 3 were waited for; matrix products, arithmetic and copies ran while one was open for 0% of the time, Pallas kernels for 14%

profile of v10, /device:TPU:0, one launch (start us, length us, event | category | flops | bytes accessed | tf_op | source)
XLA Modules:
  0.0 37.3 jit_solution(1869260541814300563)
XLA Ops:
  0.6 0.0 copy-start.2
  0.6 1.8 %outer.1 = (f32[4,8,256]{2,1,0:T(8,128)}, f32[4,8,256]{2,1,0:T(8,128)}) custom-call(f32[16]{0:T(128)} %thick_hbm.3, s32[128,256]{1,0:T(8,128)} %count_hbm.3, f32[128,256]{1,0:T(8,128)} %inertia_hbm.3, bf16[2,16,128,256]{3,2,1,0:T(8,128)(2,1)} %tend_hbm.3), custom_call_target="tpu_custom_call" | custom-call | flops 1572864 | bytes 524288 | tf_op jit(solution)/shard_map/outer/pallas_call | solution.py:129
  2.5 0.0 copy-start.3
  2.5 0.7 %collective-permute-start = (f32[4,8,256]{2,1,0:T(8,128)}, f32[4,8,256]{2,1,0:T(8,128)S(1)}, u32[]{:S(2)}, u32[]{:S(2)}) collective-permute-start(f32[4,8,256]{2,1,0:T(8,128)} %get-tuple-element.23), channel_id=1, source_target_pairs={{8,16},{16,8},{9,17},{17,9},{10,18},{18,10},{11,19},{19,11},{12,20... | collective-permute-start | bytes 98312 | tf_op jit(solution)/shard_map/ppermute | solution.py:501
  3.2 4.4 %collective-permute-start.1 = (f32[4,8,256]{2,1,0:T(8,128)}, f32[4,8,256]{2,1,0:T(8,128)S(1)}, u32[]{:S(2)}, u32[]{:S(2)}) collective-permute-start(f32[4,8,256]{2,1,0:T(8,128)} %get-tuple-element.24), channel_id=1, source_target_pairs={{0,8},{8,0},{16,24},{24,16},{1,9},{9,1},{17,25},{25,17},{2,10},{10... | collective-permute-start | bytes 98312 | tf_op jit(solution)/shard_map/ppermute | solution.py:501
  7.6 0.0 copy-done.2
  7.6 2.9 %whole.1 = (f32[4,128,256]{2,1,0:T(8,128)}, f32[128,128]{1,0:T(8,128)S(1)}) custom-call(f32[16]{0:T(128)S(1)} %copy-done.2, s32[128,256]{1,0:T(8,128)} %count_hbm.3, f32[128,256]{1,0:T(8,128)} %inertia_hbm.3, bf16[2,16,128,256]{3,2,1,0:T(8,128)(2,1)} %tend_hbm.3), custom_call_target="tpu_custom_call" | custom-call | flops 6291456 | bytes 2097152 | tf_op jit(solution)/shard_map/whole/pallas_call | solution.py:129
  10.5 0.0 collective-permute-done.far_ref
  10.5 0.0 collective-permute-done.1.near_ref
  10.5 0.1 edges.1
  10.6 4.6 %collective-permute-start.2 = (f32[24,128]{1,0:T(8,128)S(1)}, f32[24,128]{1,0:T(8,128)S(1)}, u32[]{:S(2)}, u32[]{:S(2)}) collective-permute-start(f32[24,128]{1,0:T(8,128)S(1)} %get-tuple-element.27), channel_id=1, source_target_pairs={{1,2},{2,1},{3,4},{4,3},{5,6},{6,5},{7,0},{0,7},{9,10},{10,9},{11,... | collective-permute-start | bytes 36872 | tf_op jit(solution)/shard_map/ppermute | solution.py:501
  15.2 0.0 collective-permute-start.3
  15.2 0.0 copy-start
  15.2 1.0 %copy-done = f32[4,128,256]{2,1,0:T(8,128)S(1)} copy-done((f32[4,128,256]{2,1,0:T(8,128)S(1)}, f32[4,128,256]{2,1,0:T(8,128)}, u32[]{:S(2)}) %copy-start) | copy-done | bytes 524312
  16.2 1.6 %interior.1 = (f32[4,128,256]{2,1,0:T(8,128)S(1)}, f32[5,128,256]{2,1,0:T(8,128)S(1)}, f32[4,144,128]{2,1,0:T(8,128)S(1)}, f32[8,128]{1,0:T(8,128)S(1)}) custom-call(f32[4,128,256]{2,1,0:T(8,128)S(1)} %copy-done, f32[4,8,256]{2,1,0:T(8,128)S(1)} %collective-permute-done.far_ref, f32[4,8,256]{2,1,0:T(8,128)S(1)} %collective-permute-done.1.near_ref), custom_call_target="tpu_custom_call" | custom-call | flops 9830400 | bytes 2097152 | tf_op jit(solution)/shard_map/interior/pallas_call | solution.py:273
  17.8 0.0 collective-permute-done.2.far_ref
  17.8 1.1 %collective-permute-done.3.near_ref = f32[24,128]{1,0:T(8,128)S(1)} collective-permute-done((f32[24,128]{1,0:T(8,128)S(1)}, f32[24,128]{1,0:T(8,128)S(1)}, u32[]{:S(2)}, u32[]{:S(2)}) %collective-permute-start.3) | collective-permute-done | bytes 12320 | tf_op jit(solution)/shard_map/ppermute | solution.py:501
  18.9 1.0 %strip.1 = (f32[4,128,128]{2,1,0:T(8,128)S(1)}, f32[5,128,128]{2,1,0:T(8,128)S(1)}, f32[8,128]{1,0:T(8,128)S(1)}) custom-call(f32[4,144,128]{2,1,0:T(8,128)S(1)} %get-tuple-element.25.strip_in_ref, f32[24,128]{1,0:T(8,128)S(1)} %collective-permute-done.2.far_ref, f32[24,128]{1,0:T(8,128)S(1)} %collective-permute-done.3.near_ref, ...), custom_call_target="tpu_custom_call" | custom-call | tf_op jit(solution)/shard_map/strip/pallas_call | solution.py:320
  19.9 0.1 collective-permute-start.4
  19.9 1.2 %collective-permute-done.4 = f32[8,128]{1,0:T(8,128)S(1)} collective-permute-done((f32[8,128]{1,0:T(8,128)S(1)}, f32[8,128]{1,0:T(8,128)S(1)}, u32[]{:S(2)}, u32[]{:S(2)}) %collective-permute-start.4) | collective-permute-done | bytes 4128 | tf_op jit(solution)/shard_map/ppermute | solution.py:492
  21.1 0.4 %collective-permute-start.5 = (f32[8,128]{1,0:T(8,128)S(1)}, f32[8,128]{1,0:T(8,128)S(1)}, u32[]{:S(2)}, u32[]{:S(2)}) collective-permute-start(f32[8,128]{1,0:T(8,128)S(1)} %add.3.sums_ref), channel_id=1, source_target_pairs={{0,16},{8,24},{16,0},{24,8},{1,17},{9,25},{17,1},{25,9},{2,18},{10... | collective-permute-start | bytes 12296 | tf_op jit(solution)/shard_map/ppermute | solution.py:492
  21.5 0.0 copy-done.3
  21.5 0.0 copy-start.1
  21.5 1.0 %copy-done.1 = f32[4,128,256]{2,1,0:T(8,128)S(1)} copy-done((f32[4,128,256]{2,1,0:T(8,128)S(1)}, f32[4,128,256]{2,1,0:T(8,128)}, u32[]{:S(2)}) %copy-start.1) | copy-done | bytes 524312
  22.6 0.8 %place.1 = (s16[8,80,128]{2,1,0:T(8,128)(2,1)S(1)}, f32[8,8,128]{2,1,0:T(8,128)S(1)}) custom-call(s32[8]{0:T(128)S(1)} %bitcast.2, f32[4,128,256]{2,1,0:T(8,128)S(1)} %copy-done.1), custom_call_target="tpu_custom_call" | custom-call | flops 1966080 | bytes 393216 | tf_op jit(solution)/shard_map/place/pallas_call | solution.py:376
  23.4 1.3 %collective-permute-done.5.other_ref = f32[8,128]{1,0:T(8,128)S(1)} collective-permute-done((f32[8,128]{1,0:T(8,128)S(1)}, f32[8,128]{1,0:T(8,128)S(1)}, u32[]{:S(2)}, u32[]{:S(2)}) %collective-permute-start.5) | collective-permute-done | bytes 4128 | tf_op jit(solution)/shard_map/ppermute | solution.py:492
  24.7 11.3 %all_to_all.5.arrived_ref = s16[8,80,128]{2,1,0:T(8,128)(2,1)S(1)} all-to-all(s16[8,80,128]{2,1,0:T(8,128)(2,1)S(1)} %constant_dynamic-update-slice_fusion), channel_id=1, replica_groups=mesh['lat'=4,'lon'=8] {'lon'}, dimensions={0} | all-to-all | bytes 327680 | tf_op jit(solution)/shard_map/all_to_all | solution.py:526
  36.1 1.3 %combine.1 = (f32[128,256]{1,0:T(8,128)}, f32[128,256]{1,0:T(8,128)}, f32[8,32,256]{2,1,0:T(8,128)}) custom-call(s16[8,80,128]{2,1,0:T(8,128)(2,1)S(1)} %all_to_all.5.arrived_ref, f32[4,128,256]{2,1,0:T(8,128)S(1)} %get-tuple-element.32.w_ref, f32[5,128,256]{2,1,0:T(8,128)S(1)} %get-tuple-element.33.mw_ref, f32[4,128,128]{2,1,0:T(8,128)S(1)} %get-tuple-element.34.w_edge_ref, ...), custom_call_target="tpu_custom_call" | custom-call | tf_op jit(solution)/shard_map/combine/pallas_call | solution.py:482
  (3 shorter events, 0.1 us)
Async XLA Ops:
  0.6 6.9 %copy-start.2 = (f32[16]{0:T(128)S(1)}, f32[16]{0:T(128)}, u32[]{:S(2)}) copy-start(f32[16]{0:T(128)} %thick_hbm.3) | copy-start | bytes 196
  2.5 19.0 %copy-start.3 = (s32[8,1]{0,1:T(1,128)S(1)}, s32[8,1]{0,1:T(1,128)}, u32[]{:S(2)}) copy-start(s32[8,1]{0,1:T(1,128)} %param.9) | copy-start | bytes 100
  2.5 8.0 %collective-permute-start = (f32[4,8,256]{2,1,0:T(8,128)}, f32[4,8,256]{2,1,0:T(8,128)S(1)}, u32[]{:S(2)}, u32[]{:S(2)}) collective-permute-start(f32[4,8,256]{2,1,0:T(8,128)} %get-tuple-element.23), channel_id=1, source_target_pairs={{8,16},{16,8},{9,17},{17,9},{10,18},{18,10},{11,19},{19,11},{12,20... | collective-permute-start | bytes 98312 | tf_op jit(solution)/shard_map/ppermute | solution.py:501
  3.2 7.3 %collective-permute-start.1 = (f32[4,8,256]{2,1,0:T(8,128)}, f32[4,8,256]{2,1,0:T(8,128)S(1)}, u32[]{:S(2)}, u32[]{:S(2)}) collective-permute-start(f32[4,8,256]{2,1,0:T(8,128)} %get-tuple-element.24), channel_id=1, source_target_pairs={{0,8},{8,0},{16,24},{24,16},{1,9},{9,1},{17,25},{25,17},{2,10},{10... | collective-permute-start | bytes 98312 | tf_op jit(solution)/shard_map/ppermute | solution.py:501
  10.6 7.2 %collective-permute-start.2 = (f32[24,128]{1,0:T(8,128)S(1)}, f32[24,128]{1,0:T(8,128)S(1)}, u32[]{:S(2)}, u32[]{:S(2)}) collective-permute-start(f32[24,128]{1,0:T(8,128)S(1)} %get-tuple-element.27), channel_id=1, source_target_pairs={{1,2},{2,1},{3,4},{4,3},{5,6},{6,5},{7,0},{0,7},{9,10},{10,9},{11,... | collective-permute-start | bytes 36872 | tf_op jit(solution)/shard_map/ppermute | solution.py:501
  15.2 3.7 %collective-permute-start.3 = (f32[24,128]{1,0:T(8,128)S(1)}, f32[24,128]{1,0:T(8,128)S(1)}, u32[]{:S(2)}, u32[]{:S(2)}) collective-permute-start(f32[24,128]{1,0:T(8,128)S(1)} %get-tuple-element.28), channel_id=1, source_target_pairs={{0,1},{1,0},{2,3},{3,2},{4,5},{5,4},{6,7},{7,6},{8,9},{9,8},{10,11... | collective-permute-start | bytes 36872 | tf_op jit(solution)/shard_map/ppermute | solution.py:501
  15.2 1.0 %copy-start = (f32[4,128,256]{2,1,0:T(8,128)S(1)}, f32[4,128,256]{2,1,0:T(8,128)}, u32[]{:S(2)}) copy-start(f32[4,128,256]{2,1,0:T(8,128)} %get-tuple-element.21.fields_ref) | copy-start | bytes 1572868
  19.9 1.2 %collective-permute-start.4 = (f32[8,128]{1,0:T(8,128)S(1)}, f32[8,128]{1,0:T(8,128)S(1)}, u32[]{:S(2)}, u32[]{:S(2)}) collective-permute-start(f32[8,128]{1,0:T(8,128)S(1)} %get-tuple-element.30), channel_id=1, source_target_pairs={{0,8},{8,0},{16,24},{24,16},{1,9},{9,1},{17,25},{25,17},{2,10},{10... | collective-permute-start | bytes 12296 | tf_op jit(solution)/shard_map/ppermute | solution.py:492
  21.1 3.6 %collective-permute-start.5 = (f32[8,128]{1,0:T(8,128)S(1)}, f32[8,128]{1,0:T(8,128)S(1)}, u32[]{:S(2)}, u32[]{:S(2)}) collective-permute-start(f32[8,128]{1,0:T(8,128)S(1)} %add.3.sums_ref), channel_id=1, source_target_pairs={{0,16},{8,24},{16,0},{24,8},{1,17},{9,25},{17,1},{25,9},{2,18},{10... | collective-permute-start | bytes 12296 | tf_op jit(solution)/shard_map/ppermute | solution.py:492
  21.5 1.0 %copy-start.1 = (f32[4,128,256]{2,1,0:T(8,128)S(1)}, f32[4,128,256]{2,1,0:T(8,128)}, u32[]{:S(2)}) copy-start(f32[4,128,256]{2,1,0:T(8,128)} %get-tuple-element.21.fields_ref) | copy-start | bytes 1572868

commit v11 on v10

--- a/solution.py
+++ b/solution.py
@@ -19,6 +19,7 @@
 FIELDS = 4
 GROUPS = 6
 PITCH = LANES // GROUPS
+PIECES = 2
 OUTER = 16
 TAIL = 16
 SUM_ROWS = 4
@@ -149,7 +150,7 @@
     )(thickness, level_count, inertia, tendency)
 
 
-def edges_kernel(side_ref, far_ref, near_ref, near_out_ref, far_out_ref):
+def edges_kernel(side_ref, near_ref, far_ref, near_out_ref, far_out_ref):
     even_lat = is_even("lat")
     even_lon = is_even("lon")
     near = pack_edges(near_ref, slice(None))
@@ -179,7 +180,7 @@
         out_shape=[message, message],
         compiler_params=pltpu.CompilerParams(vmem_limit_bytes=VMEM_BYTES),
         name="edges",
-    )(side, far, near)
+    )(side, near, far)
 
 
 def smooth(field):
@@ -238,8 +239,8 @@
 
 def interior_kernel(
     fields_ref,
+    near_ref,
     far_ref,
-    near_ref,
     w_ref,
     mw_ref,
     strip_ref,
@@ -283,7 +284,7 @@
             flops=300 * rows * cols, bytes_accessed=64 * rows * cols, transcendentals=0
         ),
         name="interior",
-    )(fields, far, near)
+    )(fields, near, far)
 
 
 def strip_kernel(strip_in_ref, far_ref, near_ref, inner_ref, w_ref, mw_ref, sums_ref):
@@ -413,7 +414,19 @@
 
 
 def combine_kernel(
-    arrived_ref, w_ref, mw_ref, w_edge_ref, mw_edge_ref, pressure_ref, residual_ref, held_ref
+    arrived_ref,
+    w_ref,
+    mw_ref,
+    w_edge_ref,
+    mw_edge_ref,
+    pressure_hbm,
+    residual_hbm,
+    held_hbm,
+    pressure_ref,
+    residual_ref,
+    held_ref,
+    held_sem,
+    sems,
 ):
     rows = held_ref.shape[1]
     packed = jnp.zeros((SUM_ROWS, LANES), jnp.float32)
@@ -428,6 +441,8 @@
             scale = power(tail[at : at + 1] - 15)
             whole = arrived_ref[slot, half * rows : (half + 1) * rows].astype(jnp.int32)
             held_ref[slot, :, half * LANES : (half + 1) * LANES] = whole.astype(jnp.float32) * scale
+    held_copy = pltpu.make_async_copy(held_ref, held_hbm, held_sem)
+    held_copy.start()
     quarter = lanes_of(packed.shape) // QUARTER
     totals = [
         jnp.sum(jnp.where(quarter == place, packed, 0.0), axis=1, keepdims=True)
@@ -454,25 +469,40 @@
             right[pivot] = right[pivot] - matrix[pivot, col] * right[col]
         right[pivot] = right[pivot] * matrix[pivot, pivot]
 
-    def results(w_ref, mw_ref):
-        pressure = right[0] * w_ref[0]
-        residual = mw_ref[0] - right[0] * (mw_ref[0] - mw_ref[1])
+    def results(w_ref, mw_ref, part):
+        pressure = right[0] * w_ref[0, part]
+        residual = mw_ref[0, part] - right[0] * (mw_ref[0, part] - mw_ref[1, part])
         for place in range(1, STEPS):
-            pressure = pressure + right[place] * w_ref[place]
-            residual = residual - right[place] * (mw_ref[place] - mw_ref[place + 1])
+            pressure = pressure + right[place] * w_ref[place, part]
+            image = mw_ref[place, part] - mw_ref[place + 1, part]
+            residual = residual - right[place] * image
         return pressure, residual
 
-    inner = results(w_ref, mw_ref)
-    edge = results(w_edge_ref, mw_edge_ref)
-    cols = pressure_ref.shape[1]
-    lane = lanes_of(edge[0].shape)
-    for out_ref, inside, border in zip((pressure_ref, residual_ref), inner, edge):
-        out_ref[:, :LANES] = jnp.where(lane < RIM, border, inside[:, :LANES])
-        if cols > 2 * LANES:
-            out_ref[:, LANES : cols - LANES] = inside[:, LANES : cols - LANES]
-        out_ref[:, cols - LANES :] = jnp.where(
-            lane >= LANES - RIM, turn(border, -SEAM), inside[:, cols - LANES :]
-        )
+    rows, cols = pressure_ref.shape
+    copies = []
+    for piece in range(PIECES):
+        part = slice(piece * rows // PIECES, (piece + 1) * rows // PIECES)
+        inner = results(w_ref, mw_ref, part)
+        edge = results(w_edge_ref, mw_edge_ref, part)
+        lane = lanes_of(edge[0].shape)
+        for field, (out_ref, out_hbm, inside, border) in enumerate(
+            zip((pressure_ref, residual_ref), (pressure_hbm, residual_hbm), inner, edge)
+        ):
+            out_ref[part, :LANES] = jnp.where(lane < RIM, border, inside[:, :LANES])
+            if cols > 2 * LANES:
+                out_ref[part, LANES : cols - LANES] = inside[:, LANES : cols - LANES]
+            out_ref[part, cols - LANES :] = jnp.where(
+                lane >= LANES - RIM, turn(border, -SEAM), inside[:, cols - LANES :]
+            )
+            there = pl.ds(piece * rows // PIECES, rows // PIECES)
+            copy = pltpu.make_async_copy(
+                out_ref.at[there], out_hbm.at[there], sems.at[field, piece]
+            )
+            copy.start()
+            copies.append(copy)
+    held_copy.wait()
+    for copy in copies:
+        copy.wait()
 
 
 def combine(arrived, w, mw, w_edge, mw_edge):
@@ -482,6 +512,14 @@
     return pl.pallas_call(
         combine_kernel,
         out_shape=[shape, shape, jax.ShapeDtypeStruct(held, jnp.float32)],
+        out_specs=[pl.BlockSpec(memory_space=pltpu.HBM)] * 3,
+        scratch_shapes=[
+            pltpu.VMEM((rows, cols), jnp.float32),
+            pltpu.VMEM((rows, cols), jnp.float32),
+            pltpu.VMEM(held, jnp.float32),
+            pltpu.SemaphoreType.DMA,
+            pltpu.SemaphoreType.DMA((2, PIECES)),
+        ],
         compiler_params=pltpu.CompilerParams(vmem_limit_bytes=VMEM_BYTES),
         name="combine",
     )(arrived, w, mw, w_edge, mw_edge)
@@ -509,8 +547,8 @@
     near, far = integrate(*inputs, ((0, OUTER), (rows - OUTER, OUTER)), True)
     bands = tuple((row, CHUNK) for row in range(0, rows, CHUNK))
     fields, side = integrate(*inputs, bands, False)
+    near = swap(near, "lat", 0, False)
     far = swap(far, "lat", 1, False)
-    near = swap(near, "lat", 0, False)
     near_edge, far_edge = edges(side, near, far)
     far_edge = swap(far_edge, "lon", 1, True)
     near_edge = swap(near_edge, "lon", 0, True)

time: 37.6 us -> 36.4 us (0.968)
  waiting for transfers between devices: 3.57 us -> 1.92 us
  starting transfers between devices: 10.1 us -> 10.5 us
    ppermute x2, starting transfers between devices: 0.49 us -> 3.76 us  [exchange(): return lax.ppermute(values, axis, pairs)]
    ppermute x4, starting transfers between devices: 9.62 us -> 6.76 us  [swap(): return lax.ppermute(values, axis, pairs)]
    ppermute x2, waiting for transfers between devices: 2.48 us -> 0.83 us  [exchange(): return lax.ppermute(values, axis, pairs)]
  transfers between devices with their start and end apart: 6 -> 6, of which waited for: 3 -> 2; matrix products, arithmetic and copies ran while one was open for 0% -> 0% of each run, Pallas kernels for 14% -> 15%
where the time goes in v11:
time: 36.4 us; the launch traced here: 36.1 us
  blocking collectives  11.3 us (31%)
  starting transfers between devices  10.5 us (29%)
  Pallas kernels  9.47 us (26%)
  local copies, waits for them, and re-layouts  2.1 us (6%)
  waiting for transfers between devices  1.92 us (5%)
  between operations  0.74 us (2%)
    all_to_all x1, blocking collectives, on_device(): lax.all_to_all(sent, 'lon', split_axis=0, concat_axis=0, tiled=True)  11.3 us
    ppermute x4, starting transfers between devices, swap(): return lax.ppermute(values, axis, pairs)  6.76 us
    pallas_call x2, Pallas kernels, integrate(): pl.pallas_call(functools.partial(integrate_kernel, bands, outer), in_spec...  4.73 us
    ppermute x2, starting transfers between devices, exchange(): return lax.ppermute(values, axis, pairs)  3.76 us
    unnamed x8, local copies, waits for them, and re-layouts  2.09 us
    pallas_call x1, Pallas kernels, interior(): pl.pallas_call(interior_kernel, out_shape=[jax.ShapeDtypeStruct((STEPS, r...  1.56 us
    pallas_call x1, Pallas kernels, combine(): pl.pallas_call(combine_kernel, out_shape=[shape, shape, jax.ShapeDtypeStr...  1.16 us
    ppermute x4, waiting for transfers between devices, swap(): return lax.ppermute(values, axis, pairs)  1.09 us
  transfers between devices with their start and end apart: 6, of which 2 were waited for; matrix products, arithmetic and copies ran while one was open for 0% of the time, Pallas kernels for 15%

profile of v11, /device:TPU:0, one launch (start us, length us, event | category | flops | bytes accessed | tf_op | source)
XLA Modules:
  0.0 36.1 jit_solution(13274969703595469952)
XLA Ops:
  0.6 0.0 copy-start.2
  0.6 1.8 %outer.1 = (f32[4,8,256]{2,1,0:T(8,128)}, f32[4,8,256]{2,1,0:T(8,128)}) custom-call(f32[16]{0:T(128)} %thick_hbm.3, s32[128,256]{1,0:T(8,128)} %count_hbm.3, f32[128,256]{1,0:T(8,128)} %inertia_hbm.3, bf16[2,16,128,256]{3,2,1,0:T(8,128)(2,1)} %tend_hbm.3), custom_call_target="tpu_custom_call" | custom-call | flops 1572864 | bytes 524288 | tf_op jit(solution)/shard_map/outer/pallas_call | solution.py:130
  2.5 0.0 copy-start.3
  2.5 0.5 %collective-permute-start = (f32[4,8,256]{2,1,0:T(8,128)}, f32[4,8,256]{2,1,0:T(8,128)S(1)}, u32[]{:S(2)}, u32[]{:S(2)}) collective-permute-start(f32[4,8,256]{2,1,0:T(8,128)} %get-tuple-element.23), channel_id=1, source_target_pairs={{0,8},{8,0},{16,24},{24,16},{1,9},{9,1},{17,25},{25,17},{2,10},{10... | collective-permute-start | bytes 98312 | tf_op jit(solution)/shard_map/ppermute | solution.py:539
  3.0 0.7 %collective-permute-start.1 = (f32[4,8,256]{2,1,0:T(8,128)}, f32[4,8,256]{2,1,0:T(8,128)S(1)}, u32[]{:S(2)}, u32[]{:S(2)}) collective-permute-start(f32[4,8,256]{2,1,0:T(8,128)} %get-tuple-element.24), channel_id=1, source_target_pairs={{8,16},{16,8},{9,17},{17,9},{10,18},{18,10},{11,19},{19,11},{12,20... | collective-permute-start | bytes 98312 | tf_op jit(solution)/shard_map/ppermute | solution.py:539
  3.7 0.0 copy-done.2
  3.7 2.9 %whole.1 = (f32[4,128,256]{2,1,0:T(8,128)}, f32[128,128]{1,0:T(8,128)S(1)}) custom-call(f32[16]{0:T(128)S(1)} %copy-done.2, s32[128,256]{1,0:T(8,128)} %count_hbm.3, f32[128,256]{1,0:T(8,128)} %inertia_hbm.3, bf16[2,16,128,256]{3,2,1,0:T(8,128)(2,1)} %tend_hbm.3), custom_call_target="tpu_custom_call" | custom-call | flops 6291456 | bytes 2097152 | tf_op jit(solution)/shard_map/whole/pallas_call | solution.py:130
  6.6 0.0 collective-permute-done.near_ref
  6.6 0.0 collective-permute-done.1.far_ref
  6.6 0.1 edges.1
  6.8 5.6 %collective-permute-start.2 = (f32[24,128]{1,0:T(8,128)S(1)}, f32[24,128]{1,0:T(8,128)S(1)}, u32[]{:S(2)}, u32[]{:S(2)}) collective-permute-start(f32[24,128]{1,0:T(8,128)S(1)} %get-tuple-element.27), channel_id=1, source_target_pairs={{1,2},{2,1},{3,4},{4,3},{5,6},{6,5},{7,0},{0,7},{9,10},{10,9},{11,... | collective-permute-start | bytes 36872 | tf_op jit(solution)/shard_map/ppermute | solution.py:539
  12.3 0.0 collective-permute-start.3
  12.3 0.0 copy-start
  12.3 1.0 %copy-done = f32[4,128,256]{2,1,0:T(8,128)S(1)} copy-done((f32[4,128,256]{2,1,0:T(8,128)S(1)}, f32[4,128,256]{2,1,0:T(8,128)}, u32[]{:S(2)}) %copy-start) | copy-done | bytes 524312
  13.4 1.6 %interior.1 = (f32[4,128,256]{2,1,0:T(8,128)S(1)}, f32[5,128,256]{2,1,0:T(8,128)S(1)}, f32[4,144,128]{2,1,0:T(8,128)S(1)}, f32[8,128]{1,0:T(8,128)S(1)}) custom-call(f32[4,128,256]{2,1,0:T(8,128)S(1)} %copy-done, f32[4,8,256]{2,1,0:T(8,128)S(1)} %collective-permute-done.near_ref, f32[4,8,256]{2,1,0:T(8,128)S(1)} %collective-permute-done.1.far_ref), custom_call_target="tpu_custom_call" | custom-call | flops 9830400 | bytes 2097152 | tf_op jit(solution)/shard_map/interior/pallas_call | solution.py:274
  14.9 0.0 collective-permute-done.2.far_ref
  15.0 1.1 %collective-permute-done.3.near_ref = f32[24,128]{1,0:T(8,128)S(1)} collective-permute-done((f32[24,128]{1,0:T(8,128)S(1)}, f32[24,128]{1,0:T(8,128)S(1)}, u32[]{:S(2)}, u32[]{:S(2)}) %collective-permute-start.3) | collective-permute-done | bytes 12320 | tf_op jit(solution)/shard_map/ppermute | solution.py:539
  16.0 1.0 %strip.1 = (f32[4,128,128]{2,1,0:T(8,128)S(1)}, f32[5,128,128]{2,1,0:T(8,128)S(1)}, f32[8,128]{1,0:T(8,128)S(1)}) custom-call(f32[4,144,128]{2,1,0:T(8,128)S(1)} %get-tuple-element.25.strip_in_ref, f32[24,128]{1,0:T(8,128)S(1)} %collective-permute-done.2.far_ref, f32[24,128]{1,0:T(8,128)S(1)} %collective-permute-done.3.near_ref, ...), custom_call_target="tpu_custom_call" | custom-call | tf_op jit(solution)/shard_map/strip/pallas_call | solution.py:321
  17.0 1.6 %collective-permute-start.4 = (f32[8,128]{1,0:T(8,128)S(1)}, f32[8,128]{1,0:T(8,128)S(1)}, u32[]{:S(2)}, u32[]{:S(2)}) collective-permute-start(f32[8,128]{1,0:T(8,128)S(1)} %get-tuple-element.30), channel_id=1, source_target_pairs={{0,8},{8,0},{16,24},{24,16},{1,9},{9,1},{17,25},{25,17},{2,10},{10... | collective-permute-start | bytes 12296 | tf_op jit(solution)/shard_map/ppermute | solution.py:530
  18.6 0.8 %collective-permute-done.4 = f32[8,128]{1,0:T(8,128)S(1)} collective-permute-done((f32[8,128]{1,0:T(8,128)S(1)}, f32[8,128]{1,0:T(8,128)S(1)}, u32[]{:S(2)}, u32[]{:S(2)}) %collective-permute-start.4) | collective-permute-done | bytes 4128 | tf_op jit(solution)/shard_map/ppermute | solution.py:530
  19.4 2.2 %collective-permute-start.5 = (f32[8,128]{1,0:T(8,128)S(1)}, f32[8,128]{1,0:T(8,128)S(1)}, u32[]{:S(2)}, u32[]{:S(2)}) collective-permute-start(f32[8,128]{1,0:T(8,128)S(1)} %add.3.sums_ref), channel_id=1, source_target_pairs={{0,16},{8,24},{16,0},{24,8},{1,17},{9,25},{17,1},{25,9},{2,18},{10... | collective-permute-start | bytes 12296 | tf_op jit(solution)/shard_map/ppermute | solution.py:530
  21.6 0.0 copy-done.3
  21.6 0.0 copy-start.1
  21.6 1.0 %copy-done.1 = f32[4,128,256]{2,1,0:T(8,128)S(1)} copy-done((f32[4,128,256]{2,1,0:T(8,128)S(1)}, f32[4,128,256]{2,1,0:T(8,128)}, u32[]{:S(2)}) %copy-start.1) | copy-done | bytes 524312
  22.6 0.9 %place.1 = (s16[8,80,128]{2,1,0:T(8,128)(2,1)S(1)}, f32[8,8,128]{2,1,0:T(8,128)S(1)}) custom-call(s32[8]{0:T(128)S(1)} %bitcast.2, f32[4,128,256]{2,1,0:T(8,128)S(1)} %copy-done.1), custom_call_target="tpu_custom_call" | custom-call | flops 1966080 | bytes 393216 | tf_op jit(solution)/shard_map/place/pallas_call | solution.py:377
  23.5 0.0 collective-permute-done.5.other_ref
  23.6 11.3 %all_to_all.5.arrived_ref = s16[8,80,128]{2,1,0:T(8,128)(2,1)S(1)} all-to-all(s16[8,80,128]{2,1,0:T(8,128)(2,1)S(1)} %constant_dynamic-update-slice_fusion), channel_id=1, replica_groups=mesh['lat'=4,'lon'=8] {'lon'}, dimensions={0} | all-to-all | bytes 327680 | tf_op jit(solution)/shard_map/all_to_all | solution.py:564
  34.9 1.2 %combine.1 = (f32[128,256]{1,0:T(8,128)}, f32[128,256]{1,0:T(8,128)}, f32[8,32,256]{2,1,0:T(8,128)}) custom-call(s16[8,80,128]{2,1,0:T(8,128)(2,1)S(1)} %all_to_all.5.arrived_ref, f32[4,128,256]{2,1,0:T(8,128)S(1)} %get-tuple-element.32.w_ref, f32[5,128,256]{2,1,0:T(8,128)S(1)} %get-tuple-element.33.mw_ref, f32[4,128,128]{2,1,0:T(8,128)S(1)} %get-tuple-element.34.w_edge_ref, ...), custom_call_target="tpu_custom_call" | custom-call | tf_op jit(solution)/shard_map/combine/pallas_call | solution.py:512
  (3 shorter events, 0.1 us)
Async XLA Ops:
  0.6 3.0 %copy-start.2 = (f32[16]{0:T(128)S(1)}, f32[16]{0:T(128)}, u32[]{:S(2)}) copy-start(f32[16]{0:T(128)} %thick_hbm.3) | copy-start | bytes 196
  2.5 19.1 %copy-start.3 = (s32[8,1]{0,1:T(1,128)S(1)}, s32[8,1]{0,1:T(1,128)}, u32[]{:S(2)}) copy-start(s32[8,1]{0,1:T(1,128)} %param.9) | copy-start | bytes 100
  2.5 4.1 %collective-permute-start = (f32[4,8,256]{2,1,0:T(8,128)}, f32[4,8,256]{2,1,0:T(8,128)S(1)}, u32[]{:S(2)}, u32[]{:S(2)}) collective-permute-start(f32[4,8,256]{2,1,0:T(8,128)} %get-tuple-element.23), channel_id=1, source_target_pairs={{0,8},{8,0},{16,24},{24,16},{1,9},{9,1},{17,25},{25,17},{2,10},{10... | collective-permute-start | bytes 98312 | tf_op jit(solution)/shard_map/ppermute | solution.py:539
  3.0 3.6 %collective-permute-start.1 = (f32[4,8,256]{2,1,0:T(8,128)}, f32[4,8,256]{2,1,0:T(8,128)S(1)}, u32[]{:S(2)}, u32[]{:S(2)}) collective-permute-start(f32[4,8,256]{2,1,0:T(8,128)} %get-tuple-element.24), channel_id=1, source_target_pairs={{8,16},{16,8},{9,17},{17,9},{10,18},{18,10},{11,19},{19,11},{12,20... | collective-permute-start | bytes 98312 | tf_op jit(solution)/shard_map/ppermute | solution.py:539
  6.8 8.2 %collective-permute-start.2 = (f32[24,128]{1,0:T(8,128)S(1)}, f32[24,128]{1,0:T(8,128)S(1)}, u32[]{:S(2)}, u32[]{:S(2)}) collective-permute-start(f32[24,128]{1,0:T(8,128)S(1)} %get-tuple-element.27), channel_id=1, source_target_pairs={{1,2},{2,1},{3,4},{4,3},{5,6},{6,5},{7,0},{0,7},{9,10},{10,9},{11,... | collective-permute-start | bytes 36872 | tf_op jit(solution)/shard_map/ppermute | solution.py:539
  12.3 3.7 %collective-permute-start.3 = (f32[24,128]{1,0:T(8,128)S(1)}, f32[24,128]{1,0:T(8,128)S(1)}, u32[]{:S(2)}, u32[]{:S(2)}) collective-permute-start(f32[24,128]{1,0:T(8,128)S(1)} %get-tuple-element.28), channel_id=1, source_target_pairs={{0,1},{1,0},{2,3},{3,2},{4,5},{5,4},{6,7},{7,6},{8,9},{9,8},{10,11... | collective-permute-start | bytes 36872 | tf_op jit(solution)/shard_map/ppermute | solution.py:539
  12.3 1.0 %copy-start = (f32[4,128,256]{2,1,0:T(8,128)S(1)}, f32[4,128,256]{2,1,0:T(8,128)}, u32[]{:S(2)}) copy-start(f32[4,128,256]{2,1,0:T(8,128)} %get-tuple-element.21.fields_ref) | copy-start | bytes 1572868
  17.0 2.4 %collective-permute-start.4 = (f32[8,128]{1,0:T(8,128)S(1)}, f32[8,128]{1,0:T(8,128)S(1)}, u32[]{:S(2)}, u32[]{:S(2)}) collective-permute-start(f32[8,128]{1,0:T(8,128)S(1)} %get-tuple-element.30), channel_id=1, source_target_pairs={{0,8},{8,0},{16,24},{24,16},{1,9},{9,1},{17,25},{25,17},{2,10},{10... | collective-permute-start | bytes 12296 | tf_op jit(solution)/shard_map/ppermute | solution.py:530
  19.4 4.1 %collective-permute-start.5 = (f32[8,128]{1,0:T(8,128)S(1)}, f32[8,128]{1,0:T(8,128)S(1)}, u32[]{:S(2)}, u32[]{:S(2)}) collective-permute-start(f32[8,128]{1,0:T(8,128)S(1)} %add.3.sums_ref), channel_id=1, source_target_pairs={{0,16},{8,24},{16,0},{24,8},{1,17},{9,25},{17,1},{25,9},{2,18},{10... | collective-permute-start | bytes 12296 | tf_op jit(solution)/shard_map/ppermute | solution.py:530
  21.6 1.0 %copy-start.1 = (f32[4,128,256]{2,1,0:T(8,128)S(1)}, f32[4,128,256]{2,1,0:T(8,128)}, u32[]{:S(2)}) copy-start(f32[4,128,256]{2,1,0:T(8,128)} %get-tuple-element.21.fields_ref) | copy-start | bytes 1572868

commit v12 on v11

--- a/solution.py
+++ b/solution.py
@@ -15,7 +15,7 @@
 QUARTER = LANES // 4
 EAST = 48
 SEAM = HALF + EAST
-CHUNK = 32
+CHUNK = 16
 FIELDS = 4
 GROUPS = 6
 PITCH = LANES // GROUPS
@@ -34,6 +34,15 @@
 def turn(values, amount):
     amount = amount % values.shape[1]
     return pltpu.roll(values, amount, 1) if amount else values
+
+
+def sides(near, far):
+    place = lax.axis_index("lat")
+    even = is_even("lat")
+    last = lax.axis_size("lat") - 1
+    north = jnp.where(place == 0, 0.0, jnp.where(even, far, near))
+    south = jnp.where(place == last, 0.0, jnp.where(even, near, far))
+    return north, south
 
 
 def is_even(axis):
@@ -58,7 +67,7 @@
 
 def integrate_kernel(bands, outer, thick_hbm, count_hbm, inertia_hbm, tend_hbm, *refs):
     outs, scratch = refs[:2], refs[2:]
-    thick_ref, count_ref, inertia_ref, tend_ref, thick_sem, small_sems, large_sems = scratch
+    thick_ref, count_ref, inertia_ref, tend_ref, thick_sem, small_sems, large_sems = scratch[:7]
     levels = tend_hbm.shape[1]
     thick_copy = pltpu.make_async_copy(thick_hbm, thick_ref, thick_sem)
     copies = []
@@ -101,9 +110,16 @@
         if outer:
             results.append(values)
         else:
-            fields_ref, side_ref = outs
+            fields_hbm, side_ref = outs
+            fields_ref, out_sems = scratch[7:]
             for field in range(FIELDS):
                 fields_ref[field, part] = values[field]
+            here = pl.ds(start, size)
+            done = pltpu.make_async_copy(
+                fields_ref.at[:, here], fields_hbm.at[:, here], out_sems.at[place]
+            )
+            done.start()
+            results.append(done)
             side_ref[part] = pack_edges(fields_ref, part)
         start += size
     if outer:
@@ -114,6 +130,9 @@
             tail = results[1][field][-ROWS:]
             near_ref[field] = jnp.where(even, tail, head)
             far_ref[field] = jnp.where(even, head, tail)
+    else:
+        for done in results:
+            done.wait()
 
 
 def integrate(tendency, thickness, level_count, inertia, bands, outer):
@@ -122,7 +141,14 @@
     f32 = jnp.float32
     if outer:
         out_shape = [jax.ShapeDtypeStruct((FIELDS, ROWS, cols), f32)] * 2
+        out_space = [pltpu.VMEM] * 2
+        extra = []
     else:
+        out_space = [pltpu.HBM, pltpu.VMEM]
+        extra = [
+            pltpu.VMEM((FIELDS, rows, cols), f32),
+            pltpu.SemaphoreType.DMA((len(bands),)),
+        ]
         out_shape = [
             jax.ShapeDtypeStruct((FIELDS, rows, cols), f32),
             jax.ShapeDtypeStruct((rows, LANES), f32),
@@ -131,6 +157,7 @@
         functools.partial(integrate_kernel, bands, outer),
         in_specs=[pl.BlockSpec(memory_space=pltpu.HBM)] * 4,
         out_shape=out_shape,
+        out_specs=[pl.BlockSpec(memory_space=space) for space in out_space],
         scratch_shapes=[
             pltpu.SMEM(thickness.shape, f32),
             pltpu.VMEM((rows, cols), jnp.int32),
@@ -139,6 +166,7 @@
             pltpu.SemaphoreType.DMA,
             pltpu.SemaphoreType.DMA((2, len(bands))),
             pltpu.SemaphoreType.DMA((len(bands),)),
+            *extra,
         ],
         cost_estimate=pl.CostEstimate(
             flops=6 * components * levels * rows * cols,
@@ -151,12 +179,10 @@
 
 
 def edges_kernel(side_ref, near_ref, far_ref, near_out_ref, far_out_ref):
-    even_lat = is_even("lat")
     even_lon = is_even("lon")
     near = pack_edges(near_ref, slice(None))
     far = pack_edges(far_ref, slice(None))
-    north = jnp.where(even_lat, far, near)
-    south = jnp.where(even_lat, near, far)
+    north, south = sides(near, far)
     packed = jnp.concatenate([north, side_ref[...], south], axis=0)
     size = near_out_ref.shape[0]
     lane = lanes_of(near_out_ref.shape)
@@ -247,14 +273,10 @@
     sums_ref,
 ):
     cols = fields_ref.shape[2]
-    even = is_even("lat")
     lane = lanes_of((strip_ref.shape[1], LANES))
     padded = []
     for place in range(FIELDS):
-        near = near_ref[place]
-        far = far_ref[place]
-        north = jnp.where(even, far, near)
-        south = jnp.where(even, near, far)
+        north, south = sides(near_ref[place], far_ref[place])
         values = jnp.concatenate([north, fields_ref[place], south], axis=0)
         east = turn(values[:, cols - LANES :], SEAM)
         strip_ref[place] = jnp.where(lane < HALF, values[:, :LANES], east)
@@ -530,10 +552,10 @@
     return lax.ppermute(values, axis, pairs)
 
 
-def swap(values, axis, first, ring):
+def swap(values, axis, first):
     count = lax.axis_size(axis)
     pairs = []
-    for place in range(first, count if ring else count - 1, 2):
+    for place in range(first, count, 2):
         beside = (place + 1) % count
         pairs += [(place, beside), (beside, place)]
     return lax.ppermute(values, axis, pairs)
@@ -547,11 +569,11 @@
     near, far = integrate(*inputs, ((0, OUTER), (rows - OUTER, OUTER)), True)
     bands = tuple((row, CHUNK) for row in range(0, rows, CHUNK))
     fields, side = integrate(*inputs, bands, False)
-    near = swap(near, "lat", 0, False)
-    far = swap(far, "lat", 1, False)
+    near = swap(near, "lat", 0)
+    far = swap(far, "lat", 1)
     near_edge, far_edge = edges(side, near, far)
-    far_edge = swap(far_edge, "lon", 1, True)
-    near_edge = swap(near_edge, "lon", 0, True)
+    far_edge = swap(far_edge, "lon", 1)
+    near_edge = swap(near_edge, "lon", 0)
     w, mw, strip_in, inner = interior(fields, near, far)
     w_edge, mw_edge, sums = strip(strip_in, near_edge, far_edge, inner)
     sent, scale = place(owner[:, 0], fields, lon_count)

time: 36.4 us -> 35.9 us (0.986)
  starting transfers between devices: 10.5 us -> 8.29 us
  waiting for transfers between devices: 1.92 us -> 3.43 us
    ppermute x2, starting transfers between devices: 3.76 us -> 0.56 us  [exchange(): return lax.ppermute(values, axis, pairs)]
    ppermute x2, waiting for transfers between devices: 0.83 us -> 2.33 us  [exchange(): return lax.ppermute(values, axis, pairs)]
    ppermute x4, starting transfers between devices: 6.76 us -> 7.73 us  [swap(): return lax.ppermute(values, axis, pairs)]
  transfers between devices with their start and end apart: 6 -> 6, of which waited for: 2 -> 3; matrix products, arithmetic and copies ran while one was open for 0% -> 0% of each run, Pallas kernels for 15% -> 16%
where the time goes in v12:
time: 35.9 us; the launch traced here: 35.6 us
  blocking collectives  11.3 us (31%)
  Pallas kernels  9.75 us (27%)
  starting transfers between devices  8.29 us (23%)
  waiting for transfers between devices  3.43 us (10%)
  local copies, waits for them, and re-layouts  2.1 us (6%)
  between operations  0.72 us (2%)
    all_to_all x1, blocking collectives, on_device(): lax.all_to_all(sent, 'lon', split_axis=0, concat_axis=0, tiled=True)  11.3 us
    ppermute x4, starting transfers between devices, swap(): return lax.ppermute(values, axis, pairs)  7.73 us
    pallas_call x2, Pallas kernels, integrate(): pl.pallas_call(functools.partial(integrate_kernel, bands, outer), in_spec...  5.02 us
    ppermute x2, waiting for transfers between devices, exchange(): return lax.ppermute(values, axis, pairs)  2.33 us
    unnamed x8, local copies, waits for them, and re-layouts  2.09 us
    pallas_call x1, Pallas kernels, interior(): pl.pallas_call(interior_kernel, out_shape=[jax.ShapeDtypeStruct((STEPS, r...  1.55 us
    pallas_call x1, Pallas kernels, combine(): pl.pallas_call(combine_kernel, out_shape=[shape, shape, jax.ShapeDtypeStr...  1.16 us
    ppermute x4, waiting for transfers between devices, swap(): return lax.ppermute(values, axis, pairs)  1.09 us
  transfers between devices with their start and end apart: 6, of which 3 were waited for; matrix products, arithmetic and copies ran while one was open for 0% of the time, Pallas kernels for 16%

profile of v12, /device:TPU:0, one launch (start us, length us, event | category | flops | bytes accessed | tf_op | source)
XLA Modules:
  0.0 35.6 jit_solution(1138867451814047768)
XLA Ops:
  0.6 0.0 copy-start.2
  0.6 1.8 %outer.1 = (f32[4,8,256]{2,1,0:T(8,128)}, f32[4,8,256]{2,1,0:T(8,128)}) custom-call(f32[16]{0:T(128)} %thick_hbm.3, s32[128,256]{1,0:T(8,128)} %count_hbm.3, f32[128,256]{1,0:T(8,128)} %inertia_hbm.3, bf16[2,16,128,256]{3,2,1,0:T(8,128)(2,1)} %tend_hbm.3), custom_call_target="tpu_custom_call" | custom-call | flops 1572864 | bytes 524288 | tf_op jit(solution)/shard_map/outer/pallas_call | solution.py:156
  2.5 0.0 copy-start.3
  2.5 0.5 %collective-permute-start = (f32[4,8,256]{2,1,0:T(8,128)}, f32[4,8,256]{2,1,0:T(8,128)S(1)}, u32[]{:S(2)}, u32[]{:S(2)}) collective-permute-start(f32[4,8,256]{2,1,0:T(8,128)} %get-tuple-element.23), channel_id=1, source_target_pairs={{0,8},{8,0},{16,24},{24,16},{1,9},{9,1},{17,25},{25,17},{2,10},{10... | collective-permute-start | bytes 98312 | tf_op jit(solution)/shard_map/ppermute | solution.py:561
  3.0 2.6 %collective-permute-start.1 = (f32[4,8,256]{2,1,0:T(8,128)}, f32[4,8,256]{2,1,0:T(8,128)S(1)}, u32[]{:S(2)}, u32[]{:S(2)}) collective-permute-start(f32[4,8,256]{2,1,0:T(8,128)} %get-tuple-element.24), channel_id=1, source_target_pairs={{8,16},{16,8},{24,0},{0,24},{9,17},{17,9},{25,1},{1,25},{10,18},{1... | collective-permute-start | bytes 98312 | tf_op jit(solution)/shard_map/ppermute | solution.py:561
  5.7 0.0 copy-done.2
  5.7 3.2 %whole.1 = (f32[4,128,256]{2,1,0:T(8,128)}, f32[128,128]{1,0:T(8,128)S(1)}) custom-call(f32[16]{0:T(128)S(1)} %copy-done.2, s32[128,256]{1,0:T(8,128)} %count_hbm.3, f32[128,256]{1,0:T(8,128)} %inertia_hbm.3, bf16[2,16,128,256]{3,2,1,0:T(8,128)(2,1)} %tend_hbm.3), custom_call_target="tpu_custom_call" | custom-call | flops 6291456 | bytes 2097152 | tf_op jit(solution)/shard_map/whole/pallas_call | solution.py:156
  8.8 0.0 collective-permute-done.near_ref
  8.9 0.0 collective-permute-done.1.far_ref
  8.9 0.1 edges.1
  9.0 4.6 %collective-permute-start.2 = (f32[24,128]{1,0:T(8,128)S(1)}, f32[24,128]{1,0:T(8,128)S(1)}, u32[]{:S(2)}, u32[]{:S(2)}) collective-permute-start(f32[24,128]{1,0:T(8,128)S(1)} %get-tuple-element.27), channel_id=1, source_target_pairs={{1,2},{2,1},{3,4},{4,3},{5,6},{6,5},{7,0},{0,7},{9,10},{10,9},{11,... | collective-permute-start | bytes 36872 | tf_op jit(solution)/shard_map/ppermute | solution.py:561
  13.6 0.0 collective-permute-start.3
  13.6 0.0 copy-start
  13.6 1.0 %copy-done = f32[4,128,256]{2,1,0:T(8,128)S(1)} copy-done((f32[4,128,256]{2,1,0:T(8,128)S(1)}, f32[4,128,256]{2,1,0:T(8,128)}, u32[]{:S(2)}) %copy-start) | copy-done | bytes 524312
  14.6 1.6 %interior.1 = (f32[4,128,256]{2,1,0:T(8,128)S(1)}, f32[5,128,256]{2,1,0:T(8,128)S(1)}, f32[4,144,128]{2,1,0:T(8,128)S(1)}, f32[8,128]{1,0:T(8,128)S(1)}) custom-call(f32[4,128,256]{2,1,0:T(8,128)S(1)} %copy-done, f32[4,8,256]{2,1,0:T(8,128)S(1)} %collective-permute-done.near_ref, f32[4,8,256]{2,1,0:T(8,128)S(1)} %collective-permute-done.1.far_ref), custom_call_target="tpu_custom_call" | custom-call | flops 9830400 | bytes 2097152 | tf_op jit(solution)/shard_map/interior/pallas_call | solution.py:296
  16.2 0.0 collective-permute-done.2.far_ref
  16.2 1.1 %collective-permute-done.3.near_ref = f32[24,128]{1,0:T(8,128)S(1)} collective-permute-done((f32[24,128]{1,0:T(8,128)S(1)}, f32[24,128]{1,0:T(8,128)S(1)}, u32[]{:S(2)}, u32[]{:S(2)}) %collective-permute-start.3) | collective-permute-done | bytes 12320 | tf_op jit(solution)/shard_map/ppermute | solution.py:561
  17.3 1.0 %strip.1 = (f32[4,128,128]{2,1,0:T(8,128)S(1)}, f32[5,128,128]{2,1,0:T(8,128)S(1)}, f32[8,128]{1,0:T(8,128)S(1)}) custom-call(f32[4,144,128]{2,1,0:T(8,128)S(1)} %get-tuple-element.25.strip_in_ref, f32[24,128]{1,0:T(8,128)S(1)} %collective-permute-done.2.far_ref, f32[24,128]{1,0:T(8,128)S(1)} %collective-permute-done.3.near_ref, ...), custom_call_target="tpu_custom_call" | custom-call | tf_op jit(solution)/shard_map/strip/pallas_call | solution.py:343
  18.2 0.1 collective-permute-start.4
  18.3 1.2 %collective-permute-done.4 = f32[8,128]{1,0:T(8,128)S(1)} collective-permute-done((f32[8,128]{1,0:T(8,128)S(1)}, f32[8,128]{1,0:T(8,128)S(1)}, u32[]{:S(2)}, u32[]{:S(2)}) %collective-permute-start.4) | collective-permute-done | bytes 4128 | tf_op jit(solution)/shard_map/ppermute | solution.py:552
  19.5 0.5 %collective-permute-start.5 = (f32[8,128]{1,0:T(8,128)S(1)}, f32[8,128]{1,0:T(8,128)S(1)}, u32[]{:S(2)}, u32[]{:S(2)}) collective-permute-start(f32[8,128]{1,0:T(8,128)S(1)} %add.3.sums_ref), channel_id=1, source_target_pairs={{0,16},{8,24},{16,0},{24,8},{1,17},{9,25},{17,1},{25,9},{2,18},{10... | collective-permute-start | bytes 12296 | tf_op jit(solution)/shard_map/ppermute | solution.py:552
  20.0 0.0 copy-done.3
  20.0 0.0 copy-start.1
  20.0 1.0 %copy-done.1 = f32[4,128,256]{2,1,0:T(8,128)S(1)} copy-done((f32[4,128,256]{2,1,0:T(8,128)S(1)}, f32[4,128,256]{2,1,0:T(8,128)}, u32[]{:S(2)}) %copy-start.1) | copy-done | bytes 524312
  21.0 0.9 %place.1 = (s16[8,80,128]{2,1,0:T(8,128)(2,1)S(1)}, f32[8,8,128]{2,1,0:T(8,128)S(1)}) custom-call(s32[8]{0:T(128)S(1)} %bitcast.2, f32[4,128,256]{2,1,0:T(8,128)S(1)} %copy-done.1), custom_call_target="tpu_custom_call" | custom-call | flops 1966080 | bytes 393216 | tf_op jit(solution)/shard_map/place/pallas_call | solution.py:399
  21.9 1.2 %collective-permute-done.5.other_ref = f32[8,128]{1,0:T(8,128)S(1)} collective-permute-done((f32[8,128]{1,0:T(8,128)S(1)}, f32[8,128]{1,0:T(8,128)S(1)}, u32[]{:S(2)}, u32[]{:S(2)}) %collective-permute-start.5) | collective-permute-done | bytes 4128 | tf_op jit(solution)/shard_map/ppermute | solution.py:552
  23.1 11.3 %all_to_all.5.arrived_ref = s16[8,80,128]{2,1,0:T(8,128)(2,1)S(1)} all-to-all(s16[8,80,128]{2,1,0:T(8,128)(2,1)S(1)} %constant_dynamic-update-slice_fusion), channel_id=1, replica_groups=mesh['lat'=4,'lon'=8] {'lon'}, dimensions={0} | all-to-all | bytes 327680 | tf_op jit(solution)/shard_map/all_to_all | solution.py:586
  34.5 1.2 %combine.1 = (f32[128,256]{1,0:T(8,128)}, f32[128,256]{1,0:T(8,128)}, f32[8,32,256]{2,1,0:T(8,128)}) custom-call(s16[8,80,128]{2,1,0:T(8,128)(2,1)S(1)} %all_to_all.5.arrived_ref, f32[4,128,256]{2,1,0:T(8,128)S(1)} %get-tuple-element.32.w_ref, f32[5,128,256]{2,1,0:T(8,128)S(1)} %get-tuple-element.33.mw_ref, f32[4,128,128]{2,1,0:T(8,128)S(1)} %get-tuple-element.34.w_edge_ref, ...), custom_call_target="tpu_custom_call" | custom-call | tf_op jit(solution)/shard_map/combine/pallas_call | solution.py:534
  (3 shorter events, 0.1 us)
Async XLA Ops:
  0.6 5.0 %copy-start.2 = (f32[16]{0:T(128)S(1)}, f32[16]{0:T(128)}, u32[]{:S(2)}) copy-start(f32[16]{0:T(128)} %thick_hbm.3) | copy-start | bytes 196
  2.5 17.5 %copy-start.3 = (s32[8,1]{0,1:T(1,128)S(1)}, s32[8,1]{0,1:T(1,128)}, u32[]{:S(2)}) copy-start(s32[8,1]{0,1:T(1,128)} %param.9) | copy-start | bytes 100
  2.5 6.4 %collective-permute-start = (f32[4,8,256]{2,1,0:T(8,128)}, f32[4,8,256]{2,1,0:T(8,128)S(1)}, u32[]{:S(2)}, u32[]{:S(2)}) collective-permute-start(f32[4,8,256]{2,1,0:T(8,128)} %get-tuple-element.23), channel_id=1, source_target_pairs={{0,8},{8,0},{16,24},{24,16},{1,9},{9,1},{17,25},{25,17},{2,10},{10... | collective-permute-start | bytes 98312 | tf_op jit(solution)/shard_map/ppermute | solution.py:561
  3.0 5.8 %collective-permute-start.1 = (f32[4,8,256]{2,1,0:T(8,128)}, f32[4,8,256]{2,1,0:T(8,128)S(1)}, u32[]{:S(2)}, u32[]{:S(2)}) collective-permute-start(f32[4,8,256]{2,1,0:T(8,128)} %get-tuple-element.24), channel_id=1, source_target_pairs={{8,16},{16,8},{24,0},{0,24},{9,17},{17,9},{25,1},{1,25},{10,18},{1... | collective-permute-start | bytes 98312 | tf_op jit(solution)/shard_map/ppermute | solution.py:561
  9.0 7.2 %collective-permute-start.2 = (f32[24,128]{1,0:T(8,128)S(1)}, f32[24,128]{1,0:T(8,128)S(1)}, u32[]{:S(2)}, u32[]{:S(2)}) collective-permute-start(f32[24,128]{1,0:T(8,128)S(1)} %get-tuple-element.27), channel_id=1, source_target_pairs={{1,2},{2,1},{3,4},{4,3},{5,6},{6,5},{7,0},{0,7},{9,10},{10,9},{11,... | collective-permute-start | bytes 36872 | tf_op jit(solution)/shard_map/ppermute | solution.py:561
  13.6 3.7 %collective-permute-start.3 = (f32[24,128]{1,0:T(8,128)S(1)}, f32[24,128]{1,0:T(8,128)S(1)}, u32[]{:S(2)}, u32[]{:S(2)}) collective-permute-start(f32[24,128]{1,0:T(8,128)S(1)} %get-tuple-element.28), channel_id=1, source_target_pairs={{0,1},{1,0},{2,3},{3,2},{4,5},{5,4},{6,7},{7,6},{8,9},{9,8},{10,11... | collective-permute-start | bytes 36872 | tf_op jit(solution)/shard_map/ppermute | solution.py:561
  13.6 1.0 %copy-start = (f32[4,128,256]{2,1,0:T(8,128)S(1)}, f32[4,128,256]{2,1,0:T(8,128)}, u32[]{:S(2)}) copy-start(f32[4,128,256]{2,1,0:T(8,128)} %get-tuple-element.21.fields_ref) | copy-start | bytes 1572868
  18.2 1.2 %collective-permute-start.4 = (f32[8,128]{1,0:T(8,128)S(1)}, f32[8,128]{1,0:T(8,128)S(1)}, u32[]{:S(2)}, u32[]{:S(2)}) collective-permute-start(f32[8,128]{1,0:T(8,128)S(1)} %get-tuple-element.30), channel_id=1, source_target_pairs={{0,8},{8,0},{16,24},{24,16},{1,9},{9,1},{17,25},{25,17},{2,10},{10... | collective-permute-start | bytes 12296 | tf_op jit(solution)/shard_map/ppermute | solution.py:552
  19.5 3.6 %collective-permute-start.5 = (f32[8,128]{1,0:T(8,128)S(1)}, f32[8,128]{1,0:T(8,128)S(1)}, u32[]{:S(2)}, u32[]{:S(2)}) collective-permute-start(f32[8,128]{1,0:T(8,128)S(1)} %add.3.sums_ref), channel_id=1, source_target_pairs={{0,16},{8,24},{16,0},{24,8},{1,17},{9,25},{17,1},{25,9},{2,18},{10... | collective-permute-start | bytes 12296 | tf_op jit(solution)/shard_map/ppermute | solution.py:552
  20.0 1.0 %copy-start.1 = (f32[4,128,256]{2,1,0:T(8,128)S(1)}, f32[4,128,256]{2,1,0:T(8,128)}, u32[]{:S(2)}) copy-start(f32[4,128,256]{2,1,0:T(8,128)} %get-tuple-element.21.fields_ref) | copy-start | bytes 1572868

commit v13 on v8

--- a/solution.py
+++ b/solution.py
@@ -19,6 +19,8 @@
 FIELDS = 4
 GROUPS = 6
 PITCH = LANES // GROUPS
+PIECES = 2
+OUTER = 16
 TAIL = 16
 SUM_ROWS = 4
 VMEM_BYTES = 16 * 1024 * 1024
@@ -32,6 +34,15 @@
 def turn(values, amount):
     amount = amount % values.shape[1]
     return pltpu.roll(values, amount, 1) if amount else values
+
+
+def sides(near, far):
+    place = lax.axis_index("lat")
+    even = is_even("lat")
+    last = lax.axis_size("lat") - 1
+    north = jnp.where(place == 0, 0.0, jnp.where(even, far, near))
+    south = jnp.where(place == last, 0.0, jnp.where(even, near, far))
+    return north, south
 
 
 def is_even(axis):
@@ -141,20 +152,13 @@
 
 
 def edges_kernel(outer_ref, middle_ref, near_ref, far_ref, near_out_ref, far_out_ref):
-    even_lat = is_even("lat")
     even_lon = is_even("lon")
     near = pack_edges(near_ref, slice(None))
     far = pack_edges(far_ref, slice(None))
     half = outer_ref.shape[0] // 2
+    north, south = sides(near, far)
     packed = jnp.concatenate(
-        [
-            jnp.where(even_lat, far, near),
-            outer_ref[:half],
-            middle_ref[...],
-            outer_ref[half:],
-            jnp.where(even_lat, near, far),
-        ],
-        axis=0,
+        [north, outer_ref[:half], middle_ref[...], outer_ref[half:], south], axis=0
     )
     size = near_out_ref.shape[0]
     lane = lanes_of(near_out_ref.shape)
@@ -247,22 +251,18 @@
 ):
     half = outer_ref.shape[1] // 2
     cols = outer_ref.shape[2]
-    even = is_even("lat")
     lane = lanes_of((strip_ref.shape[1], LANES))
     padded = []
     for place in range(FIELDS):
-        near = near_ref[place]
-        far = far_ref[place]
-        values = jnp.concatenate(
-            [
-                jnp.where(even, far, near),
-                outer_ref[place, :half],
-                middle_ref[place],
-                outer_ref[place, half:],
-                jnp.where(even, near, far),
-            ],
-            axis=0,
-        )
+        north, south = sides(near_ref[place], far_ref[place])
+        pieces = [
+            north,
+            outer_ref[place, :half],
+            middle_ref[place],
+            outer_ref[place, half:],
+            south,
+        ]
+        values = jnp.concatenate(pieces, axis=0)
         east = turn(values[:, cols - LANES :], SEAM)
         strip_ref[place] = jnp.where(lane < HALF, values[:, :LANES], east)
         padded.append(values)
@@ -295,7 +295,7 @@
     )(outer, middle, near, far)
 
 
-def strip_kernel(strip_in_ref, near_ref, far_ref, inner_ref, w_ref, mw_ref, sums_ref):
+def strip_kernel(strip_in_ref, far_ref, near_ref, inner_ref, w_ref, mw_ref, sums_ref):
     even = is_even("lon")
     near = near_ref[...]
     far = far_ref[...]
@@ -335,7 +335,7 @@
         ],
         compiler_params=pltpu.CompilerParams(vmem_limit_bytes=VMEM_BYTES),
         name="strip",
-    )(strip_in, near, far, inner)
+    )(strip_in, far, near, inner)
 
 
 def power(exponent):
@@ -428,22 +428,55 @@
     )(sums, other, scale)
 
 
-def combine_kernel(
-    arrived_ref, w_ref, mw_ref, w_edge_ref, mw_edge_ref, pressure_ref, residual_ref, held_ref
-):
-    rows = held_ref.shape[1]
+def tally_kernel(arrived_ref, sums_ref):
     packed = jnp.zeros((SUM_ROWS, LANES), jnp.float32)
-    for slot in range(held_ref.shape[0]):
+    for slot in range(arrived_ref.shape[0]):
         tail = arrived_ref[slot, arrived_ref.shape[1] - TAIL :].astype(jnp.int32)
         digits = tail.astype(jnp.float32)
         high = digits[SUM_ROWS : 2 * SUM_ROWS]
         low = digits[2 * SUM_ROWS : 3 * SUM_ROWS]
         packed = packed + (high + low * 2.0**-15) * power(tail[:SUM_ROWS] - 14)
+    sums_ref[:SUM_ROWS] = packed
+    sums_ref[SUM_ROWS:] = jnp.zeros((ROWS - SUM_ROWS, LANES), jnp.float32)
+
+
+def tally(arrived):
+    return pl.pallas_call(
+        tally_kernel,
+        out_shape=jax.ShapeDtypeStruct((ROWS, LANES), jnp.float32),
+        compiler_params=pltpu.CompilerParams(vmem_limit_bytes=VMEM_BYTES),
+        name="tally",
+    )(arrived)
+
+
+def combine_kernel(
+    sums_ref,
+    other_ref,
+    arrived_ref,
+    w_ref,
+    mw_ref,
+    w_edge_ref,
+    mw_edge_ref,
+    pressure_hbm,
+    residual_hbm,
+    held_hbm,
+    pressure_ref,
+    residual_ref,
+    held_ref,
+    held_sem,
+    sems,
+):
+    rows = held_ref.shape[1]
+    for slot in range(held_ref.shape[0]):
+        tail = arrived_ref[slot, arrived_ref.shape[1] - TAIL :].astype(jnp.int32)
         for half in range(held_ref.shape[2] // LANES):
             at = 3 * SUM_ROWS + half
             scale = power(tail[at : at + 1] - 15)
             whole = arrived_ref[slot, half * rows : (half + 1) * rows].astype(jnp.int32)
             held_ref[slot, :, half * LANES : (half + 1) * LANES] = whole.astype(jnp.float32) * scale
+    held_copy = pltpu.make_async_copy(held_ref, held_hbm, held_sem)
+    held_copy.start()
+    packed = jnp.where(is_even("lat"), other_ref[:SUM_ROWS], sums_ref[:SUM_ROWS])
     quarter = lanes_of(packed.shape) // QUARTER
     totals = [
         jnp.sum(jnp.where(quarter == place, packed, 0.0), axis=1, keepdims=True)
@@ -470,48 +503,73 @@
             right[pivot] = right[pivot] - matrix[pivot, col] * right[col]
         right[pivot] = right[pivot] * matrix[pivot, pivot]
 
-    def results(w_ref, mw_ref):
-        pressure = right[0] * w_ref[0]
-        residual = mw_ref[0] - right[0] * (mw_ref[0] - mw_ref[1])
+    def results(w_ref, mw_ref, part):
+        pressure = right[0] * w_ref[0, part]
+        residual = mw_ref[0, part] - right[0] * (mw_ref[0, part] - mw_ref[1, part])
         for place in range(1, STEPS):
-            pressure = pressure + right[place] * w_ref[place]
-            residual = residual - right[place] * (mw_ref[place] - mw_ref[place + 1])
+            pressure = pressure + right[place] * w_ref[place, part]
+            image = mw_ref[place, part] - mw_ref[place + 1, part]
+            residual = residual - right[place] * image
         return pressure, residual
 
-    inner = results(w_ref, mw_ref)
-    edge = results(w_edge_ref, mw_edge_ref)
-    cols = pressure_ref.shape[1]
-    lane = lanes_of(edge[0].shape)
-    for out_ref, inside, border in zip((pressure_ref, residual_ref), inner, edge):
-        out_ref[:, :LANES] = jnp.where(lane < RIM, border, inside[:, :LANES])
-        if cols > 2 * LANES:
-            out_ref[:, LANES : cols - LANES] = inside[:, LANES : cols - LANES]
-        out_ref[:, cols - LANES :] = jnp.where(
-            lane >= LANES - RIM, turn(border, -SEAM), inside[:, cols - LANES :]
-        )
-
-
-def combine(arrived, w, mw, w_edge, mw_edge):
+    rows, cols = pressure_ref.shape
+    copies = []
+    for piece in range(PIECES):
+        part = slice(piece * rows // PIECES, (piece + 1) * rows // PIECES)
+        inner = results(w_ref, mw_ref, part)
+        edge = results(w_edge_ref, mw_edge_ref, part)
+        lane = lanes_of(edge[0].shape)
+        for field, (out_ref, out_hbm, inside, border) in enumerate(
+            zip((pressure_ref, residual_ref), (pressure_hbm, residual_hbm), inner, edge)
+        ):
+            out_ref[part, :LANES] = jnp.where(lane < RIM, border, inside[:, :LANES])
+            if cols > 2 * LANES:
+                out_ref[part, LANES : cols - LANES] = inside[:, LANES : cols - LANES]
+            out_ref[part, cols - LANES :] = jnp.where(
+                lane >= LANES - RIM, turn(border, -SEAM), inside[:, cols - LANES :]
+            )
+            there = pl.ds(piece * rows // PIECES, rows // PIECES)
+            copy = pltpu.make_async_copy(
+                out_ref.at[there], out_hbm.at[there], sems.at[field, piece]
+            )
+            copy.start()
+            copies.append(copy)
+    held_copy.wait()
+    for copy in copies:
+        copy.wait()
+
+
+def combine(sums, other, arrived, w, mw, w_edge, mw_edge):
     rows, cols = w.shape[1:]
     shape = jax.ShapeDtypeStruct((rows, cols), jnp.float32)
     held = (arrived.shape[0], (arrived.shape[1] - TAIL) * LANES // cols, cols)
     return pl.pallas_call(
         combine_kernel,
         out_shape=[shape, shape, jax.ShapeDtypeStruct(held, jnp.float32)],
+        out_specs=[pl.BlockSpec(memory_space=pltpu.HBM)] * 3,
+        scratch_shapes=[
+            pltpu.VMEM((rows, cols), jnp.float32),
+            pltpu.VMEM((rows, cols), jnp.float32),
+            pltpu.VMEM(held, jnp.float32),
+            pltpu.SemaphoreType.DMA,
+            pltpu.SemaphoreType.DMA((2, PIECES)),
+        ],
         compiler_params=pltpu.CompilerParams(vmem_limit_bytes=VMEM_BYTES),
         name="combine",
-    )(arrived, w, mw, w_edge, mw_edge)
-
-
-def exchange(values, axis, distance):
-    pairs = [(place, place ^ distance) for place in range(lax.axis_size(axis))]
-    return lax.ppermute(values, axis, pairs)
-
-
-def swap(values, axis, first, ring):
+    )(sums, other, arrived, w, mw, w_edge, mw_edge)
+
+
+def exchange_odd(values, distance):
+    pairs = [
+        (place, place ^ distance if place % 2 else place) for place in range(lax.axis_size("lat"))
+    ]
+    return lax.ppermute(values, "lat", pairs)
+
+
+def swap(values, axis, first):
     count = lax.axis_size(axis)
     pairs = []
-    for place in range(first, count if ring else count - 1, 2):
+    for place in range(first, count, 2):
         beside = (place + 1) % count
         pairs += [(place, beside), (beside, place)]
     return lax.ppermute(values, axis, pairs)
@@ -521,27 +579,32 @@
     lat_count = lax.axis_size("lat")
     lon_count = lax.axis_size("lon")
     rows = level_count.shape[0]
-    tall = min(CHUNK, rows // 4)
+    tall = OUTER
     inputs = (tendency, thickness, level_count, inertia)
     outer, outer_side, near, far = integrate(*inputs, ((0, tall), (rows - tall, tall)), True)
-    bands = tuple((row, tall) for row in range(tall, rows - tall, tall))
+    bands = tuple(
+        (row, min(CHUNK, rows - tall - row)) for row in range(tall, rows - tall, CHUNK)
+    )
     middle, middle_side = integrate(*inputs, bands, False)
-    near = swap(near, "lat", 0, False)
-    far = swap(far, "lat", 1, False)
+    near = swap(near, "lat", 0)
+    far = swap(far, "lat", 1)
     near_edge, far_edge = edges(outer_side, middle_side, near, far)
-    near_edge = swap(near_edge, "lon", 0, True)
-    far_edge = swap(far_edge, "lon", 1, True)
+    far_edge = swap(far_edge, "lon", 1)
+    near_edge = swap(near_edge, "lon", 0)
     w, mw, strip_in, inner = interior(outer, middle, near, far)
     w_edge, mw_edge, sums = strip(strip_in, near_edge, far_edge, inner)
     sent, scale = place(owner[:, 0], outer, middle, lon_count)
-    shift = 1
+    sums = sums + swap(sums, "lat", 0)
+    shift = 2
     while 2 * shift < lat_count:
-        sums = sums + exchange(sums, "lat", shift)
+        sums = sums + exchange_odd(sums, shift)
         shift *= 2
-    tail = seal(sums, exchange(sums, "lat", shift), scale)
+    tail = seal(sums, exchange_odd(sums, shift), scale)
     sent = lax.dynamic_update_slice(sent, tail, (0, sent.shape[1] - TAIL, 0))
     arrived = lax.all_to_all(sent, "lon", split_axis=0, concat_axis=0, tiled=True)
-    pressure, residual, held = combine(arrived, w, mw, w_edge, mw_edge)
+    sums = tally(arrived)
+    other = swap(sums, "lat", 0)
+    pressure, residual, held = combine(sums, other, arrived, w, mw, w_edge, mw_edge)
     held = held.reshape((1, 1, lon_count, 2, held.shape[1] // 2, held.shape[2]))
     return (held, pressure, residual)
 

time: 37.4 us -> 36.5 us (0.976)
  starting transfers between devices: 11.7 us -> 9.16 us
  waiting for transfers between devices: 1.11 us -> 3.1 us
  blocking collectives: 12.3 us -> 11.9 us
    ppermute x2 -> x1, starting transfers between devices: 4.37 us -> 0.65 us  [exchange_odd(): return lax.ppermute(values, 'lat', pairs)]
    ppermute x4 -> x6, waiting for transfers between devices: 0.29 us -> 3.09 us  [swap(): return lax.ppermute(values, axis, pairs)]
    ppermute x4 -> x6, starting transfers between devices: 7.29 us -> 8.51 us  [swap(): return lax.ppermute(values, axis, pairs)]
    ppermute x2 -> x1, waiting for transfers between devices: 0.83 us -> 0.01 us  [exchange_odd(): return lax.ppermute(values, 'lat', pairs)]
    all_to_all x1, blocking collectives: 12.3 us -> 11.9 us  [on_device(): lax.all_to_all(sent, 'lon', split_axis=0, concat_axis=0, tiled=True)]
  transfers between devices with their start and end apart: 6 -> 7, of which waited for: 2 -> 3; matrix products, arithmetic and copies ran while one was open for 0% -> 0% of each run, Pallas kernels for 12% -> 14%
where the time goes in v13:
time: 36.5 us; the launch traced here: 36.3 us
  blocking collectives  11.9 us (33%)
  Pallas kernels  9.36 us (26%)
  starting transfers between devices  9.16 us (25%)
  waiting for transfers between devices  3.1 us (8%)
  local copies, waits for them, and re-layouts  2.02 us (6%)
  between operations  0.78 us (2%)
    all_to_all x1, blocking collectives, on_device(): lax.all_to_all(sent, 'lon', split_axis=0, concat_axis=0, tiled=True)  11.9 us
    ppermute x6, starting transfers between devices, swap(): return lax.ppermute(values, axis, pairs)  8.51 us
    pallas_call x2, Pallas kernels, integrate(): pl.pallas_call(functools.partial(integrate_kernel, bands, outer), in_spec...  4.55 us
    ppermute x6, waiting for transfers between devices, swap(): return lax.ppermute(values, axis, pairs)  3.09 us
    unnamed x12, local copies, waits for them, and re-layouts  2.01 us
    pallas_call x1, Pallas kernels, interior(): pl.pallas_call(interior_kernel, out_shape=[jax.ShapeDtypeStruct((STEPS, r...  1.57 us
    pallas_call x1, Pallas kernels, combine(): pl.pallas_call(combine_kernel, out_shape=[shape, shape, jax.ShapeDtypeStr...  1.15 us
    pallas_call x1, Pallas kernels, strip(): pl.pallas_call(strip_kernel, out_shape=[jax.ShapeDtypeStruct((STEPS, rows...  0.97 us
  transfers between devices with their start and end apart: 7, of which 3 were waited for; matrix products, arithmetic and copies ran while one was open for 0% of the time, Pallas kernels for 14%

profile of v13, /device:TPU:0, one launch (start us, length us, event | category | flops | bytes accessed | tf_op | source)
XLA Modules:
  0.0 36.3 jit_solution(2112833875001013561)
XLA Ops:
  0.6 0.0 copy-start.4
  0.6 2.0 %outer.1 = (f32[4,32,256]{2,1,0:T(8,128)}, f32[32,128]{1,0:T(8,128)}, f32[4,8,256]{2,1,0:T(8,128)}, f32[4,8,256]{2,1,0:T(8,128)}) custom-call(f32[16]{0:T(128)} %thick_hbm.3, s32[128,256]{1,0:T(8,128)} %count_hbm.3, f32[128,256]{1,0:T(8,128)} %inertia_hbm.3, bf16[2,16,128,256]{3,2,1,0:T(8,128)(2,1)} %tend_hbm.3), custom_call_target="tpu_custom_call" | custom-call | flops 1572864 | bytes 524288 | tf_op jit(solution)/shard_map/outer/pallas_call | solution.py:127
  2.6 0.0 copy-start.3
  2.6 0.0 copy-start.2
  2.7 0.0 copy-start.5
  2.7 0.5 %collective-permute-start = (f32[4,8,256]{2,1,0:T(8,128)}, f32[4,8,256]{2,1,0:T(8,128)S(1)}, u32[]{:S(2)}, u32[]{:S(2)}) collective-permute-start(f32[4,8,256]{2,1,0:T(8,128)} %get-tuple-element.26), channel_id=1, source_target_pairs={{0,8},{8,0},{16,24},{24,16},{1,9},{9,1},{17,25},{25,17},{2,10},{10... | collective-permute-start | bytes 98312 | tf_op jit(solution)/shard_map/ppermute | solution.py:575
  3.2 2.6 %collective-permute-start.1 = (f32[4,8,256]{2,1,0:T(8,128)}, f32[4,8,256]{2,1,0:T(8,128)S(1)}, u32[]{:S(2)}, u32[]{:S(2)}) collective-permute-start(f32[4,8,256]{2,1,0:T(8,128)} %get-tuple-element.27), channel_id=1, source_target_pairs={{8,16},{16,8},{24,0},{0,24},{9,17},{17,9},{25,1},{1,25},{10,18},{1... | collective-permute-start | bytes 98312 | tf_op jit(solution)/shard_map/ppermute | solution.py:575
  5.8 0.0 copy-done.4
  5.8 2.6 %middle.1 = (f32[4,96,256]{2,1,0:T(8,128)}, f32[96,128]{1,0:T(8,128)S(1)}) custom-call(f32[16]{0:T(128)S(1)} %copy-done.4, s32[128,256]{1,0:T(8,128)} %count_hbm.3, f32[128,256]{1,0:T(8,128)} %inertia_hbm.3, bf16[2,16,128,256]{3,2,1,0:T(8,128)(2,1)} %tend_hbm.3), custom_call_target="tpu_custom_call" | custom-call | flops 4718592 | bytes 1572864 | tf_op jit(solution)/shard_map/middle/pallas_call | solution.py:127
  8.4 0.0 collective-permute-done.near_ref
  8.4 0.0 collective-permute-done.1.far_ref
  8.4 0.0 copy-done.3
  8.4 0.1 edges.1
  8.6 4.6 %collective-permute-start.2 = (f32[24,128]{1,0:T(8,128)S(1)}, f32[24,128]{1,0:T(8,128)S(1)}, u32[]{:S(2)}, u32[]{:S(2)}) collective-permute-start(f32[24,128]{1,0:T(8,128)S(1)} %get-tuple-element.31), channel_id=1, source_target_pairs={{1,2},{2,1},{3,4},{4,3},{5,6},{6,5},{7,0},{0,7},{9,10},{10,9},{11,... | collective-permute-start | bytes 36872 | tf_op jit(solution)/shard_map/ppermute | solution.py:575
  13.1 0.0 collective-permute-start.3
  13.2 0.0 copy-done.2
  13.2 0.0 copy-start
  13.2 1.0 %copy-done = f32[4,96,256]{2,1,0:T(8,128)S(1)} copy-done((f32[4,96,256]{2,1,0:T(8,128)S(1)}, f32[4,96,256]{2,1,0:T(8,128)}, u32[]{:S(2)}) %copy-start) | copy-done | bytes 393240
  14.2 1.6 %interior.1 = (f32[4,128,256]{2,1,0:T(8,128)S(1)}, f32[5,128,256]{2,1,0:T(8,128)S(1)}, f32[4,144,128]{2,1,0:T(8,128)S(1)}, f32[8,128]{1,0:T(8,128)S(1)}) custom-call(f32[4,32,256]{2,1,0:T(8,128)S(1)} %copy-done.2, f32[4,96,256]{2,1,0:T(8,128)S(1)} %copy-done, f32[4,8,256]{2,1,0:T(8,128)S(1)} %collective-permute-done.near_ref, ...), custom_call_target="tpu_custom_call" | custom-call | flops 9830400 | bytes 2097152 | tf_op jit(solution)/shard_map/interior/pallas_call | solution.py:282
  15.7 0.0 collective-permute-done.2.far_ref
  15.7 1.1 %collective-permute-done.3.near_ref = f32[24,128]{1,0:T(8,128)S(1)} collective-permute-done((f32[24,128]{1,0:T(8,128)S(1)}, f32[24,128]{1,0:T(8,128)S(1)}, u32[]{:S(2)}, u32[]{:S(2)}) %collective-permute-start.3) | collective-permute-done | bytes 12320 | tf_op jit(solution)/shard_map/ppermute | solution.py:575
  16.8 1.0 %strip.1 = (f32[4,128,128]{2,1,0:T(8,128)S(1)}, f32[5,128,128]{2,1,0:T(8,128)S(1)}, f32[8,128]{1,0:T(8,128)S(1)}) custom-call(f32[4,144,128]{2,1,0:T(8,128)S(1)} %get-tuple-element.28.strip_in_ref, f32[24,128]{1,0:T(8,128)S(1)} %collective-permute-done.2.far_ref, f32[24,128]{1,0:T(8,128)S(1)} %collective-permute-done.3.near_ref, ...), custom_call_target="tpu_custom_call" | custom-call | tf_op jit(solution)/shard_map/strip/pallas_call | solution.py:329
  17.8 0.1 collective-permute-start.4
  17.9 1.2 %collective-permute-done.4 = f32[8,128]{1,0:T(8,128)S(1)} collective-permute-done((f32[8,128]{1,0:T(8,128)S(1)}, f32[8,128]{1,0:T(8,128)S(1)}, u32[]{:S(2)}, u32[]{:S(2)}) %collective-permute-start.4) | collective-permute-done | bytes 4128 | tf_op jit(solution)/shard_map/ppermute | solution.py:575
  19.0 0.7 %collective-permute-start.5 = (f32[8,128]{1,0:T(8,128)S(1)}, f32[8,128]{1,0:T(8,128)S(1)}, u32[]{:S(2)}, u32[]{:S(2)}) collective-permute-start(f32[8,128]{1,0:T(8,128)S(1)} %add.3.sums_ref), channel_id=1, source_target_pairs={{0,0},{8,24},{16,16},{24,8},{1,1},{9,25},{17,17},{25,9},{2,2},{10,... | collective-permute-start | bytes 12296 | tf_op jit(solution)/shard_map/ppermute | solution.py:566
  19.7 0.0 copy-done.5
  19.7 0.0 copy-start.1
  19.7 1.0 %copy-done.1 = f32[4,96,256]{2,1,0:T(8,128)S(1)} copy-done((f32[4,96,256]{2,1,0:T(8,128)S(1)}, f32[4,96,256]{2,1,0:T(8,128)}, u32[]{:S(2)}) %copy-start.1) | copy-done | bytes 393240
  20.7 0.9 %place.1 = (s16[8,80,128]{2,1,0:T(8,128)(2,1)S(1)}, f32[8,8,128]{2,1,0:T(8,128)S(1)}) custom-call(s32[8]{0:T(128)S(1)} %bitcast.2, f32[4,32,256]{2,1,0:T(8,128)S(1)} %copy-done.2, f32[4,96,256]{2,1,0:T(8,128)S(1)} %copy-done.1), custom_call_target="tpu_custom_call" | custom-call | flops 1966080 | bytes 393216 | tf_op jit(solution)/shard_map/place/pallas_call | solution.py:394
  21.6 0.0 collective-permute-done.5.other_ref
  21.6 11.9 %all_to_all.5.arrived_ref = s16[8,80,128]{2,1,0:T(8,128)(2,1)S(1)} all-to-all(s16[8,80,128]{2,1,0:T(8,128)(2,1)S(1)} %constant_dynamic-update-slice_fusion), channel_id=1, replica_groups=mesh['lat'=4,'lon'=8] {'lon'}, dimensions={0} | all-to-all | bytes 327680 | tf_op jit(solution)/shard_map/all_to_all | solution.py:604
  33.5 0.1 tally.1.sums_ref
  33.6 0.7 %collective-permute-start.6 = (f32[8,128]{1,0:T(8,128)S(1)}, f32[8,128]{1,0:T(8,128)S(1)}, u32[]{:S(2)}, u32[]{:S(2)}) collective-permute-start(f32[8,128]{1,0:T(8,128)S(1)} %tally.1.sums_ref), channel_id=1, source_target_pairs={{0,8},{8,0},{16,24},{24,16},{1,9},{9,1},{17,25},{25,17},{2,10},{10... | collective-permute-start | bytes 12296 | tf_op jit(solution)/shard_map/ppermute | solution.py:575
  34.3 0.8 %collective-permute-done.6.other_ref = f32[8,128]{1,0:T(8,128)S(1)} collective-permute-done((f32[8,128]{1,0:T(8,128)S(1)}, f32[8,128]{1,0:T(8,128)S(1)}, u32[]{:S(2)}, u32[]{:S(2)}) %collective-permute-start.6) | collective-permute-done | bytes 4128 | tf_op jit(solution)/shard_map/ppermute | solution.py:575
  35.1 1.2 %combine.1 = (f32[128,256]{1,0:T(8,128)}, f32[128,256]{1,0:T(8,128)}, f32[8,32,256]{2,1,0:T(8,128)}) custom-call(f32[8,128]{1,0:T(8,128)S(1)} %tally.1.sums_ref, f32[8,128]{1,0:T(8,128)S(1)} %collective-permute-done.6.other_ref, s16[8,80,128]{2,1,0:T(8,128)(2,1)S(1)} %all_to_all.5.arrived_ref, f32[4,128,256]{2,1,0:T(8,128)S(1)} %get-tuple-element.36.w_ref, ...), custom_call_target="tpu_custom_call" | custom-call | tf_op jit(solution)/shard_map/combine/pallas_call | solution.py:546
  (3 shorter events, 0.1 us)
Async XLA Ops:
  0.6 5.2 %copy-start.4 = (f32[16]{0:T(128)S(1)}, f32[16]{0:T(128)}, u32[]{:S(2)}) copy-start(f32[16]{0:T(128)} %thick_hbm.3) | copy-start | bytes 196
  2.6 5.8 %copy-start.3 = (f32[32,128]{1,0:T(8,128)S(1)}, f32[32,128]{1,0:T(8,128)}, u32[]{:S(2)}) copy-start(f32[32,128]{1,0:T(8,128)} %get-tuple-element.29.outer_ref) | copy-start | bytes 49156
  2.6 10.5 %copy-start.2 = (f32[4,32,256]{2,1,0:T(8,128)S(1)}, f32[4,32,256]{2,1,0:T(8,128)}, u32[]{:S(2)}) copy-start(f32[4,32,256]{2,1,0:T(8,128)} %get-tuple-element.23.outer_ref) | copy-start | bytes 393220
  2.7 17.0 %copy-start.5 = (s32[8,1]{0,1:T(1,128)S(1)}, s32[8,1]{0,1:T(1,128)}, u32[]{:S(2)}) copy-start(s32[8,1]{0,1:T(1,128)} %param.9) | copy-start | bytes 100
  2.7 5.7 %collective-permute-start = (f32[4,8,256]{2,1,0:T(8,128)}, f32[4,8,256]{2,1,0:T(8,128)S(1)}, u32[]{:S(2)}, u32[]{:S(2)}) collective-permute-start(f32[4,8,256]{2,1,0:T(8,128)} %get-tuple-element.26), channel_id=1, source_target_pairs={{0,8},{8,0},{16,24},{24,16},{1,9},{9,1},{17,25},{25,17},{2,10},{10... | collective-permute-start | bytes 98312 | tf_op jit(solution)/shard_map/ppermute | solution.py:575
  3.2 5.2 %collective-permute-start.1 = (f32[4,8,256]{2,1,0:T(8,128)}, f32[4,8,256]{2,1,0:T(8,128)S(1)}, u32[]{:S(2)}, u32[]{:S(2)}) collective-permute-start(f32[4,8,256]{2,1,0:T(8,128)} %get-tuple-element.27), channel_id=1, source_target_pairs={{8,16},{16,8},{24,0},{0,24},{9,17},{17,9},{25,1},{1,25},{10,18},{1... | collective-permute-start | bytes 98312 | tf_op jit(solution)/shard_map/ppermute | solution.py:575
  8.6 7.1 %collective-permute-start.2 = (f32[24,128]{1,0:T(8,128)S(1)}, f32[24,128]{1,0:T(8,128)S(1)}, u32[]{:S(2)}, u32[]{:S(2)}) collective-permute-start(f32[24,128]{1,0:T(8,128)S(1)} %get-tuple-element.31), channel_id=1, source_target_pairs={{1,2},{2,1},{3,4},{4,3},{5,6},{6,5},{7,0},{0,7},{9,10},{10,9},{11,... | collective-permute-start | bytes 36872 | tf_op jit(solution)/shard_map/ppermute | solution.py:575
  13.1 3.7 %collective-permute-start.3 = (f32[24,128]{1,0:T(8,128)S(1)}, f32[24,128]{1,0:T(8,128)S(1)}, u32[]{:S(2)}, u32[]{:S(2)}) collective-permute-start(f32[24,128]{1,0:T(8,128)S(1)} %get-tuple-element.32), channel_id=1, source_target_pairs={{0,1},{1,0},{2,3},{3,2},{4,5},{5,4},{6,7},{7,6},{8,9},{9,8},{10,11... | collective-permute-start | bytes 36872 | tf_op jit(solution)/shard_map/ppermute | solution.py:575
  13.2 1.0 %copy-start = (f32[4,96,256]{2,1,0:T(8,128)S(1)}, f32[4,96,256]{2,1,0:T(8,128)}, u32[]{:S(2)}) copy-start(f32[4,96,256]{2,1,0:T(8,128)} %get-tuple-element.24.middle_ref) | copy-start | bytes 1179652
  17.8 1.2 %collective-permute-start.4 = (f32[8,128]{1,0:T(8,128)S(1)}, f32[8,128]{1,0:T(8,128)S(1)}, u32[]{:S(2)}, u32[]{:S(2)}) collective-permute-start(f32[8,128]{1,0:T(8,128)S(1)} %get-tuple-element.34), channel_id=1, source_target_pairs={{0,8},{8,0},{16,24},{24,16},{1,9},{9,1},{17,25},{25,17},{2,10},{10... | collective-permute-start | bytes 12296 | tf_op jit(solution)/shard_map/ppermute | solution.py:575
  19.0 2.5 %collective-permute-start.5 = (f32[8,128]{1,0:T(8,128)S(1)}, f32[8,128]{1,0:T(8,128)S(1)}, u32[]{:S(2)}, u32[]{:S(2)}) collective-permute-start(f32[8,128]{1,0:T(8,128)S(1)} %add.3.sums_ref), channel_id=1, source_target_pairs={{0,0},{8,24},{16,16},{24,8},{1,1},{9,25},{17,17},{25,9},{2,2},{10,... | collective-permute-start | bytes 12296 | tf_op jit(solution)/shard_map/ppermute | solution.py:566
  19.7 1.0 %copy-start.1 = (f32[4,96,256]{2,1,0:T(8,128)S(1)}, f32[4,96,256]{2,1,0:T(8,128)}, u32[]{:S(2)}) copy-start(f32[4,96,256]{2,1,0:T(8,128)} %get-tuple-element.24.middle_ref) | copy-start | bytes 1179652
  33.6 1.5 %collective-permute-start.6 = (f32[8,128]{1,0:T(8,128)S(1)}, f32[8,128]{1,0:T(8,128)S(1)}, u32[]{:S(2)}, u32[]{:S(2)}) collective-permute-start(f32[8,128]{1,0:T(8,128)S(1)} %tally.1.sums_ref), channel_id=1, source_target_pairs={{0,8},{8,0},{16,24},{24,16},{1,9},{9,1},{17,25},{25,17},{2,10},{10... | collective-permute-start | bytes 12296 | tf_op jit(solution)/shard_map/ppermute | solution.py:575

commit v14 on v12

--- a/solution.py
+++ b/solution.py
@@ -1,5 +1,3 @@
-import functools
-
 import jax
 import jax.numpy as jnp
 from jax import lax
@@ -15,7 +13,7 @@
 QUARTER = LANES // 4
 EAST = 48
 SEAM = HALF + EAST
-CHUNK = 16
+CHUNK = 32
 FIELDS = 4
 GROUPS = 6
 PITCH = LANES // GROUPS
@@ -65,38 +63,11 @@
     return packed
 
 
-def integrate_kernel(bands, outer, thick_hbm, count_hbm, inertia_hbm, tend_hbm, *refs):
-    outs, scratch = refs[:2], refs[2:]
-    thick_ref, count_ref, inertia_ref, tend_ref, thick_sem, small_sems, large_sems = scratch[:7]
-    levels = tend_hbm.shape[1]
-    thick_copy = pltpu.make_async_copy(thick_hbm, thick_ref, thick_sem)
-    copies = []
-    start = 0
+def integrate_bands(bands, thick_ref, count_ref, tend_ref, waits, finish):
+    levels = tend_ref.shape[1]
     for place, (row, size) in enumerate(bands):
-        there = pl.ds(row, size)
-        here = pl.ds(start, size)
-        count_copy = pltpu.make_async_copy(
-            count_hbm.at[there], count_ref.at[here], small_sems.at[0, place]
-        )
-        inertia_copy = pltpu.make_async_copy(
-            inertia_hbm.at[there], inertia_ref.at[here], small_sems.at[1, place]
-        )
-        tend_copy = pltpu.make_async_copy(
-            tend_hbm.at[:, :, there], tend_ref.at[:, :, here], large_sems.at[place]
-        )
-        copies.append((count_copy, inertia_copy, tend_copy))
-        start += size
-    thick_copy.start()
-    for group in copies:
-        for copy in group:
-            copy.start()
-    thick_copy.wait()
-    start = 0
-    results = []
-    for place, (row, size) in enumerate(bands):
-        part = slice(start, start + size)
-        for copy in copies[place]:
-            copy.wait()
+        part = slice(row, row + size)
+        waits[place]()
         count = count_ref[part]
         first = jnp.zeros(count.shape, jnp.float32)
         second = jnp.zeros(count.shape, jnp.float32)
@@ -106,75 +77,166 @@
             depth = depth + layer
             first = first + layer * tend_ref[0, level, part].astype(jnp.float32)
             second = second + layer * tend_ref[1, level, part].astype(jnp.float32)
-        values = (first, second, depth, inertia_ref[part])
-        if outer:
-            results.append(values)
-        else:
-            fields_hbm, side_ref = outs
-            fields_ref, out_sems = scratch[7:]
-            for field in range(FIELDS):
-                fields_ref[field, part] = values[field]
-            here = pl.ds(start, size)
-            done = pltpu.make_async_copy(
-                fields_ref.at[:, here], fields_hbm.at[:, here], out_sems.at[place]
+        finish(place, part, (first, second, depth))
+
+
+def outer_kernel(
+    thick_hbm,
+    count_hbm,
+    inertia_hbm,
+    tend_hbm,
+    near_ref,
+    far_ref,
+    thick_ref,
+    count_ref,
+    tend_ref,
+    thick_sem,
+    sems,
+):
+    rows = count_hbm.shape[0]
+    even = is_even("lat")
+    starts = (0, rows - OUTER)
+    bands = [(place * OUTER, OUTER) for place in range(2)]
+
+    def pair(source, target, place, kind):
+        there = pl.ds(starts[place], OUTER)
+        here = pl.ds(place * OUTER, OUTER)
+        if kind == 0:
+            return pltpu.make_async_copy(
+                source.at[:, :, there], target.at[:, :, here], sems.at[kind, place]
             )
-            done.start()
-            results.append(done)
-            side_ref[part] = pack_edges(fields_ref, part)
-        start += size
-    if outer:
-        near_ref, far_ref = outs
-        even = is_even("lat")
-        for field in range(FIELDS):
-            head = results[0][field][:ROWS]
-            tail = results[1][field][-ROWS:]
-            near_ref[field] = jnp.where(even, tail, head)
-            far_ref[field] = jnp.where(even, head, tail)
-    else:
-        for done in results:
-            done.wait()
-
-
-def integrate(tendency, thickness, level_count, inertia, bands, outer):
+        return pltpu.make_async_copy(source.at[there], target.at[here], sems.at[kind, place])
+
+    tends = [pair(tend_hbm, tend_ref, place, 0) for place in range(2)]
+    counts = [pair(count_hbm, count_ref, place, 1) for place in range(2)]
+    thick = pltpu.make_async_copy(thick_hbm, thick_ref, thick_sem)
+    last = rows - ROWS
+    near_row = pl.multiple_of(jnp.where(even, last, 0), ROWS)
+    far_row = pl.multiple_of(jnp.where(even, 0, last), ROWS)
+    inertias = [
+        pltpu.make_async_copy(
+            inertia_hbm.at[pl.ds(row, ROWS)], ref.at[FIELDS - 1], sems.at[2, place]
+        )
+        for place, (row, ref) in enumerate(((near_row, near_ref), (far_row, far_ref)))
+    ]
+    for copy in (tends[0], counts[0], thick, tends[1], counts[1], inertias[0], inertias[1]):
+        copy.start()
+    thick.wait()
+    results = []
+
+    def wait(place):
+        def run():
+            counts[place].wait()
+            tends[place].wait()
+
+        return run
+
+    integrate_bands(
+        bands,
+        thick_ref,
+        count_ref,
+        tend_ref,
+        [wait(place) for place in range(2)],
+        lambda place, part, values: results.append(values),
+    )
+    for field in range(FIELDS - 1):
+        head = results[0][field][:ROWS]
+        tail = results[1][field][-ROWS:]
+        near_ref[field] = jnp.where(even, tail, head)
+        far_ref[field] = jnp.where(even, head, tail)
+    for copy in inertias:
+        copy.wait()
+
+
+def whole_kernel(
+    thick_hbm,
+    count_hbm,
+    inertia_hbm,
+    tend_hbm,
+    fields_ref,
+    side_ref,
+    thick_ref,
+    count_ref,
+    tend_ref,
+    sems,
+    band_sems,
+):
+    rows = count_hbm.shape[0]
+    bands = [(row, CHUNK) for row in range(0, rows, CHUNK)]
+    tends = []
+    for place, (row, size) in enumerate(bands):
+        part = pl.ds(row, size)
+        tends.append(
+            pltpu.make_async_copy(
+                tend_hbm.at[:, :, part], tend_ref.at[:, :, part], band_sems.at[place]
+            )
+        )
+    count = pltpu.make_async_copy(count_hbm, count_ref, sems.at[0])
+    thick = pltpu.make_async_copy(thick_hbm, thick_ref, sems.at[1])
+    inertia = pltpu.make_async_copy(inertia_hbm, fields_ref.at[FIELDS - 1], sems.at[2])
+    for copy in [tends[0], count, thick, inertia] + tends[1:]:
+        copy.start()
+    for copy in (count, thick, inertia):
+        copy.wait()
+
+    def finish(place, part, values):
+        for field in range(FIELDS - 1):
+            fields_ref[field, part] = values[field]
+        side_ref[part] = pack_edges(fields_ref, part)
+
+    integrate_bands(
+        bands, thick_ref, count_ref, tend_ref, [copy.wait for copy in tends], finish
+    )
+
+
+def integrate_cost(tendency, rows):
     components, levels, _, cols = tendency.shape
-    rows = sum(size for _, size in bands)
+    return pl.CostEstimate(
+        flops=6 * components * levels * rows * cols,
+        bytes_accessed=2 * components * levels * rows * cols,
+        transcendentals=0,
+    )
+
+
+def integrate_outer(tendency, thickness, level_count, inertia):
+    components, levels, _, cols = tendency.shape
     f32 = jnp.float32
-    if outer:
-        out_shape = [jax.ShapeDtypeStruct((FIELDS, ROWS, cols), f32)] * 2
-        out_space = [pltpu.VMEM] * 2
-        extra = []
-    else:
-        out_space = [pltpu.HBM, pltpu.VMEM]
-        extra = [
-            pltpu.VMEM((FIELDS, rows, cols), f32),
-            pltpu.SemaphoreType.DMA((len(bands),)),
-        ]
-        out_shape = [
+    return pl.pallas_call(
+        outer_kernel,
+        in_specs=[pl.BlockSpec(memory_space=pltpu.HBM)] * 4,
+        out_shape=[jax.ShapeDtypeStruct((FIELDS, ROWS, cols), f32)] * 2,
+        scratch_shapes=[
+            pltpu.SMEM(thickness.shape, f32),
+            pltpu.VMEM((2 * OUTER, cols), jnp.int32),
+            pltpu.VMEM((components, levels, 2 * OUTER, cols), tendency.dtype),
+            pltpu.SemaphoreType.DMA,
+            pltpu.SemaphoreType.DMA((3, 2)),
+        ],
+        cost_estimate=integrate_cost(tendency, 2 * OUTER),
+        name="outer",
+    )(thickness, level_count, inertia, tendency)
+
+
+def integrate(tendency, thickness, level_count, inertia):
+    rows, cols = level_count.shape
+    f32 = jnp.float32
+    return pl.pallas_call(
+        whole_kernel,
+        in_specs=[pl.BlockSpec(memory_space=pltpu.HBM)] * 4,
+        out_shape=[
             jax.ShapeDtypeStruct((FIELDS, rows, cols), f32),
             jax.ShapeDtypeStruct((rows, LANES), f32),
-        ]
-    return pl.pallas_call(
-        functools.partial(integrate_kernel, bands, outer),
-        in_specs=[pl.BlockSpec(memory_space=pltpu.HBM)] * 4,
-        out_shape=out_shape,
-        out_specs=[pl.BlockSpec(memory_space=space) for space in out_space],
+        ],
         scratch_shapes=[
             pltpu.SMEM(thickness.shape, f32),
             pltpu.VMEM((rows, cols), jnp.int32),
-            pltpu.VMEM((rows, cols), f32),
-            pltpu.VMEM((components, levels, rows, cols), tendency.dtype),
-            pltpu.SemaphoreType.DMA,
-            pltpu.SemaphoreType.DMA((2, len(bands))),
-            pltpu.SemaphoreType.DMA((len(bands),)),
-            *extra,
-        ],
-        cost_estimate=pl.CostEstimate(
-            flops=6 * components * levels * rows * cols,
-            bytes_accessed=2 * components * levels * rows * cols,
-            transcendentals=0,
-        ),
-        compiler_params=None if outer else pltpu.CompilerParams(vmem_limit_bytes=WHOLE_BYTES),
-        name="outer" if outer else "whole",
+            pltpu.VMEM(tendency.shape, tendency.dtype),
+            pltpu.SemaphoreType.DMA((3,)),
+            pltpu.SemaphoreType.DMA((rows // CHUNK,)),
+        ],
+        cost_estimate=integrate_cost(tendency, rows),
+        compiler_params=pltpu.CompilerParams(vmem_limit_bytes=WHOLE_BYTES),
+        name="whole",
     )(thickness, level_count, inertia, tendency)
 
 
@@ -271,7 +333,9 @@
     mw_ref,
     strip_ref,
     sums_ref,
+    forcing_ref,
 ):
+    forcing_ref[...] = fields_ref[:2]
     cols = fields_ref.shape[2]
     lane = lanes_of((strip_ref.shape[1], LANES))
     padded = []
@@ -300,6 +364,7 @@
             jax.ShapeDtypeStruct((STEPS + 1, rows, cols), f32),
             jax.ShapeDtypeStruct((FIELDS, rows + 2 * ROWS, LANES), f32),
             jax.ShapeDtypeStruct((ROWS, LANES), f32),
+            jax.ShapeDtypeStruct((2, rows, cols), f32),
         ],
         compiler_params=pltpu.CompilerParams(vmem_limit_bytes=VMEM_BYTES),
         cost_estimate=pl.CostEstimate(
@@ -451,18 +516,27 @@
     sems,
 ):
     rows = held_ref.shape[1]
-    packed = jnp.zeros((SUM_ROWS, LANES), jnp.float32)
-    for slot in range(held_ref.shape[0]):
-        tail = arrived_ref[slot, arrived_ref.shape[1] - TAIL :].astype(jnp.int32)
-        digits = tail.astype(jnp.float32)
-        high = digits[SUM_ROWS : 2 * SUM_ROWS]
-        low = digits[2 * SUM_ROWS : 3 * SUM_ROWS]
-        packed = packed + (high + low * 2.0**-15) * power(tail[:SUM_ROWS] - 14)
+    slots = held_ref.shape[0]
+    tails = []
+    for slot in range(slots):
+        tails.append(arrived_ref[slot, arrived_ref.shape[1] - TAIL :].astype(jnp.int32))
+    scales = jnp.concatenate([tail[3 * SUM_ROWS :] for tail in tails], axis=0)
+    scales = power(scales - 15)
+    exponents = jnp.concatenate([tail[:SUM_ROWS] for tail in tails], axis=0)
+    high = jnp.concatenate([tail[SUM_ROWS : 2 * SUM_ROWS] for tail in tails], axis=0)
+    low = jnp.concatenate([tail[2 * SUM_ROWS : 3 * SUM_ROWS] for tail in tails], axis=0)
+    digits = high.astype(jnp.float32) + low.astype(jnp.float32) * 2.0**-15
+    sums = digits * power(exponents - 14)
+    packed = sums[:SUM_ROWS]
+    for slot in range(1, slots):
+        packed = packed + sums[slot * SUM_ROWS : (slot + 1) * SUM_ROWS]
+    spare = TAIL - 3 * SUM_ROWS
+    for slot in range(slots):
         for half in range(held_ref.shape[2] // LANES):
-            at = 3 * SUM_ROWS + half
-            scale = power(tail[at : at + 1] - 15)
+            at = slot * spare + half
             whole = arrived_ref[slot, half * rows : (half + 1) * rows].astype(jnp.int32)
-            held_ref[slot, :, half * LANES : (half + 1) * LANES] = whole.astype(jnp.float32) * scale
+            whole = whole.astype(jnp.float32) * scales[at : at + 1]
+            held_ref[slot, :, half * LANES : (half + 1) * LANES] = whole
     held_copy = pltpu.make_async_copy(held_ref, held_hbm, held_sem)
     held_copy.start()
     quarter = lanes_of(packed.shape) // QUARTER
@@ -564,19 +638,17 @@
 def on_device(tendency, thickness, level_count, block_mask, owner, inertia):
     lat_count = lax.axis_size("lat")
     lon_count = lax.axis_size("lon")
-    rows = level_count.shape[0]
     inputs = (tendency, thickness, level_count, inertia)
-    near, far = integrate(*inputs, ((0, OUTER), (rows - OUTER, OUTER)), True)
-    bands = tuple((row, CHUNK) for row in range(0, rows, CHUNK))
-    fields, side = integrate(*inputs, bands, False)
+    near, far = integrate_outer(*inputs)
+    fields, side = integrate(*inputs)
     near = swap(near, "lat", 0)
     far = swap(far, "lat", 1)
     near_edge, far_edge = edges(side, near, far)
     far_edge = swap(far_edge, "lon", 1)
     near_edge = swap(near_edge, "lon", 0)
-    w, mw, strip_in, inner = interior(fields, near, far)
+    w, mw, strip_in, inner, forcing = interior(fields, near, far)
     w_edge, mw_edge, sums = strip(strip_in, near_edge, far_edge, inner)
-    sent, scale = place(owner[:, 0], fields, lon_count)
+    sent, scale = place(owner[:, 0], forcing, lon_count)
     shift = 1
     while 2 * shift < lat_count:
         sums = sums + exchange(sums, "lat", shift)

time: 35.9 us -> 35.8 us (level)
  waiting for transfers between devices: 3.43 us -> 4.49 us
  local copies, waits for them, and re-layouts: 2.1 us -> 1.06 us
    ppermute x2, waiting for transfers between devices: 2.33 us -> 3.4 us  [exchange(): return lax.ppermute(values, axis, pairs)]
    unnamed x8 -> x6, local copies, waits for them, and re-layouts: 2.09 us -> 1.05 us
where the time goes in v14:
time: 35.8 us; the launch traced here: 35.5 us
  blocking collectives  11.3 us (32%)
  Pallas kernels  9.59 us (27%)
  starting transfers between devices  8.29 us (23%)
  waiting for transfers between devices  4.49 us (13%)
  local copies, waits for them, and re-layouts  1.06 us (3%)
  between operations  0.72 us (2%)
    all_to_all x1, blocking collectives, on_device(): lax.all_to_all(sent, 'lon', split_axis=0, concat_axis=0, tiled=True)  11.3 us
    ppermute x4, starting transfers between devices, swap(): return lax.ppermute(values, axis, pairs)  7.73 us
    ppermute x2, waiting for transfers between devices, exchange(): return lax.ppermute(values, axis, pairs)  3.4 us
    pallas_call x1, Pallas kernels, integrate(): pl.pallas_call(whole_kernel, in_specs=[pl.BlockSpec(memory_space=pltpu.HB...  3.12 us
    pallas_call x1, Pallas kernels, integrate_outer(): pl.pallas_call(outer_kernel, in_specs=[pl.BlockSpec(memory_space=pltpu.HB...  1.79 us
    pallas_call x1, Pallas kernels, interior(): pl.pallas_call(interior_kernel, out_shape=[jax.ShapeDtypeStruct((STEPS, r...  1.56 us
    pallas_call x1, Pallas kernels, combine(): pl.pallas_call(combine_kernel, out_shape=[shape, shape, jax.ShapeDtypeStr...  1.12 us
    ppermute x4, waiting for transfers between devices, swap(): return lax.ppermute(values, axis, pairs)  1.09 us
  transfers between devices with their start and end apart: 6, of which 3 were waited for; matrix products, arithmetic and copies ran while one was open for 0% of the time, Pallas kernels for 16%

profile of v14, /device:TPU:0, one launch (start us, length us, event | category | flops | bytes accessed | tf_op | source)
XLA Modules:
  0.0 35.5 jit_solution(15472191376775230476)
XLA Ops:
  0.6 0.0 copy-start.1
  0.6 1.8 %outer.1 = (f32[4,8,256]{2,1,0:T(8,128)}, f32[4,8,256]{2,1,0:T(8,128)}) custom-call(f32[16]{0:T(128)} %thick_hbm.3, s32[128,256]{1,0:T(8,128)} %count_hbm.3, f32[128,256]{1,0:T(8,128)} %inertia_hbm.3, bf16[2,16,128,256]{3,2,1,0:T(8,128)(2,1)} %tend_hbm.3), custom_call_target="tpu_custom_call" | custom-call | flops 1572864 | bytes 524288 | tf_op jit(solution)/shard_map/outer/pallas_call | solution.py:204
  2.4 0.0 copy-start.2
  2.5 0.5 %collective-permute-start = (f32[4,8,256]{2,1,0:T(8,128)}, f32[4,8,256]{2,1,0:T(8,128)S(1)}, u32[]{:S(2)}, u32[]{:S(2)}) collective-permute-start(f32[4,8,256]{2,1,0:T(8,128)} %get-tuple-element.23), channel_id=1, source_target_pairs={{0,8},{8,0},{16,24},{24,16},{1,9},{9,1},{17,25},{25,17},{2,10},{10... | collective-permute-start | bytes 98312 | tf_op jit(solution)/shard_map/ppermute | solution.py:635
  3.0 2.6 %collective-permute-start.1 = (f32[4,8,256]{2,1,0:T(8,128)}, f32[4,8,256]{2,1,0:T(8,128)S(1)}, u32[]{:S(2)}, u32[]{:S(2)}) collective-permute-start(f32[4,8,256]{2,1,0:T(8,128)} %get-tuple-element.24), channel_id=1, source_target_pairs={{8,16},{16,8},{24,0},{0,24},{9,17},{17,9},{25,1},{1,25},{10,18},{1... | collective-permute-start | bytes 98312 | tf_op jit(solution)/shard_map/ppermute | solution.py:635
  5.6 0.0 copy-done.1
  5.6 3.1 %whole.1 = (f32[4,128,256]{2,1,0:T(8,128)}, f32[128,128]{1,0:T(8,128)S(1)}) custom-call(f32[16]{0:T(128)S(1)} %copy-done.1, s32[128,256]{1,0:T(8,128)} %count_hbm.3, f32[128,256]{1,0:T(8,128)} %inertia_hbm.3, bf16[2,16,128,256]{3,2,1,0:T(8,128)(2,1)} %tend_hbm.3), custom_call_target="tpu_custom_call" | custom-call | flops 6291456 | bytes 2097152 | tf_op jit(solution)/shard_map/whole/pallas_call | solution.py:223
  8.7 0.0 collective-permute-done.near_ref
  8.8 0.0 collective-permute-done.1.far_ref
  8.8 0.1 edges.1
  8.9 4.6 %collective-permute-start.2 = (f32[24,128]{1,0:T(8,128)S(1)}, f32[24,128]{1,0:T(8,128)S(1)}, u32[]{:S(2)}, u32[]{:S(2)}) collective-permute-start(f32[24,128]{1,0:T(8,128)S(1)} %get-tuple-element.29), channel_id=1, source_target_pairs={{1,2},{2,1},{3,4},{4,3},{5,6},{6,5},{7,0},{0,7},{9,10},{10,9},{11,... | collective-permute-start | bytes 36872 | tf_op jit(solution)/shard_map/ppermute | solution.py:635
  13.5 0.0 collective-permute-start.3
  13.5 0.0 copy-start
  13.5 1.0 %copy-done = f32[4,128,256]{2,1,0:T(8,128)S(1)} copy-done((f32[4,128,256]{2,1,0:T(8,128)S(1)}, f32[4,128,256]{2,1,0:T(8,128)}, u32[]{:S(2)}) %copy-start) | copy-done | bytes 524312
  14.5 1.6 %interior.1 = (f32[4,128,256]{2,1,0:T(8,128)S(1)}, f32[5,128,256]{2,1,0:T(8,128)S(1)}, f32[4,144,128]{2,1,0:T(8,128)S(1)}, f32[8,128]{1,0:T(8,128)S(1)}, f32[2,128,256]{2,1,0:T(8,128)S(1)}) custom-call(f32[4,128,256]{2,1,0:T(8,128)S(1)} %copy-done, f32[4,8,256]{2,1,0:T(8,128)S(1)} %collective-permute-done.near_ref, ...), custom_call_target="tpu_custom_call" | custom-call | flops 9830400 | bytes 2097152 | tf_op jit(solution)/shard_map/interior/pallas_call | solution.py:360
  16.1 0.0 collective-permute-done.2.far_ref
  16.1 1.1 %collective-permute-done.3.near_ref = f32[24,128]{1,0:T(8,128)S(1)} collective-permute-done((f32[24,128]{1,0:T(8,128)S(1)}, f32[24,128]{1,0:T(8,128)S(1)}, u32[]{:S(2)}, u32[]{:S(2)}) %collective-permute-start.3) | collective-permute-done | bytes 12320 | tf_op jit(solution)/shard_map/ppermute | solution.py:635
  17.2 1.0 %strip.1 = (f32[4,128,128]{2,1,0:T(8,128)S(1)}, f32[5,128,128]{2,1,0:T(8,128)S(1)}, f32[8,128]{1,0:T(8,128)S(1)}) custom-call(f32[4,144,128]{2,1,0:T(8,128)S(1)} %get-tuple-element.27.strip_in_ref, f32[24,128]{1,0:T(8,128)S(1)} %collective-permute-done.2.far_ref, f32[24,128]{1,0:T(8,128)S(1)} %collective-permute-done.3.near_ref, ...), custom_call_target="tpu_custom_call" | custom-call | tf_op jit(solution)/shard_map/strip/pallas_call | solution.py:408
  18.1 0.1 collective-permute-start.4
  18.2 1.2 %collective-permute-done.4 = f32[8,128]{1,0:T(8,128)S(1)} collective-permute-done((f32[8,128]{1,0:T(8,128)S(1)}, f32[8,128]{1,0:T(8,128)S(1)}, u32[]{:S(2)}, u32[]{:S(2)}) %collective-permute-start.4) | collective-permute-done | bytes 4128 | tf_op jit(solution)/shard_map/ppermute | solution.py:626
  19.4 0.5 %collective-permute-start.5 = (f32[8,128]{1,0:T(8,128)S(1)}, f32[8,128]{1,0:T(8,128)S(1)}, u32[]{:S(2)}, u32[]{:S(2)}) collective-permute-start(f32[8,128]{1,0:T(8,128)S(1)} %add.3.sums_ref), channel_id=1, source_target_pairs={{0,16},{8,24},{16,0},{24,8},{1,17},{9,25},{17,1},{25,9},{2,18},{10... | collective-permute-start | bytes 12296 | tf_op jit(solution)/shard_map/ppermute | solution.py:626
  19.9 0.0 copy-done.2
  19.9 0.8 %place.1 = (s16[8,80,128]{2,1,0:T(8,128)(2,1)S(1)}, f32[8,8,128]{2,1,0:T(8,128)S(1)}) custom-call(s32[8]{0:T(128)S(1)} %bitcast.2, f32[2,128,256]{2,1,0:T(8,128)S(1)} %get-tuple-element.25.fields_ref), custom_call_target="tpu_custom_call" | custom-call | flops 1966080 | bytes 393216 | tf_op jit(solution)/shard_map/place/pallas_call | solution.py:464
  20.7 2.2 %collective-permute-done.5.other_ref = f32[8,128]{1,0:T(8,128)S(1)} collective-permute-done((f32[8,128]{1,0:T(8,128)S(1)}, f32[8,128]{1,0:T(8,128)S(1)}, u32[]{:S(2)}, u32[]{:S(2)}) %collective-permute-start.5) | collective-permute-done | bytes 4128 | tf_op jit(solution)/shard_map/ppermute | solution.py:626
  23.0 11.3 %all_to_all.5.arrived_ref = s16[8,80,128]{2,1,0:T(8,128)(2,1)S(1)} all-to-all(s16[8,80,128]{2,1,0:T(8,128)(2,1)S(1)} %constant_dynamic-update-slice_fusion), channel_id=1, replica_groups=mesh['lat'=4,'lon'=8] {'lon'}, dimensions={0} | all-to-all | bytes 327680 | tf_op jit(solution)/shard_map/all_to_all | solution.py:658
  34.4 1.1 %combine.1 = (f32[128,256]{1,0:T(8,128)}, f32[128,256]{1,0:T(8,128)}, f32[8,32,256]{2,1,0:T(8,128)}) custom-call(s16[8,80,128]{2,1,0:T(8,128)(2,1)S(1)} %all_to_all.5.arrived_ref, f32[4,128,256]{2,1,0:T(8,128)S(1)} %get-tuple-element.34.w_ref, f32[5,128,256]{2,1,0:T(8,128)S(1)} %get-tuple-element.35.mw_ref, f32[4,128,128]{2,1,0:T(8,128)S(1)} %get-tuple-element.36.w_edge_ref, ...), custom_call_target="tpu_custom_call" | custom-call | tf_op jit(solution)/shard_map/combine/pallas_call | solution.py:608
  (3 shorter events, 0.1 us)
Async XLA Ops:
  0.6 5.0 %copy-start.1 = (f32[16]{0:T(128)S(1)}, f32[16]{0:T(128)}, u32[]{:S(2)}) copy-start(f32[16]{0:T(128)} %thick_hbm.3) | copy-start | bytes 196
  2.4 17.4 %copy-start.2 = (s32[8,1]{0,1:T(1,128)S(1)}, s32[8,1]{0,1:T(1,128)}, u32[]{:S(2)}) copy-start(s32[8,1]{0,1:T(1,128)} %param.9) | copy-start | bytes 100
  2.5 6.3 %collective-permute-start = (f32[4,8,256]{2,1,0:T(8,128)}, f32[4,8,256]{2,1,0:T(8,128)S(1)}, u32[]{:S(2)}, u32[]{:S(2)}) collective-permute-start(f32[4,8,256]{2,1,0:T(8,128)} %get-tuple-element.23), channel_id=1, source_target_pairs={{0,8},{8,0},{16,24},{24,16},{1,9},{9,1},{17,25},{25,17},{2,10},{10... | collective-permute-start | bytes 98312 | tf_op jit(solution)/shard_map/ppermute | solution.py:635
  3.0 5.8 %collective-permute-start.1 = (f32[4,8,256]{2,1,0:T(8,128)}, f32[4,8,256]{2,1,0:T(8,128)S(1)}, u32[]{:S(2)}, u32[]{:S(2)}) collective-permute-start(f32[4,8,256]{2,1,0:T(8,128)} %get-tuple-element.24), channel_id=1, source_target_pairs={{8,16},{16,8},{24,0},{0,24},{9,17},{17,9},{25,1},{1,25},{10,18},{1... | collective-permute-start | bytes 98312 | tf_op jit(solution)/shard_map/ppermute | solution.py:635
  8.9 7.2 %collective-permute-start.2 = (f32[24,128]{1,0:T(8,128)S(1)}, f32[24,128]{1,0:T(8,128)S(1)}, u32[]{:S(2)}, u32[]{:S(2)}) collective-permute-start(f32[24,128]{1,0:T(8,128)S(1)} %get-tuple-element.29), channel_id=1, source_target_pairs={{1,2},{2,1},{3,4},{4,3},{5,6},{6,5},{7,0},{0,7},{9,10},{10,9},{11,... | collective-permute-start | bytes 36872 | tf_op jit(solution)/shard_map/ppermute | solution.py:635
  13.5 3.7 %collective-permute-start.3 = (f32[24,128]{1,0:T(8,128)S(1)}, f32[24,128]{1,0:T(8,128)S(1)}, u32[]{:S(2)}, u32[]{:S(2)}) collective-permute-start(f32[24,128]{1,0:T(8,128)S(1)} %get-tuple-element.30), channel_id=1, source_target_pairs={{0,1},{1,0},{2,3},{3,2},{4,5},{5,4},{6,7},{7,6},{8,9},{9,8},{10,11... | collective-permute-start | bytes 36872 | tf_op jit(solution)/shard_map/ppermute | solution.py:635
  13.5 1.0 %copy-start = (f32[4,128,256]{2,1,0:T(8,128)S(1)}, f32[4,128,256]{2,1,0:T(8,128)}, u32[]{:S(2)}) copy-start(f32[4,128,256]{2,1,0:T(8,128)} %get-tuple-element.22.fields_ref) | copy-start | bytes 1572868
  18.1 1.2 %collective-permute-start.4 = (f32[8,128]{1,0:T(8,128)S(1)}, f32[8,128]{1,0:T(8,128)S(1)}, u32[]{:S(2)}, u32[]{:S(2)}) collective-permute-start(f32[8,128]{1,0:T(8,128)S(1)} %get-tuple-element.32), channel_id=1, source_target_pairs={{0,8},{8,0},{16,24},{24,16},{1,9},{9,1},{17,25},{25,17},{2,10},{10... | collective-permute-start | bytes 12296 | tf_op jit(solution)/shard_map/ppermute | solution.py:626
  19.4 3.6 %collective-permute-start.5 = (f32[8,128]{1,0:T(8,128)S(1)}, f32[8,128]{1,0:T(8,128)S(1)}, u32[]{:S(2)}, u32[]{:S(2)}) collective-permute-start(f32[8,128]{1,0:T(8,128)S(1)} %add.3.sums_ref), channel_id=1, source_target_pairs={{0,16},{8,24},{16,0},{24,8},{1,17},{9,25},{17,1},{25,9},{2,18},{10... | collective-permute-start | bytes 12296 | tf_op jit(solution)/shard_map/ppermute | solution.py:626

commit v15 on v14

--- a/solution.py
+++ b/solution.py
@@ -1,3 +1,5 @@
+import functools
+
 import jax
 import jax.numpy as jnp
 from jax import lax
@@ -11,12 +13,10 @@
 LANES = 128
 HALF = LANES // 2
 QUARTER = LANES // 4
-EAST = 48
-SEAM = HALF + EAST
+FOLD = 4
+PITCH = LANES // FOLD
 CHUNK = 32
 FIELDS = 4
-GROUPS = 6
-PITCH = LANES // GROUPS
 PIECES = 2
 OUTER = 16
 TAIL = 16
@@ -240,29 +240,37 @@
     )(thickness, level_count, inertia, tendency)
 
 
+def folded_rows(tall):
+    return (tall - 2 * ROWS) // FOLD + 2 * ROWS
+
+
+def fold(values, shift, first, last):
+    size = folded_rows(values.shape[0])
+    lane = lanes_of((size, LANES))
+    folded = jnp.zeros((size, LANES), jnp.float32)
+    for part in range(FOLD):
+        start = part * (size - 2 * ROWS)
+        rows = turn(values[start : start + size], part * PITCH + shift)
+        here = (lane >= part * PITCH + first) & (lane < part * PITCH + last)
+        folded = jnp.where(here, rows, folded)
+    return folded
+
+
 def edges_kernel(side_ref, near_ref, far_ref, near_out_ref, far_out_ref):
     even_lon = is_even("lon")
     near = pack_edges(near_ref, slice(None))
     far = pack_edges(far_ref, slice(None))
     north, south = sides(near, far)
     packed = jnp.concatenate([north, side_ref[...], south], axis=0)
-    size = near_out_ref.shape[0]
-    lane = lanes_of(near_out_ref.shape)
-    west = jnp.zeros(near_out_ref.shape, jnp.float32)
-    east = jnp.zeros(near_out_ref.shape, jnp.float32)
-    for group in range(GROUPS):
-        rows = packed[group * size : (group + 1) * size]
-        at = group * PITCH
-        here = (lane >= at) & (lane < at + PITCH)
-        west = jnp.where(here, turn(rows, at), west)
-        east = jnp.where(here, turn(rows, at - HALF), east)
+    west = fold(packed, 0, 0, PITCH)
+    east = fold(packed, -HALF, 0, PITCH)
     near_out_ref[...] = jnp.where(even_lon, east, west)
     far_out_ref[...] = jnp.where(even_lon, west, east)
 
 
 def edges(side, near, far):
     rows = side.shape[0] + 2 * ROWS
-    message = jax.ShapeDtypeStruct((rows // GROUPS, LANES), jnp.float32)
+    message = jax.ShapeDtypeStruct((folded_rows(rows), LANES), jnp.float32)
     return pl.pallas_call(
         edges_kernel,
         out_shape=[message, message],
@@ -331,19 +339,22 @@
     far_ref,
     w_ref,
     mw_ref,
-    strip_ref,
+    near_strip_ref,
+    far_strip_ref,
     sums_ref,
     forcing_ref,
 ):
     forcing_ref[...] = fields_ref[:2]
     cols = fields_ref.shape[2]
-    lane = lanes_of((strip_ref.shape[1], LANES))
+    even = is_even("lon")
     padded = []
     for place in range(FIELDS):
         north, south = sides(near_ref[place], far_ref[place])
         values = jnp.concatenate([north, fields_ref[place], south], axis=0)
-        east = turn(values[:, cols - LANES :], SEAM)
-        strip_ref[place] = jnp.where(lane < HALF, values[:, :LANES], east)
+        west = fold(values[:, :LANES], RIM, RIM, 3 * RIM)
+        east = fold(values[:, cols - LANES :], 2 * RIM, 0, 2 * RIM)
+        near_strip_ref[place] = jnp.where(even, east, west)
+        far_strip_ref[place] = jnp.where(even, west, east)
         padded.append(values)
     ws, mws = basis(*padded)
     for place, values in enumerate(ws):
@@ -362,7 +373,8 @@
         out_shape=[
             jax.ShapeDtypeStruct((STEPS, rows, cols), f32),
             jax.ShapeDtypeStruct((STEPS + 1, rows, cols), f32),
-            jax.ShapeDtypeStruct((FIELDS, rows + 2 * ROWS, LANES), f32),
+            jax.ShapeDtypeStruct((FIELDS, folded_rows(rows + 2 * ROWS), LANES), f32),
+            jax.ShapeDtypeStruct((FIELDS, folded_rows(rows + 2 * ROWS), LANES), f32),
             jax.ShapeDtypeStruct((ROWS, LANES), f32),
             jax.ShapeDtypeStruct((2, rows, cols), f32),
         ],
@@ -374,47 +386,44 @@
     )(fields, near, far)
 
 
-def strip_kernel(strip_in_ref, far_ref, near_ref, inner_ref, w_ref, mw_ref, sums_ref):
+def strip_kernel(near, strip_in_ref, message_ref, before_ref, w_ref, mw_ref, sums_ref):
     even = is_even("lon")
-    near = near_ref[...]
-    far = far_ref[...]
-    from_east = jnp.where(even, near, far)
-    from_west = jnp.where(even, far, near)
-    lane = lanes_of(near.shape)
+    eastern = even if near else jnp.logical_not(even)
+    message = message_ref[...]
+    column = lax.rem(lanes_of(message.shape), PITCH)
+    first = jnp.where(eastern, 2 * RIM, 0)
+    halo = (column >= first) & (column < first + RIM)
     padded = []
     for place in range(FIELDS):
-        halo = []
-        for group in range(GROUPS):
-            at = group * PITCH + place * RIM
-            east = turn(from_east, SEAM - at)
-            west = turn(from_west, LANES - RIM - at)
-            west = jnp.where(lane >= LANES - RIM, west, 0.0)
-            halo.append(jnp.where(lane < SEAM + RIM, east, west))
-        halo = jnp.concatenate(halo, axis=0)
-        padded.append(jnp.where(lanes_of(halo.shape) < SEAM, strip_in_ref[place], halo))
+        at = place * RIM
+        beyond = jnp.where(eastern, turn(message, 2 * RIM - at), turn(message, -at))
+        padded.append(jnp.where(halo, beyond, strip_in_ref[place]))
     ws, mws = basis(*padded)
     for place, values in enumerate(ws):
         w_ref[place] = values
     for place, values in enumerate(mws):
         mw_ref[place] = values
-    lane = lanes_of(ws[0].shape)
-    edge = (lane < RIM) | ((lane >= SEAM - RIM) & (lane < SEAM))
-    sums_ref[...] = inner_ref[...] + moments(ws, mws, edge)
-
-
-def strip(strip_in, near, far, inner):
+    column = lax.rem(lanes_of(ws[0].shape), PITCH)
+    edge = (column >= RIM) & (column < 2 * RIM)
+    sums_ref[...] = before_ref[...] + moments(ws, mws, edge)
+
+
+def strip(near, strip_in, message, before):
     rows = strip_in.shape[1] - 2 * ROWS
     f32 = jnp.float32
     return pl.pallas_call(
-        strip_kernel,
+        functools.partial(strip_kernel, near),
         out_shape=[
             jax.ShapeDtypeStruct((STEPS, rows, LANES), f32),
             jax.ShapeDtypeStruct((STEPS + 1, rows, LANES), f32),
             jax.ShapeDtypeStruct((ROWS, LANES), f32),
         ],
         compiler_params=pltpu.CompilerParams(vmem_limit_bytes=VMEM_BYTES),
-        name="strip",
-    )(strip_in, far, near, inner)
+        cost_estimate=pl.CostEstimate(
+            flops=300 * rows * LANES, bytes_accessed=64 * rows * LANES, transcendentals=0
+        ),
+        name="near_strip" if near else "far_strip",
+    )(strip_in, message, before)
 
 
 def power(exponent):
@@ -504,8 +513,10 @@
     arrived_ref,
     w_ref,
     mw_ref,
-    w_edge_ref,
-    mw_edge_ref,
+    near_w_ref,
+    near_mw_ref,
+    far_w_ref,
+    far_mw_ref,
     pressure_hbm,
     residual_hbm,
     held_hbm,
@@ -575,20 +586,31 @@
         return pressure, residual
 
     rows, cols = pressure_ref.shape
+    even = is_even("lon")
+    near = results(near_w_ref, near_mw_ref, slice(None))
+    far = results(far_w_ref, far_mw_ref, slice(None))
+    west = [jnp.where(even, b, a) for a, b in zip(near, far)]
+    east = [jnp.where(even, a, b) for a, b in zip(near, far)]
+
+    def unfold(values, parts, lane):
+        return jnp.concatenate([turn(values, lane - RIM - part * PITCH) for part in parts], axis=0)
+
     copies = []
     for piece in range(PIECES):
         part = slice(piece * rows // PIECES, (piece + 1) * rows // PIECES)
         inner = results(w_ref, mw_ref, part)
-        edge = results(w_edge_ref, mw_edge_ref, part)
-        lane = lanes_of(edge[0].shape)
-        for field, (out_ref, out_hbm, inside, border) in enumerate(
-            zip((pressure_ref, residual_ref), (pressure_hbm, residual_hbm), inner, edge)
+        parts = range(piece * FOLD // PIECES, (piece + 1) * FOLD // PIECES)
+        lane = lanes_of((rows // PIECES, LANES))
+        for field, (out_ref, out_hbm, inside) in enumerate(
+            zip((pressure_ref, residual_ref), (pressure_hbm, residual_hbm), inner)
         ):
+            border = unfold(west[field], parts, 0)
             out_ref[part, :LANES] = jnp.where(lane < RIM, border, inside[:, :LANES])
             if cols > 2 * LANES:
                 out_ref[part, LANES : cols - LANES] = inside[:, LANES : cols - LANES]
+            border = unfold(east[field], parts, LANES - RIM)
             out_ref[part, cols - LANES :] = jnp.where(
-                lane >= LANES - RIM, turn(border, -SEAM), inside[:, cols - LANES :]
+                lane >= LANES - RIM, border, inside[:, cols - LANES :]
             )
             there = pl.ds(piece * rows // PIECES, rows // PIECES)
             copy = pltpu.make_async_copy(
@@ -601,7 +623,7 @@
         copy.wait()
 
 
-def combine(arrived, w, mw, w_edge, mw_edge):
+def combine(arrived, w, mw, near, far):
     rows, cols = w.shape[1:]
     shape = jax.ShapeDtypeStruct((rows, cols), jnp.float32)
     held = (arrived.shape[0], (arrived.shape[1] - TAIL) * LANES // cols, cols)
@@ -618,7 +640,7 @@
         ],
         compiler_params=pltpu.CompilerParams(vmem_limit_bytes=VMEM_BYTES),
         name="combine",
-    )(arrived, w, mw, w_edge, mw_edge)
+    )(arrived, w, mw, *near, *far)
 
 
 def exchange(values, axis, distance):
@@ -646,8 +668,9 @@
     near_edge, far_edge = edges(side, near, far)
     far_edge = swap(far_edge, "lon", 1)
     near_edge = swap(near_edge, "lon", 0)
-    w, mw, strip_in, inner, forcing = interior(fields, near, far)
-    w_edge, mw_edge, sums = strip(strip_in, near_edge, far_edge, inner)
+    w, mw, near_strip, far_strip, sums, forcing = interior(fields, near, far)
+    *near_results, sums = strip(True, near_strip, near_edge, sums)
+    *far_results, sums = strip(False, far_strip, far_edge, sums)
     sent, scale = place(owner[:, 0], forcing, lon_count)
     shift = 1
     while 2 * shift < lat_count:
@@ -656,7 +679,7 @@
     tail = seal(sums, exchange(sums, "lat", shift), scale)
     sent = lax.dynamic_update_slice(sent, tail, (0, sent.shape[1] - TAIL, 0))
     arrived = lax.all_to_all(sent, "lon", split_axis=0, concat_axis=0, tiled=True)
-    pressure, residual, held = combine(arrived, w, mw, w_edge, mw_edge)
+    pressure, residual, held = combine(arrived, w, mw, near_results, far_results)
     held = held.reshape((1, 1, lon_count, 2, held.shape[1] // 2, held.shape[2]))
     return (held, pressure, residual)
 

time: 35.8 us -> 36.2 us (1.011)
  waiting for transfers between devices: 4.49 us -> 3.39 us
  Pallas kernels: 9.59 us -> 10.2 us
  starting transfers between devices: 8.29 us -> 8.8 us
  blocking collectives: 11.3 us -> 11.7 us
    ppermute x4, waiting for transfers between devices: 1.09 us -> 0.01 us  [swap(): return lax.ppermute(values, axis, pairs)]
    ppermute x4, starting transfers between devices: 7.73 us -> 8.27 us  [swap(): return lax.ppermute(values, axis, pairs)]
    pallas_call x1 -> x2, Pallas kernels: 0.98 us -> 1.43 us  [strip(): pl.pallas_call(functools.partial(strip_kernel, near), out_shape=[jax.Shap...]
  transfers between devices with their start and end apart: 6 -> 6, of which waited for: 3 -> 2; matrix products, arithmetic and copies ran while one was open for 0% -> 0% of each run, Pallas kernels for 16% -> 18%
where the time goes in v15:
time: 36.2 us; the launch traced here: 35.9 us
  blocking collectives  11.7 us (32%)
  Pallas kernels  10.2 us (28%)
  starting transfers between devices  8.8 us (24%)
  waiting for transfers between devices  3.39 us (9%)
  local copies, waits for them, and re-layouts  1.06 us (3%)
  between operations  0.73 us (2%)
    all_to_all x1, blocking collectives, on_device(): lax.all_to_all(sent, 'lon', split_axis=0, concat_axis=0, tiled=True)  11.7 us
    ppermute x4, starting transfers between devices, swap(): return lax.ppermute(values, axis, pairs)  8.27 us
    ppermute x2, waiting for transfers between devices, exchange(): return lax.ppermute(values, axis, pairs)  3.38 us
    pallas_call x1, Pallas kernels, integrate(): pl.pallas_call(whole_kernel, in_specs=[pl.BlockSpec(memory_space=pltpu.HB...  3.12 us
    pallas_call x1, Pallas kernels, integrate_outer(): pl.pallas_call(outer_kernel, in_specs=[pl.BlockSpec(memory_space=pltpu.HB...  1.79 us
    pallas_call x1, Pallas kernels, interior(): pl.pallas_call(interior_kernel, out_shape=[jax.ShapeDtypeStruct((STEPS, r...  1.71 us
    pallas_call x2, Pallas kernels, strip(): pl.pallas_call(functools.partial(strip_kernel, near), out_shape=[jax.Shap...  1.43 us
    pallas_call x1, Pallas kernels, combine(): pl.pallas_call(combine_kernel, out_shape=[shape, shape, jax.ShapeDtypeStr...  1.14 us
  transfers between devices with their start and end apart: 6, of which 2 were waited for; matrix products, arithmetic and copies ran while one was open for 0% of the time, Pallas kernels for 18%

profile of v15, /device:TPU:0, one launch (start us, length us, event | category | flops | bytes accessed | tf_op | source)
XLA Modules:
  0.0 35.9 jit_solution(10520637901141108033)
XLA Ops:
  0.6 0.0 copy-start.1
  0.6 1.8 %outer.1 = (f32[4,8,256]{2,1,0:T(8,128)}, f32[4,8,256]{2,1,0:T(8,128)}) custom-call(f32[16]{0:T(128)} %thick_hbm.3, s32[128,256]{1,0:T(8,128)} %count_hbm.3, f32[128,256]{1,0:T(8,128)} %inertia_hbm.3, bf16[2,16,128,256]{3,2,1,0:T(8,128)(2,1)} %tend_hbm.3), custom_call_target="tpu_custom_call" | custom-call | flops 1572864 | bytes 524288 | tf_op jit(solution)/shard_map/outer/pallas_call | solution.py:204
  2.4 0.0 copy-start.2
  2.5 0.5 %collective-permute-start = (f32[4,8,256]{2,1,0:T(8,128)}, f32[4,8,256]{2,1,0:T(8,128)S(1)}, u32[]{:S(2)}, u32[]{:S(2)}) collective-permute-start(f32[4,8,256]{2,1,0:T(8,128)} %get-tuple-element.27), channel_id=1, source_target_pairs={{0,8},{8,0},{16,24},{24,16},{1,9},{9,1},{17,25},{25,17},{2,10},{10... | collective-permute-start | bytes 98312 | tf_op jit(solution)/shard_map/ppermute | solution.py:657
  3.0 2.6 %collective-permute-start.1 = (f32[4,8,256]{2,1,0:T(8,128)}, f32[4,8,256]{2,1,0:T(8,128)S(1)}, u32[]{:S(2)}, u32[]{:S(2)}) collective-permute-start(f32[4,8,256]{2,1,0:T(8,128)} %get-tuple-element.28), channel_id=1, source_target_pairs={{8,16},{16,8},{24,0},{0,24},{9,17},{17,9},{25,1},{1,25},{10,18},{1... | collective-permute-start | bytes 98312 | tf_op jit(solution)/shard_map/ppermute | solution.py:657
  5.6 0.0 copy-done.1
  5.6 3.1 %whole.1 = (f32[4,128,256]{2,1,0:T(8,128)}, f32[128,128]{1,0:T(8,128)S(1)}) custom-call(f32[16]{0:T(128)S(1)} %copy-done.1, s32[128,256]{1,0:T(8,128)} %count_hbm.3, f32[128,256]{1,0:T(8,128)} %inertia_hbm.3, bf16[2,16,128,256]{3,2,1,0:T(8,128)(2,1)} %tend_hbm.3), custom_call_target="tpu_custom_call" | custom-call | flops 6291456 | bytes 2097152 | tf_op jit(solution)/shard_map/whole/pallas_call | solution.py:223
  8.7 0.0 collective-permute-done.near_ref
  8.8 0.0 collective-permute-done.1.far_ref
  8.8 0.2 edges.1
  8.9 1.5 %collective-permute-start.3 = (f32[48,128]{1,0:T(8,128)S(1)}, f32[48,128]{1,0:T(8,128)S(1)}, u32[]{:S(2)}, u32[]{:S(2)}) collective-permute-start(f32[48,128]{1,0:T(8,128)S(1)} %get-tuple-element.35), channel_id=1, source_target_pairs={{0,1},{1,0},{2,3},{3,2},{4,5},{5,4},{6,7},{7,6},{8,9},{9,8},{10,11... | collective-permute-start | bytes 73736 | tf_op jit(solution)/shard_map/ppermute | solution.py:657
  10.5 3.6 %collective-permute-start.2 = (f32[48,128]{1,0:T(8,128)S(1)}, f32[48,128]{1,0:T(8,128)S(1)}, u32[]{:S(2)}, u32[]{:S(2)}) collective-permute-start(f32[48,128]{1,0:T(8,128)S(1)} %get-tuple-element.33), channel_id=1, source_target_pairs={{1,2},{2,1},{3,4},{4,3},{5,6},{6,5},{7,0},{0,7},{9,10},{10,9},{11,... | collective-permute-start | bytes 73736 | tf_op jit(solution)/shard_map/ppermute | solution.py:657
  14.0 0.0 copy-start
  14.0 1.0 %copy-done = f32[4,128,256]{2,1,0:T(8,128)S(1)} copy-done((f32[4,128,256]{2,1,0:T(8,128)S(1)}, f32[4,128,256]{2,1,0:T(8,128)}, u32[]{:S(2)}) %copy-start) | copy-done | bytes 524312
  15.1 1.7 %interior.1 = (f32[4,128,256]{2,1,0:T(8,128)S(1)}, f32[5,128,256]{2,1,0:T(8,128)S(1)}, f32[4,48,128]{2,1,0:T(8,128)S(1)}, f32[4,48,128]{2,1,0:T(8,128)S(1)}, f32...) custom-call(f32[4,128,256]{2,1,0:T(8,128)S(1)} %copy-done, f32[4,8,256]{2,1,0:T(8,128)S(1)} %collective-permute-done.near_ref, ...), custom_call_target="tpu_custom_call" | custom-call | flops 9830400 | bytes 2097152 | tf_op jit(solution)/shard_map/interior/pallas_call | solution.py:371
  16.8 0.0 collective-permute-done.3.message_ref
  16.8 0.7 %near_strip.1 = (f32[4,32,128]{2,1,0:T(8,128)S(1)}, f32[5,32,128]{2,1,0:T(8,128)S(1)}, f32[8,128]{1,0:T(8,128)S(1)}) custom-call(f32[4,48,128]{2,1,0:T(8,128)S(1)} %get-tuple-element.34.strip_in_ref, f32[48,128]{1,0:T(8,128)S(1)} %collective-permute-done.3.message_ref, f32[8,128]{1,0:T(8,128)S(1)} %get-tuple-element.36.before_ref), custom_call_target="tpu_custom_call" | custom-call | flops 1228800 | bytes 262144 | tf_op jit(solution)/shard_map/near_strip/pallas_call | solution.py:414
  17.5 0.0 collective-permute-done.2.message_ref
  17.5 0.7 %far_strip.1 = (f32[4,32,128]{2,1,0:T(8,128)S(1)}, f32[5,32,128]{2,1,0:T(8,128)S(1)}, f32[8,128]{1,0:T(8,128)S(1)}) custom-call(f32[4,48,128]{2,1,0:T(8,128)S(1)} %get-tuple-element.31.strip_in_ref, f32[48,128]{1,0:T(8,128)S(1)} %collective-permute-done.2.message_ref, f32[8,128]{1,0:T(8,128)S(1)} %get-tuple-element.37.before_ref), custom_call_target="tpu_custom_call" | custom-call | flops 1228800 | bytes 262144 | tf_op jit(solution)/shard_map/far_strip/pallas_call | solution.py:414
  18.2 0.0 collective-permute-start.4
  18.3 1.2 %collective-permute-done.4 = f32[8,128]{1,0:T(8,128)S(1)} collective-permute-done((f32[8,128]{1,0:T(8,128)S(1)}, f32[8,128]{1,0:T(8,128)S(1)}, u32[]{:S(2)}, u32[]{:S(2)}) %collective-permute-start.4) | collective-permute-done | bytes 4128 | tf_op jit(solution)/shard_map/ppermute | solution.py:648
  19.4 0.5 %collective-permute-start.5 = (f32[8,128]{1,0:T(8,128)S(1)}, f32[8,128]{1,0:T(8,128)S(1)}, u32[]{:S(2)}, u32[]{:S(2)}) collective-permute-start(f32[8,128]{1,0:T(8,128)S(1)} %add.3.sums_ref), channel_id=1, source_target_pairs={{0,16},{8,24},{16,0},{24,8},{1,17},{9,25},{17,1},{25,9},{2,18},{10... | collective-permute-start | bytes 12296 | tf_op jit(solution)/shard_map/ppermute | solution.py:648
  19.9 0.0 copy-done.2
  19.9 0.9 %place.1 = (s16[8,80,128]{2,1,0:T(8,128)(2,1)S(1)}, f32[8,8,128]{2,1,0:T(8,128)S(1)}) custom-call(s32[8]{0:T(128)S(1)} %bitcast.2, f32[2,128,256]{2,1,0:T(8,128)S(1)} %get-tuple-element.29.fields_ref), custom_call_target="tpu_custom_call" | custom-call | flops 1966080 | bytes 393216 | tf_op jit(solution)/shard_map/place/pallas_call | solution.py:473
  20.8 2.2 %collective-permute-done.5.other_ref = f32[8,128]{1,0:T(8,128)S(1)} collective-permute-done((f32[8,128]{1,0:T(8,128)S(1)}, f32[8,128]{1,0:T(8,128)S(1)}, u32[]{:S(2)}, u32[]{:S(2)}) %collective-permute-start.5) | collective-permute-done | bytes 4128 | tf_op jit(solution)/shard_map/ppermute | solution.py:648
  23.1 11.7 %all_to_all.5.arrived_ref = s16[8,80,128]{2,1,0:T(8,128)(2,1)S(1)} all-to-all(s16[8,80,128]{2,1,0:T(8,128)(2,1)S(1)} %constant_dynamic-update-slice_fusion), channel_id=1, replica_groups=mesh['lat'=4,'lon'=8] {'lon'}, dimensions={0} | all-to-all | bytes 327680 | tf_op jit(solution)/shard_map/all_to_all | solution.py:681
  34.8 1.1 %combine.1 = (f32[128,256]{1,0:T(8,128)}, f32[128,256]{1,0:T(8,128)}, f32[8,32,256]{2,1,0:T(8,128)}) custom-call(s16[8,80,128]{2,1,0:T(8,128)(2,1)S(1)} %all_to_all.5.arrived_ref, f32[4,128,256]{2,1,0:T(8,128)S(1)} %get-tuple-element.40.w_ref, f32[5,128,256]{2,1,0:T(8,128)S(1)} %get-tuple-element.41.mw_ref, f32[4,32,128]{2,1,0:T(8,128)S(1)} %get-tuple-element.42.near_w_ref, ...), custom_call_target="tpu_custom_call" | custom-call | tf_op jit(solution)/shard_map/combine/pallas_call | solution.py:630
  (3 shorter events, 0.1 us)
Async XLA Ops:
  0.6 5.0 %copy-start.1 = (f32[16]{0:T(128)S(1)}, f32[16]{0:T(128)}, u32[]{:S(2)}) copy-start(f32[16]{0:T(128)} %thick_hbm.3) | copy-start | bytes 196
  2.4 17.5 %copy-start.2 = (s32[8,1]{0,1:T(1,128)S(1)}, s32[8,1]{0,1:T(1,128)}, u32[]{:S(2)}) copy-start(s32[8,1]{0,1:T(1,128)} %param.9) | copy-start | bytes 100
  2.5 6.3 %collective-permute-start = (f32[4,8,256]{2,1,0:T(8,128)}, f32[4,8,256]{2,1,0:T(8,128)S(1)}, u32[]{:S(2)}, u32[]{:S(2)}) collective-permute-start(f32[4,8,256]{2,1,0:T(8,128)} %get-tuple-element.27), channel_id=1, source_target_pairs={{0,8},{8,0},{16,24},{24,16},{1,9},{9,1},{17,25},{25,17},{2,10},{10... | collective-permute-start | bytes 98312 | tf_op jit(solution)/shard_map/ppermute | solution.py:657
  3.0 5.8 %collective-permute-start.1 = (f32[4,8,256]{2,1,0:T(8,128)}, f32[4,8,256]{2,1,0:T(8,128)S(1)}, u32[]{:S(2)}, u32[]{:S(2)}) collective-permute-start(f32[4,8,256]{2,1,0:T(8,128)} %get-tuple-element.28), channel_id=1, source_target_pairs={{8,16},{16,8},{24,0},{0,24},{9,17},{17,9},{25,1},{1,25},{10,18},{1... | collective-permute-start | bytes 98312 | tf_op jit(solution)/shard_map/ppermute | solution.py:657
  8.9 7.9 %collective-permute-start.3 = (f32[48,128]{1,0:T(8,128)S(1)}, f32[48,128]{1,0:T(8,128)S(1)}, u32[]{:S(2)}, u32[]{:S(2)}) collective-permute-start(f32[48,128]{1,0:T(8,128)S(1)} %get-tuple-element.35), channel_id=1, source_target_pairs={{0,1},{1,0},{2,3},{3,2},{4,5},{5,4},{6,7},{7,6},{8,9},{9,8},{10,11... | collective-permute-start | bytes 73736 | tf_op jit(solution)/shard_map/ppermute | solution.py:657
  10.5 7.0 %collective-permute-start.2 = (f32[48,128]{1,0:T(8,128)S(1)}, f32[48,128]{1,0:T(8,128)S(1)}, u32[]{:S(2)}, u32[]{:S(2)}) collective-permute-start(f32[48,128]{1,0:T(8,128)S(1)} %get-tuple-element.33), channel_id=1, source_target_pairs={{1,2},{2,1},{3,4},{4,3},{5,6},{6,5},{7,0},{0,7},{9,10},{10,9},{11,... | collective-permute-start | bytes 73736 | tf_op jit(solution)/shard_map/ppermute | solution.py:657
  14.0 1.0 %copy-start = (f32[4,128,256]{2,1,0:T(8,128)S(1)}, f32[4,128,256]{2,1,0:T(8,128)}, u32[]{:S(2)}) copy-start(f32[4,128,256]{2,1,0:T(8,128)} %get-tuple-element.26.fields_ref) | copy-start | bytes 1572868
  18.2 1.2 %collective-permute-start.4 = (f32[8,128]{1,0:T(8,128)S(1)}, f32[8,128]{1,0:T(8,128)S(1)}, u32[]{:S(2)}, u32[]{:S(2)}) collective-permute-start(f32[8,128]{1,0:T(8,128)S(1)} %get-tuple-element.38), channel_id=1, source_target_pairs={{0,8},{8,0},{16,24},{24,16},{1,9},{9,1},{17,25},{25,17},{2,10},{10... | collective-permute-start | bytes 12296 | tf_op jit(solution)/shard_map/ppermute | solution.py:648
  19.4 3.6 %collective-permute-start.5 = (f32[8,128]{1,0:T(8,128)S(1)}, f32[8,128]{1,0:T(8,128)S(1)}, u32[]{:S(2)}, u32[]{:S(2)}) collective-permute-start(f32[8,128]{1,0:T(8,128)S(1)} %add.3.sums_ref), channel_id=1, source_target_pairs={{0,16},{8,24},{16,0},{24,8},{1,17},{9,25},{17,1},{25,9},{2,18},{10... | collective-permute-start | bytes 12296 | tf_op jit(solution)/shard_map/ppermute | solution.py:648

commit v16 on v15

--- a/solution.py
+++ b/solution.py
@@ -380,7 +380,7 @@
         ],
         compiler_params=pltpu.CompilerParams(vmem_limit_bytes=VMEM_BYTES),
         cost_estimate=pl.CostEstimate(
-            flops=300 * rows * cols, bytes_accessed=64 * rows * cols, transcendentals=0
+            flops=300000 * rows * cols, bytes_accessed=64 * rows * cols, transcendentals=0
         ),
         name="interior",
     )(fields, near, far)

time: 36.2 us -> 35.6 us (0.983)
  blocking collectives: 11.7 us -> 10.6 us
  waiting for transfers between devices: 3.39 us -> 4.48 us
  starting transfers between devices: 8.8 us -> 8.27 us
    ppermute x4, waiting for transfers between devices: 0.01 us -> 1.08 us  [swap(): return lax.ppermute(values, axis, pairs)]
    all_to_all x1, blocking collectives: 11.7 us -> 10.6 us  [on_device(): lax.all_to_all(sent, 'lon', split_axis=0, concat_axis=0, tiled=True)]
    ppermute x4, starting transfers between devices: 8.27 us -> 7.74 us  [swap(): return lax.ppermute(values, axis, pairs)]
  transfers between devices with their start and end apart: 6 -> 6, of which waited for: 2 -> 3; matrix products, arithmetic and copies ran while one was open for 0% -> 0% of each run, Pallas kernels for 18% -> 18%
where the time goes in v16:
time: 35.6 us; the launch traced here: 35.4 us
  blocking collectives  10.6 us (30%)
  Pallas kernels  10.2 us (29%)
  starting transfers between devices  8.27 us (23%)
  waiting for transfers between devices  4.48 us (13%)
  local copies, waits for them, and re-layouts  1.06 us (3%)
  between operations  0.72 us (2%)
    all_to_all x1, blocking collectives, on_device(): lax.all_to_all(sent, 'lon', split_axis=0, concat_axis=0, tiled=True)  10.6 us
    ppermute x4, starting transfers between devices, swap(): return lax.ppermute(values, axis, pairs)  7.74 us
    ppermute x2, waiting for transfers between devices, exchange(): return lax.ppermute(values, axis, pairs)  3.4 us
    pallas_call x1, Pallas kernels, integrate(): pl.pallas_call(whole_kernel, in_specs=[pl.BlockSpec(memory_space=pltpu.HB...  3.12 us
    pallas_call x1, Pallas kernels, integrate_outer(): pl.pallas_call(outer_kernel, in_specs=[pl.BlockSpec(memory_space=pltpu.HB...  1.79 us
    pallas_call x1, Pallas kernels, interior(): pl.pallas_call(interior_kernel, out_shape=[jax.ShapeDtypeStruct((STEPS, r...  1.71 us
    pallas_call x2, Pallas kernels, strip(): pl.pallas_call(functools.partial(strip_kernel, near), out_shape=[jax.Shap...  1.42 us
    pallas_call x1, Pallas kernels, combine(): pl.pallas_call(combine_kernel, out_shape=[shape, shape, jax.ShapeDtypeStr...  1.14 us
  transfers between devices with their start and end apart: 6, of which 3 were waited for; matrix products, arithmetic and copies ran while one was open for 0% of the time, Pallas kernels for 18%

profile of v16, /device:TPU:0, one launch (start us, length us, event | category | flops | bytes accessed | tf_op | source)
XLA Modules:
  0.0 35.4 jit_solution(2593242800628635031)
XLA Ops:
  0.6 0.0 copy-start
  0.6 1.8 %outer.1 = (f32[4,8,256]{2,1,0:T(8,128)}, f32[4,8,256]{2,1,0:T(8,128)}) custom-call(f32[16]{0:T(128)} %thick_hbm.3, s32[128,256]{1,0:T(8,128)} %count_hbm.3, f32[128,256]{1,0:T(8,128)} %inertia_hbm.3, bf16[2,16,128,256]{3,2,1,0:T(8,128)(2,1)} %tend_hbm.3), custom_call_target="tpu_custom_call" | custom-call | flops 1572864 | bytes 524288 | tf_op jit(solution)/shard_map/outer/pallas_call | solution.py:204
  2.4 0.5 %collective-permute-start = (f32[4,8,256]{2,1,0:T(8,128)}, f32[4,8,256]{2,1,0:T(8,128)S(1)}, u32[]{:S(2)}, u32[]{:S(2)}) collective-permute-start(f32[4,8,256]{2,1,0:T(8,128)} %get-tuple-element.27), channel_id=1, source_target_pairs={{0,8},{8,0},{16,24},{24,16},{1,9},{9,1},{17,25},{25,17},{2,10},{10... | collective-permute-start | bytes 98312 | tf_op jit(solution)/shard_map/ppermute | solution.py:657
  3.0 2.6 %collective-permute-start.1 = (f32[4,8,256]{2,1,0:T(8,128)}, f32[4,8,256]{2,1,0:T(8,128)S(1)}, u32[]{:S(2)}, u32[]{:S(2)}) collective-permute-start(f32[4,8,256]{2,1,0:T(8,128)} %get-tuple-element.28), channel_id=1, source_target_pairs={{8,16},{16,8},{24,0},{0,24},{9,17},{17,9},{25,1},{1,25},{10,18},{1... | collective-permute-start | bytes 98312 | tf_op jit(solution)/shard_map/ppermute | solution.py:657
  5.6 0.0 copy-done
  5.6 3.1 %whole.1 = (f32[4,128,256]{2,1,0:T(8,128)}, f32[128,128]{1,0:T(8,128)S(1)}) custom-call(f32[16]{0:T(128)S(1)} %copy-done, s32[128,256]{1,0:T(8,128)} %count_hbm.3, f32[128,256]{1,0:T(8,128)} %inertia_hbm.3, bf16[2,16,128,256]{3,2,1,0:T(8,128)(2,1)} %tend_hbm.3), custom_call_target="tpu_custom_call" | custom-call | flops 6291456 | bytes 2097152 | tf_op jit(solution)/shard_map/whole/pallas_call | solution.py:223
  8.7 0.0 collective-permute-done.near_ref
  8.7 0.0 collective-permute-done.1.far_ref
  8.8 0.2 edges.1
  8.9 4.6 %collective-permute-start.2 = (f32[48,128]{1,0:T(8,128)S(1)}, f32[48,128]{1,0:T(8,128)S(1)}, u32[]{:S(2)}, u32[]{:S(2)}) collective-permute-start(f32[48,128]{1,0:T(8,128)S(1)} %get-tuple-element.33), channel_id=1, source_target_pairs={{1,2},{2,1},{3,4},{4,3},{5,6},{6,5},{7,0},{0,7},{9,10},{10,9},{11,... | collective-permute-start | bytes 73736 | tf_op jit(solution)/shard_map/ppermute | solution.py:657
  13.5 0.0 collective-permute-start.3
  13.5 0.0 copy-start.2
  13.5 1.0 %copy-done.2 = f32[4,128,256]{2,1,0:T(8,128)S(1)} copy-done((f32[4,128,256]{2,1,0:T(8,128)S(1)}, f32[4,128,256]{2,1,0:T(8,128)}, u32[]{:S(2)}) %copy-start.2) | copy-done | bytes 524312
  14.5 0.0 copy-start.1
  14.5 1.7 %interior.1 = (f32[4,128,256]{2,1,0:T(8,128)S(1)}, f32[5,128,256]{2,1,0:T(8,128)S(1)}, f32[4,48,128]{2,1,0:T(8,128)S(1)}, f32[4,48,128]{2,1,0:T(8,128)S(1)}, f32...) custom-call(f32[4,128,256]{2,1,0:T(8,128)S(1)} %copy-done.2, f32[4,8,256]{2,1,0:T(8,128)S(1)} %collective-permute-done.near_ref, ...), custom_call_target="tpu_custom_call" | custom-call | flops 9830400000 | bytes 2097152 | tf_op jit(solution)/shard_map/interior/pallas_call | solution.py:371
  16.2 1.1 %collective-permute-done.3.message_ref = f32[48,128]{1,0:T(8,128)S(1)} collective-permute-done((f32[48,128]{1,0:T(8,128)S(1)}, f32[48,128]{1,0:T(8,128)S(1)}, u32[]{:S(2)}, u32[]{:S(2)}) %collective-permute-start.3) | collective-permute-done | bytes 24608 | tf_op jit(solution)/shard_map/ppermute | solution.py:657
  17.3 0.7 %near_strip.1 = (f32[4,32,128]{2,1,0:T(8,128)S(1)}, f32[5,32,128]{2,1,0:T(8,128)S(1)}, f32[8,128]{1,0:T(8,128)S(1)}) custom-call(f32[4,48,128]{2,1,0:T(8,128)S(1)} %get-tuple-element.34.strip_in_ref, f32[48,128]{1,0:T(8,128)S(1)} %collective-permute-done.3.message_ref, f32[8,128]{1,0:T(8,128)S(1)} %get-tuple-element.36.before_ref), custom_call_target="tpu_custom_call" | custom-call | flops 1228800 | bytes 262144 | tf_op jit(solution)/shard_map/near_strip/pallas_call | solution.py:414
  18.0 0.0 collective-permute-done.2.message_ref
  18.0 0.7 %far_strip.1 = (f32[4,32,128]{2,1,0:T(8,128)S(1)}, f32[5,32,128]{2,1,0:T(8,128)S(1)}, f32[8,128]{1,0:T(8,128)S(1)}) custom-call(f32[4,48,128]{2,1,0:T(8,128)S(1)} %get-tuple-element.31.strip_in_ref, f32[48,128]{1,0:T(8,128)S(1)} %collective-permute-done.2.message_ref, f32[8,128]{1,0:T(8,128)S(1)} %get-tuple-element.37.before_ref), custom_call_target="tpu_custom_call" | custom-call | flops 1228800 | bytes 262144 | tf_op jit(solution)/shard_map/far_strip/pallas_call | solution.py:414
  18.7 0.0 collective-permute-start.4
  18.8 1.2 %collective-permute-done.4 = f32[8,128]{1,0:T(8,128)S(1)} collective-permute-done((f32[8,128]{1,0:T(8,128)S(1)}, f32[8,128]{1,0:T(8,128)S(1)}, u32[]{:S(2)}, u32[]{:S(2)}) %collective-permute-start.4) | collective-permute-done | bytes 4128 | tf_op jit(solution)/shard_map/ppermute | solution.py:648
  19.9 0.5 %collective-permute-start.5 = (f32[8,128]{1,0:T(8,128)S(1)}, f32[8,128]{1,0:T(8,128)S(1)}, u32[]{:S(2)}, u32[]{:S(2)}) collective-permute-start(f32[8,128]{1,0:T(8,128)S(1)} %add.3.sums_ref), channel_id=1, source_target_pairs={{0,16},{8,24},{16,0},{24,8},{1,17},{9,25},{17,1},{25,9},{2,18},{10... | collective-permute-start | bytes 12296 | tf_op jit(solution)/shard_map/ppermute | solution.py:648
  20.4 0.0 copy-done.1
  20.4 0.8 %place.1 = (s16[8,80,128]{2,1,0:T(8,128)(2,1)S(1)}, f32[8,8,128]{2,1,0:T(8,128)S(1)}) custom-call(s32[8]{0:T(128)S(1)} %bitcast.2, f32[2,128,256]{2,1,0:T(8,128)S(1)} %get-tuple-element.29.fields_ref), custom_call_target="tpu_custom_call" | custom-call | flops 1966080 | bytes 393216 | tf_op jit(solution)/shard_map/place/pallas_call | solution.py:473
  21.3 2.2 %collective-permute-done.5.other_ref = f32[8,128]{1,0:T(8,128)S(1)} collective-permute-done((f32[8,128]{1,0:T(8,128)S(1)}, f32[8,128]{1,0:T(8,128)S(1)}, u32[]{:S(2)}, u32[]{:S(2)}) %collective-permute-start.5) | collective-permute-done | bytes 4128 | tf_op jit(solution)/shard_map/ppermute | solution.py:648
  23.6 10.6 %all_to_all.5.arrived_ref = s16[8,80,128]{2,1,0:T(8,128)(2,1)S(1)} all-to-all(s16[8,80,128]{2,1,0:T(8,128)(2,1)S(1)} %constant_dynamic-update-slice_fusion), channel_id=1, replica_groups=mesh['lat'=4,'lon'=8] {'lon'}, dimensions={0} | all-to-all | bytes 327680 | tf_op jit(solution)/shard_map/all_to_all | solution.py:681
  34.2 1.1 %combine.1 = (f32[128,256]{1,0:T(8,128)}, f32[128,256]{1,0:T(8,128)}, f32[8,32,256]{2,1,0:T(8,128)}) custom-call(s16[8,80,128]{2,1,0:T(8,128)(2,1)S(1)} %all_to_all.5.arrived_ref, f32[4,128,256]{2,1,0:T(8,128)S(1)} %get-tuple-element.40.w_ref, f32[5,128,256]{2,1,0:T(8,128)S(1)} %get-tuple-element.41.mw_ref, f32[4,32,128]{2,1,0:T(8,128)S(1)} %get-tuple-element.42.near_w_ref, ...), custom_call_target="tpu_custom_call" | custom-call | tf_op jit(solution)/shard_map/combine/pallas_call | solution.py:630
  (3 shorter events, 0.1 us)
Async XLA Ops:
  0.6 5.0 %copy-start = (f32[16]{0:T(128)S(1)}, f32[16]{0:T(128)}, u32[]{:S(2)}) copy-start(f32[16]{0:T(128)} %thick_hbm.3) | copy-start | bytes 196
  2.4 6.3 %collective-permute-start = (f32[4,8,256]{2,1,0:T(8,128)}, f32[4,8,256]{2,1,0:T(8,128)S(1)}, u32[]{:S(2)}, u32[]{:S(2)}) collective-permute-start(f32[4,8,256]{2,1,0:T(8,128)} %get-tuple-element.27), channel_id=1, source_target_pairs={{0,8},{8,0},{16,24},{24,16},{1,9},{9,1},{17,25},{25,17},{2,10},{10... | collective-permute-start | bytes 98312 | tf_op jit(solution)/shard_map/ppermute | solution.py:657
  3.0 5.8 %collective-permute-start.1 = (f32[4,8,256]{2,1,0:T(8,128)}, f32[4,8,256]{2,1,0:T(8,128)S(1)}, u32[]{:S(2)}, u32[]{:S(2)}) collective-permute-start(f32[4,8,256]{2,1,0:T(8,128)} %get-tuple-element.28), channel_id=1, source_target_pairs={{8,16},{16,8},{24,0},{0,24},{9,17},{17,9},{25,1},{1,25},{10,18},{1... | collective-permute-start | bytes 98312 | tf_op jit(solution)/shard_map/ppermute | solution.py:657
  8.9 9.1 %collective-permute-start.2 = (f32[48,128]{1,0:T(8,128)S(1)}, f32[48,128]{1,0:T(8,128)S(1)}, u32[]{:S(2)}, u32[]{:S(2)}) collective-permute-start(f32[48,128]{1,0:T(8,128)S(1)} %get-tuple-element.33), channel_id=1, source_target_pairs={{1,2},{2,1},{3,4},{4,3},{5,6},{6,5},{7,0},{0,7},{9,10},{10,9},{11,... | collective-permute-start | bytes 73736 | tf_op jit(solution)/shard_map/ppermute | solution.py:657
  13.5 3.8 %collective-permute-start.3 = (f32[48,128]{1,0:T(8,128)S(1)}, f32[48,128]{1,0:T(8,128)S(1)}, u32[]{:S(2)}, u32[]{:S(2)}) collective-permute-start(f32[48,128]{1,0:T(8,128)S(1)} %get-tuple-element.35), channel_id=1, source_target_pairs={{0,1},{1,0},{2,3},{3,2},{4,5},{5,4},{6,7},{7,6},{8,9},{9,8},{10,11... | collective-permute-start | bytes 73736 | tf_op jit(solution)/shard_map/ppermute | solution.py:657
  13.5 1.0 %copy-start.2 = (f32[4,128,256]{2,1,0:T(8,128)S(1)}, f32[4,128,256]{2,1,0:T(8,128)}, u32[]{:S(2)}) copy-start(f32[4,128,256]{2,1,0:T(8,128)} %get-tuple-element.26.fields_ref) | copy-start | bytes 1572868
  14.5 5.9 %copy-start.1 = (s32[8,1]{0,1:T(1,128)S(1)}, s32[8,1]{0,1:T(1,128)}, u32[]{:S(2)}) copy-start(s32[8,1]{0,1:T(1,128)} %param.9) | copy-start | bytes 100
  18.7 1.2 %collective-permute-start.4 = (f32[8,128]{1,0:T(8,128)S(1)}, f32[8,128]{1,0:T(8,128)S(1)}, u32[]{:S(2)}, u32[]{:S(2)}) collective-permute-start(f32[8,128]{1,0:T(8,128)S(1)} %get-tuple-element.38), channel_id=1, source_target_pairs={{0,8},{8,0},{16,24},{24,16},{1,9},{9,1},{17,25},{25,17},{2,10},{10... | collective-permute-start | bytes 12296 | tf_op jit(solution)/shard_map/ppermute | solution.py:648
  19.9 3.6 %collective-permute-start.5 = (f32[8,128]{1,0:T(8,128)S(1)}, f32[8,128]{1,0:T(8,128)S(1)}, u32[]{:S(2)}, u32[]{:S(2)}) collective-permute-start(f32[8,128]{1,0:T(8,128)S(1)} %add.3.sums_ref), channel_id=1, source_target_pairs={{0,16},{8,24},{16,0},{24,8},{1,17},{9,25},{17,1},{25,9},{2,18},{10... | collective-permute-start | bytes 12296 | tf_op jit(solution)/shard_map/ppermute | solution.py:648

commit v17 on v16

--- a/solution.py
+++ b/solution.py
@@ -297,18 +297,18 @@
     mws = [scaled[own]]
     ws = []
     vector = scaled * inverse
+    ws.append(vector[own])
     for step in range(STEPS):
-        ws.append(vector[own])
         weighed = depth * vector
         scaled = depth * smooth(vector) + smooth(weighed) - 2.0 * weighed
         mws.append(scaled[own])
-        if step + 1 < STEPS:
-            vector = scaled * inverse
-    return ws, mws
+        vector = scaled * inverse
+        ws.append(vector[own])
+    return ws, mws, diag[own]
 
 
 def moments(ws, mws, mask):
-    ws = [jnp.where(mask, values, 0.0) for values in ws]
+    ws = [jnp.where(mask, values, 0.0) for values in ws[:STEPS]]
     images = [mws[place] - mws[place + 1] for place in range(STEPS)]
     pairs = [ws[place] * mws[0] for place in range(STEPS)]
     for low in range(STEPS):
@@ -338,7 +338,7 @@
     near_ref,
     far_ref,
     w_ref,
-    mw_ref,
+    diag_ref,
     near_strip_ref,
     far_strip_ref,
     sums_ref,
@@ -356,11 +356,10 @@
         near_strip_ref[place] = jnp.where(even, east, west)
         far_strip_ref[place] = jnp.where(even, west, east)
         padded.append(values)
-    ws, mws = basis(*padded)
+    ws, mws, diag = basis(*padded)
     for place, values in enumerate(ws):
         w_ref[place] = values
-    for place, values in enumerate(mws):
-        mw_ref[place] = values
+    diag_ref[...] = diag
     lane = lanes_of(ws[0].shape)
     sums_ref[...] = moments(ws, mws, (lane >= RIM) & (lane < cols - RIM))
 
@@ -371,8 +370,8 @@
     return pl.pallas_call(
         interior_kernel,
         out_shape=[
-            jax.ShapeDtypeStruct((STEPS, rows, cols), f32),
             jax.ShapeDtypeStruct((STEPS + 1, rows, cols), f32),
+            jax.ShapeDtypeStruct((rows, cols), f32),
             jax.ShapeDtypeStruct((FIELDS, folded_rows(rows + 2 * ROWS), LANES), f32),
             jax.ShapeDtypeStruct((FIELDS, folded_rows(rows + 2 * ROWS), LANES), f32),
             jax.ShapeDtypeStruct((ROWS, LANES), f32),
@@ -386,7 +385,7 @@
     )(fields, near, far)
 
 
-def strip_kernel(near, strip_in_ref, message_ref, before_ref, w_ref, mw_ref, sums_ref):
+def strip_kernel(near, strip_in_ref, message_ref, before_ref, w_ref, diag_ref, sums_ref):
     even = is_even("lon")
     eastern = even if near else jnp.logical_not(even)
     message = message_ref[...]
@@ -398,11 +397,10 @@
         at = place * RIM
         beyond = jnp.where(eastern, turn(message, 2 * RIM - at), turn(message, -at))
         padded.append(jnp.where(halo, beyond, strip_in_ref[place]))
-    ws, mws = basis(*padded)
+    ws, mws, diag = basis(*padded)
     for place, values in enumerate(ws):
         w_ref[place] = values
-    for place, values in enumerate(mws):
-        mw_ref[place] = values
+    diag_ref[...] = diag
     column = lax.rem(lanes_of(ws[0].shape), PITCH)
     edge = (column >= RIM) & (column < 2 * RIM)
     sums_ref[...] = before_ref[...] + moments(ws, mws, edge)
@@ -414,8 +412,8 @@
     return pl.pallas_call(
         functools.partial(strip_kernel, near),
         out_shape=[
-            jax.ShapeDtypeStruct((STEPS, rows, LANES), f32),
             jax.ShapeDtypeStruct((STEPS + 1, rows, LANES), f32),
+            jax.ShapeDtypeStruct((rows, LANES), f32),
             jax.ShapeDtypeStruct((ROWS, LANES), f32),
         ],
         compiler_params=pltpu.CompilerParams(vmem_limit_bytes=VMEM_BYTES),
@@ -512,11 +510,11 @@
 def combine_kernel(
     arrived_ref,
     w_ref,
-    mw_ref,
+    diag_ref,
     near_w_ref,
-    near_mw_ref,
+    near_diag_ref,
     far_w_ref,
-    far_mw_ref,
+    far_diag_ref,
     pressure_hbm,
     residual_hbm,
     held_hbm,
@@ -576,19 +574,26 @@
             right[pivot] = right[pivot] - matrix[pivot, col] * right[col]
         right[pivot] = right[pivot] * matrix[pivot, pivot]
 
-    def results(w_ref, mw_ref, part):
-        pressure = right[0] * w_ref[0, part]
-        residual = mw_ref[0, part] - right[0] * (mw_ref[0, part] - mw_ref[1, part])
+    left = [1.0 - right[0]]
+    for place in range(1, STEPS):
+        left.append(right[place - 1] - right[place])
+    left.append(right[STEPS - 1])
+
+    def results(w_ref, diag_ref, part):
+        vector = w_ref[0, part]
+        pressure = right[0] * vector
+        residual = left[0] * vector
         for place in range(1, STEPS):
-            pressure = pressure + right[place] * w_ref[place, part]
-            image = mw_ref[place, part] - mw_ref[place + 1, part]
-            residual = residual - right[place] * image
-        return pressure, residual
+            vector = w_ref[place, part]
+            pressure = pressure + right[place] * vector
+            residual = residual + left[place] * vector
+        residual = residual + left[STEPS] * w_ref[STEPS, part]
+        return pressure, diag_ref[part] * residual
 
     rows, cols = pressure_ref.shape
     even = is_even("lon")
-    near = results(near_w_ref, near_mw_ref, slice(None))
-    far = results(far_w_ref, far_mw_ref, slice(None))
+    near = results(near_w_ref, near_diag_ref, slice(None))
+    far = results(far_w_ref, far_diag_ref, slice(None))
     west = [jnp.where(even, b, a) for a, b in zip(near, far)]
     east = [jnp.where(even, a, b) for a, b in zip(near, far)]
 
@@ -598,7 +603,7 @@
     copies = []
     for piece in range(PIECES):
         part = slice(piece * rows // PIECES, (piece + 1) * rows // PIECES)
-        inner = results(w_ref, mw_ref, part)
+        inner = results(w_ref, diag_ref, part)
         parts = range(piece * FOLD // PIECES, (piece + 1) * FOLD // PIECES)
         lane = lanes_of((rows // PIECES, LANES))
         for field, (out_ref, out_hbm, inside) in enumerate(
@@ -623,7 +628,7 @@
         copy.wait()
 
 
-def combine(arrived, w, mw, near, far):
+def combine(arrived, w, diag, near, far):
     rows, cols = w.shape[1:]
     shape = jax.ShapeDtypeStruct((rows, cols), jnp.float32)
     held = (arrived.shape[0], (arrived.shape[1] - TAIL) * LANES // cols, cols)
@@ -640,7 +645,7 @@
         ],
         compiler_params=pltpu.CompilerParams(vmem_limit_bytes=VMEM_BYTES),
         name="combine",
-    )(arrived, w, mw, *near, *far)
+    )(arrived, w, diag, *near, *far)
 
 
 def exchange(values, axis, distance):
@@ -668,7 +673,7 @@
     near_edge, far_edge = edges(side, near, far)
     far_edge = swap(far_edge, "lon", 1)
     near_edge = swap(near_edge, "lon", 0)
-    w, mw, near_strip, far_strip, sums, forcing = interior(fields, near, far)
+    w, diag, near_strip, far_strip, sums, forcing = interior(fields, near, far)
     *near_results, sums = strip(True, near_strip, near_edge, sums)
     *far_results, sums = strip(False, far_strip, far_edge, sums)
     sent, scale = place(owner[:, 0], forcing, lon_count)
@@ -679,7 +684,7 @@
     tail = seal(sums, exchange(sums, "lat", shift), scale)
     sent = lax.dynamic_update_slice(sent, tail, (0, sent.shape[1] - TAIL, 0))
     arrived = lax.all_to_all(sent, "lon", split_axis=0, concat_axis=0, tiled=True)
-    pressure, residual, held = combine(arrived, w, mw, near_results, far_results)
+    pressure, residual, held = combine(arrived, w, diag, near_results, far_results)
     held = held.reshape((1, 1, lon_count, 2, held.shape[1] // 2, held.shape[2]))
     return (held, pressure, residual)
 

time: 35.6 us -> 35.6 us (level)
  no operation moved by 1% of the time
where the time goes in v17:
time: 35.6 us; the launch traced here: 35.4 us
  blocking collectives  10.6 us (30%)
  Pallas kernels  10.3 us (29%)
  starting transfers between devices  8.27 us (23%)
  waiting for transfers between devices  4.42 us (12%)
  local copies, waits for them, and re-layouts  1.06 us (3%)
  between operations  0.72 us (2%)
    all_to_all x1, blocking collectives, on_device(): lax.all_to_all(sent, 'lon', split_axis=0, concat_axis=0, tiled=True)  10.6 us
    ppermute x4, starting transfers between devices, swap(): return lax.ppermute(values, axis, pairs)  7.74 us
    ppermute x2, waiting for transfers between devices, exchange(): return lax.ppermute(values, axis, pairs)  3.38 us
    pallas_call x1, Pallas kernels, integrate(): pl.pallas_call(whole_kernel, in_specs=[pl.BlockSpec(memory_space=pltpu.HB...  3.12 us
    pallas_call x1, Pallas kernels, integrate_outer(): pl.pallas_call(outer_kernel, in_specs=[pl.BlockSpec(memory_space=pltpu.HB...  1.79 us
    pallas_call x1, Pallas kernels, interior(): pl.pallas_call(interior_kernel, out_shape=[jax.ShapeDtypeStruct((STEPS +...  1.73 us
    pallas_call x2, Pallas kernels, strip(): pl.pallas_call(functools.partial(strip_kernel, near), out_shape=[jax.Shap...  1.43 us
    pallas_call x1, Pallas kernels, combine(): pl.pallas_call(combine_kernel, out_shape=[shape, shape, jax.ShapeDtypeStr...  1.15 us
  transfers between devices with their start and end apart: 6, of which 3 were waited for; matrix products, arithmetic and copies ran while one was open for 0% of the time, Pallas kernels for 18%

profile of v17, /device:TPU:0, one launch (start us, length us, event | category | flops | bytes accessed | tf_op | source)
XLA Modules:
  0.0 35.4 jit_solution(16210139143597105531)
XLA Ops:
  0.6 0.0 copy-start
  0.6 1.8 %outer.1 = (f32[4,8,256]{2,1,0:T(8,128)}, f32[4,8,256]{2,1,0:T(8,128)}) custom-call(f32[16]{0:T(128)} %thick_hbm.3, s32[128,256]{1,0:T(8,128)} %count_hbm.3, f32[128,256]{1,0:T(8,128)} %inertia_hbm.3, bf16[2,16,128,256]{3,2,1,0:T(8,128)(2,1)} %tend_hbm.3), custom_call_target="tpu_custom_call" | custom-call | flops 1572864 | bytes 524288 | tf_op jit(solution)/shard_map/outer/pallas_call | solution.py:204
  2.4 0.5 %collective-permute-start = (f32[4,8,256]{2,1,0:T(8,128)}, f32[4,8,256]{2,1,0:T(8,128)S(1)}, u32[]{:S(2)}, u32[]{:S(2)}) collective-permute-start(f32[4,8,256]{2,1,0:T(8,128)} %get-tuple-element.27), channel_id=1, source_target_pairs={{0,8},{8,0},{16,24},{24,16},{1,9},{9,1},{17,25},{25,17},{2,10},{10... | collective-permute-start | bytes 98312 | tf_op jit(solution)/shard_map/ppermute | solution.py:662
  3.0 2.6 %collective-permute-start.1 = (f32[4,8,256]{2,1,0:T(8,128)}, f32[4,8,256]{2,1,0:T(8,128)S(1)}, u32[]{:S(2)}, u32[]{:S(2)}) collective-permute-start(f32[4,8,256]{2,1,0:T(8,128)} %get-tuple-element.28), channel_id=1, source_target_pairs={{8,16},{16,8},{24,0},{0,24},{9,17},{17,9},{25,1},{1,25},{10,18},{1... | collective-permute-start | bytes 98312 | tf_op jit(solution)/shard_map/ppermute | solution.py:662
  5.6 0.0 copy-done
  5.6 3.1 %whole.1 = (f32[4,128,256]{2,1,0:T(8,128)}, f32[128,128]{1,0:T(8,128)S(1)}) custom-call(f32[16]{0:T(128)S(1)} %copy-done, s32[128,256]{1,0:T(8,128)} %count_hbm.3, f32[128,256]{1,0:T(8,128)} %inertia_hbm.3, bf16[2,16,128,256]{3,2,1,0:T(8,128)(2,1)} %tend_hbm.3), custom_call_target="tpu_custom_call" | custom-call | flops 6291456 | bytes 2097152 | tf_op jit(solution)/shard_map/whole/pallas_call | solution.py:223
  8.7 0.0 collective-permute-done.near_ref
  8.7 0.0 collective-permute-done.1.far_ref
  8.8 0.2 edges.1
  8.9 4.6 %collective-permute-start.2 = (f32[48,128]{1,0:T(8,128)S(1)}, f32[48,128]{1,0:T(8,128)S(1)}, u32[]{:S(2)}, u32[]{:S(2)}) collective-permute-start(f32[48,128]{1,0:T(8,128)S(1)} %get-tuple-element.33), channel_id=1, source_target_pairs={{1,2},{2,1},{3,4},{4,3},{5,6},{6,5},{7,0},{0,7},{9,10},{10,9},{11,... | collective-permute-start | bytes 73736 | tf_op jit(solution)/shard_map/ppermute | solution.py:662
  13.5 0.0 collective-permute-start.3
  13.5 0.0 copy-start.2
  13.5 1.0 %copy-done.2 = f32[4,128,256]{2,1,0:T(8,128)S(1)} copy-done((f32[4,128,256]{2,1,0:T(8,128)S(1)}, f32[4,128,256]{2,1,0:T(8,128)}, u32[]{:S(2)}) %copy-start.2) | copy-done | bytes 524312
  14.5 0.0 copy-start.1
  14.5 1.7 %interior.1 = (f32[5,128,256]{2,1,0:T(8,128)S(1)}, f32[128,256]{1,0:T(8,128)S(1)}, f32[4,48,128]{2,1,0:T(8,128)S(1)}, f32[4,48,128]{2,1,0:T(8,128)S(1)}, f32[8,1...) custom-call(f32[4,128,256]{2,1,0:T(8,128)S(1)} %copy-done.2, f32[4,8,256]{2,1,0:T(8,128)S(1)} %collective-permute-done.near_ref, ...), custom_call_target="tpu_custom_call" | custom-call | flops 9830400000 | bytes 2097152 | tf_op jit(solution)/shard_map/interior/pallas_call | solution.py:370
  16.3 1.0 %collective-permute-done.3.message_ref = f32[48,128]{1,0:T(8,128)S(1)} collective-permute-done((f32[48,128]{1,0:T(8,128)S(1)}, f32[48,128]{1,0:T(8,128)S(1)}, u32[]{:S(2)}, u32[]{:S(2)}) %collective-permute-start.3) | collective-permute-done | bytes 24608 | tf_op jit(solution)/shard_map/ppermute | solution.py:662
  17.3 0.7 %near_strip.1 = (f32[5,32,128]{2,1,0:T(8,128)S(1)}, f32[32,128]{1,0:T(8,128)S(1)}, f32[8,128]{1,0:T(8,128)S(1)}) custom-call(f32[4,48,128]{2,1,0:T(8,128)S(1)} %get-tuple-element.34.strip_in_ref, f32[48,128]{1,0:T(8,128)S(1)} %collective-permute-done.3.message_ref, f32[8,128]{1,0:T(8,128)S(1)} %get-tuple-element.36.before_ref), custom_call_target="tpu_custom_call" | custom-call | flops 1228800 | bytes 262144 | tf_op jit(solution)/shard_map/near_strip/pallas_call | solution.py:412
  18.0 0.0 collective-permute-done.2.message_ref
  18.0 0.7 %far_strip.1 = (f32[5,32,128]{2,1,0:T(8,128)S(1)}, f32[32,128]{1,0:T(8,128)S(1)}, f32[8,128]{1,0:T(8,128)S(1)}) custom-call(f32[4,48,128]{2,1,0:T(8,128)S(1)} %get-tuple-element.31.strip_in_ref, f32[48,128]{1,0:T(8,128)S(1)} %collective-permute-done.2.message_ref, f32[8,128]{1,0:T(8,128)S(1)} %get-tuple-element.37.before_ref), custom_call_target="tpu_custom_call" | custom-call | flops 1228800 | bytes 262144 | tf_op jit(solution)/shard_map/far_strip/pallas_call | solution.py:412
  18.7 0.0 collective-permute-start.4
  18.8 1.2 %collective-permute-done.4 = f32[8,128]{1,0:T(8,128)S(1)} collective-permute-done((f32[8,128]{1,0:T(8,128)S(1)}, f32[8,128]{1,0:T(8,128)S(1)}, u32[]{:S(2)}, u32[]{:S(2)}) %collective-permute-start.4) | collective-permute-done | bytes 4128 | tf_op jit(solution)/shard_map/ppermute | solution.py:653
  19.9 0.5 %collective-permute-start.5 = (f32[8,128]{1,0:T(8,128)S(1)}, f32[8,128]{1,0:T(8,128)S(1)}, u32[]{:S(2)}, u32[]{:S(2)}) collective-permute-start(f32[8,128]{1,0:T(8,128)S(1)} %add.3.sums_ref), channel_id=1, source_target_pairs={{0,16},{8,24},{16,0},{24,8},{1,17},{9,25},{17,1},{25,9},{2,18},{10... | collective-permute-start | bytes 12296 | tf_op jit(solution)/shard_map/ppermute | solution.py:653
  20.4 0.0 copy-done.1
  20.4 0.9 %place.1 = (s16[8,80,128]{2,1,0:T(8,128)(2,1)S(1)}, f32[8,8,128]{2,1,0:T(8,128)S(1)}) custom-call(s32[8]{0:T(128)S(1)} %bitcast.2, f32[2,128,256]{2,1,0:T(8,128)S(1)} %get-tuple-element.29.fields_ref), custom_call_target="tpu_custom_call" | custom-call | flops 1966080 | bytes 393216 | tf_op jit(solution)/shard_map/place/pallas_call | solution.py:471
  21.3 2.2 %collective-permute-done.5.other_ref = f32[8,128]{1,0:T(8,128)S(1)} collective-permute-done((f32[8,128]{1,0:T(8,128)S(1)}, f32[8,128]{1,0:T(8,128)S(1)}, u32[]{:S(2)}, u32[]{:S(2)}) %collective-permute-start.5) | collective-permute-done | bytes 4128 | tf_op jit(solution)/shard_map/ppermute | solution.py:653
  23.6 10.6 %all_to_all.5.arrived_ref = s16[8,80,128]{2,1,0:T(8,128)(2,1)S(1)} all-to-all(s16[8,80,128]{2,1,0:T(8,128)(2,1)S(1)} %constant_dynamic-update-slice_fusion), channel_id=1, replica_groups=mesh['lat'=4,'lon'=8] {'lon'}, dimensions={0} | all-to-all | bytes 327680 | tf_op jit(solution)/shard_map/all_to_all | solution.py:686
  34.2 1.2 %combine.1 = (f32[128,256]{1,0:T(8,128)}, f32[128,256]{1,0:T(8,128)}, f32[8,32,256]{2,1,0:T(8,128)}) custom-call(s16[8,80,128]{2,1,0:T(8,128)(2,1)S(1)} %all_to_all.5.arrived_ref, f32[5,128,256]{2,1,0:T(8,128)S(1)} %get-tuple-element.40.w_ref, f32[128,256]{1,0:T(8,128)S(1)} %get-tuple-element.41.diag_ref, f32[5,32,128]{2,1,0:T(8,128)S(1)} %get-tuple-element.42.near_w_ref, ...), custom_call_target="tpu_custom_call" | custom-call | tf_op jit(solution)/shard_map/combine/pallas_call | solution.py:635
  (3 shorter events, 0.1 us)
Async XLA Ops:
  0.6 5.0 %copy-start = (f32[16]{0:T(128)S(1)}, f32[16]{0:T(128)}, u32[]{:S(2)}) copy-start(f32[16]{0:T(128)} %thick_hbm.3) | copy-start | bytes 196
  2.4 6.3 %collective-permute-start = (f32[4,8,256]{2,1,0:T(8,128)}, f32[4,8,256]{2,1,0:T(8,128)S(1)}, u32[]{:S(2)}, u32[]{:S(2)}) collective-permute-start(f32[4,8,256]{2,1,0:T(8,128)} %get-tuple-element.27), channel_id=1, source_target_pairs={{0,8},{8,0},{16,24},{24,16},{1,9},{9,1},{17,25},{25,17},{2,10},{10... | collective-permute-start | bytes 98312 | tf_op jit(solution)/shard_map/ppermute | solution.py:662
  3.0 5.8 %collective-permute-start.1 = (f32[4,8,256]{2,1,0:T(8,128)}, f32[4,8,256]{2,1,0:T(8,128)S(1)}, u32[]{:S(2)}, u32[]{:S(2)}) collective-permute-start(f32[4,8,256]{2,1,0:T(8,128)} %get-tuple-element.28), channel_id=1, source_target_pairs={{8,16},{16,8},{24,0},{0,24},{9,17},{17,9},{25,1},{1,25},{10,18},{1... | collective-permute-start | bytes 98312 | tf_op jit(solution)/shard_map/ppermute | solution.py:662
  8.9 9.1 %collective-permute-start.2 = (f32[48,128]{1,0:T(8,128)S(1)}, f32[48,128]{1,0:T(8,128)S(1)}, u32[]{:S(2)}, u32[]{:S(2)}) collective-permute-start(f32[48,128]{1,0:T(8,128)S(1)} %get-tuple-element.33), channel_id=1, source_target_pairs={{1,2},{2,1},{3,4},{4,3},{5,6},{6,5},{7,0},{0,7},{9,10},{10,9},{11,... | collective-permute-start | bytes 73736 | tf_op jit(solution)/shard_map/ppermute | solution.py:662
  13.5 3.8 %collective-permute-start.3 = (f32[48,128]{1,0:T(8,128)S(1)}, f32[48,128]{1,0:T(8,128)S(1)}, u32[]{:S(2)}, u32[]{:S(2)}) collective-permute-start(f32[48,128]{1,0:T(8,128)S(1)} %get-tuple-element.35), channel_id=1, source_target_pairs={{0,1},{1,0},{2,3},{3,2},{4,5},{5,4},{6,7},{7,6},{8,9},{9,8},{10,11... | collective-permute-start | bytes 73736 | tf_op jit(solution)/shard_map/ppermute | solution.py:662
  13.5 1.0 %copy-start.2 = (f32[4,128,256]{2,1,0:T(8,128)S(1)}, f32[4,128,256]{2,1,0:T(8,128)}, u32[]{:S(2)}) copy-start(f32[4,128,256]{2,1,0:T(8,128)} %get-tuple-element.26.fields_ref) | copy-start | bytes 1572868
  14.5 5.9 %copy-start.1 = (s32[8,1]{0,1:T(1,128)S(1)}, s32[8,1]{0,1:T(1,128)}, u32[]{:S(2)}) copy-start(s32[8,1]{0,1:T(1,128)} %param.9) | copy-start | bytes 100
  18.7 1.2 %collective-permute-start.4 = (f32[8,128]{1,0:T(8,128)S(1)}, f32[8,128]{1,0:T(8,128)S(1)}, u32[]{:S(2)}, u32[]{:S(2)}) collective-permute-start(f32[8,128]{1,0:T(8,128)S(1)} %get-tuple-element.38), channel_id=1, source_target_pairs={{0,8},{8,0},{16,24},{24,16},{1,9},{9,1},{17,25},{25,17},{2,10},{10... | collective-permute-start | bytes 12296 | tf_op jit(solution)/shard_map/ppermute | solution.py:653
  19.9 3.6 %collective-permute-start.5 = (f32[8,128]{1,0:T(8,128)S(1)}, f32[8,128]{1,0:T(8,128)S(1)}, u32[]{:S(2)}, u32[]{:S(2)}) collective-permute-start(f32[8,128]{1,0:T(8,128)S(1)} %add.3.sums_ref), channel_id=1, source_target_pairs={{0,16},{8,24},{16,0},{24,8},{1,17},{9,25},{17,1},{25,9},{2,18},{10... | collective-permute-start | bytes 12296 | tf_op jit(solution)/shard_map/ppermute | solution.py:653

commit v18 on v16

--- a/solution.py
+++ b/solution.py
@@ -160,33 +160,47 @@
     tend_ref,
     sems,
     band_sems,
+    count_sems,
 ):
     rows = count_hbm.shape[0]
     bands = [(row, CHUNK) for row in range(0, rows, CHUNK)]
     tends = []
+    counts = []
     for place, (row, size) in enumerate(bands):
         part = pl.ds(row, size)
+        counts.append(
+            pltpu.make_async_copy(count_hbm.at[part], count_ref.at[part], count_sems.at[place])
+        )
         tends.append(
             pltpu.make_async_copy(
                 tend_hbm.at[:, :, part], tend_ref.at[:, :, part], band_sems.at[place]
             )
         )
-    count = pltpu.make_async_copy(count_hbm, count_ref, sems.at[0])
-    thick = pltpu.make_async_copy(thick_hbm, thick_ref, sems.at[1])
-    inertia = pltpu.make_async_copy(inertia_hbm, fields_ref.at[FIELDS - 1], sems.at[2])
-    for copy in [tends[0], count, thick, inertia] + tends[1:]:
+    thick = pltpu.make_async_copy(thick_hbm, thick_ref, sems.at[0])
+    inertia = pltpu.make_async_copy(inertia_hbm, fields_ref.at[FIELDS - 1], sems.at[1])
+    order = [tends[0], counts[0], thick, tends[1], counts[1], inertia]
+    for place in range(2, len(bands)):
+        order += [tends[place], counts[place]]
+    for copy in order:
         copy.start()
-    for copy in (count, thick, inertia):
-        copy.wait()
+    thick.wait()
+
+    def wait(place):
+        def run():
+            counts[place].wait()
+            tends[place].wait()
+
+        return run
 
     def finish(place, part, values):
+        if place == 0:
+            inertia.wait()
         for field in range(FIELDS - 1):
             fields_ref[field, part] = values[field]
         side_ref[part] = pack_edges(fields_ref, part)
 
-    integrate_bands(
-        bands, thick_ref, count_ref, tend_ref, [copy.wait for copy in tends], finish
-    )
+    waits = [wait(place) for place in range(len(bands))]
+    integrate_bands(bands, thick_ref, count_ref, tend_ref, waits, finish)
 
 
 def integrate_cost(tendency, rows):
@@ -231,7 +245,8 @@
             pltpu.SMEM(thickness.shape, f32),
             pltpu.VMEM((rows, cols), jnp.int32),
             pltpu.VMEM(tendency.shape, tendency.dtype),
-            pltpu.SemaphoreType.DMA((3,)),
+            pltpu.SemaphoreType.DMA((2,)),
+            pltpu.SemaphoreType.DMA((rows // CHUNK,)),
             pltpu.SemaphoreType.DMA((rows // CHUNK,)),
         ],
         cost_estimate=integrate_cost(tendency, rows),

time: 35.6 us -> 35.5 us (level)
  no operation moved by 1% of the time
where the time goes in v18:
time: 35.5 us; the launch traced here: 35.3 us
  blocking collectives  10.6 us (30%)
  Pallas kernels  10.1 us (28%)
  starting transfers between devices  8.29 us (23%)
  waiting for transfers between devices  4.47 us (13%)
  local copies, waits for them, and re-layouts  1.06 us (3%)
  between operations  0.72 us (2%)
    all_to_all x1, blocking collectives, on_device(): lax.all_to_all(sent, 'lon', split_axis=0, concat_axis=0, tiled=True)  10.6 us
    ppermute x4, starting transfers between devices, swap(): return lax.ppermute(values, axis, pairs)  7.74 us
    ppermute x2, waiting for transfers between devices, exchange(): return lax.ppermute(values, axis, pairs)  3.39 us
    pallas_call x1, Pallas kernels, integrate(): pl.pallas_call(whole_kernel, in_specs=[pl.BlockSpec(memory_space=pltpu.HB...  3.03 us
    pallas_call x1, Pallas kernels, integrate_outer(): pl.pallas_call(outer_kernel, in_specs=[pl.BlockSpec(memory_space=pltpu.HB...  1.79 us
    pallas_call x1, Pallas kernels, interior(): pl.pallas_call(interior_kernel, out_shape=[jax.ShapeDtypeStruct((STEPS, r...  1.71 us
    pallas_call x2, Pallas kernels, strip(): pl.pallas_call(functools.partial(strip_kernel, near), out_shape=[jax.Shap...  1.42 us
    pallas_call x1, Pallas kernels, combine(): pl.pallas_call(combine_kernel, out_shape=[shape, shape, jax.ShapeDtypeStr...  1.14 us
  transfers between devices with their start and end apart: 6, of which 3 were waited for; matrix products, arithmetic and copies ran while one was open for 0% of the time, Pallas kernels for 18%

profile of v18, /device:TPU:0, one launch (start us, length us, event | category | flops | bytes accessed | tf_op | source)
XLA Modules:
  0.0 35.3 jit_solution(8941300696801142775)
XLA Ops:
  0.6 0.0 copy-start
  0.6 1.8 %outer.1 = (f32[4,8,256]{2,1,0:T(8,128)}, f32[4,8,256]{2,1,0:T(8,128)}) custom-call(f32[16]{0:T(128)} %thick_hbm.3, s32[128,256]{1,0:T(8,128)} %count_hbm.3, f32[128,256]{1,0:T(8,128)} %inertia_hbm.3, bf16[2,16,128,256]{3,2,1,0:T(8,128)(2,1)} %tend_hbm.3), custom_call_target="tpu_custom_call" | custom-call | flops 1572864 | bytes 524288 | tf_op jit(solution)/shard_map/outer/pallas_call | solution.py:218
  2.4 0.5 %collective-permute-start = (f32[4,8,256]{2,1,0:T(8,128)}, f32[4,8,256]{2,1,0:T(8,128)S(1)}, u32[]{:S(2)}, u32[]{:S(2)}) collective-permute-start(f32[4,8,256]{2,1,0:T(8,128)} %get-tuple-element.27), channel_id=1, source_target_pairs={{0,8},{8,0},{16,24},{24,16},{1,9},{9,1},{17,25},{25,17},{2,10},{10... | collective-permute-start | bytes 98312 | tf_op jit(solution)/shard_map/ppermute | solution.py:672
  3.0 2.6 %collective-permute-start.1 = (f32[4,8,256]{2,1,0:T(8,128)}, f32[4,8,256]{2,1,0:T(8,128)S(1)}, u32[]{:S(2)}, u32[]{:S(2)}) collective-permute-start(f32[4,8,256]{2,1,0:T(8,128)} %get-tuple-element.28), channel_id=1, source_target_pairs={{8,16},{16,8},{24,0},{0,24},{9,17},{17,9},{25,1},{1,25},{10,18},{1... | collective-permute-start | bytes 98312 | tf_op jit(solution)/shard_map/ppermute | solution.py:672
  5.6 0.0 copy-done
  5.6 3.0 %whole.1 = (f32[4,128,256]{2,1,0:T(8,128)}, f32[128,128]{1,0:T(8,128)S(1)}) custom-call(f32[16]{0:T(128)S(1)} %copy-done, s32[128,256]{1,0:T(8,128)} %count_hbm.3, f32[128,256]{1,0:T(8,128)} %inertia_hbm.3, bf16[2,16,128,256]{3,2,1,0:T(8,128)(2,1)} %tend_hbm.3), custom_call_target="tpu_custom_call" | custom-call | flops 6291456 | bytes 2097152 | tf_op jit(solution)/shard_map/whole/pallas_call | solution.py:237
  8.6 0.0 collective-permute-done.near_ref
  8.6 0.0 collective-permute-done.1.far_ref
  8.7 0.2 edges.1
  8.8 4.6 %collective-permute-start.2 = (f32[48,128]{1,0:T(8,128)S(1)}, f32[48,128]{1,0:T(8,128)S(1)}, u32[]{:S(2)}, u32[]{:S(2)}) collective-permute-start(f32[48,128]{1,0:T(8,128)S(1)} %get-tuple-element.33), channel_id=1, source_target_pairs={{1,2},{2,1},{3,4},{4,3},{5,6},{6,5},{7,0},{0,7},{9,10},{10,9},{11,... | collective-permute-start | bytes 73736 | tf_op jit(solution)/shard_map/ppermute | solution.py:672
  13.4 0.0 collective-permute-start.3
  13.4 0.0 copy-start.2
  13.4 1.0 %copy-done.2 = f32[4,128,256]{2,1,0:T(8,128)S(1)} copy-done((f32[4,128,256]{2,1,0:T(8,128)S(1)}, f32[4,128,256]{2,1,0:T(8,128)}, u32[]{:S(2)}) %copy-start.2) | copy-done | bytes 524312
  14.4 0.0 copy-start.1
  14.4 1.7 %interior.1 = (f32[4,128,256]{2,1,0:T(8,128)S(1)}, f32[5,128,256]{2,1,0:T(8,128)S(1)}, f32[4,48,128]{2,1,0:T(8,128)S(1)}, f32[4,48,128]{2,1,0:T(8,128)S(1)}, f32...) custom-call(f32[4,128,256]{2,1,0:T(8,128)S(1)} %copy-done.2, f32[4,8,256]{2,1,0:T(8,128)S(1)} %collective-permute-done.near_ref, ...), custom_call_target="tpu_custom_call" | custom-call | flops 9830400000 | bytes 2097152 | tf_op jit(solution)/shard_map/interior/pallas_call | solution.py:386
  16.1 1.1 %collective-permute-done.3.message_ref = f32[48,128]{1,0:T(8,128)S(1)} collective-permute-done((f32[48,128]{1,0:T(8,128)S(1)}, f32[48,128]{1,0:T(8,128)S(1)}, u32[]{:S(2)}, u32[]{:S(2)}) %collective-permute-start.3) | collective-permute-done | bytes 24608 | tf_op jit(solution)/shard_map/ppermute | solution.py:672
  17.2 0.7 %near_strip.1 = (f32[4,32,128]{2,1,0:T(8,128)S(1)}, f32[5,32,128]{2,1,0:T(8,128)S(1)}, f32[8,128]{1,0:T(8,128)S(1)}) custom-call(f32[4,48,128]{2,1,0:T(8,128)S(1)} %get-tuple-element.34.strip_in_ref, f32[48,128]{1,0:T(8,128)S(1)} %collective-permute-done.3.message_ref, f32[8,128]{1,0:T(8,128)S(1)} %get-tuple-element.36.before_ref), custom_call_target="tpu_custom_call" | custom-call | flops 1228800 | bytes 262144 | tf_op jit(solution)/shard_map/near_strip/pallas_call | solution.py:429
  17.9 0.0 collective-permute-done.2.message_ref
  17.9 0.7 %far_strip.1 = (f32[4,32,128]{2,1,0:T(8,128)S(1)}, f32[5,32,128]{2,1,0:T(8,128)S(1)}, f32[8,128]{1,0:T(8,128)S(1)}) custom-call(f32[4,48,128]{2,1,0:T(8,128)S(1)} %get-tuple-element.31.strip_in_ref, f32[48,128]{1,0:T(8,128)S(1)} %collective-permute-done.2.message_ref, f32[8,128]{1,0:T(8,128)S(1)} %get-tuple-element.37.before_ref), custom_call_target="tpu_custom_call" | custom-call | flops 1228800 | bytes 262144 | tf_op jit(solution)/shard_map/far_strip/pallas_call | solution.py:429
  18.6 0.0 collective-permute-start.4
  18.7 1.2 %collective-permute-done.4 = f32[8,128]{1,0:T(8,128)S(1)} collective-permute-done((f32[8,128]{1,0:T(8,128)S(1)}, f32[8,128]{1,0:T(8,128)S(1)}, u32[]{:S(2)}, u32[]{:S(2)}) %collective-permute-start.4) | collective-permute-done | bytes 4128 | tf_op jit(solution)/shard_map/ppermute | solution.py:663
  19.8 0.5 %collective-permute-start.5 = (f32[8,128]{1,0:T(8,128)S(1)}, f32[8,128]{1,0:T(8,128)S(1)}, u32[]{:S(2)}, u32[]{:S(2)}) collective-permute-start(f32[8,128]{1,0:T(8,128)S(1)} %add.3.sums_ref), channel_id=1, source_target_pairs={{0,16},{8,24},{16,0},{24,8},{1,17},{9,25},{17,1},{25,9},{2,18},{10... | collective-permute-start | bytes 12296 | tf_op jit(solution)/shard_map/ppermute | solution.py:663
  20.4 0.0 copy-done.1
  20.4 0.8 %place.1 = (s16[8,80,128]{2,1,0:T(8,128)(2,1)S(1)}, f32[8,8,128]{2,1,0:T(8,128)S(1)}) custom-call(s32[8]{0:T(128)S(1)} %bitcast.2, f32[2,128,256]{2,1,0:T(8,128)S(1)} %get-tuple-element.29.fields_ref), custom_call_target="tpu_custom_call" | custom-call | flops 1966080 | bytes 393216 | tf_op jit(solution)/shard_map/place/pallas_call | solution.py:488
  21.2 2.2 %collective-permute-done.5.other_ref = f32[8,128]{1,0:T(8,128)S(1)} collective-permute-done((f32[8,128]{1,0:T(8,128)S(1)}, f32[8,128]{1,0:T(8,128)S(1)}, u32[]{:S(2)}, u32[]{:S(2)}) %collective-permute-start.5) | collective-permute-done | bytes 4128 | tf_op jit(solution)/shard_map/ppermute | solution.py:663
  23.5 10.6 %all_to_all.5.arrived_ref = s16[8,80,128]{2,1,0:T(8,128)(2,1)S(1)} all-to-all(s16[8,80,128]{2,1,0:T(8,128)(2,1)S(1)} %constant_dynamic-update-slice_fusion), channel_id=1, replica_groups=mesh['lat'=4,'lon'=8] {'lon'}, dimensions={0} | all-to-all | bytes 327680 | tf_op jit(solution)/shard_map/all_to_all | solution.py:696
  34.1 1.1 %combine.1 = (f32[128,256]{1,0:T(8,128)}, f32[128,256]{1,0:T(8,128)}, f32[8,32,256]{2,1,0:T(8,128)}) custom-call(s16[8,80,128]{2,1,0:T(8,128)(2,1)S(1)} %all_to_all.5.arrived_ref, f32[4,128,256]{2,1,0:T(8,128)S(1)} %get-tuple-element.40.w_ref, f32[5,128,256]{2,1,0:T(8,128)S(1)} %get-tuple-element.41.mw_ref, f32[4,32,128]{2,1,0:T(8,128)S(1)} %get-tuple-element.42.near_w_ref, ...), custom_call_target="tpu_custom_call" | custom-call | tf_op jit(solution)/shard_map/combine/pallas_call | solution.py:645
  (3 shorter events, 0.1 us)
Async XLA Ops:
  0.6 5.0 %copy-start = (f32[16]{0:T(128)S(1)}, f32[16]{0:T(128)}, u32[]{:S(2)}) copy-start(f32[16]{0:T(128)} %thick_hbm.3) | copy-start | bytes 196
  2.4 6.2 %collective-permute-start = (f32[4,8,256]{2,1,0:T(8,128)}, f32[4,8,256]{2,1,0:T(8,128)S(1)}, u32[]{:S(2)}, u32[]{:S(2)}) collective-permute-start(f32[4,8,256]{2,1,0:T(8,128)} %get-tuple-element.27), channel_id=1, source_target_pairs={{0,8},{8,0},{16,24},{24,16},{1,9},{9,1},{17,25},{25,17},{2,10},{10... | collective-permute-start | bytes 98312 | tf_op jit(solution)/shard_map/ppermute | solution.py:672
  3.0 5.7 %collective-permute-start.1 = (f32[4,8,256]{2,1,0:T(8,128)}, f32[4,8,256]{2,1,0:T(8,128)S(1)}, u32[]{:S(2)}, u32[]{:S(2)}) collective-permute-start(f32[4,8,256]{2,1,0:T(8,128)} %get-tuple-element.28), channel_id=1, source_target_pairs={{8,16},{16,8},{24,0},{0,24},{9,17},{17,9},{25,1},{1,25},{10,18},{1... | collective-permute-start | bytes 98312 | tf_op jit(solution)/shard_map/ppermute | solution.py:672
  8.8 9.1 %collective-permute-start.2 = (f32[48,128]{1,0:T(8,128)S(1)}, f32[48,128]{1,0:T(8,128)S(1)}, u32[]{:S(2)}, u32[]{:S(2)}) collective-permute-start(f32[48,128]{1,0:T(8,128)S(1)} %get-tuple-element.33), channel_id=1, source_target_pairs={{1,2},{2,1},{3,4},{4,3},{5,6},{6,5},{7,0},{0,7},{9,10},{10,9},{11,... | collective-permute-start | bytes 73736 | tf_op jit(solution)/shard_map/ppermute | solution.py:672
  13.4 3.8 %collective-permute-start.3 = (f32[48,128]{1,0:T(8,128)S(1)}, f32[48,128]{1,0:T(8,128)S(1)}, u32[]{:S(2)}, u32[]{:S(2)}) collective-permute-start(f32[48,128]{1,0:T(8,128)S(1)} %get-tuple-element.35), channel_id=1, source_target_pairs={{0,1},{1,0},{2,3},{3,2},{4,5},{5,4},{6,7},{7,6},{8,9},{9,8},{10,11... | collective-permute-start | bytes 73736 | tf_op jit(solution)/shard_map/ppermute | solution.py:672
  13.4 1.0 %copy-start.2 = (f32[4,128,256]{2,1,0:T(8,128)S(1)}, f32[4,128,256]{2,1,0:T(8,128)}, u32[]{:S(2)}) copy-start(f32[4,128,256]{2,1,0:T(8,128)} %get-tuple-element.26.fields_ref) | copy-start | bytes 1572868
  14.4 5.9 %copy-start.1 = (s32[8,1]{0,1:T(1,128)S(1)}, s32[8,1]{0,1:T(1,128)}, u32[]{:S(2)}) copy-start(s32[8,1]{0,1:T(1,128)} %param.9) | copy-start | bytes 100
  18.6 1.2 %collective-permute-start.4 = (f32[8,128]{1,0:T(8,128)S(1)}, f32[8,128]{1,0:T(8,128)S(1)}, u32[]{:S(2)}, u32[]{:S(2)}) collective-permute-start(f32[8,128]{1,0:T(8,128)S(1)} %get-tuple-element.38), channel_id=1, source_target_pairs={{0,8},{8,0},{16,24},{24,16},{1,9},{9,1},{17,25},{25,17},{2,10},{10... | collective-permute-start | bytes 12296 | tf_op jit(solution)/shard_map/ppermute | solution.py:663
  19.8 3.6 %collective-permute-start.5 = (f32[8,128]{1,0:T(8,128)S(1)}, f32[8,128]{1,0:T(8,128)S(1)}, u32[]{:S(2)}, u32[]{:S(2)}) collective-permute-start(f32[8,128]{1,0:T(8,128)S(1)} %add.3.sums_ref), channel_id=1, source_target_pairs={{0,16},{8,24},{16,0},{24,8},{1,17},{9,25},{17,1},{25,9},{2,18},{10... | collective-permute-start | bytes 12296 | tf_op jit(solution)/shard_map/ppermute | solution.py:663
